TPU v7x, 128 devices: a whole 4x4x4 slice. The times are simulated.
128 devices in a mesh: dp: 16 (over z, x_hi, core), tensor: 8 (over y, x_lo).
Axes of the slice: x: 4 (x_hi: 2, x_lo: 2; x = x_hi * 2 + x_lo), y: 4, z: 4, core: 2. Of those that a mesh axis runs over, the one named last changes fastest.
Arguments:
- query_states: bfloat16 [16, 512, 8192], P('dp', None, 'tensor'), may hold values from -110 to 110
- key_states: bfloat16 [16, 512, 1024], P('dp', None, 'tensor'), may hold values from -4 to 4
- value_states: bfloat16 [16, 512, 1024], P('dp', None, 'tensor'), may hold values from -6 to 6
- segment_ids: int32 [16, 512], P('dp', 'tensor'), may hold values from 0 to 7, never falling along the last dimension, each value on 1 to 256 neighbouring positions
- pair_margins: float32 [16, 4], P('dp'), may hold values from -6 to 6
- upstream: bfloat16 [16, 512, 8192], P('dp', 'tensor'), may hold values from -6 to 6
- out_weight: bfloat16 [8192, 8192], P('tensor', 'dp'), may hold values from -0.0625 to 0.0625
Outputs:
- query_grad: bfloat16 [16, 512, 8192], P('dp', None, 'tensor')
- key_grad: bfloat16 [16, 512, 1024], P('dp', None, 'tensor')
- value_grad: bfloat16 [16, 512, 1024], P('dp', None, 'tensor')
- out_weight_grad: float32 [8192, 8192], P('tensor', 'dp')
Inputs may be any that keep to these rules, and one draw needn't show every extreme that they name: `segment_ids`: every row holds all 8 responses, each of 1 to 256 positions in order.
All inputs are finite; a program needn't handle non-finite values.
Results may differ from a plain program's by a relative error of at most 0.015.
Values may be sent and summed in bfloat16 or wider, within the bound.
No kernel may reach another device: no remote copies, remote signals or barrier semaphores. Data moves between devices by JAX's collectives and lax.ppermute only.
A program may use at most 128 MiB of HBM per device.

v0:
```python
import jax
import jax.numpy as jnp
from jax import lax
from jax.sharding import PartitionSpec as P

HEADS = 64
KV_HEADS = 8
HD = 128


def shards(query_states, key_states, value_states, segment_ids, pair_margins, upstream, out_weight):
    row_count, seq_local, model_width = upstream.shape
    length = query_states.shape[1]
    head_width = query_states.shape[2]
    kv_local = key_states.shape[2] // HD
    group_size = HEADS // KV_HEADS
    score_scale = HD ** (-0.5)
    whole_segs = lax.all_gather(segment_ids, "tensor", axis=1, tiled=True)
    sigma = jax.nn.sigmoid(-pair_margins)
    onehot = (
        segment_ids[:, :, None] // 2 == jnp.arange(sigma.shape[1], dtype=jnp.int32)[None, None, :]
    ).astype(jnp.float32)
    coeff = jnp.sum(onehot * sigma[:, None, :], axis=2)
    signs = jnp.where(segment_ids % 2 == 0, -1.0, 1.0).astype(jnp.float32)
    output_grad = (upstream.astype(jnp.float32) * (signs * coeff)[:, :, None]).astype(jnp.bfloat16)
    weight_full = lax.all_gather(out_weight, "dp", axis=1, tiled=True)
    query_heads = query_states.reshape(row_count, length, kv_local, group_size, HD)
    key_heads = key_states.reshape(row_count, length, kv_local, HD)
    value_heads = value_states.reshape(row_count, length, kv_local, HD)
    position = jnp.arange(length, dtype=jnp.int32)
    allowed = (whole_segs[:, :, None] == whole_segs[:, None, :]) & (
        position[None, None, :] <= position[None, :, None]
    )
    scores = (
        jnp.einsum("rigmd,rjgd->rgmij", query_heads, key_heads, preferred_element_type=jnp.float32)
        * score_scale
    )
    scores = jnp.where(allowed[:, None, None], scores, -1e30)
    highest = jnp.max(scores, axis=-1, keepdims=True)
    expo = jnp.exp(scores - highest)
    probs = expo / jnp.sum(expo, axis=-1, keepdims=True)
    probs_low = probs.astype(jnp.bfloat16)
    attn_out = jnp.einsum(
        "rgmij,rjgd->rigmd", probs_low, value_heads, preferred_element_type=jnp.float32
    )
    attn_out = attn_out.astype(jnp.bfloat16).reshape(row_count, length, head_width)
    block_grad = lax.all_gather(output_grad, "tensor", axis=1, tiled=True)
    partial_value = jnp.einsum(
        "rte,he->rth", block_grad, weight_full, preferred_element_type=jnp.float32
    )
    wgrad_acc = jnp.einsum("rth,rte->he", attn_out, block_grad, preferred_element_type=jnp.float32)
    weight_grad = lax.psum_scatter(
        wgrad_acc.astype(jnp.bfloat16), "dp", scatter_dimension=1, tiled=True
    ).astype(jnp.float32)
    attn_grad = partial_value.astype(jnp.bfloat16)
    grad_heads = attn_grad.reshape(row_count, length, kv_local, group_size, HD)
    prob_grad = jnp.einsum(
        "rigmd,rjgd->rgmij", grad_heads, value_heads, preferred_element_type=jnp.float32
    )
    delta = jnp.sum(probs * prob_grad, axis=-1, keepdims=True)
    score_grad = (score_scale * probs * (prob_grad - delta)).astype(jnp.bfloat16)
    query_grad = jnp.einsum(
        "rgmij,rjgd->rigmd", score_grad, key_heads, preferred_element_type=jnp.float32
    )
    query_grad = query_grad.astype(jnp.bfloat16).reshape(row_count, length, head_width)
    key_grad = jnp.einsum(
        "rgmij,rigmd->rjgd", score_grad, query_heads, preferred_element_type=jnp.float32
    )
    key_grad = key_grad.astype(jnp.bfloat16).reshape(row_count, length, kv_local * HD)
    value_grad = jnp.einsum(
        "rgmij,rigmd->rjgd", probs_low, grad_heads, preferred_element_type=jnp.float32
    )
    value_grad = value_grad.astype(jnp.bfloat16).reshape(row_count, length, kv_local * HD)
    return (query_grad, key_grad, value_grad, weight_grad)


def solution(mesh):
    in_specs = (
        P("dp", None, "tensor"),
        P("dp", None, "tensor"),
        P("dp", None, "tensor"),
        P("dp", "tensor"),
        P("dp", None),
        P("dp", "tensor", None),
        P("tensor", "dp"),
    )
    out_specs = (
        P("dp", None, "tensor"),
        P("dp", None, "tensor"),
        P("dp", None, "tensor"),
        P("tensor", "dp"),
    )
    return jax.shard_map(shards, mesh=mesh, in_specs=in_specs, out_specs=out_specs, check_vma=False)
```

profile of v0, /device:TPU:1, one launch (start us, length us, event | category | flops | bytes accessed | tf_op | source)
XLA Modules:
  0.0 500.5 jit_solution(11753365866720476348)
XLA Ops:
  7.2 0.0 copy-start
  7.2 0.0 all-gather.3.cloned.1.call-start
  7.2 0.7 divide_bitcast_fusion
  7.9 1.2 dynamic-slice
  9.8 0.8 bitcast_dynamic-update-slice_fusion
  10.6 0.1 select_reduce_fusion
  10.6 0.7 fusion.30
  11.3 2.4 multiply_convert_fusion
  13.7 0.0 all-gather.3.cloned.1.call-update
  13.8 0.0 all-gather.5.cloned.1.call-start
  13.8 0.7 all-gather.5.cloned.1.call-update
  14.5 0.0 reduce-scatter.2.cloned.1.call-start
  14.6 1.5 copy.43
  16.1 9.9 %all-reduce = s32[512]{0:T(512)S(1)} all-reduce(s32[512]{0:T(512)S(1)} %get-tuple-element.14), channel_id=1, replica_groups=mesh['dp'=16,'tensor'=8] {'tensor'}, use_global_device_ids=true, to_apply=%add | all-reduce | flops 512 | bytes 4096 | tf_op jit(solution)/shard_map/eq | solution.py:31
  26.0 0.2 fusion.20
  26.2 0.0 copy-done
  26.2 2.0 fusion.8
  28.2 0.0 copy-start.1
  28.2 3.2 copy-done.1
  31.4 1.8 fusion.7
  33.2 0.0 copy-start.7
  33.2 0.0 copy-start.6
  33.2 152.3 %all-gather.3.cloned.1.call-done = bf16[1,512,8192]{2,1,0:T(8,128)(2,1)} async-done(((bf16[1,64,8192]{2,1,0:T(8,128)(2,1)}), bf16[1,512,8192]{2,1,0:T(8,128)(2,1)}) %all-gather.3.cloned.1.call-update) | async-done | bytes 8388624 | tf_op jit(solution)/shard_map/all_gather | solution.py:47
  185.4 122.9 %all-gather.5.cloned.1.call-done = bf16[1024,8192]{1,0:T(8,128)(2,1)} async-done(((bf16[1024,512]{1,0:T(8,128)(2,1)}), bf16[1024,8192]{1,0:T(8,128)(2,1)}) %all-gather.5.cloned.1.call-update) | async-done | bytes 16777232 | tf_op jit(solution)/shard_map/all_gather | solution.py:26
  308.4 14.8 %fusion.10 = bf16[512,1024]{1,0:T(8,128)(2,1)S(1)} fusion(bf16[1024,8192]{1,0:T(8,128)(2,1)} %all-gather.5.cloned.1.call-done, bf16[1,512,8192]{2,1,0:T(8,128)(2,1)} %all-gather.3.cloned.1.call-done), kind=kOutput, calls=%fused_computation.17 | convolution fusion | flops 8590458880 | bytes 26214400 | tf_op jit(solution)/shard_map/rte,he->rth/dot_general | solution.py:48
  323.2 0.0 copy-done.6
  323.2 0.0 copy-start.2
  323.2 1.3 fusion.17
  324.5 0.0 copy-done.7
  324.5 2.1 copy-done.2
  326.6 0.0 copy-start.3
  326.6 3.4 convert_bitcast_fusion
  330.0 0.0 copy-done.3
  330.0 0.0 copy-start.4
  330.0 1.9 copy-done.4
  331.9 0.8 convolution_convert_fusion.1
  332.7 15.3 %convolution_convert_fusion = bf16[1024,8192]{1,0:T(8,128)(2,1)} fusion(bf16[512,1024]{0,1:T(8,128)(2,1)S(1)} %bitcast.143, bf16[1,512,8192]{2,1,0:T(8,128)(2,1)} %all-gather.3.cloned.1.call-done), kind=kOutput, calls=%fused_computation | convolution fusion | flops 8598323200 | bytes 26214400 | tf_op jit(solution)/shard_map/rth,rte->he/dot_general | solution.py:51
  348.0 0.0 reduce-scatter.2.cloned.1.call-update
  348.0 8.2 %copy.36 = bf16[8,512,512]{2,0,1:T(8,128)(2,1)} copy(bf16[8,512,512]{1,2,0:T(8,128)(2,1)} %copy-done.4) | data formatting | bytes 8388608 | tf_op jit(solution)/shard_map/reshape.39
  356.2 0.3 copy.44
  356.4 10.4 %fusion.9 = bf16[8,512,512]{1,2,0:T(8,128)(2,1)S(1)} fusion(f32[512,8,512]{0,2,1:T(8,128)} %copy-done.3, f32[8,512]{1,0:T(8,128)} %get-tuple-element.13, f32[8,512]{1,0:T(8,128)} %copy-done.7, f32[8,512]{1,0:T(8,128)S(1)} %get-tuple-element.16, f32[512,512,8]{1,0,2:T(8,128)} %copy-done.1, pred[512,512]{0,1:T(8,128)(4,1)S(1)} %fusion.20), kind=kLoop, calls=%fused_computation.14 | loop fusion | flops 16777216 | bytes 21282816 | tf_op jit(solution)/shard_map/reshape.33
  366.8 0.0 copy-start.5
  366.8 2.2 copy-done.5
  369.0 0.8 convolution_convert_fusion.2
  369.8 1.3 copy.31
  371.2 3.8 fusion.15
  374.9 0.8 copy.32
  375.7 4.1 fusion.16
  379.8 111.3 %reduce-scatter.2.cloned.1.call-done = bf16[1024,512]{1,0:T(8,128)(2,1)} async-done(((bf16[1024,8192]{1,0:T(8,128)(2,1)}), bf16[1024,512]{1,0:T(8,128)(2,1)}) %reduce-scatter.2.cloned.1.call-update) | async-done | bytes 1048592 | tf_op jit(solution)/shard_map/reduce_scatter | solution.py:52
  491.2 2.8 convert_element_type.89
  (1 shorter events, 0.0 us)
Async XLA Ops:
  7.2 19.0 %copy-start = (bf16[1,512,128]{2,1,0:T(8,128)(2,1)S(1)}, bf16[1,512,128]{2,1,0:T(8,128)(2,1)}, u32[]{:S(2)}) copy-start(bf16[1,512,128]{2,1,0:T(8,128)(2,1)} %param.8) | copy-start | bytes 393220
  7.2 178.3 %all-gather.3.cloned.1.call-start = ((), (), s32[]{:S(2)}) async-start(), calls=%async_computation.1 | async-start | bytes 9437184 | tf_op jit(solution)/shard_map/all_gather | solution.py:47
  13.8 294.6 %all-gather.5.cloned.1.call-start = ((), (), s32[]{:S(2)}) async-start(), calls=%async_computation.2 | async-start | bytes 17825792 | tf_op jit(solution)/shard_map/all_gather | solution.py:26
  14.5 476.6 %reduce-scatter.2.cloned.1.call-start = ((), (), s32[]{:S(2)}) async-start(), calls=%async_computation.3 | async-start | bytes 17825792 | tf_op jit(solution)/shard_map/reduce_scatter | solution.py:52
  28.2 3.2 copy-start.1
  33.2 291.3 %copy-start.7 = (f32[8,512]{1,0:T(8,128)}, f32[8,512]{1,0:T(8,128)S(1)}, u32[]{:S(2)}) copy-start(f32[8,512]{1,0:T(8,128)S(1)} %fusion.7) | copy-start | bytes 49156
  33.2 290.1 %copy-start.6 = (bf16[1,512,128]{2,1,0:T(8,128)(2,1)S(1)}, bf16[1,512,128]{2,1,0:T(8,128)(2,1)}, u32[]{:S(2)}) copy-start(bf16[1,512,128]{2,1,0:T(8,128)(2,1)} %param.9) | copy-start | bytes 393220
  323.2 3.4 copy-start.2
  326.6 3.4 copy-start.3
  330.0 1.9 copy-start.4
  366.8 2.2 copy-start.5
Sparse Core Ops, SparseCore 0:
  13.9 171.5 all-gather.2
  187.8 120.5 all-gather.4
  348.1 143.0 reduce-scatter.1
where the time goes:
time: 501 us
  waiting for transfers between devices  387 us (77%)
  matrix products  42.8 us (9%)
  other arithmetic  23.1 us (5%)
  local copies, waits for them, and re-layouts  22.8 us (5%)
  between operations  14.6 us (3%)
  blocking collectives  9.92 us (2%)
    all_gather x1, waiting for transfers between devices, shards(): block_grad = lax.all_gather(output_grad, 'tensor', axis=1, tiled=True)  152 us
    all_gather x1, waiting for transfers between devices, shards(): weight_full = lax.all_gather(out_weight, 'dp', axis=1, tiled=True)  123 us
    reduce_scatter x1, waiting for transfers between devices, shards(): lax.psum_scatter(wgrad_acc.astype(jnp.bfloat16), 'dp', scatter_dimension=...  111 us
    dot_general x1, matrix products, shards(): jnp.einsum('rth,rte->he', attn_out, block_grad, preferred_element_type=jn...  15.3 us
    dot_general x1, matrix products, shards(): jnp.einsum('rte,he->rth', block_grad, weight_full, preferred_element_type...  14.8 us
    unnamed x22, local copies, waits for them, and re-layouts  14.6 us
    another operation x2, other arithmetic  13.7 us
  transfers between devices with their start and end apart: 3, of which 3 were waited for; matrix products, arithmetic and copies ran while one was open for 7% of the time, Pallas kernels for 0%

commit v1 on v0

v1 whole, which is shorter than its diff:
```python
import functools

import jax
import jax.numpy as jnp
from jax import lax
from jax.experimental import pallas as pl
from jax.experimental.pallas import tpu as pltpu
from jax.sharding import PartitionSpec as P

HD = 128
F32 = jnp.float32
BF16 = jnp.bfloat16
SCALE = HD ** (-0.5)
LIGHT = pl.CostEstimate(flops=0, bytes_accessed=0, transcendentals=0)
VMEM_MOST = 60 * 1024 * 1024


def by_dp(step):
    return [(i, step(i)) for i in range(16)]


def by_tensor(step):
    return [(i, step(i)) for i in range(8)]


SIBLING = by_dp(lambda i: i ^ 1)
ACROSS = by_dp(lambda i: i ^ 2)
PAIR = by_tensor(lambda i: i ^ 1)
Y_UP = by_tensor(lambda i: (i + 2) % 8)
Y_DOWN = by_tensor(lambda i: (i - 2) % 8)
Z_GROUPS = [[z * 4 + j for z in range(4)] for j in range(4)]


def sibling(x):
    return lax.ppermute(x, "dp", SIBLING)


def across(x):
    return lax.ppermute(x, "dp", ACROSS)


def pair(x):
    return lax.ppermute(x, "tensor", PAIR)


def y_up(x):
    return lax.ppermute(x, "tensor", Y_UP)


def y_down(x):
    return lax.ppermute(x, "tensor", Y_DOWN)


def nn(a, b):
    return lax.dot_general(a, b, (((1,), (0,)), ((), ())), preferred_element_type=F32)


def nt(a, b):
    return lax.dot_general(a, b, (((1,), (1,)), ((), ())), preferred_element_type=F32)


def params():
    return pltpu.CompilerParams(vmem_limit_bytes=VMEM_MOST, dimension_semantics=("arbitrary",))


SMEM = functools.partial(pl.BlockSpec, memory_space=pltpu.SMEM)


def whole(shape):
    return pl.BlockSpec(shape, lambda i: (0,) * len(shape))


def prep_kernel(place, margins, segs, up, own, to_sibling, to_across):
    h, c = place[2], place[3]
    seg = segs[...]
    margin = jnp.full(seg.shape, margins[0, 0], F32)
    for p in range(1, margins.shape[1]):
        margin = jnp.where((seg >> 1) == p, margins[0, p], margin)
    factor = jax.nn.sigmoid(-margin) * jnp.where((seg & 1) == 0, -1.0, 1.0)
    width = own.shape[1]
    factor = jnp.concatenate([factor] * (width // factor.shape[1]), axis=1)

    def grad(hh, cc):
        start = pl.multiple_of((hh * 2 + cc) * width, width)
        return (up[:, pl.ds(start, width)].astype(F32) * factor).astype(BF16)

    own[...] = grad(h, c)
    to_sibling[...] = grad(h, 1 - c)
    to_across[0] = grad(1 - h, c)
    to_across[1] = grad(1 - h, 1 - c)


def prep(place, margins, segs, up):
    seq, model = up.shape
    width = model // 16
    shape = jax.ShapeDtypeStruct((seq, 4 * width), BF16)
    col = pl.BlockSpec((seq, width), lambda i: (0, i))
    return pl.pallas_call(
        prep_kernel,
        grid=(4,),
        in_specs=[SMEM(), SMEM(), whole(segs.shape), pl.BlockSpec((seq, 4 * width), lambda i: (0, i))],
        out_specs=[col, col, pl.BlockSpec((2, seq, width), lambda i: (0, 0, i))],
        out_shape=[shape, shape, jax.ShapeDtypeStruct((2, seq, 4 * width), BF16)],
        compiler_params=params(),
        cost_estimate=LIGHT,
        name="prep",
    )(place, margins, segs, up)


def key_range(block):
    return max(0, block - 2) * HD, (block + 1) * HD


def two_heads(ref, block):
    rows = slice(block * HD, (block + 1) * HD)
    return jnp.concatenate([ref[rows, :HD], ref[rows, HD:]], axis=0)


def twice(x):
    return jnp.concatenate([x, x], axis=1)


def forward_kernel(place, segs, q, k, v, out, stats, bias, v_t):
    y, low = place[0], place[1]
    blocks = q.shape[0] // HD

    @pl.when(pl.program_id(0) == 0)
    def _():
        v_t[...] = v[...].astype(F32).T.astype(BF16)
        for b in range(blocks):
            first, last = key_range(b)
            of_query = segs[b * HD : (b + 1) * HD, :].astype(F32).T[:1]
            of_key = segs[first:last, :].astype(F32)
            shape = (last - first, HD)
            query_at = lax.broadcasted_iota(jnp.int32, shape, 1) + b * HD
            key_at = lax.broadcasted_iota(jnp.int32, shape, 0) + first
            seen = (of_key == of_query) & (key_at <= query_at)
            bias[b, : last - first] = jnp.where(seen, 0.0, -1e30)

    for b in range(blocks):
        first, last = key_range(b)
        q2 = two_heads(q, b)
        s = nt(k[first:last], q2) * SCALE + twice(bias[b, : last - first])
        highest = jnp.max(s, axis=0, keepdims=True)
        e = jnp.exp(s - highest)
        inverse = 1.0 / jnp.sum(e, axis=0, keepdims=True)
        stats[0, b : b + 1] = highest
        stats[0, blocks + b : blocks + b + 1] = inverse
        a = nn(v_t[:, first:last], (e * inverse).astype(BF16))
        at = pl.multiple_of(lax.rem(b - y + 4, 4) * HD, HD)
        for i in range(2):
            x = a[:, i * HD : (i + 1) * HD]
            x = jnp.where(low == 0, x, pltpu.roll(x, HD // 2, 1))
            out[i * HD : (i + 1) * HD, pl.ds(at, HD)] = x.astype(BF16)


def forward(place, segs, q, k, v):
    length, wide = q.shape
    pairs, blocks = wide // (2 * HD), length // HD
    bias_shape = (blocks, 3 * HD, HD)
    return pl.pallas_call(
        forward_kernel,
        grid=(pairs,),
        in_specs=[
            SMEM(),
            whole(segs.shape),
            pl.BlockSpec((length, 2 * HD), lambda i: (0, i)),
            whole(k.shape),
            whole(v.shape),
        ],
        out_specs=[
            pl.BlockSpec((2 * HD, length), lambda i: (i, 0)),
            pl.BlockSpec((1, 2 * blocks, 2 * HD), lambda i: (i, 0, 0)),
            whole(bias_shape),
        ],
        out_shape=[
            jax.ShapeDtypeStruct((wide, length), BF16),
            jax.ShapeDtypeStruct((pairs, 2 * blocks, 2 * HD), F32),
            jax.ShapeDtypeStruct(bias_shape, F32),
        ],
        scratch_shapes=[pltpu.VMEM((HD, length), BF16)],
        compiler_params=params(),
        cost_estimate=LIGHT,
        name="attend",
    )(place, segs, q, k, v)


def backward_kernel(place, q, k, v, stats, bias, *rest):
    terms, (dq, dk, dv, k_t, dk_sum, dv_sum) = rest[:6], rest[6:]
    y, low = place[0], place[1]
    blocks = q.shape[0] // HD
    half = HD // 2

    @pl.when(pl.program_id(0) == 0)
    def _():
        k_t[...] = k[...].astype(F32).T.astype(BF16)
        dk_sum[...] = jnp.zeros_like(dk_sum)
        dv_sum[...] = jnp.zeros_like(dv_sum)

    for b in range(blocks):
        first, last = key_range(b)
        rows = pl.ds(pl.multiple_of(lax.rem(b - y + 4, 4) * half, half), half)
        same = terms[0][rows] + terms[1][rows].astype(F32) + terms[2][rows].astype(F32)
        flip = terms[3][rows] + terms[4][rows].astype(F32) + terms[5][rows].astype(F32)
        grad = jnp.concatenate([jnp.where(low == 0, same, flip), jnp.where(low == 0, flip, same)], axis=0).astype(BF16)
        grad = jnp.concatenate([grad[:, :HD], grad[:, HD:]], axis=0)
        q2 = two_heads(q, b)
        s = nt(k[first:last], q2) * SCALE + twice(bias[b, : last - first])
        p = jnp.exp(s - stats[0, b : b + 1]) * stats[0, blocks + b : blocks + b + 1]
        dp = nt(v[first:last], grad)
        delta = jnp.sum(p * dp, axis=0, keepdims=True)
        ds = (SCALE * p * (dp - delta)).astype(BF16)
        dv_sum[first:last] += nn(p.astype(BF16), grad)
        dk_sum[first:last] += nn(ds, q2)
        x = nn(k_t[:, first:last], ds)
        for i in range(2):
            dq[b * HD : (b + 1) * HD, i * HD : (i + 1) * HD] = x[:, i * HD : (i + 1) * HD].T.astype(BF16)

    @pl.when(pl.program_id(0) == pl.num_programs(0) - 1)
    def _():
        dk[...] = dk_sum[...].astype(BF16)
        dv[...] = dv_sum[...].astype(BF16)


def backward(place, q, k, v, stats, bias, terms):
    length, wide = q.shape
    pairs, blocks = wide // (2 * HD), length // HD
    two = pl.BlockSpec((length, 2 * HD), lambda i: (0, i))
    return pl.pallas_call(
        backward_kernel,
        grid=(pairs,),
        in_specs=[
            SMEM(),
            two,
            whole(k.shape),
            whole(v.shape),
            pl.BlockSpec((1, 2 * blocks, 2 * HD), lambda i: (i, 0, 0)),
            whole(bias.shape),
        ]
        + [pl.BlockSpec((length // 2, 2 * HD), lambda i: (0, i))] * 6,
        out_specs=[two, whole(k.shape), whole(v.shape)],
        out_shape=[jax.ShapeDtypeStruct(x.shape, BF16) for x in (q, k, v)],
        scratch_shapes=[pltpu.VMEM((HD, length), BF16), pltpu.VMEM(k.shape, F32), pltpu.VMEM(v.shape, F32)],
        compiler_params=params(),
        cost_estimate=LIGHT,
        name="attend_grad",
    )(place, q, k, v, stats, bias, *terms)


def partial_kernel(*refs):
    blocks, (weight, keep, give, x) = refs[:4], refs[4:]
    seq = blocks[0].shape[1]
    half = 4 * seq
    width = weight.shape[2]

    @pl.when(pl.program_id(0) == 0)
    def _():
        for i in range(2):
            for j, block in enumerate(blocks):
                x[i * half + j * seq : i * half + (j + 1) * seq] = block[i]

    total = nt(x[:, :width], weight[0])
    for j in range(1, 4):
        total += nt(x[:, j * width : (j + 1) * width], weight[j])
    keep[...] = total[:half]
    give[...] = total[half:].astype(BF16)


def partial(blocks, weight):
    _, seq, cols = blocks[0].shape
    heads = weight.shape[1]
    tile = heads // 4
    out = pl.BlockSpec((4 * seq, tile), lambda i: (0, i))
    return pl.pallas_call(
        partial_kernel,
        grid=(4,),
        in_specs=[whole(blocks[0].shape)] * 4 + [pl.BlockSpec((4, tile, cols // 4), lambda i: (0, i, 0))],
        out_specs=[out, out],
        out_shape=[jax.ShapeDtypeStruct((4 * seq, heads), F32), jax.ShapeDtypeStruct((4 * seq, heads), BF16)],
        scratch_shapes=[pltpu.VMEM((8 * seq, cols), BF16)],
        compiler_params=params(),
        cost_estimate=LIGHT,
        name="partial_grad",
    )(*blocks, weight)


def wgrad_kernel(has_start, *refs):
    same, flip, outs = refs[:4], refs[4:8], refs[8:10]
    start = refs[10] if has_start else None
    out, x = refs[-2:]
    seq = same[0].shape[1]
    for i in range(2):
        for j in range(4):
            at = (i * 8 + j * 2) * seq
            x[at : at + seq] = same[j][i]
            x[at + seq : at + 2 * seq] = flip[j][i]
    half = 8 * seq
    tile = 256
    for m in range(0, out.shape[1], tile):
        total = nn(outs[0][m : m + tile], x[:half]) + nn(outs[1][m : m + tile], x[half:])
        if has_start:
            total += start[0, m : m + tile]
        out[0, m : m + tile] = total.astype(out.dtype)


def wgrad(same, flip, outs, start):
    _, seq, cols = same[0].shape
    heads = outs[0].shape[0]
    width = cols // 4
    col = pl.BlockSpec((2, seq, width), lambda i: (0, 0, i))
    result = pl.BlockSpec((1, heads, width), lambda i: (i, 0, 0))
    return pl.pallas_call(
        functools.partial(wgrad_kernel, start is not None),
        grid=(4,),
        in_specs=[col] * 8 + [whole(outs[0].shape)] * 2 + ([] if start is None else [result]),
        out_specs=result,
        out_shape=jax.ShapeDtypeStruct((4, heads, width), F32 if start is None else BF16),
        scratch_shapes=[pltpu.VMEM((16 * seq, width), BF16)],
        compiler_params=params(),
        cost_estimate=LIGHT,
        name="weight_grad",
    )(*same, *flip, *outs, *([] if start is None else [start]))


def named(name, fn, x):
    with jax.named_scope("t_" + name):
        return fn(x)


def after(x, *others):
    return lax.optimization_barrier((x, *others))[0]


def gather_ids(ids):
    low = lax.axis_index("tensor") % 2
    y = lax.axis_index("tensor") // 2
    partner = named("ids_pair", pair, ids)
    both = jnp.where(low == 0, jnp.stack([ids, partner]), jnp.stack([partner, ids]))
    behind = named("ids_up", y_up, both)
    ahead = named("ids_down", y_down, both)
    far = named("ids_far", lambda x: lax.ppermute(x, "tensor", by_tensor(lambda i: (i + 4) % 8)), both)
    ring = jnp.stack([both, ahead, far, behind] * 2).reshape(8, -1)
    return lax.dynamic_slice(ring, ((4 - y) % 4, 0), (4, ring.shape[1])).reshape(-1)


def shards(query_states, key_states, value_states, segment_ids, pair_margins, upstream, out_weight):
    d = lax.axis_index("dp")
    t = lax.axis_index("tensor")
    place = jnp.stack([t // 2, t % 2, (d // 2) % 2, d % 2]).astype(jnp.int32)
    query, key, value = query_states[0], key_states[0], value_states[0]

    segs = jnp.broadcast_to(segment_ids[0][:, None], (segment_ids.shape[1], HD))
    own, to_sibling, to_across = prep(place, pair_margins, segs, upstream[0])
    heads, width = out_weight.shape
    weight = lax.all_gather(out_weight, "dp", axis=0, tiled=True, axis_index_groups=Z_GROUPS).reshape(4, heads, width)

    from_sibling = named("near_sibling", sibling, to_sibling)
    near = jnp.stack([own, from_sibling])
    from_across = named("other_across", across, to_across)
    other = jnp.stack([from_across[0], named("other_sibling", sibling, from_across[1])])
    near_pair = named("near_pair", pair, near)
    other_pair = named("other_pair", pair, other)

    def to_row(name, blocks):
        keep, give = partial(blocks, weight)
        total = (keep + named(name + "_sibling", sibling, give).astype(F32)).astype(BF16)
        return named(name + "_across", across, total), total

    def for_row(name, blocks):
        keep, give = partial(blocks, weight)
        return keep, named(name + "_sibling", sibling, give)

    n, o, p, q = near, other, other_pair, near_pair
    n_up, n_down = named("n_up", y_up, n), named("n_down", y_down, n)

    ids = gather_ids(after(segment_ids[0], from_sibling))
    whole_segs = jnp.broadcast_to(ids[:, None], (ids.shape[0], HD))
    attn_out, stats, bias = forward(place, whole_segs, after(query, other, n_up, n_down), key, value)
    out_across = named("out_across", across, attn_out)

    n_far, o_down = named("n_far", y_up, after(n_up, n_down)), named("o_down", y_down, after(o, q, ids))
    o_up, o_far = named("o_up", y_up, after(o, n_up, n_down, p, attn_out)), named("o_far", y_down, after(o_down, attn_out))
    p = after(p, n_far, o_down)
    p_up, p_down = named("p_up", y_up, p), named("p_down", y_down, p)
    terms_same = for_row("sum_near", [n, n_down, n_far, after(n_up, o_up, o_far)])
    p_far, q_down = named("p_far", y_up, after(p_up, terms_same[0])), named("q_down", y_down, after(q, o_up, o_far, terms_same[0]))
    sent_same, sum_other = to_row("sum_other", [o, o_down, o_far, after(o_up, p_up, p_down)])
    q_up, q_far = named("q_up", y_up, after(q, p_up, p_down, sum_other)), named("q_far", y_down, after(q_down, sum_other))
    near_blocks = [n, n_down, n_far, n_up]
    other_blocks = [o, o_down, o_far, o_up]
    other_pair_blocks = [p, p_down, p_far, p_up]
    near_pair_blocks = [q, q_down, q_far, q_up]
    sent_flip, sum_other_pair = to_row("sum_other_pair", [p, p_down, after(p_far, q_down), p_up])
    out_near = named("out_near", sibling, after(attn_out, o_up, o_far))
    out_other = named("out_other", sibling, after(out_across, o_up, o_far))
    first = wgrad(other_blocks, other_pair_blocks, (out_across, after(out_other, sum_other_pair)), None)
    total = wgrad(near_blocks, near_pair_blocks, (attn_out, out_near), after(first, sent_same))
    terms_flip = for_row("sum_near_pair", near_pair_blocks)
    terms = [*terms_same, sent_same, *terms_flip, sent_flip]
    weight_grad = lax.psum_scatter(
        total.reshape(4 * heads, width), "dp", scatter_dimension=0, tiled=True, axis_index_groups=Z_GROUPS
    )
    dq, dk, dv = backward(place, query, key, value, stats, bias, terms)
    return (dq[None], dk[None], dv[None], weight_grad.astype(F32))


def solution(mesh):
    in_specs = (
        P("dp", None, "tensor"),
        P("dp", None, "tensor"),
        P("dp", None, "tensor"),
        P("dp", "tensor"),
        P("dp", None),
        P("dp", "tensor", None),
        P("tensor", "dp"),
    )
    out_specs = (
        P("dp", None, "tensor"),
        P("dp", None, "tensor"),
        P("dp", None, "tensor"),
        P("tensor", "dp"),
    )
    return jax.shard_map(shards, mesh=mesh, in_specs=in_specs, out_specs=out_specs, check_vma=False)
```

time: 501 us -> 207 us (0.41)
  waiting for transfers between devices: 387 us -> 64.8 us
  Pallas kernels: 0 us -> 66.5 us
  starting transfers between devices: 0.12 us -> 43 us
  matrix products: 42.8 us -> 0 us
  other arithmetic: 23.1 us -> 8.73 us
  local copies, waits for them, and re-layouts: 22.8 us -> 9.01 us
  blocking collectives: 9.92 us -> 0 us
    all_gather x2 -> x1, waiting for transfers between devices: 275 us -> 0.01 us  [shards(): lax.all_gather(out_weight, 'dp', axis=0, tiled=True, axis_index_groups=Z_...]
    reduce_scatter x1, waiting for transfers between devices: 111 us -> 19.8 us  [shards(): lax.psum_scatter(total.reshape(4 * heads, width), 'dp', scatter_dimension...]
    pallas_call x0 -> x9, Pallas kernels: none -> 66.5 us  [the longest x4 25.3 us: partial(): pl.pallas_call(partial_kernel, grid=(4,), in_specs=[whole(blocks[0].shape...]
    ppermute x0 -> x30, waiting for transfers between devices: none -> 44.3 us  [the longest x3 17.6 us: pair(): return lax.ppermute(x, 'tensor', PAIR)]
    ppermute x0 -> x30, starting transfers between devices: none -> 42.9 us  [the longest x8 17.1 us: sibling(): return lax.ppermute(x, 'dp', SIBLING)]
    dot_general x8 -> x0, matrix products: 42.8 us -> none  [the longest x1 15.3 us: shards(): jnp.einsum('rth,rte->he', attn_out, block_grad, preferred_element_type=jn...]
    another operation x2 -> x3, other arithmetic: 13.7 us -> 1.64 us  [the longest x1 1 us: shards(): near = jnp.stack([own, from_sibling])]
    eq x1 -> x0, blocking collectives: 9.92 us -> none  [shards(): whole_segs[:, :, None] == whole_segs[:, None, :]]
  transfers between devices with their start and end apart: 3 -> 32, of which waited for: 3 -> 11; matrix products, arithmetic and copies ran while one was open for 7% -> 4% of each run, Pallas kernels for 0% -> 27%
where the time goes in v1:
time: 207 us; the launch traced here: 206 us
  Pallas kernels  66.5 us (32%)
  waiting for transfers between devices  64.8 us (31%)
  starting transfers between devices  43 us (21%)
  between operations  14.4 us (7%)
  local copies, waits for them, and re-layouts  9.01 us (4%)
  other arithmetic  8.73 us (4%)
    pallas_call x4, Pallas kernels, partial(): pl.pallas_call(partial_kernel, grid=(4,), in_specs=[whole(blocks[0].shape...  25.3 us
    reduce_scatter x1, waiting for transfers between devices, shards(): lax.psum_scatter(total.reshape(4 * heads, width), 'dp', scatter_dimension...  19.8 us
    pallas_call x2, Pallas kernels, wgrad(): pl.pallas_call(functools.partial(wgrad_kernel, start is not None), grid=(...  19.6 us
    ppermute x3, waiting for transfers between devices, pair(): return lax.ppermute(x, 'tensor', PAIR)  17.6 us
    ppermute x8, starting transfers between devices, sibling(): return lax.ppermute(x, 'dp', SIBLING)  17.1 us
    ppermute x4, waiting for transfers between devices, across(): return lax.ppermute(x, 'dp', ACROSS)  11.7 us
    ppermute x7, starting transfers between devices, y_down(): return lax.ppermute(x, 'tensor', Y_DOWN)  11.4 us
    ppermute x7, waiting for transfers between devices, y_up(): return lax.ppermute(x, 'tensor', Y_UP)  9.97 us
  transfers between devices with their start and end apart: 32, of which 11 were waited for; matrix products, arithmetic and copies ran while one was open for 4% of the time, Pallas kernels for 27%

profile of v1, /device:TPU:1, one launch (start us, length us, event | category | flops | bytes accessed | tf_op | source)
XLA Modules:
  0.0 206.3 jit_solution(12282858701860615340)
XLA Ops:
  7.2 0.7 all-gather.2.cloned.1.call-update
  8.0 0.6 pad_add_fusion.place
  8.6 1.3 broadcast_in_dim.21.segs
  9.9 3.4 %prep.1 = (bf16[64,2048]{1,0:T(8,128)(2,1)}, bf16[64,2048]{1,0:T(8,128)(2,1)}, bf16[2,64,2048]{2,1,0:T(8,128)(2,1)}) custom-call(s32[4]{0:T(128)} %pad_add_fusion.place, f32[1,4]{1,0:T(1,128)} %margins.1, s32[64,128]{1,0:T(8,128)} %broadcast_in_dim.21.segs, bf16[64,8192]{1,0:T(8,128)(2,1)} %bitcast.32), custom_call_target="tpu_custom_call" | custom-call | tf_op jit(solution)/shard_map/prep/pallas_call | solution.py:98
  13.3 3.6 %collective-permute-start.5 = (bf16[2,64,2048]{2,1,0:T(8,128)(2,1)}, bf16[2,64,2048]{2,1,0:T(8,128)(2,1)S(1)}, u32[]{:S(2)}, u32[]{:S(2)}) collective-permute-start(bf16[2,64,2048]{2,1,0:T(8,128)(2,1)} %get-tuple-element.41), channel_id=1, source_target_pairs={{0,16},{8,24},{16,0},{24,8},{32,48},{40,56},{48,32},{56,40},{64,80... | collective-permute-start | bytes 1572872 | tf_op jit(solution)/shard_map/t_other_across/ppermute | solution.py:39
  16.9 1.0 collective-permute-start
  17.9 1.4 collective-permute-done
  19.2 1.0 pad_maximum_fusion.1.refs_0_
  20.3 0.4 collective-permute-start.12
  20.6 2.7 %collective-permute-start.8 = (bf16[2,64,2048]{2,1,0:T(8,128)(2,1)S(1)}, bf16[2,64,2048]{2,1,0:T(8,128)(2,1)S(1)}, u32[]{:S(2)}, u32[]{:S(2)}) collective-permute-start(bf16[2,64,2048]{2,1,0:T(8,128)(2,1)S(1)} %pad_maximum_fusion.1.refs_0_), channel_id=1, source_target_pairs={{0,6},{1,7},{2,0},{3,1},{4,2},{5,3},{6,4},{7,5},{8,14},{9,15},{10,... | collective-permute-start | bytes 1572872 | tf_op jit(solution)/shard_map/t_n_down/ppermute | solution.py:51
  23.4 4.9 %collective-permute-done.5 = bf16[2,64,2048]{2,1,0:T(8,128)(2,1)S(1)} collective-permute-done((bf16[2,64,2048]{2,1,0:T(8,128)(2,1)}, bf16[2,64,2048]{2,1,0:T(8,128)(2,1)S(1)}, u32[]{:S(2)}, u32[]{:S(2)}) %collective-permute-start.5) | collective-permute-done | bytes 524320 | tf_op jit(solution)/shard_map/t_other_across/ppermute | solution.py:39
  28.3 3.1 %collective-permute-start.6 = (bf16[64,2048]{1,0:T(8,128)(2,1)S(1)}, bf16[64,2048]{1,0:T(8,128)(2,1)S(1)}, u32[]{:S(2)}, u32[]{:S(2)}) collective-permute-start(bf16[64,2048]{1,0:T(8,128)(2,1)S(1)} %get-tuple-element.75), channel_id=1, source_target_pairs={{0,8},{8,0},{16,24},{24,16},{32,40},{40,32},{48,56},{56,48},{64,72... | collective-permute-start | bytes 786440 | tf_op jit(solution)/shard_map/t_other_sibling/ppermute | solution.py:35
  31.4 1.2 collective-permute-done.6
  32.7 7.4 %collective-permute-done.12.refs_0_.refs_4_ = bf16[2,64,2048]{2,1,0:T(8,128)(2,1)S(1)} collective-permute-done((bf16[2,64,2048]{2,1,0:T(8,128)(2,1)S(1)}, bf16[2,64,2048]{2,1,0:T(8,128)(2,1)S(1)}, u32[]{:S(2)}, u32[]{:S(2)}) %collective-permute-start.12) | collective-permute-done | bytes 524320 | tf_op jit(solution)/shard_map/t_near_pair/ppermute | solution.py:43
  40.1 2.7 %collective-permute-start.13 = (bf16[2,64,2048]{2,1,0:T(8,128)(2,1)S(1)}, bf16[2,64,2048]{2,1,0:T(8,128)(2,1)}, u32[]{:S(2)}, u32[]{:S(2)}) collective-permute-start(bf16[2,64,2048]{2,1,0:T(8,128)(2,1)S(1)} %pad_maximum_fusion.refs_0_), channel_id=1, source_target_pairs={{0,6},{1,7},{2,0},{3,1},{4,2},{5,3},{6,4},{7,5},{8,14},{9,15},{10,... | collective-permute-start | bytes 1572872 | tf_op jit(solution)/shard_map/t_o_down/ppermute | solution.py:51
  42.8 1.2 collective-permute-start.10
  44.1 0.4 collective-permute-start.1
  44.5 10.1 %collective-permute-done.1 = s32[64]{0:T(128)S(1)} collective-permute-done((s32[64]{0:T(128)S(1)}, s32[64]{0:T(128)S(1)}, u32[]{:S(2)}, u32[]{:S(2)}) %collective-permute-start.1) | collective-permute-done | bytes 288 | tf_op jit(solution)/shard_map/t_ids_pair/ppermute | solution.py:43
  54.8 1.6 collective-permute-start.3
  56.4 2.5 %collective-permute-done.4 = s32[2,64]{1,0:T(2,128)S(1)} collective-permute-done((s32[2,64]{1,0:T(2,128)S(1)}, s32[2,64]{1,0:T(2,128)S(1)}, u32[]{:S(2)}, u32[]{:S(2)}) %collective-permute-start.4) | collective-permute-done | bytes 544 | tf_op jit(solution)/shard_map/t_ids_up/ppermute | solution.py:47
  58.8 0.1 select_n.63
  58.9 0.1 stack.84
  59.0 0.1 stack.83
  59.1 2.5 %collective-permute-done.2 = s32[2,64]{1,0:T(2,128)S(1)} collective-permute-done((s32[2,64]{1,0:T(2,128)S(1)}, s32[2,64]{1,0:T(2,128)S(1)}, u32[]{:S(2)}, u32[]{:S(2)}) %collective-permute-start.2) | collective-permute-done | bytes 544 | tf_op jit(solution)/shard_map/t_ids_down/ppermute | solution.py:51
  61.5 0.1 stack.82
  61.7 0.8 broadcast_in_dim.23.segs
  62.5 8.8 %attend.1 = (bf16[1024,512]{1,0:T(8,128)(2,1)}, f32[4,8,256]{2,1,0:T(8,128)}, f32[4,384,128]{2,1,0:T(8,128)}) custom-call(s32[4]{0:T(128)} %pad_add_fusion.place, s32[512,128]{1,0:T(8,128)} %broadcast_in_dim.23.segs, bf16[512,1024]{1,0:T(8,128)(2,1)} %bitcast.30, bf16[512,128]{1,0:T(8,128)(2,1)} %bitcast.33, bf16[512,128]{1,0:T(8,128)(2,1)} %bitcast.35), custom_call_target="tpu_custom_call" | custom-call | tf_op jit(solution)/shard_map/attend/pallas_call | solution.py:161
  71.4 2.7 %collective-permute-start.14 = (bf16[2,64,2048]{2,1,0:T(8,128)(2,1)}, bf16[2,64,2048]{2,1,0:T(8,128)(2,1)}, u32[]{:S(2)}, u32[]{:S(2)}) collective-permute-start(bf16[2,64,2048]{2,1,0:T(8,128)(2,1)} %collective-permute-done.13.refs_1_), channel_id=1, source_target_pairs={{0,6},{1,7},{2,0},{3,1},{4,2},{5,3},{6,4},{7,5},{8,14},{9,15},{10,... | collective-permute-start | bytes 1572872 | tf_op jit(solution)/shard_map/t_o_far/ppermute | solution.py:51
  74.0 1.8 collective-permute-start.28
  75.9 2.6 %collective-permute-start.17 = (bf16[2,64,2048]{2,1,0:T(8,128)(2,1)}, bf16[2,64,2048]{2,1,0:T(8,128)(2,1)}, u32[]{:S(2)}, u32[]{:S(2)}) collective-permute-start(bf16[2,64,2048]{2,1,0:T(8,128)(2,1)} %collective-permute-done.10.refs_0_.refs_4_), channel_id=1, source_target_pairs={{0,6},{1,7},{2,0},{3,1},{4,2},{5,3},{6,4},{7,5},{8,14},{9,15},{10,... | collective-permute-start | bytes 1572872 | tf_op jit(solution)/shard_map/t_p_down/ppermute | solution.py:51
  78.5 3.3 %collective-permute-done.11.refs_3_ = bf16[2,64,2048]{2,1,0:T(8,128)(2,1)S(1)} collective-permute-done((bf16[2,64,2048]{2,1,0:T(8,128)(2,1)S(1)}, bf16[2,64,2048]{2,1,0:T(8,128)(2,1)S(1)}, u32[]{:S(2)}, u32[]{:S(2)}) %collective-permute-start.11) | collective-permute-done | bytes 524320 | tf_op jit(solution)/shard_map/t_o_up/ppermute | solution.py:47
  81.8 0.8 copy-done.7
  82.6 6.3 %partial_grad.4 = (f32[256,1024]{1,0:T(8,128)}, bf16[256,1024]{1,0:T(8,128)(2,1)}) custom-call(bf16[2,64,2048]{2,1,0:T(8,128)(2,1)} %copy-done, bf16[2,64,2048]{2,1,0:T(8,128)(2,1)} %copy-done.3, bf16[2,64,2048]{2,1,0:T(8,128)(2,1)} %copy-done.5, bf16[2,64,2048]{2,1,0:T(8,128)(2,1)} %copy-done.4, bf16[4,1024,512]{2,1,0:T(8,128)(2,1)} %bitcast.25), custom_call_target="tpu_custom_call" | custom-call | tf_op jit(solution)/shard_map/partial_grad/pallas_call | solution.py:274
  88.9 4.2 %collective-permute-done.16.refs_3_.refs_7_ = bf16[2,64,2048]{2,1,0:T(8,128)(2,1)} collective-permute-done((bf16[2,64,2048]{2,1,0:T(8,128)(2,1)}, bf16[2,64,2048]{2,1,0:T(8,128)(2,1)}, u32[]{:S(2)}, u32[]{:S(2)}) %collective-permute-start.16) | collective-permute-done | bytes 524320 | tf_op jit(solution)/shard_map/t_p_up/ppermute | solution.py:47
  93.1 0.5 collective-permute-start.20
  93.6 1.0 collective-permute-start.24
  94.6 6.3 %partial_grad.5 = (f32[256,1024]{1,0:T(8,128)}, bf16[256,1024]{1,0:T(8,128)(2,1)}) custom-call(bf16[2,64,2048]{2,1,0:T(8,128)(2,1)} %copy-done.1, bf16[2,64,2048]{2,1,0:T(8,128)(2,1)} %collective-permute-done.13.refs_1_, bf16[2,64,2048]{2,1,0:T(8,128)(2,1)} %collective-permute-done.14.refs_2_, bf16[2,64,2048]{2,1,0:T(8,128)(2,1)} %copy-done.7, ...), custom_call_target="tpu_custom_call" | custom-call | tf_op jit(solution)/shard_map/partial_grad/pallas_call | solution.py:274
  100.9 7.0 %collective-permute-start.18 = (bf16[256,1024]{1,0:T(8,128)(2,1)}, bf16[256,1024]{1,0:T(8,128)(2,1)}, u32[]{:S(2)}, u32[]{:S(2)}) collective-permute-start(bf16[256,1024]{1,0:T(8,128)(2,1)} %get-tuple-element.57), channel_id=1, source_target_pairs={{0,8},{8,0},{16,24},{24,16},{32,40},{40,32},{48,56},{56,48},{64,72... | collective-permute-start | bytes 1572872 | tf_op jit(solution)/shard_map/t_sum_other_sibling/ppermute | solution.py:35
  107.9 0.1 collective-permute-start.29
  108.0 0.8 copy-done.8
  108.9 6.3 %partial_grad.7 = (f32[256,1024]{1,0:T(8,128)}, bf16[256,1024]{1,0:T(8,128)(2,1)}) custom-call(bf16[2,64,2048]{2,1,0:T(8,128)(2,1)} %collective-permute-done.10.refs_0_.refs_4_, bf16[2,64,2048]{2,1,0:T(8,128)(2,1)} %collective-permute-done.17.refs_1_.refs_5_, bf16[2,64,2048]{2,1,0:T(8,128)(2,1)} %copy-done.8, ...), custom_call_target="tpu_custom_call" | custom-call | tf_op jit(solution)/shard_map/partial_grad/pallas_call | solution.py:274
  115.2 4.1 %collective-permute-start.25 = (bf16[256,1024]{1,0:T(8,128)(2,1)}, bf16[256,1024]{1,0:T(8,128)(2,1)S(1)}, u32[]{:S(2)}, u32[]{:S(2)}) collective-permute-start(bf16[256,1024]{1,0:T(8,128)(2,1)} %get-tuple-element.66), channel_id=1, source_target_pairs={{0,8},{8,0},{16,24},{24,16},{32,40},{40,32},{48,56},{56,48},{64,72... | collective-permute-start | bytes 1572872 | tf_op jit(solution)/shard_map/t_sum_other_pair_sibling/ppermute | solution.py:35
  119.3 0.2 collective-permute-start.27
  119.5 2.0 add_convert_fusion.1
  121.6 1.7 collective-permute-start.19
  123.3 0.2 collective-permute-start.21
  123.5 1.3 collective-permute-start.22
  124.8 2.2 %add_convert_fusion = bf16[256,1024]{1,0:T(8,128)(2,1)} fusion(f32[256,1024]{1,0:T(8,128)} %get-tuple-element.65, bf16[256,1024]{1,0:T(8,128)(2,1)S(1)} %collective-permute-done.25), kind=kLoop, calls=%fused_computation | loop fusion | flops 786432 | bytes 2097152 | tf_op jit(solution)/shard_map/convert_element_type | solution.py:366
  127.0 1.1 copy-done.11
  128.1 9.3 %weight_grad.2.refs_10_ = f32[4,1024,512]{2,1,0:T(8,128)} custom-call(bf16[2,64,2048]{2,1,0:T(8,128)(2,1)} %copy-done.1, bf16[2,64,2048]{2,1,0:T(8,128)(2,1)} %collective-permute-done.13.refs_1_, bf16[2,64,2048]{2,1,0:T(8,128)(2,1)} %collective-permute-done.14.refs_2_, bf16[2,64,2048]{2,1,0:T(8,128)(2,1)} %copy-done.7, ...), custom_call_target="tpu_custom_call" | custom-call | tf_op jit(solution)/shard_map/weight_grad/pallas_call | solution.py:312
  137.4 0.8 copy-done.9
  138.3 0.8 copy-done.10
  139.1 10.3 %weight_grad.3 = bf16[4,1024,512]{2,1,0:T(8,128)(2,1)} custom-call(bf16[2,64,2048]{2,1,0:T(8,128)(2,1)} %copy-done, bf16[2,64,2048]{2,1,0:T(8,128)(2,1)} %copy-done.3, bf16[2,64,2048]{2,1,0:T(8,128)(2,1)} %copy-done.5, bf16[2,64,2048]{2,1,0:T(8,128)(2,1)} %copy-done.4, bf16[2,64,2048]{2,1,0:T(8,128)(2,1)} %copy-done.2, bf16[2,64,2048]{2,1,0:T(8,128)(2,1)} %copy-done.6, ...), custom_call_target="tpu_custom_call" | custom-call | tf_op jit(solution)/shard_map/weight_grad/pallas_call | solution.py:312
  149.4 1.0 copy-done.19
  150.4 1.1 collective-permute-start.15
  151.6 1.2 collective-permute-start.26
  152.8 6.3 %partial_grad.6 = (f32[256,1024]{1,0:T(8,128)}, bf16[256,1024]{1,0:T(8,128)(2,1)}) custom-call(bf16[2,64,2048]{2,1,0:T(8,128)(2,1)} %copy-done.2, bf16[2,64,2048]{2,1,0:T(8,128)(2,1)} %copy-done.6, bf16[2,64,2048]{2,1,0:T(8,128)(2,1)} %copy-done.9, bf16[2,64,2048]{2,1,0:T(8,128)(2,1)} %copy-done.10, bf16[4,1024,512]{2,1,0:T(8,128)(2,1)} %bitcast.28), custom_call_target="tpu_custom_call" | custom-call | tf_op jit(solution)/shard_map/partial_grad/pallas_call | solution.py:274
  159.1 0.5 collective-permute-start.23
  159.6 6.8 %collective-permute-done.26.rest_5_ = bf16[256,1024]{1,0:T(8,128)(2,1)S(1)} collective-permute-done((bf16[256,1024]{1,0:T(8,128)(2,1)S(1)}, bf16[256,1024]{1,0:T(8,128)(2,1)S(1)}, u32[]{:S(2)}, u32[]{:S(2)}) %collective-permute-start.26) | collective-permute-done | bytes 524320 | tf_op jit(solution)/shard_map/t_sum_other_pair_across/ppermute | solution.py:39
  166.4 0.8 copy-done.15
  167.3 0.2 copy-done.16
  167.5 9.4 %attend_grad.1 = (bf16[512,1024]{1,0:T(8,128)(2,1)}, bf16[512,128]{1,0:T(8,128)(2,1)}, bf16[512,128]{1,0:T(8,128)(2,1)}) custom-call(s32[4]{0:T(128)} %pad_add_fusion.place, bf16[512,1024]{1,0:T(8,128)(2,1)} %bitcast.31, bf16[512,128]{1,0:T(8,128)(2,1)} %bitcast.34, bf16[512,128]{1,0:T(8,128)(2,1)} %bitcast.36, f32[4,8,256]{2,1,0:T(8,128)} %get-tuple-element.44.stats, ...), custom_call_target="tpu_custom_call" | custom-call | tf_op jit(solution)/shard_map/attend_grad/pallas_call | solution.py:229
  176.8 19.8 %reduce-scatter.2.cloned.1.call-done = bf16[1024,512]{1,0:T(8,128)(2,1)} async-done(((bf16[4096,512]{1,0:T(8,128)(2,1)}), bf16[1024,512]{1,0:T(8,128)(2,1)}) %reduce-scatter.2.cloned.1.call-update) | async-done | bytes 1048592 | tf_op jit(solution)/shard_map/reduce_scatter | solution.py:400
  196.7 2.8 %convert_element_type.19 = f32[1024,512]{1,0:T(8,128)} convert(bf16[1024,512]{1,0:T(8,128)(2,1)} %reduce-scatter.2.cloned.1.call-done) | non-fusion elementwise | flops 524288 | bytes 3145728 | tf_op jit(solution)/shard_map/convert_element_type | solution.py:404
  (68 shorter events, 0.6 us)
Async XLA Ops:
  7.2 36.9 %copy-start.18 = (s32[1,64]{1,0:T(1,128)S(1)}, s32[1,64]{1,0:T(1,128)}, u32[]{:S(2)}) copy-start(s32[1,64]{1,0:T(1,128)} %param.10) | copy-start | bytes 772
  7.2 75.4 %all-gather.2.cloned.1.call-start = ((), (), s32[]{:S(2)}) async-start(), calls=%async_computation.1 | async-start | bytes 5242880 | tf_op jit(solution)/shard_map/all_gather | solution.py:355
  7.9 188.7 %reduce-scatter.2.cloned.1.call-start = ((), (), s32[]{:S(2)}) async-start(), calls=%async_computation.2 | async-start | bytes 5242880 | tf_op jit(solution)/shard_map/reduce_scatter | solution.py:400
  13.3 14.9 %collective-permute-start.5 = (bf16[2,64,2048]{2,1,0:T(8,128)(2,1)}, bf16[2,64,2048]{2,1,0:T(8,128)(2,1)S(1)}, u32[]{:S(2)}, u32[]{:S(2)}) collective-permute-start(bf16[2,64,2048]{2,1,0:T(8,128)(2,1)} %get-tuple-element.41), channel_id=1, source_target_pairs={{0,16},{8,24},{16,0},{24,8},{32,48},{40,56},{48,32},{56,40},{64,80... | collective-permute-start | bytes 1572872 | tf_op jit(solution)/shard_map/t_other_across/ppermute | solution.py:39
  16.9 2.3 %collective-permute-start = (bf16[64,2048]{1,0:T(8,128)(2,1)}, bf16[64,2048]{1,0:T(8,128)(2,1)S(1)}, u32[]{:S(2)}, u32[]{:S(2)}) collective-permute-start(bf16[64,2048]{1,0:T(8,128)(2,1)} %get-tuple-element.39), channel_id=1, source_target_pairs={{0,8},{8,0},{16,24},{24,16},{32,40},{40,32},{48,56},{56,48},{64,72... | collective-permute-start | bytes 786440 | tf_op jit(solution)/shard_map/t_near_sibling/ppermute | solution.py:35
  20.2 62.3 %copy-start = (bf16[2,64,2048]{2,1,0:T(8,128)(2,1)}, bf16[2,64,2048]{2,1,0:T(8,128)(2,1)S(1)}, u32[]{:S(2)}) copy-start(bf16[2,64,2048]{2,1,0:T(8,128)(2,1)S(1)} %pad_maximum_fusion.1.refs_0_) | copy-start | bytes 1572868
  20.3 19.8 %collective-permute-start.12 = (bf16[2,64,2048]{2,1,0:T(8,128)(2,1)S(1)}, bf16[2,64,2048]{2,1,0:T(8,128)(2,1)S(1)}, u32[]{:S(2)}, u32[]{:S(2)}) collective-permute-start(bf16[2,64,2048]{2,1,0:T(8,128)(2,1)S(1)} %pad_maximum_fusion.1.refs_0_), channel_id=1, source_target_pairs={{0,1},{1,0},{2,3},{3,2},{4,5},{5,4},{6,7},{7,6},{8,9},{9,8},{10,11... | collective-permute-start | bytes 1572872 | tf_op jit(solution)/shard_map/t_near_pair/ppermute | solution.py:43
  20.6 23.4 %collective-permute-start.8 = (bf16[2,64,2048]{2,1,0:T(8,128)(2,1)S(1)}, bf16[2,64,2048]{2,1,0:T(8,128)(2,1)S(1)}, u32[]{:S(2)}, u32[]{:S(2)}) collective-permute-start(bf16[2,64,2048]{2,1,0:T(8,128)(2,1)S(1)} %pad_maximum_fusion.1.refs_0_), channel_id=1, source_target_pairs={{0,6},{1,7},{2,0},{3,1},{4,2},{5,3},{6,4},{7,5},{8,14},{9,15},{10,... | collective-permute-start | bytes 1572872 | tf_op jit(solution)/shard_map/t_n_down/ppermute | solution.py:51
  23.4 20.6 %collective-permute-start.7 = (bf16[2,64,2048]{2,1,0:T(8,128)(2,1)S(1)}, bf16[2,64,2048]{2,1,0:T(8,128)(2,1)S(1)}, u32[]{:S(2)}, u32[]{:S(2)}) collective-permute-start(bf16[2,64,2048]{2,1,0:T(8,128)(2,1)S(1)} %pad_maximum_fusion.1.refs_0_), channel_id=1, source_target_pairs={{0,2},{1,3},{2,4},{3,5},{4,6},{5,7},{6,0},{7,1},{8,10},{9,11},{10,... | collective-permute-start | bytes 1572872 | tf_op jit(solution)/shard_map/t_n_up/ppermute | solution.py:47
  28.3 4.3 %collective-permute-start.6 = (bf16[64,2048]{1,0:T(8,128)(2,1)S(1)}, bf16[64,2048]{1,0:T(8,128)(2,1)S(1)}, u32[]{:S(2)}, u32[]{:S(2)}) collective-permute-start(bf16[64,2048]{1,0:T(8,128)(2,1)S(1)} %get-tuple-element.75), channel_id=1, source_target_pairs={{0,8},{8,0},{16,24},{24,16},{32,40},{40,32},{48,56},{56,48},{64,72... | collective-permute-start | bytes 786440 | tf_op jit(solution)/shard_map/t_other_sibling/ppermute | solution.py:35
  32.7 61.9 %copy-start.1 = (bf16[2,64,2048]{2,1,0:T(8,128)(2,1)}, bf16[2,64,2048]{2,1,0:T(8,128)(2,1)S(1)}, u32[]{:S(2)}) copy-start(bf16[2,64,2048]{2,1,0:T(8,128)(2,1)S(1)} %pad_maximum_fusion.refs_0_) | copy-start | bytes 1572868
  40.1 83.4 %copy-start.2 = (bf16[2,64,2048]{2,1,0:T(8,128)(2,1)}, bf16[2,64,2048]{2,1,0:T(8,128)(2,1)S(1)}, u32[]{:S(2)}) copy-start(bf16[2,64,2048]{2,1,0:T(8,128)(2,1)S(1)} %collective-permute-done.12.refs_0_.refs_4_) | copy-start | bytes 1572868
  40.1 31.1 %collective-permute-start.13 = (bf16[2,64,2048]{2,1,0:T(8,128)(2,1)S(1)}, bf16[2,64,2048]{2,1,0:T(8,128)(2,1)}, u32[]{:S(2)}, u32[]{:S(2)}) collective-permute-start(bf16[2,64,2048]{2,1,0:T(8,128)(2,1)S(1)} %pad_maximum_fusion.refs_0_), channel_id=1, source_target_pairs={{0,6},{1,7},{2,0},{3,1},{4,2},{5,3},{6,4},{7,5},{8,14},{9,15},{10,... | collective-permute-start | bytes 1572872 | tf_op jit(solution)/shard_map/t_o_down/ppermute | solution.py:51
  42.8 28.4 %collective-permute-start.10 = (bf16[2,64,2048]{2,1,0:T(8,128)(2,1)S(1)}, bf16[2,64,2048]{2,1,0:T(8,128)(2,1)}, u32[]{:S(2)}, u32[]{:S(2)}) collective-permute-start(bf16[2,64,2048]{2,1,0:T(8,128)(2,1)S(1)} %pad_maximum_fusion.refs_0_), channel_id=1, source_target_pairs={{0,1},{1,0},{2,3},{3,2},{4,5},{5,4},{6,7},{7,6},{8,9},{9,8},{10,11... | collective-permute-start | bytes 1572872 | tf_op jit(solution)/shard_map/t_other_pair/ppermute | solution.py:43
  44.0 38.6 %copy-start.3 = (bf16[2,64,2048]{2,1,0:T(8,128)(2,1)}, bf16[2,64,2048]{2,1,0:T(8,128)(2,1)S(1)}, u32[]{:S(2)}) copy-start(bf16[2,64,2048]{2,1,0:T(8,128)(2,1)S(1)} %collective-permute-done.8.refs_1_) | copy-start | bytes 1572868
  44.0 38.6 %copy-start.4 = (bf16[2,64,2048]{2,1,0:T(8,128)(2,1)}, bf16[2,64,2048]{2,1,0:T(8,128)(2,1)S(1)}, u32[]{:S(2)}) copy-start(bf16[2,64,2048]{2,1,0:T(8,128)(2,1)S(1)} %collective-permute-done.7.refs_3_) | copy-start | bytes 1572868
  44.0 30.0 %collective-permute-start.9 = (bf16[2,64,2048]{2,1,0:T(8,128)(2,1)S(1)}, bf16[2,64,2048]{2,1,0:T(8,128)(2,1)S(1)}, u32[]{:S(2)}, u32[]{:S(2)}) collective-permute-start(bf16[2,64,2048]{2,1,0:T(8,128)(2,1)S(1)} %collective-permute-done.7.refs_3_), channel_id=1, source_target_pairs={{0,2},{1,3},{2,4},{3,5},{4,6},{5,7},{6,0},{7,1},{8,10},{9,11},{10,... | collective-permute-start | bytes 1572872 | tf_op jit(solution)/shard_map/t_n_far/ppermute | solution.py:47
  44.1 10.5 %collective-permute-start.1 = (s32[64]{0:T(128)S(1)}, s32[64]{0:T(128)S(1)}, u32[]{:S(2)}, u32[]{:S(2)}) collective-permute-start(s32[64]{0:T(128)S(1)} %bitcast.41), channel_id=1, source_target_pairs={{0,1},{1,0},{2,3},{3,2},{4,5},{5,4},{6,7},{7,6},{8,9},{9,8},{10,11... | collective-permute-start | bytes 776 | tf_op jit(solution)/shard_map/t_ids_pair/ppermute | solution.py:43
  54.7 4.2 %collective-permute-start.4 = (s32[2,64]{1,0:T(2,128)S(1)}, s32[2,64]{1,0:T(2,128)S(1)}, u32[]{:S(2)}, u32[]{:S(2)}) collective-permute-start(s32[2,64]{1,0:T(2,128)S(1)} %add_select_fusion.1), channel_id=1, source_target_pairs={{0,2},{1,3},{2,4},{3,5},{4,6},{5,7},{6,0},{7,1},{8,10},{9,11},{10,... | collective-permute-start | bytes 1544 | tf_op jit(solution)/shard_map/t_ids_up/ppermute | solution.py:47
  54.8 4.3 %collective-permute-start.3 = (s32[2,64]{1,0:T(2,128)S(1)}, s32[2,64]{1,0:T(2,128)S(1)}, u32[]{:S(2)}, u32[]{:S(2)}) collective-permute-start(s32[2,64]{1,0:T(2,128)S(1)} %add_select_fusion.1), channel_id=1, source_target_pairs={{0,4},{1,5},{2,6},{3,7},{4,0},{5,1},{6,2},{7,3},{8,12},{9,13},{10,... | collective-permute-start | bytes 1544 | tf_op jit(solution)/shard_map/t_ids_far/ppermute | solution.py:341
  58.8 2.7 %collective-permute-start.2 = (s32[2,64]{1,0:T(2,128)S(1)}, s32[2,64]{1,0:T(2,128)S(1)}, u32[]{:S(2)}, u32[]{:S(2)}) collective-permute-start(s32[2,64]{1,0:T(2,128)S(1)} %add_select_fusion.1), channel_id=1, source_target_pairs={{0,6},{1,7},{2,0},{3,1},{4,2},{5,3},{6,4},{7,5},{8,14},{9,15},{10,... | collective-permute-start | bytes 1544 | tf_op jit(solution)/shard_map/t_ids_down/ppermute | solution.py:51
  71.3 10.5 %collective-permute-start.11 = (bf16[2,64,2048]{2,1,0:T(8,128)(2,1)S(1)}, bf16[2,64,2048]{2,1,0:T(8,128)(2,1)S(1)}, u32[]{:S(2)}, u32[]{:S(2)}) collective-permute-start(bf16[2,64,2048]{2,1,0:T(8,128)(2,1)S(1)} %pad_maximum_fusion.refs_0_), channel_id=1, source_target_pairs={{0,2},{1,3},{2,4},{3,5},{4,6},{5,7},{6,0},{7,1},{8,10},{9,11},{10,... | collective-permute-start | bytes 1572872 | tf_op jit(solution)/shard_map/t_o_up/ppermute | solution.py:47
  71.4 11.2 %collective-permute-start.14 = (bf16[2,64,2048]{2,1,0:T(8,128)(2,1)}, bf16[2,64,2048]{2,1,0:T(8,128)(2,1)}, u32[]{:S(2)}, u32[]{:S(2)}) collective-permute-start(bf16[2,64,2048]{2,1,0:T(8,128)(2,1)} %collective-permute-done.13.refs_1_), channel_id=1, source_target_pairs={{0,6},{1,7},{2,0},{3,1},{4,2},{5,3},{6,4},{7,5},{8,14},{9,15},{10,... | collective-permute-start | bytes 1572872 | tf_op jit(solution)/shard_map/t_o_far/ppermute | solution.py:51
  74.0 8.6 %copy-start.5 = (bf16[2,64,2048]{2,1,0:T(8,128)(2,1)}, bf16[2,64,2048]{2,1,0:T(8,128)(2,1)S(1)}, u32[]{:S(2)}) copy-start(bf16[2,64,2048]{2,1,0:T(8,128)(2,1)S(1)} %collective-permute-done.9.refs_2_) | copy-start | bytes 1572868
  74.0 19.1 %collective-permute-start.16 = (bf16[2,64,2048]{2,1,0:T(8,128)(2,1)}, bf16[2,64,2048]{2,1,0:T(8,128)(2,1)}, u32[]{:S(2)}, u32[]{:S(2)}) collective-permute-start(bf16[2,64,2048]{2,1,0:T(8,128)(2,1)} %collective-permute-done.10.refs_0_.refs_4_), channel_id=1, source_target_pairs={{0,2},{1,3},{2,4},{3,5},{4,6},{5,7},{6,0},{7,1},{8,10},{9,11},{10,... | collective-permute-start | bytes 1572872 | tf_op jit(solution)/shard_map/t_p_up/ppermute | solution.py:47
  74.0 33.9 %collective-permute-start.28 = (bf16[1024,512]{1,0:T(8,128)(2,1)}, bf16[1024,512]{1,0:T(8,128)(2,1)}, u32[]{:S(2)}, u32[]{:S(2)}) collective-permute-start(bf16[1024,512]{1,0:T(8,128)(2,1)} %get-tuple-element.70.refs_8_), channel_id=1, source_target_pairs={{0,16},{8,24},{16,0},{24,8},{32,48},{40,56},{48,32},{56,40},{64,80... | collective-permute-start | bytes 3145736 | tf_op jit(solution)/shard_map/t_out_across/ppermute | solution.py:39
  75.9 18.7 %collective-permute-start.17 = (bf16[2,64,2048]{2,1,0:T(8,128)(2,1)}, bf16[2,64,2048]{2,1,0:T(8,128)(2,1)}, u32[]{:S(2)}, u32[]{:S(2)}) collective-permute-start(bf16[2,64,2048]{2,1,0:T(8,128)(2,1)} %collective-permute-done.10.refs_0_.refs_4_), channel_id=1, source_target_pairs={{0,6},{1,7},{2,0},{3,1},{4,2},{5,3},{6,4},{7,5},{8,14},{9,15},{10,... | collective-permute-start | bytes 1572872 | tf_op jit(solution)/shard_map/t_p_down/ppermute | solution.py:51
  81.8 0.8 copy-start.7
  93.1 14.9 %collective-permute-start.20 = (bf16[2,64,2048]{2,1,0:T(8,128)(2,1)S(1)}, bf16[2,64,2048]{2,1,0:T(8,128)(2,1)S(1)}, u32[]{:S(2)}, u32[]{:S(2)}) collective-permute-start(bf16[2,64,2048]{2,1,0:T(8,128)(2,1)S(1)} %collective-permute-done.12.refs_0_.refs_4_), channel_id=1, source_target_pairs={{0,6},{1,7},{2,0},{3,1},{4,2},{5,3},{6,4},{7,5},{8,14},{9,15},{10,... | collective-permute-start | bytes 1572872 | tf_op jit(solution)/shard_map/t_q_down/ppermute | solution.py:51
  93.6 14.4 %collective-permute-start.24 = (bf16[2,64,2048]{2,1,0:T(8,128)(2,1)}, bf16[2,64,2048]{2,1,0:T(8,128)(2,1)S(1)}, u32[]{:S(2)}, u32[]{:S(2)}) collective-permute-start(bf16[2,64,2048]{2,1,0:T(8,128)(2,1)} %collective-permute-done.16.refs_3_.refs_7_), channel_id=1, source_target_pairs={{0,2},{1,3},{2,4},{3,5},{4,6},{5,7},{6,0},{7,1},{8,10},{9,11},{10,... | collective-permute-start | bytes 1572872 | tf_op jit(solution)/shard_map/t_p_far/ppermute | solution.py:47
  100.9 18.6 %copy-start.12 = (f32[256,1024]{1,0:T(8,128)S(1)}, f32[256,1024]{1,0:T(8,128)}, u32[]{:S(2)}) copy-start(f32[256,1024]{1,0:T(8,128)} %get-tuple-element.56) | copy-start | bytes 3145732
  100.9 18.6 %collective-permute-start.18 = (bf16[256,1024]{1,0:T(8,128)(2,1)}, bf16[256,1024]{1,0:T(8,128)(2,1)}, u32[]{:S(2)}, u32[]{:S(2)}) collective-permute-start(bf16[256,1024]{1,0:T(8,128)(2,1)} %get-tuple-element.57), channel_id=1, source_target_pairs={{0,8},{8,0},{16,24},{24,16},{32,40},{40,32},{48,56},{56,48},{64,72... | collective-permute-start | bytes 1572872 | tf_op jit(solution)/shard_map/t_sum_other_sibling/ppermute | solution.py:35
  107.9 19.1 %collective-permute-start.29 = (bf16[1024,512]{1,0:T(8,128)(2,1)}, bf16[1024,512]{1,0:T(8,128)(2,1)S(1)}, u32[]{:S(2)}, u32[]{:S(2)}) collective-permute-start(bf16[1024,512]{1,0:T(8,128)(2,1)} %collective-permute-done.28.refs_8_), channel_id=1, source_target_pairs={{0,8},{8,0},{16,24},{24,16},{32,40},{40,32},{48,56},{56,48},{64,72... | collective-permute-start | bytes 3145736 | tf_op jit(solution)/shard_map/t_out_other/ppermute | solution.py:35
  108.0 15.3 %copy-start.6 = (bf16[2,64,2048]{2,1,0:T(8,128)(2,1)}, bf16[2,64,2048]{2,1,0:T(8,128)(2,1)S(1)}, u32[]{:S(2)}) copy-start(bf16[2,64,2048]{2,1,0:T(8,128)(2,1)S(1)} %collective-permute-done.20.refs_1_.refs_5_) | copy-start | bytes 1572868
  108.0 0.8 copy-start.8
  115.2 8.3 %collective-permute-start.25 = (bf16[256,1024]{1,0:T(8,128)(2,1)}, bf16[256,1024]{1,0:T(8,128)(2,1)S(1)}, u32[]{:S(2)}, u32[]{:S(2)}) collective-permute-start(bf16[256,1024]{1,0:T(8,128)(2,1)} %get-tuple-element.66), channel_id=1, source_target_pairs={{0,8},{8,0},{16,24},{24,16},{32,40},{40,32},{48,56},{56,48},{64,72... | collective-permute-start | bytes 1572872 | tf_op jit(solution)/shard_map/t_sum_other_pair_sibling/ppermute | solution.py:35
  119.3 18.1 %collective-permute-start.27 = (bf16[1024,512]{1,0:T(8,128)(2,1)}, bf16[1024,512]{1,0:T(8,128)(2,1)}, u32[]{:S(2)}, u32[]{:S(2)}) collective-permute-start(bf16[1024,512]{1,0:T(8,128)(2,1)} %get-tuple-element.70.refs_8_), channel_id=1, source_target_pairs={{0,8},{8,0},{16,24},{24,16},{32,40},{40,32},{48,56},{56,48},{64,72... | collective-permute-start | bytes 3145736 | tf_op jit(solution)/shard_map/t_out_near/ppermute | solution.py:35
  121.6 15.8 %collective-permute-start.19 = (bf16[256,1024]{1,0:T(8,128)(2,1)}, bf16[256,1024]{1,0:T(8,128)(2,1)S(1)}, u32[]{:S(2)}, u32[]{:S(2)}) collective-permute-start(bf16[256,1024]{1,0:T(8,128)(2,1)} %add_convert_fusion.1), channel_id=1, source_target_pairs={{0,16},{8,24},{16,0},{24,8},{32,48},{40,56},{48,32},{56,40},{64,80... | collective-permute-start | bytes 1572872 | tf_op jit(solution)/shard_map/t_sum_other_across/ppermute | solution.py:39
  123.3 14.1 %collective-permute-start.21 = (bf16[2,64,2048]{2,1,0:T(8,128)(2,1)S(1)}, bf16[2,64,2048]{2,1,0:T(8,128)(2,1)S(1)}, u32[]{:S(2)}, u32[]{:S(2)}) collective-permute-start(bf16[2,64,2048]{2,1,0:T(8,128)(2,1)S(1)} %collective-permute-done.20.refs_1_.refs_5_), channel_id=1, source_target_pairs={{0,6},{1,7},{2,0},{3,1},{4,2},{5,3},{6,4},{7,5},{8,14},{9,15},{10,... | collective-permute-start | bytes 1572872 | tf_op jit(solution)/shard_map/t_q_far/ppermute | solution.py:51
  123.5 13.9 %collective-permute-start.22 = (bf16[2,64,2048]{2,1,0:T(8,128)(2,1)S(1)}, bf16[2,64,2048]{2,1,0:T(8,128)(2,1)S(1)}, u32[]{:S(2)}, u32[]{:S(2)}) collective-permute-start(bf16[2,64,2048]{2,1,0:T(8,128)(2,1)S(1)} %collective-permute-done.12.refs_0_.refs_4_), channel_id=1, source_target_pairs={{0,2},{1,3},{2,4},{3,5},{4,6},{5,7},{6,0},{7,1},{8,10},{9,11},{10,... | collective-permute-start | bytes 1572872 | tf_op jit(solution)/shard_map/t_q_up/ppermute | solution.py:47
  127.0 1.1 copy-start.11
  137.4 21.8 %copy-start.13 = (bf16[256,1024]{1,0:T(8,128)(2,1)}, bf16[256,1024]{1,0:T(8,128)(2,1)S(1)}, u32[]{:S(2)}) copy-start(bf16[256,1024]{1,0:T(8,128)(2,1)S(1)} %collective-permute-done.19.rest_2_) | copy-start | bytes 1572868
  137.4 0.9 copy-start.9
  138.3 0.8 copy-start.10
  149.4 1.0 copy-start.19
  149.4 2.1 %copy-start.17 = (bf16[256,1024]{1,0:T(8,128)(2,1)S(1)}, bf16[256,1024]{1,0:T(8,128)(2,1)}, u32[]{:S(2)}) copy-start(bf16[256,1024]{1,0:T(8,128)(2,1)} %add_convert_fusion) | copy-start | bytes 1572868
  150.4 9.2 %collective-permute-start.15 = (bf16[256,1024]{1,0:T(8,128)(2,1)S(1)}, bf16[256,1024]{1,0:T(8,128)(2,1)S(1)}, u32[]{:S(2)}, u32[]{:S(2)}) collective-permute-start(bf16[256,1024]{1,0:T(8,128)(2,1)S(1)} %copy-done.19), channel_id=1, source_target_pairs={{0,8},{8,0},{16,24},{24,16},{32,40},{40,32},{48,56},{56,48},{64,72... | collective-permute-start | bytes 1572872 | tf_op jit(solution)/shard_map/t_sum_near_sibling/ppermute | solution.py:35
  151.6 14.9 %collective-permute-start.26 = (bf16[256,1024]{1,0:T(8,128)(2,1)S(1)}, bf16[256,1024]{1,0:T(8,128)(2,1)S(1)}, u32[]{:S(2)}, u32[]{:S(2)}) collective-permute-start(bf16[256,1024]{1,0:T(8,128)(2,1)S(1)} %copy-done.17), channel_id=1, source_target_pairs={{0,16},{8,24},{16,0},{24,8},{32,48},{40,56},{48,32},{56,40},{64,80... | collective-permute-start | bytes 1572872 | tf_op jit(solution)/shard_map/t_sum_other_pair_across/ppermute | solution.py:39
  159.1 7.3 %collective-permute-start.23 = (bf16[256,1024]{1,0:T(8,128)(2,1)}, bf16[256,1024]{1,0:T(8,128)(2,1)S(1)}, u32[]{:S(2)}, u32[]{:S(2)}) collective-permute-start(bf16[256,1024]{1,0:T(8,128)(2,1)} %get-tuple-element.62), channel_id=1, source_target_pairs={{0,8},{8,0},{16,24},{24,16},{32,40},{40,32},{48,56},{56,48},{64,72... | collective-permute-start | bytes 1572872 | tf_op jit(solution)/shard_map/t_sum_near_pair_sibling/ppermute | solution.py:35
  159.6 6.8 %copy-start.14 = (bf16[256,1024]{1,0:T(8,128)(2,1)}, bf16[256,1024]{1,0:T(8,128)(2,1)S(1)}, u32[]{:S(2)}) copy-start(bf16[256,1024]{1,0:T(8,128)(2,1)S(1)} %collective-permute-done.15.rest_1_) | copy-start | bytes 1572868
  166.4 0.8 copy-start.15
  166.4 1.0 copy-start.16
Sparse Core Ops, SparseCore 0:
  9.7 51.6 all-gather.1
  149.6 47.0 reduce-scatter.1

commit v2 on v1

--- a/solution.py
+++ b/solution.py
@@ -25,6 +25,7 @@
 
 SIBLING = by_dp(lambda i: i ^ 1)
 ACROSS = by_dp(lambda i: i ^ 2)
+DIAGONAL = by_dp(lambda i: i ^ 3)
 PAIR = by_tensor(lambda i: i ^ 1)
 Y_UP = by_tensor(lambda i: (i + 2) % 8)
 Y_DOWN = by_tensor(lambda i: (i - 2) % 8)
@@ -39,6 +40,10 @@
     return lax.ppermute(x, "dp", ACROSS)
 
 
+def diagonal(x):
+    return lax.ppermute(x, "dp", DIAGONAL)
+
+
 def pair(x):
     return lax.ppermute(x, "tensor", PAIR)
 
@@ -70,37 +75,38 @@
     return pl.BlockSpec(shape, lambda i: (0,) * len(shape))
 
 
-def prep_kernel(place, margins, segs, up, own, to_sibling, to_across):
+def prep_kernel(place, margins, segs, up, own, to_sibling, to_across, to_diagonal):
     h, c = place[2], place[3]
     seg = segs[...]
     margin = jnp.full(seg.shape, margins[0, 0], F32)
     for p in range(1, margins.shape[1]):
         margin = jnp.where((seg >> 1) == p, margins[0, p], margin)
     factor = jax.nn.sigmoid(-margin) * jnp.where((seg & 1) == 0, -1.0, 1.0)
-    width = own.shape[1]
+    width = own.shape[2]
     factor = jnp.concatenate([factor] * (width // factor.shape[1]), axis=1)
 
-    def grad(hh, cc):
-        start = pl.multiple_of((hh * 2 + cc) * width, width)
-        return (up[:, pl.ds(start, width)].astype(F32) * factor).astype(BF16)
-
-    own[...] = grad(h, c)
-    to_sibling[...] = grad(h, 1 - c)
-    to_across[0] = grad(1 - h, c)
-    to_across[1] = grad(1 - h, 1 - c)
+    def put(ref, hh, cc):
+        for e in range(2):
+            start = pl.multiple_of((hh * 2 + cc) * 2 * width, 2 * width) + e * width
+            ref[e] = (up[:, pl.ds(start, width)].astype(F32) * factor).astype(BF16)
+
+    put(own, h, c)
+    put(to_sibling, h, 1 - c)
+    put(to_across, 1 - h, c)
+    put(to_diagonal, 1 - h, 1 - c)
 
 
 def prep(place, margins, segs, up):
     seq, model = up.shape
-    width = model // 16
-    shape = jax.ShapeDtypeStruct((seq, 4 * width), BF16)
-    col = pl.BlockSpec((seq, width), lambda i: (0, i))
+    width = model // 32
+    shape = jax.ShapeDtypeStruct((2, seq, 4 * width), BF16)
+    col = pl.BlockSpec((2, seq, width), lambda i: (0, 0, i))
     return pl.pallas_call(
         prep_kernel,
         grid=(4,),
-        in_specs=[SMEM(), SMEM(), whole(segs.shape), pl.BlockSpec((seq, 4 * width), lambda i: (0, i))],
-        out_specs=[col, col, pl.BlockSpec((2, seq, width), lambda i: (0, 0, i))],
-        out_shape=[shape, shape, jax.ShapeDtypeStruct((2, seq, 4 * width), BF16)],
+        in_specs=[SMEM(), SMEM(), whole(segs.shape), pl.BlockSpec((seq, 8 * width), lambda i: (0, i))],
+        out_specs=[col] * 4,
+        out_shape=[shape] * 4,
         compiler_params=params(),
         cost_estimate=LIGHT,
         name="prep",
@@ -248,78 +254,85 @@
 
 
 def partial_kernel(*refs):
-    blocks, (weight, keep, give, x) = refs[:4], refs[4:]
-    seq = blocks[0].shape[1]
+    pieces, (weight, keep, give, x) = refs[:8], refs[8:]
+    _, _, seq, cols = pieces[0].shape
     half = 4 * seq
-    width = weight.shape[2]
+    width = weight.shape[2] // 2
 
     @pl.when(pl.program_id(0) == 0)
     def _():
-        for i in range(2):
-            for j, block in enumerate(blocks):
-                x[i * half + j * seq : i * half + (j + 1) * seq] = block[i]
-
-    total = nt(x[:, :width], weight[0])
-    for j in range(1, 4):
-        total += nt(x[:, j * width : (j + 1) * width], weight[j])
+        for e in range(2):
+            for i in range(2):
+                for j in range(4):
+                    at = i * half + j * seq
+                    x[at : at + seq, e * cols : (e + 1) * cols] = pieces[e * 4 + j][0, i]
+
+    w = jnp.concatenate([weight[j, :, e * width : (e + 1) * width] for e in range(2) for j in range(4)], axis=1)
+    total = nt(x[...], w)
     keep[...] = total[:half]
     give[...] = total[half:].astype(BF16)
 
 
-def partial(blocks, weight):
-    _, seq, cols = blocks[0].shape
+def partial(pieces, weight):
+    _, _, seq, cols = pieces[0][0].shape
     heads = weight.shape[1]
-    tile = heads // 4
+    tile = heads // 2
     out = pl.BlockSpec((4 * seq, tile), lambda i: (0, i))
+
+    def spec(index):
+        return pl.BlockSpec((1, 2, seq, cols), lambda i: (index, 0, 0, 0))
+
     return pl.pallas_call(
         partial_kernel,
-        grid=(4,),
-        in_specs=[whole(blocks[0].shape)] * 4 + [pl.BlockSpec((4, tile, cols // 4), lambda i: (0, i, 0))],
+        grid=(2,),
+        in_specs=[spec(index) for _, index in pieces] + [pl.BlockSpec((4, tile, cols // 2), lambda i: (0, i, 0))],
         out_specs=[out, out],
         out_shape=[jax.ShapeDtypeStruct((4 * seq, heads), F32), jax.ShapeDtypeStruct((4 * seq, heads), BF16)],
-        scratch_shapes=[pltpu.VMEM((8 * seq, cols), BF16)],
+        scratch_shapes=[pltpu.VMEM((8 * seq, 2 * cols), BF16)],
         compiler_params=params(),
         cost_estimate=LIGHT,
         name="partial_grad",
-    )(*blocks, weight)
-
-
-def wgrad_kernel(has_start, *refs):
-    same, flip, outs = refs[:4], refs[4:8], refs[8:10]
-    start = refs[10] if has_start else None
-    out, x = refs[-2:]
-    seq = same[0].shape[1]
+    )(*[x for x, _ in pieces], weight)
+
+
+def wgrad_kernel(*refs):
+    near, other, flip, outs, (out, x) = refs[:4], refs[4:8], refs[8:12], refs[12:16], refs[16:]
+    _, _, seq, cols = near[0].shape
+    length = 8 * seq
     for i in range(2):
         for j in range(4):
-            at = (i * 8 + j * 2) * seq
-            x[at : at + seq] = same[j][i]
-            x[at + seq : at + 2 * seq] = flip[j][i]
-    half = 8 * seq
+            for row, block in ((i, near[j][0, i]), (2 + i, other[j][0, i])):
+                at = row * length + 2 * j * seq
+                x[at : at + seq] = block
+            for row, block in ((i, flip[j][0, i]), (2 + i, flip[j][1, i])):
+                at = row * length + (2 * j + 1) * seq
+                x[at : at + seq] = block
     tile = 256
+    width = out.shape[2]
     for m in range(0, out.shape[1], tile):
-        total = nn(outs[0][m : m + tile], x[:half]) + nn(outs[1][m : m + tile], x[half:])
-        if has_start:
-            total += start[0, m : m + tile]
-        out[0, m : m + tile] = total.astype(out.dtype)
-
-
-def wgrad(same, flip, outs, start):
-    _, seq, cols = same[0].shape
+        total = nn(outs[0][m : m + tile], x[:length])
+        for r in range(1, 4):
+            total += nn(outs[r][m : m + tile], x[r * length : (r + 1) * length])
+        for k in range(cols // width):
+            out[k, m : m + tile] = total[:, k * width : (k + 1) * width].astype(BF16)
+
+
+def wgrad(half, near, other, flip, outs):
+    _, _, seq, cols = near[0].shape
     heads = outs[0].shape[0]
-    width = cols // 4
-    col = pl.BlockSpec((2, seq, width), lambda i: (0, 0, i))
-    result = pl.BlockSpec((1, heads, width), lambda i: (i, 0, 0))
+    wide = cols // 2
+    same = pl.BlockSpec((1, 2, seq, wide), lambda i: (half, 0, 0, i))
     return pl.pallas_call(
-        functools.partial(wgrad_kernel, start is not None),
-        grid=(4,),
-        in_specs=[col] * 8 + [whole(outs[0].shape)] * 2 + ([] if start is None else [result]),
-        out_specs=result,
-        out_shape=jax.ShapeDtypeStruct((4, heads, width), F32 if start is None else BF16),
-        scratch_shapes=[pltpu.VMEM((16 * seq, width), BF16)],
+        wgrad_kernel,
+        grid=(2,),
+        in_specs=[same] * 8 + [pl.BlockSpec((2, 2, seq, wide), lambda i: (0, 0, 0, i))] * 4 + [whole(outs[0].shape)] * 4,
+        out_specs=pl.BlockSpec((2, heads, wide // 2), lambda i: (i, 0, 0)),
+        out_shape=jax.ShapeDtypeStruct((4, heads, wide // 2), BF16),
+        scratch_shapes=[pltpu.VMEM((32 * seq, wide), BF16)],
         compiler_params=params(),
         cost_estimate=LIGHT,
         name="weight_grad",
-    )(*same, *flip, *outs, *([] if start is None else [start]))
+    )(*near, *other, *flip, *outs)
 
 
 def named(name, fn, x):
@@ -331,77 +344,84 @@
     return lax.optimization_barrier((x, *others))[0]
 
 
-def gather_ids(ids):
-    low = lax.axis_index("tensor") % 2
-    y = lax.axis_index("tensor") // 2
-    partner = named("ids_pair", pair, ids)
-    both = jnp.where(low == 0, jnp.stack([ids, partner]), jnp.stack([partner, ids]))
-    behind = named("ids_up", y_up, both)
-    ahead = named("ids_down", y_down, both)
-    far = named("ids_far", lambda x: lax.ppermute(x, "tensor", by_tensor(lambda i: (i + 4) % 8)), both)
-    ring = jnp.stack([both, ahead, far, behind] * 2).reshape(8, -1)
-    return lax.dynamic_slice(ring, ((4 - y) % 4, 0), (4, ring.shape[1])).reshape(-1)
-
-
 def shards(query_states, key_states, value_states, segment_ids, pair_margins, upstream, out_weight):
     d = lax.axis_index("dp")
     t = lax.axis_index("tensor")
-    place = jnp.stack([t // 2, t % 2, (d // 2) % 2, d % 2]).astype(jnp.int32)
+    y, low = t // 2, t % 2
+    place = jnp.stack([y, low, (d // 2) % 2, d % 2]).astype(jnp.int32)
     query, key, value = query_states[0], key_states[0], value_states[0]
-
-    segs = jnp.broadcast_to(segment_ids[0][:, None], (segment_ids.shape[1], HD))
-    own, to_sibling, to_across = prep(place, pair_margins, segs, upstream[0])
     heads, width = out_weight.shape
     weight = lax.all_gather(out_weight, "dp", axis=0, tiled=True, axis_index_groups=Z_GROUPS).reshape(4, heads, width)
 
-    from_sibling = named("near_sibling", sibling, to_sibling)
-    near = jnp.stack([own, from_sibling])
+    ids = segment_ids[0]
+    partner = named("ids_pair", pair, ids)
+    segs = jnp.broadcast_to(ids[:, None], (ids.shape[0], HD))
+    own, to_sibling, to_across, to_diagonal = prep(place, pair_margins, segs, upstream[0])
+
     from_across = named("other_across", across, to_across)
-    other = jnp.stack([from_across[0], named("other_sibling", sibling, from_across[1])])
-    near_pair = named("near_pair", pair, near)
-    other_pair = named("other_pair", pair, other)
-
-    def to_row(name, blocks):
-        keep, give = partial(blocks, weight)
+    from_diagonal = named("other_diagonal", diagonal, to_diagonal)
+    near = jnp.stack([own, named("near_sibling", sibling, after(to_sibling, partner))], axis=1)
+    n_up, n_down = named("n_up", y_up, near), named("n_down", y_down, near)
+    both = jnp.where(low == 0, jnp.stack([ids, partner]), jnp.stack([partner, ids]))
+    both = after(both, near)
+    ids_up = named("ids_up", y_up, both)
+    ids_down = named("ids_down", y_down, both)
+    ids_far = named("ids_far", lambda x: lax.ppermute(x, "tensor", by_tensor(lambda i: (i + 4) % 8)), both)
+    ring = jnp.stack([both, ids_down, ids_far, ids_up] * 2).reshape(8, -1)
+    ids = lax.dynamic_slice(ring, ((4 - y) % 4, 0), (4, ring.shape[1])).reshape(-1)
+    whole_segs = jnp.broadcast_to(ids[:, None], (ids.shape[0], HD))
+
+    other = jnp.stack([after(from_across, n_up, n_down, ids_up, ids_down, ids_far), from_diagonal], axis=1)
+    flips = [named("pair_%d" % e, pair, jnp.stack([near[e], other[e]])) for e in range(2)]
+
+    def to_row(name, pieces):
+        keep, give = partial(pieces, weight)
         total = (keep + named(name + "_sibling", sibling, give).astype(F32)).astype(BF16)
         return named(name + "_across", across, total), total
 
-    def for_row(name, blocks):
-        keep, give = partial(blocks, weight)
+    def for_row(name, pieces):
+        keep, give = partial(pieces, weight)
         return keep, named(name + "_sibling", sibling, give)
 
-    n, o, p, q = near, other, other_pair, near_pair
-    n_up, n_down = named("n_up", y_up, n), named("n_down", y_down, n)
-
-    ids = gather_ids(after(segment_ids[0], from_sibling))
-    whole_segs = jnp.broadcast_to(ids[:, None], (ids.shape[0], HD))
+    n, o, p, q = near, other, flips[0], flips[1]
     attn_out, stats, bias = forward(place, whole_segs, after(query, other, n_up, n_down), key, value)
-    out_across = named("out_across", across, attn_out)
-
-    n_far, o_down = named("n_far", y_up, after(n_up, n_down)), named("o_down", y_down, after(o, q, ids))
+    out_across = named("out_across", across, after(attn_out, q))
+
+    n_far, o_down = named("n_far", y_up, after(n_up, n_down)), named("o_down", y_down, after(o, ids))
     o_up, o_far = named("o_up", y_up, after(o, n_up, n_down, p, attn_out)), named("o_far", y_down, after(o_down, attn_out))
     p = after(p, n_far, o_down)
     p_up, p_down = named("p_up", y_up, p), named("p_down", y_down, p)
-    terms_same = for_row("sum_near", [n, n_down, n_far, after(n_up, o_up, o_far)])
-    p_far, q_down = named("p_far", y_up, after(p_up, terms_same[0])), named("q_down", y_down, after(q, o_up, o_far, terms_same[0]))
-    sent_same, sum_other = to_row("sum_other", [o, o_down, o_far, after(o_up, p_up, p_down)])
-    q_up, q_far = named("q_up", y_up, after(q, p_up, p_down, sum_other)), named("q_far", y_down, after(q_down, sum_other))
     near_blocks = [n, n_down, n_far, n_up]
     other_blocks = [o, o_down, o_far, o_up]
-    other_pair_blocks = [p, p_down, p_far, p_up]
-    near_pair_blocks = [q, q_down, q_far, q_up]
-    sent_flip, sum_other_pair = to_row("sum_other_pair", [p, p_down, after(p_far, q_down), p_up])
+    terms_same = for_row("sum_near", [(x, e) for e in range(2) for x in [n, n_down, n_far, after(n_up, o_up, o_far)]])
+    p_far = named("p_far", y_up, p_up)
+    q_down = named("q_down", y_down, after(q, o_up, o_far))
+    sent_same, sum_other = to_row("sum_other", [(x, e) for e in range(2) for x in [o, o_down, o_far, after(o_up, p_up, p_down)]])
+    q_up, q_far = named("q_up", y_up, after(q, p_up, p_down)), named("q_far", y_down, q_down)
     out_near = named("out_near", sibling, after(attn_out, o_up, o_far))
     out_other = named("out_other", sibling, after(out_across, o_up, o_far))
-    first = wgrad(other_blocks, other_pair_blocks, (out_across, after(out_other, sum_other_pair)), None)
-    total = wgrad(near_blocks, near_pair_blocks, (attn_out, out_near), after(first, sent_same))
-    terms_flip = for_row("sum_near_pair", near_pair_blocks)
+    outs = (attn_out, out_near, out_across, out_other)
+    flip_blocks = [[p, p_down, after(p_far, q_down), p_up], [q, q_down, q_far, q_up]]
+
+    def sum_z(x):
+        return lax.psum_scatter(
+            x.reshape(4 * heads, width // 2), "dp", scatter_dimension=0, tiled=True, axis_index_groups=Z_GROUPS
+        )
+
+    first = wgrad(0, near_blocks, other_blocks, flip_blocks[0], (*outs[:3], after(out_other, sum_other, q_up)))
+    first_sum = sum_z(first)
+
+    def flipped(row):
+        return [(x, row) for e in range(2) for x in flip_blocks[e]]
+
+    sent_flip, sum_other_flip = to_row("sum_other_flip", flipped(1))
+    last = wgrad(1, near_blocks, other_blocks, flip_blocks[1], (*outs[:3], after(out_other, sum_other_flip)))
+    last_sum = sum_z(last)
+    terms_flip = for_row("sum_near_flip", [(after(x, last) if i == 0 else x, r) for i, (x, r) in enumerate(flipped(0))])
     terms = [*terms_same, sent_same, *terms_flip, sent_flip]
-    weight_grad = lax.psum_scatter(
-        total.reshape(4 * heads, width), "dp", scatter_dimension=0, tiled=True, axis_index_groups=Z_GROUPS
-    )
     dq, dk, dv = backward(place, query, key, value, stats, bias, terms)
-    return (dq[None], dk[None], dv[None], weight_grad.astype(F32))
+    weight_grad = jnp.concatenate([first_sum, last_sum], axis=1).astype(F32)
+    return (dq[None], dk[None], dv[None], weight_grad)
 
 
 def solution(mesh):

time: 207 us -> 217 us (1.048)
  waiting for transfers between devices: 64.8 us -> 83.1 us
  local copies, waits for them, and re-layouts: 9.01 us -> 5.02 us
  Pallas kernels: 66.5 us -> 62.7 us
  other arithmetic: 8.73 us -> 11.7 us
  starting transfers between devices: 43 us -> 40.2 us
    ppermute x7, waiting for transfers between devices: 9.97 us -> 31.2 us  [y_up(): return lax.ppermute(x, 'tensor', Y_UP)]
    ppermute x4, waiting for transfers between devices: 11.7 us -> 32 us  [across(): return lax.ppermute(x, 'dp', ACROSS)]
    reduce_scatter x1 -> x2, waiting for transfers between devices: 19.8 us -> 0.04 us  [sum_z(): lax.psum_scatter(x.reshape(4 * heads, width // 2), 'dp', scatter_dimensio...]
    ppermute x3, waiting for transfers between devices: 17.6 us -> 2.04 us  [pair(): return lax.ppermute(x, 'tensor', PAIR)]
    ppermute x7, waiting for transfers between devices: 2.47 us -> 12.9 us  [y_down(): return lax.ppermute(x, 'tensor', Y_DOWN)]
    ppermute x8 -> x7, starting transfers between devices: 17.1 us -> 11.7 us  [sibling(): return lax.ppermute(x, 'dp', SIBLING)]
    another operation x3 -> x7, other arithmetic: 1.64 us -> 6.17 us  [the longest x2 2.65 us: shards(): jnp.stack([near[e], other[e]])]
    unnamed x40 -> x38, local copies, waits for them, and re-layouts: 6.42 us -> 2.48 us
  transfers between devices with their start and end apart: 32 -> 33, of which waited for: 11 -> 16; matrix products, arithmetic and copies ran while one was open for 4% -> 5% of each run, Pallas kernels for 27% -> 25%
where the time goes in v2:
time: 217 us
  waiting for transfers between devices  83.1 us (38%)
  Pallas kernels  62.7 us (29%)
  starting transfers between devices  40.2 us (19%)
  between operations  14 us (6%)
  other arithmetic  11.7 us (5%)
  local copies, waits for them, and re-layouts  5.02 us (2%)
    ppermute x4, waiting for transfers between devices, across(): return lax.ppermute(x, 'dp', ACROSS)  32 us
    ppermute x7, waiting for transfers between devices, y_up(): return lax.ppermute(x, 'tensor', Y_UP)  31.2 us
    pallas_call x4, Pallas kernels, partial(): pl.pallas_call(partial_kernel, grid=(2,), in_specs=[spec(index) for _, in...  23.2 us
    pallas_call x2, Pallas kernels, wgrad(): pl.pallas_call(wgrad_kernel, grid=(2,), in_specs=[same] * 8 + [pl.BlockSp...  18 us
    ppermute x7, waiting for transfers between devices, y_down(): return lax.ppermute(x, 'tensor', Y_DOWN)  12.9 us
    ppermute x7, starting transfers between devices, sibling(): return lax.ppermute(x, 'dp', SIBLING)  11.7 us
    ppermute x7, starting transfers between devices, y_down(): return lax.ppermute(x, 'tensor', Y_DOWN)  10.6 us
    pallas_call x1, Pallas kernels, backward(): pl.pallas_call(backward_kernel, grid=(pairs,), in_specs=[SMEM(), two, who...  9.28 us
  transfers between devices with their start and end apart: 33, of which 16 were waited for; matrix products, arithmetic and copies ran while one was open for 5% of the time, Pallas kernels for 25%

profile of v2, /device:TPU:1, one launch (start us, length us, event | category | flops | bytes accessed | tf_op | source)
XLA Modules:
  0.0 216.7 jit_solution(11411161098648782881)
XLA Ops:
  7.2 0.7 all-gather.2.cloned.1.call-update
  8.0 2.1 collective-permute-start
  10.1 0.6 pad_add_fusion.place
  10.7 1.3 broadcast_in_dim.21.segs
  12.0 3.4 %prep.1 = (bf16[2,64,1024]{2,1,0:T(8,128)(2,1)}, bf16[2,64,1024]{2,1,0:T(8,128)(2,1)}, bf16[2,64,1024]{2,1,0:T(8,128)(2,1)}, bf16[2,64,1024]{2,1,0:T(8,128)(2,1)}) custom-call(s32[4]{0:T(128)} %pad_add_fusion.place, f32[1,4]{1,0:T(1,128)} %margins.1, s32[64,128]{1,0:T(8,128)} %broadcast_in_dim.21.segs, bf16[64,8192]{1,0:T(8,128)(2,1)} %bitcast.30), custom_call_target="tpu_custom_call" | custom-call | tf_op jit(solution)/shard_map/prep/pallas_call | solution.py:104
  15.4 1.0 collective-permute-start.1
  16.5 1.4 collective-permute-done.1
  17.8 1.0 pad_maximum_fusion.refs_0_.refs_4_
  18.8 1.4 collective-permute-start.6
  20.2 1.5 collective-permute-start.7
  21.7 2.5 %collective-permute-start.5 = (bf16[2,64,1024]{2,1,0:T(8,128)(2,1)}, bf16[2,64,1024]{2,1,0:T(8,128)(2,1)S(1)}, u32[]{:S(2)}, u32[]{:S(2)}) collective-permute-start(bf16[2,64,1024]{2,1,0:T(8,128)(2,1)} %get-tuple-element.45), channel_id=1, source_target_pairs={{0,16},{8,24},{16,0},{24,8},{32,48},{40,56},{48,32},{56,40},{64,80... | collective-permute-start | bytes 786440 | tf_op jit(solution)/shard_map/t_other_across/ppermute | solution.py:40
  24.2 1.5 collective-permute-start.8
  25.7 1.6 collective-permute-start.2
  27.3 3.2 %collective-permute-done.5 = bf16[2,64,1024]{2,1,0:T(8,128)(2,1)S(1)} collective-permute-done((bf16[2,64,1024]{2,1,0:T(8,128)(2,1)}, bf16[2,64,1024]{2,1,0:T(8,128)(2,1)S(1)}, u32[]{:S(2)}, u32[]{:S(2)}) %collective-permute-start.5) | collective-permute-done | bytes 262176 | tf_op jit(solution)/shard_map/t_other_across/ppermute | solution.py:40
  30.5 1.4 collective-permute-start.3
  31.9 1.3 collective-permute-done.2
  33.2 1.3 collective-permute-start.4
  34.4 1.0 fusion.3
  35.5 1.9 collective-permute-done.4
  37.4 0.8 fusion.1
  38.3 0.9 pad_maximum_fusion.3
  39.1 0.3 collective-permute-start.19
  39.9 1.5 collective-permute-start.12
  41.5 1.8 pad_maximum_fusion.2
  43.2 1.1 collective-permute-start.10
  44.4 0.8 broadcast_in_dim.23.segs
  45.2 8.8 %attend.1 = (bf16[1024,512]{1,0:T(8,128)(2,1)}, f32[4,8,256]{2,1,0:T(8,128)}, f32[4,384,128]{2,1,0:T(8,128)}) custom-call(s32[4]{0:T(128)} %pad_add_fusion.place, s32[512,128]{1,0:T(8,128)} %broadcast_in_dim.23.segs, bf16[512,1024]{1,0:T(8,128)(2,1)} %bitcast.28, bf16[512,128]{1,0:T(8,128)(2,1)} %bitcast.39, bf16[512,128]{1,0:T(8,128)(2,1)} %bitcast.41), custom_call_target="tpu_custom_call" | custom-call | tf_op jit(solution)/shard_map/attend/pallas_call | solution.py:167
  54.0 2.5 %collective-permute-start.24 = (bf16[1024,512]{1,0:T(8,128)(2,1)}, bf16[1024,512]{1,0:T(8,128)(2,1)}, u32[]{:S(2)}, u32[]{:S(2)}) collective-permute-start(bf16[1024,512]{1,0:T(8,128)(2,1)} %get-tuple-element.65.refs_12_), channel_id=1, source_target_pairs={{0,16},{8,24},{16,0},{24,8},{32,48},{40,56},{48,32},{56,40},{64,80... | collective-permute-start | bytes 3145736 | tf_op jit(solution)/shard_map/t_out_across/ppermute | solution.py:40
  56.5 0.1 collective-permute-start.9
  56.7 2.5 %collective-permute-start.13 = (bf16[2,2,64,1024]{3,2,1,0:T(8,128)(2,1)S(1)}, bf16[2,2,64,1024]{3,2,1,0:T(8,128)(2,1)S(1)}, u32[]{:S(2)}, u32[]{:S(2)}) collective-permute-start(bf16[2,2,64,1024]{3,2,1,0:T(8,128)(2,1)S(1)} %collective-permute-done.12.refs_1_.refs_5_), channel_id=1, source_target_pairs={{0,6},{1,7},{2,0},{3,1},{4,2},{5,3},{6,4},{7,5},{8,14},{9,15},{10,... | collective-permute-start | bytes 1572872 | tf_op jit(solution)/shard_map/t_o_far/ppermute | solution.py:56
  59.2 2.0 collective-permute-done.10.refs_0_.refs_8_
  61.2 0.5 collective-permute-start.11
  61.7 6.1 %collective-permute-done.9.refs_2_.refs_6_ = bf16[2,2,64,1024]{3,2,1,0:T(8,128)(2,1)S(1)} collective-permute-done((bf16[2,2,64,1024]{3,2,1,0:T(8,128)(2,1)S(1)}, bf16[2,2,64,1024]{3,2,1,0:T(8,128)(2,1)S(1)}, u32[]{:S(2)}, u32[]{:S(2)}) %collective-permute-start.9) | collective-permute-done | bytes 524320 | tf_op jit(solution)/shard_map/t_n_far/ppermute | solution.py:52
  67.9 2.7 %collective-permute-start.16 = (bf16[2,2,64,1024]{3,2,1,0:T(8,128)(2,1)S(1)}, bf16[2,2,64,1024]{3,2,1,0:T(8,128)(2,1)S(1)}, u32[]{:S(2)}, u32[]{:S(2)}) collective-permute-start(bf16[2,2,64,1024]{3,2,1,0:T(8,128)(2,1)S(1)} %collective-permute-done.10.refs_0_.refs_8_), channel_id=1, source_target_pairs={{0,6},{1,7},{2,0},{3,1},{4,2},{5,3},{6,4},{7,5},{8,14},{9,15},{10,... | collective-permute-start | bytes 1572872 | tf_op jit(solution)/shard_map/t_p_down/ppermute | solution.py:56
  70.6 8.7 %collective-permute-done.11.refs_3_.refs_7_ = bf16[2,2,64,1024]{3,2,1,0:T(8,128)(2,1)S(1)} collective-permute-done((bf16[2,2,64,1024]{3,2,1,0:T(8,128)(2,1)S(1)}, bf16[2,2,64,1024]{3,2,1,0:T(8,128)(2,1)S(1)}, u32[]{:S(2)}, u32[]{:S(2)}) %collective-permute-start.11) | collective-permute-done | bytes 524320 | tf_op jit(solution)/shard_map/t_o_up/ppermute | solution.py:52
  79.2 6.0 %collective-permute-done.24.refs_14_ = bf16[1024,512]{1,0:T(8,128)(2,1)} collective-permute-done((bf16[1024,512]{1,0:T(8,128)(2,1)}, bf16[1024,512]{1,0:T(8,128)(2,1)}, u32[]{:S(2)}, u32[]{:S(2)}) %collective-permute-start.24) | collective-permute-done | bytes 1048608 | tf_op jit(solution)/shard_map/t_out_across/ppermute | solution.py:40
  85.2 3.8 %collective-permute-start.25 = (bf16[1024,512]{1,0:T(8,128)(2,1)}, bf16[1024,512]{1,0:T(8,128)(2,1)}, u32[]{:S(2)}, u32[]{:S(2)}) collective-permute-start(bf16[1024,512]{1,0:T(8,128)(2,1)} %collective-permute-done.24.refs_14_), channel_id=1, source_target_pairs={{0,8},{8,0},{16,24},{24,16},{32,40},{40,32},{48,56},{56,48},{64,72... | collective-permute-start | bytes 3145736 | tf_op jit(solution)/shard_map/t_out_other/ppermute | solution.py:36
  89.0 1.4 collective-permute-done.15.refs_3_.refs_11_
  90.5 0.8 copy-done.11
  91.3 5.8 %partial_grad.5 = (f32[256,1024]{1,0:T(8,128)}, bf16[256,1024]{1,0:T(8,128)(2,1)}) custom-call(bf16[2,2,64,1024]{3,2,1,0:T(8,128)(2,1)} %copy-done.1, bf16[2,2,64,1024]{3,2,1,0:T(8,128)(2,1)} %copy-done.4, bf16[2,2,64,1024]{3,2,1,0:T(8,128)(2,1)} %copy-done.6, bf16[2,2,64,1024]{3,2,1,0:T(8,128)(2,1)} %copy-done.7, bf16[2,2,64,1024]{3,2,1,0:T(8,128)(2,1)} %copy-done.1, ...), custom_call_target="tpu_custom_call" | custom-call | tf_op jit(solution)/shard_map/partial_grad/pallas_call | solution.py:285
  97.1 4.3 %collective-permute-start.17 = (bf16[256,1024]{1,0:T(8,128)(2,1)}, bf16[256,1024]{1,0:T(8,128)(2,1)S(1)}, u32[]{:S(2)}, u32[]{:S(2)}) collective-permute-start(bf16[256,1024]{1,0:T(8,128)(2,1)} %get-tuple-element.61), channel_id=1, source_target_pairs={{0,8},{8,0},{16,24},{24,16},{32,40},{40,32},{48,56},{56,48},{64,72... | collective-permute-start | bytes 1572872 | tf_op jit(solution)/shard_map/t_sum_other_sibling/ppermute | solution.py:36
  101.4 0.7 collective-permute-done.26.refs_2_.refs_10_
  102.0 1.1 collective-permute-done.17
  103.1 1.4 add_convert_fusion.1
  104.5 12.4 %collective-permute-done.22.refs_7_.refs_11_ = bf16[2,2,64,1024]{3,2,1,0:T(8,128)(2,1)S(1)} collective-permute-done((bf16[2,2,64,1024]{3,2,1,0:T(8,128)(2,1)S(1)}, bf16[2,2,64,1024]{3,2,1,0:T(8,128)(2,1)S(1)}, u32[]{:S(2)}, u32[]{:S(2)}) %collective-permute-start.22) | collective-permute-done | bytes 524320 | tf_op jit(solution)/shard_map/t_q_up/ppermute | solution.py:52
  116.9 9.0 %weight_grad.3 = bf16[4,1024,256]{2,1,0:T(8,128)(2,1)} custom-call(bf16[2,2,64,1024]{3,2,1,0:T(8,128)(2,1)} %copy-done, bf16[2,2,64,1024]{3,2,1,0:T(8,128)(2,1)} %copy-done.3, bf16[2,2,64,1024]{3,2,1,0:T(8,128)(2,1)} %copy-done.5, bf16[2,2,64,1024]{3,2,1,0:T(8,128)(2,1)} %copy-done.2, bf16[2,2,64,1024]{3,2,1,0:T(8,128)(2,1)} %copy-done.1, ...), custom_call_target="tpu_custom_call" | custom-call | tf_op jit(solution)/shard_map/weight_grad/pallas_call | solution.py:325
  126.0 0.8 collective-permute-start.21
  126.7 11.6 %collective-permute-done.21.refs_6_.refs_10_ = bf16[2,2,64,1024]{3,2,1,0:T(8,128)(2,1)S(1)} collective-permute-done((bf16[2,2,64,1024]{3,2,1,0:T(8,128)(2,1)}, bf16[2,2,64,1024]{3,2,1,0:T(8,128)(2,1)S(1)}, u32[]{:S(2)}, u32[]{:S(2)}) %collective-permute-start.21) | collective-permute-done | bytes 524320 | tf_op jit(solution)/shard_map/t_q_far/ppermute | solution.py:56
  138.4 0.8 copy-done.13
  139.2 5.7 %partial_grad.6 = (f32[256,1024]{1,0:T(8,128)}, bf16[256,1024]{1,0:T(8,128)(2,1)}) custom-call(bf16[2,2,64,1024]{3,2,1,0:T(8,128)(2,1)} %copy-done.10, bf16[2,2,64,1024]{3,2,1,0:T(8,128)(2,1)} %copy-done.11, bf16[2,2,64,1024]{3,2,1,0:T(8,128)(2,1)} %collective-permute-done.26.refs_2_.refs_10_, ...), custom_call_target="tpu_custom_call" | custom-call | tf_op jit(solution)/shard_map/partial_grad/pallas_call | solution.py:285
  144.9 2.2 %collective-permute-start.27 = (bf16[256,1024]{1,0:T(8,128)(2,1)}, bf16[256,1024]{1,0:T(8,128)(2,1)S(1)}, u32[]{:S(2)}, u32[]{:S(2)}) collective-permute-start(bf16[256,1024]{1,0:T(8,128)(2,1)} %get-tuple-element.69), channel_id=1, source_target_pairs={{0,8},{8,0},{16,24},{24,16},{32,40},{40,32},{48,56},{56,48},{64,72... | collective-permute-start | bytes 1572872 | tf_op jit(solution)/shard_map/t_sum_other_flip_sibling/ppermute | solution.py:36
  147.2 1.7 collective-permute-done.27
  148.9 1.4 add_convert_fusion
  150.3 9.0 %weight_grad.2 = bf16[4,1024,256]{2,1,0:T(8,128)(2,1)} custom-call(bf16[2,2,64,1024]{3,2,1,0:T(8,128)(2,1)} %copy-done, bf16[2,2,64,1024]{3,2,1,0:T(8,128)(2,1)} %copy-done.3, bf16[2,2,64,1024]{3,2,1,0:T(8,128)(2,1)} %copy-done.5, bf16[2,2,64,1024]{3,2,1,0:T(8,128)(2,1)} %copy-done.2, bf16[2,2,64,1024]{3,2,1,0:T(8,128)(2,1)} %copy-done.1, ...), custom_call_target="tpu_custom_call" | custom-call | tf_op jit(solution)/shard_map/weight_grad/pallas_call | solution.py:325
  159.3 5.7 %partial_grad.4 = (f32[256,1024]{1,0:T(8,128)}, bf16[256,1024]{1,0:T(8,128)(2,1)}) custom-call(bf16[2,2,64,1024]{3,2,1,0:T(8,128)(2,1)} %copy-done, bf16[2,2,64,1024]{3,2,1,0:T(8,128)(2,1)} %copy-done.3, bf16[2,2,64,1024]{3,2,1,0:T(8,128)(2,1)} %copy-done.5, bf16[2,2,64,1024]{3,2,1,0:T(8,128)(2,1)} %copy-done.2, bf16[2,2,64,1024]{3,2,1,0:T(8,128)(2,1)} %copy-done, ...), custom_call_target="tpu_custom_call" | custom-call | tf_op jit(solution)/shard_map/partial_grad/pallas_call | solution.py:285
  165.0 0.4 collective-permute-start.14
  165.4 6.0 %partial_grad.7 = (f32[256,1024]{1,0:T(8,128)}, bf16[256,1024]{1,0:T(8,128)(2,1)}) custom-call(bf16[2,2,64,1024]{3,2,1,0:T(8,128)(2,1)} %copy-done.10, bf16[2,2,64,1024]{3,2,1,0:T(8,128)(2,1)} %copy-done.11, bf16[2,2,64,1024]{3,2,1,0:T(8,128)(2,1)} %collective-permute-done.26.refs_2_.refs_10_, ...), custom_call_target="tpu_custom_call" | custom-call | tf_op jit(solution)/shard_map/partial_grad/pallas_call | solution.py:285
  171.4 0.4 collective-permute-start.29
  171.8 2.6 %collective-permute-start.18 = (bf16[256,1024]{1,0:T(8,128)(2,1)S(1)}, bf16[256,1024]{1,0:T(8,128)(2,1)S(1)}, u32[]{:S(2)}, u32[]{:S(2)}) collective-permute-start(bf16[256,1024]{1,0:T(8,128)(2,1)S(1)} %add_convert_fusion.1), channel_id=1, source_target_pairs={{0,16},{8,24},{16,0},{24,8},{32,48},{40,56},{48,32},{56,40},{64,80... | collective-permute-start | bytes 1572872 | tf_op jit(solution)/shard_map/t_sum_other_across/ppermute | solution.py:40
  174.4 11.6 %collective-permute-done.29.rest_5_ = bf16[256,1024]{1,0:T(8,128)(2,1)S(1)} collective-permute-done((bf16[256,1024]{1,0:T(8,128)(2,1)S(1)}, bf16[256,1024]{1,0:T(8,128)(2,1)S(1)}, u32[]{:S(2)}, u32[]{:S(2)}) %collective-permute-start.29) | collective-permute-done | bytes 524320 | tf_op jit(solution)/shard_map/t_sum_other_flip_across/ppermute | solution.py:40
  186.0 11.2 %collective-permute-done.18.rest_2_ = bf16[256,1024]{1,0:T(8,128)(2,1)S(1)} collective-permute-done((bf16[256,1024]{1,0:T(8,128)(2,1)S(1)}, bf16[256,1024]{1,0:T(8,128)(2,1)S(1)}, u32[]{:S(2)}, u32[]{:S(2)}) %collective-permute-start.18) | collective-permute-done | bytes 524320 | tf_op jit(solution)/shard_map/t_sum_other_across/ppermute | solution.py:40
  197.3 0.8 copy-done.17
  198.0 9.3 %attend_grad.1 = (bf16[512,1024]{1,0:T(8,128)(2,1)}, bf16[512,128]{1,0:T(8,128)(2,1)}, bf16[512,128]{1,0:T(8,128)(2,1)}) custom-call(s32[4]{0:T(128)} %pad_add_fusion.place, bf16[512,1024]{1,0:T(8,128)(2,1)} %bitcast.29, bf16[512,128]{1,0:T(8,128)(2,1)} %bitcast.40, bf16[512,128]{1,0:T(8,128)(2,1)} %bitcast.42, f32[4,8,256]{2,1,0:T(8,128)} %get-tuple-element.49.stats, ...), custom_call_target="tpu_custom_call" | custom-call | tf_op jit(solution)/shard_map/attend_grad/pallas_call | solution.py:235
  207.4 2.8 %maximum_convert_fusion = f32[1024,512]{1,0:T(8,128)} fusion(bf16[1024,256]{1,0:T(8,128)(2,1)} %reduce-scatter.5.cloned.1.call-done, bf16[1024,256]{1,0:T(8,128)(2,1)} %reduce-scatter.3.cloned.1.call-done), kind=kLoop, calls=%fused_computation | loop fusion | flops 2097152 | bytes 3145728 | tf_op jit(solution)/shard_map/convert_element_type | solution.py:423
  (71 shorter events, 0.7 us)
Async XLA Ops:
  7.2 18.5 %copy-start.18 = (s32[1,64]{1,0:T(1,128)S(1)}, s32[1,64]{1,0:T(1,128)}, u32[]{:S(2)}) copy-start(s32[1,64]{1,0:T(1,128)} %param.10) | copy-start | bytes 772
  7.2 84.1 %all-gather.2.cloned.1.call-start = ((), (), s32[]{:S(2)}) async-start(), calls=%async_computation.2 | async-start | bytes 5242880 | tf_op jit(solution)/shard_map/all_gather | solution.py:354
  7.9 199.4 %reduce-scatter.3.cloned.1.call-start = ((), (), s32[]{:S(2)}) async-start(), calls=%async_computation.3 | async-start | bytes 2621440 | tf_op jit(solution)/shard_map/reduce_scatter | solution.py:407
  8.0 7.5 %collective-permute-start = (s32[64]{0:T(128)}, s32[64]{0:T(128)S(1)}, u32[]{:S(2)}, u32[]{:S(2)}) collective-permute-start(s32[64]{0:T(128)} %bitcast.43), channel_id=1, source_target_pairs={{0,1},{1,0},{2,3},{3,2},{4,5},{5,4},{6,7},{7,6},{8,9},{9,8},{10,11... | collective-permute-start | bytes 776 | tf_op jit(solution)/shard_map/t_ids_pair/ppermute | solution.py:48
  15.4 2.4 %collective-permute-start.1 = (bf16[2,64,1024]{2,1,0:T(8,128)(2,1)}, bf16[2,64,1024]{2,1,0:T(8,128)(2,1)S(1)}, u32[]{:S(2)}, u32[]{:S(2)}) collective-permute-start(bf16[2,64,1024]{2,1,0:T(8,128)(2,1)} %get-tuple-element.43), channel_id=1, source_target_pairs={{0,8},{8,0},{16,24},{24,16},{32,40},{40,32},{48,56},{56,48},{64,72... | collective-permute-start | bytes 786440 | tf_op jit(solution)/shard_map/t_near_sibling/ppermute | solution.py:36
  18.8 21.1 %copy-start = (bf16[2,2,64,1024]{3,2,1,0:T(8,128)(2,1)}, bf16[2,2,64,1024]{3,2,1,0:T(8,128)(2,1)S(1)}, u32[]{:S(2)}) copy-start(bf16[2,2,64,1024]{3,2,1,0:T(8,128)(2,1)S(1)} %pad_maximum_fusion.refs_0_.refs_4_) | copy-start | bytes 1572868
  18.8 18.6 %collective-permute-start.6 = (bf16[2,2,64,1024]{3,2,1,0:T(8,128)(2,1)S(1)}, bf16[2,2,64,1024]{3,2,1,0:T(8,128)(2,1)S(1)}, u32[]{:S(2)}, u32[]{:S(2)}) collective-permute-start(bf16[2,2,64,1024]{3,2,1,0:T(8,128)(2,1)S(1)} %pad_maximum_fusion.refs_0_.refs_4_), channel_id=1, source_target_pairs={{0,2},{1,3},{2,4},{3,5},{4,6},{5,7},{6,0},{7,1},{8,10},{9,11},{10,... | collective-permute-start | bytes 1572872 | tf_op jit(solution)/shard_map/t_n_up/ppermute | solution.py:52
  20.2 17.2 %collective-permute-start.7 = (bf16[2,2,64,1024]{3,2,1,0:T(8,128)(2,1)S(1)}, bf16[2,2,64,1024]{3,2,1,0:T(8,128)(2,1)S(1)}, u32[]{:S(2)}, u32[]{:S(2)}) collective-permute-start(bf16[2,2,64,1024]{3,2,1,0:T(8,128)(2,1)S(1)} %pad_maximum_fusion.refs_0_.refs_4_), channel_id=1, source_target_pairs={{0,6},{1,7},{2,0},{3,1},{4,2},{5,3},{6,4},{7,5},{8,14},{9,15},{10,... | collective-permute-start | bytes 1572872 | tf_op jit(solution)/shard_map/t_n_down/ppermute | solution.py:56
  21.7 8.8 %collective-permute-start.5 = (bf16[2,64,1024]{2,1,0:T(8,128)(2,1)}, bf16[2,64,1024]{2,1,0:T(8,128)(2,1)S(1)}, u32[]{:S(2)}, u32[]{:S(2)}) collective-permute-start(bf16[2,64,1024]{2,1,0:T(8,128)(2,1)} %get-tuple-element.45), channel_id=1, source_target_pairs={{0,16},{8,24},{16,0},{24,8},{32,48},{40,56},{48,32},{56,40},{64,80... | collective-permute-start | bytes 786440 | tf_op jit(solution)/shard_map/t_other_across/ppermute | solution.py:40
  24.2 13.2 %collective-permute-start.8 = (bf16[2,64,1024]{2,1,0:T(8,128)(2,1)}, bf16[2,64,1024]{2,1,0:T(8,128)(2,1)S(1)}, u32[]{:S(2)}, u32[]{:S(2)}) collective-permute-start(bf16[2,64,1024]{2,1,0:T(8,128)(2,1)} %get-tuple-element.47), channel_id=1, source_target_pairs={{0,24},{8,16},{16,8},{24,0},{32,56},{40,48},{48,40},{56,32},{64,88... | collective-permute-start | bytes 786440 | tf_op jit(solution)/shard_map/t_other_diagonal/ppermute | solution.py:44
  25.7 7.5 %collective-permute-start.2 = (s32[2,64]{1,0:T(2,128)S(1)}, s32[2,64]{1,0:T(2,128)S(1)}, u32[]{:S(2)}, u32[]{:S(2)}) collective-permute-start(s32[2,64]{1,0:T(2,128)S(1)} %add_select_fusion), channel_id=1, source_target_pairs={{0,6},{1,7},{2,0},{3,1},{4,2},{5,3},{6,4},{7,5},{8,14},{9,15},{10,... | collective-permute-start | bytes 1544 | tf_op jit(solution)/shard_map/t_ids_down/ppermute | solution.py:56
  30.5 5.0 %collective-permute-start.3 = (s32[2,64]{1,0:T(2,128)S(1)}, s32[2,64]{1,0:T(2,128)S(1)}, u32[]{:S(2)}, u32[]{:S(2)}) collective-permute-start(s32[2,64]{1,0:T(2,128)S(1)} %add_select_fusion), channel_id=1, source_target_pairs={{0,4},{1,5},{2,6},{3,7},{4,0},{5,1},{6,2},{7,3},{8,12},{9,13},{10,... | collective-permute-start | bytes 1544 | tf_op jit(solution)/shard_map/t_ids_far/ppermute | solution.py:369
  33.2 4.2 %collective-permute-start.4 = (s32[2,64]{1,0:T(2,128)S(1)}, s32[2,64]{1,0:T(2,128)S(1)}, u32[]{:S(2)}, u32[]{:S(2)}) collective-permute-start(s32[2,64]{1,0:T(2,128)S(1)} %add_select_fusion), channel_id=1, source_target_pairs={{0,2},{1,3},{2,4},{3,5},{4,6},{5,7},{6,0},{7,1},{8,10},{9,11},{10,... | collective-permute-start | bytes 1544 | tf_op jit(solution)/shard_map/t_ids_up/ppermute | solution.py:52
  37.4 19.1 %copy-start.2 = (bf16[2,2,64,1024]{3,2,1,0:T(8,128)(2,1)}, bf16[2,2,64,1024]{3,2,1,0:T(8,128)(2,1)S(1)}, u32[]{:S(2)}) copy-start(bf16[2,2,64,1024]{3,2,1,0:T(8,128)(2,1)S(1)} %collective-permute-done.6.refs_3_.refs_7_) | copy-start | bytes 1572868
  37.4 5.8 %copy-start.3 = (bf16[2,2,64,1024]{3,2,1,0:T(8,128)(2,1)}, bf16[2,2,64,1024]{3,2,1,0:T(8,128)(2,1)S(1)}, u32[]{:S(2)}) copy-start(bf16[2,2,64,1024]{3,2,1,0:T(8,128)(2,1)S(1)} %collective-permute-done.7.refs_1_.refs_5_) | copy-start | bytes 1572868
  39.1 14.8 %collective-permute-start.19 = (bf16[2,2,64,1024]{3,2,1,0:T(8,128)(2,1)}, bf16[2,2,64,1024]{3,2,1,0:T(8,128)(2,1)S(1)}, u32[]{:S(2)}, u32[]{:S(2)}) collective-permute-start(bf16[2,2,64,1024]{3,2,1,0:T(8,128)(2,1)} %pad_maximum_fusion.3), channel_id=1, source_target_pairs={{0,1},{1,0},{2,3},{3,2},{4,5},{5,4},{6,7},{7,6},{8,9},{9,8},{10,11... | collective-permute-start | bytes 1572872 | tf_op jit(solution)/shard_map/t_pair_1/ppermute | solution.py:48
  39.9 51.4 %copy-start.1 = (bf16[2,2,64,1024]{3,2,1,0:T(8,128)(2,1)}, bf16[2,2,64,1024]{3,2,1,0:T(8,128)(2,1)S(1)}, u32[]{:S(2)}) copy-start(bf16[2,2,64,1024]{3,2,1,0:T(8,128)(2,1)S(1)} %pad_maximum_fusion.1.refs_0_.refs_4_) | copy-start | bytes 1572868
  39.9 16.7 %collective-permute-start.12 = (bf16[2,2,64,1024]{3,2,1,0:T(8,128)(2,1)S(1)}, bf16[2,2,64,1024]{3,2,1,0:T(8,128)(2,1)S(1)}, u32[]{:S(2)}, u32[]{:S(2)}) collective-permute-start(bf16[2,2,64,1024]{3,2,1,0:T(8,128)(2,1)S(1)} %pad_maximum_fusion.1.refs_0_.refs_4_), channel_id=1, source_target_pairs={{0,6},{1,7},{2,0},{3,1},{4,2},{5,3},{6,4},{7,5},{8,14},{9,15},{10,... | collective-permute-start | bytes 1572872 | tf_op jit(solution)/shard_map/t_o_down/ppermute | solution.py:56
  43.2 18.0 %collective-permute-start.10 = (bf16[2,2,64,1024]{3,2,1,0:T(8,128)(2,1)}, bf16[2,2,64,1024]{3,2,1,0:T(8,128)(2,1)S(1)}, u32[]{:S(2)}, u32[]{:S(2)}) collective-permute-start(bf16[2,2,64,1024]{3,2,1,0:T(8,128)(2,1)} %pad_maximum_fusion.2), channel_id=1, source_target_pairs={{0,1},{1,0},{2,3},{3,2},{4,5},{5,4},{6,7},{7,6},{8,9},{9,8},{10,11... | collective-permute-start | bytes 1572872 | tf_op jit(solution)/shard_map/t_pair_0/ppermute | solution.py:48
  54.0 5.2 %copy-start.8 = (bf16[2,2,64,1024]{3,2,1,0:T(8,128)(2,1)}, bf16[2,2,64,1024]{3,2,1,0:T(8,128)(2,1)S(1)}, u32[]{:S(2)}) copy-start(bf16[2,2,64,1024]{3,2,1,0:T(8,128)(2,1)S(1)} %collective-permute-done.19.refs_4_.refs_8_) | copy-start | bytes 1572868
  54.0 31.3 %collective-permute-start.24 = (bf16[1024,512]{1,0:T(8,128)(2,1)}, bf16[1024,512]{1,0:T(8,128)(2,1)}, u32[]{:S(2)}, u32[]{:S(2)}) collective-permute-start(bf16[1024,512]{1,0:T(8,128)(2,1)} %get-tuple-element.65.refs_12_), channel_id=1, source_target_pairs={{0,16},{8,24},{16,0},{24,8},{32,48},{40,56},{48,32},{56,40},{64,80... | collective-permute-start | bytes 3145736 | tf_op jit(solution)/shard_map/t_out_across/ppermute | solution.py:40
  56.5 11.4 %collective-permute-start.9 = (bf16[2,2,64,1024]{3,2,1,0:T(8,128)(2,1)S(1)}, bf16[2,2,64,1024]{3,2,1,0:T(8,128)(2,1)S(1)}, u32[]{:S(2)}, u32[]{:S(2)}) collective-permute-start(bf16[2,2,64,1024]{3,2,1,0:T(8,128)(2,1)S(1)} %collective-permute-done.6.refs_3_.refs_7_), channel_id=1, source_target_pairs={{0,2},{1,3},{2,4},{3,5},{4,6},{5,7},{6,0},{7,1},{8,10},{9,11},{10,... | collective-permute-start | bytes 1572872 | tf_op jit(solution)/shard_map/t_n_far/ppermute | solution.py:52
  56.7 34.6 %copy-start.4 = (bf16[2,2,64,1024]{3,2,1,0:T(8,128)(2,1)}, bf16[2,2,64,1024]{3,2,1,0:T(8,128)(2,1)S(1)}, u32[]{:S(2)}) copy-start(bf16[2,2,64,1024]{3,2,1,0:T(8,128)(2,1)S(1)} %collective-permute-done.12.refs_1_.refs_5_) | copy-start | bytes 1572868
  56.7 13.9 %collective-permute-start.13 = (bf16[2,2,64,1024]{3,2,1,0:T(8,128)(2,1)S(1)}, bf16[2,2,64,1024]{3,2,1,0:T(8,128)(2,1)S(1)}, u32[]{:S(2)}, u32[]{:S(2)}) collective-permute-start(bf16[2,2,64,1024]{3,2,1,0:T(8,128)(2,1)S(1)} %collective-permute-done.12.refs_1_.refs_5_), channel_id=1, source_target_pairs={{0,6},{1,7},{2,0},{3,1},{4,2},{5,3},{6,4},{7,5},{8,14},{9,15},{10,... | collective-permute-start | bytes 1572872 | tf_op jit(solution)/shard_map/t_o_far/ppermute | solution.py:56
  61.2 18.0 %copy-start.10 = (bf16[2,2,64,1024]{3,2,1,0:T(8,128)(2,1)}, bf16[2,2,64,1024]{3,2,1,0:T(8,128)(2,1)S(1)}, u32[]{:S(2)}) copy-start(bf16[2,2,64,1024]{3,2,1,0:T(8,128)(2,1)S(1)} %collective-permute-done.10.refs_0_.refs_8_) | copy-start | bytes 1572868
  61.2 18.0 %collective-permute-start.11 = (bf16[2,2,64,1024]{3,2,1,0:T(8,128)(2,1)S(1)}, bf16[2,2,64,1024]{3,2,1,0:T(8,128)(2,1)S(1)}, u32[]{:S(2)}, u32[]{:S(2)}) collective-permute-start(bf16[2,2,64,1024]{3,2,1,0:T(8,128)(2,1)S(1)} %pad_maximum_fusion.1.refs_0_.refs_4_), channel_id=1, source_target_pairs={{0,2},{1,3},{2,4},{3,5},{4,6},{5,7},{6,0},{7,1},{8,10},{9,11},{10,... | collective-permute-start | bytes 1572872 | tf_op jit(solution)/shard_map/t_o_up/ppermute | solution.py:52
  67.9 29.2 %copy-start.5 = (bf16[2,2,64,1024]{3,2,1,0:T(8,128)(2,1)}, bf16[2,2,64,1024]{3,2,1,0:T(8,128)(2,1)S(1)}, u32[]{:S(2)}) copy-start(bf16[2,2,64,1024]{3,2,1,0:T(8,128)(2,1)S(1)} %collective-permute-done.9.refs_2_.refs_6_) | copy-start | bytes 1572868
  67.9 22.6 %collective-permute-start.15 = (bf16[2,2,64,1024]{3,2,1,0:T(8,128)(2,1)S(1)}, bf16[2,2,64,1024]{3,2,1,0:T(8,128)(2,1)}, u32[]{:S(2)}, u32[]{:S(2)}) collective-permute-start(bf16[2,2,64,1024]{3,2,1,0:T(8,128)(2,1)S(1)} %collective-permute-done.10.refs_0_.refs_8_), channel_id=1, source_target_pairs={{0,2},{1,3},{2,4},{3,5},{4,6},{5,7},{6,0},{7,1},{8,10},{9,11},{10,... | collective-permute-start | bytes 1572872 | tf_op jit(solution)/shard_map/t_p_up/ppermute | solution.py:52
  67.9 22.6 %collective-permute-start.16 = (bf16[2,2,64,1024]{3,2,1,0:T(8,128)(2,1)S(1)}, bf16[2,2,64,1024]{3,2,1,0:T(8,128)(2,1)S(1)}, u32[]{:S(2)}, u32[]{:S(2)}) collective-permute-start(bf16[2,2,64,1024]{3,2,1,0:T(8,128)(2,1)S(1)} %collective-permute-done.10.refs_0_.refs_8_), channel_id=1, source_target_pairs={{0,6},{1,7},{2,0},{3,1},{4,2},{5,3},{6,4},{7,5},{8,14},{9,15},{10,... | collective-permute-start | bytes 1572872 | tf_op jit(solution)/shard_map/t_p_down/ppermute | solution.py:56
  70.6 20.7 %copy-start.6 = (bf16[2,2,64,1024]{3,2,1,0:T(8,128)(2,1)}, bf16[2,2,64,1024]{3,2,1,0:T(8,128)(2,1)S(1)}, u32[]{:S(2)}) copy-start(bf16[2,2,64,1024]{3,2,1,0:T(8,128)(2,1)S(1)} %collective-permute-done.13.refs_2_.refs_6_) | copy-start | bytes 1572868
  79.2 12.1 %copy-start.7 = (bf16[2,2,64,1024]{3,2,1,0:T(8,128)(2,1)}, bf16[2,2,64,1024]{3,2,1,0:T(8,128)(2,1)S(1)}, u32[]{:S(2)}) copy-start(bf16[2,2,64,1024]{3,2,1,0:T(8,128)(2,1)S(1)} %collective-permute-done.11.refs_3_.refs_7_) | copy-start | bytes 1572868
  79.2 22.1 %collective-permute-start.20 = (bf16[2,2,64,1024]{3,2,1,0:T(8,128)(2,1)}, bf16[2,2,64,1024]{3,2,1,0:T(8,128)(2,1)}, u32[]{:S(2)}, u32[]{:S(2)}) collective-permute-start(bf16[2,2,64,1024]{3,2,1,0:T(8,128)(2,1)} %copy-done.8), channel_id=1, source_target_pairs={{0,6},{1,7},{2,0},{3,1},{4,2},{5,3},{6,4},{7,5},{8,14},{9,15},{10,... | collective-permute-start | bytes 1572872 | tf_op jit(solution)/shard_map/t_q_down/ppermute | solution.py:56
  85.2 31.6 %collective-permute-start.25 = (bf16[1024,512]{1,0:T(8,128)(2,1)}, bf16[1024,512]{1,0:T(8,128)(2,1)}, u32[]{:S(2)}, u32[]{:S(2)}) collective-permute-start(bf16[1024,512]{1,0:T(8,128)(2,1)} %collective-permute-done.24.refs_14_), channel_id=1, source_target_pairs={{0,8},{8,0},{16,24},{24,16},{32,40},{40,32},{48,56},{56,48},{64,72... | collective-permute-start | bytes 3145736 | tf_op jit(solution)/shard_map/t_out_other/ppermute | solution.py:36
  89.0 27.8 %collective-permute-start.23 = (bf16[1024,512]{1,0:T(8,128)(2,1)}, bf16[1024,512]{1,0:T(8,128)(2,1)}, u32[]{:S(2)}, u32[]{:S(2)}) collective-permute-start(bf16[1024,512]{1,0:T(8,128)(2,1)} %get-tuple-element.65.refs_12_), channel_id=1, source_target_pairs={{0,8},{8,0},{16,24},{24,16},{32,40},{40,32},{48,56},{56,48},{64,72... | collective-permute-start | bytes 3145736 | tf_op jit(solution)/shard_map/t_out_near/ppermute | solution.py:36
  90.5 0.8 copy-start.11
  91.3 10.8 %collective-permute-start.26 = (bf16[2,2,64,1024]{3,2,1,0:T(8,128)(2,1)}, bf16[2,2,64,1024]{3,2,1,0:T(8,128)(2,1)}, u32[]{:S(2)}, u32[]{:S(2)}) collective-permute-start(bf16[2,2,64,1024]{3,2,1,0:T(8,128)(2,1)} %collective-permute-done.15.refs_3_.refs_11_), channel_id=1, source_target_pairs={{0,2},{1,3},{2,4},{3,5},{4,6},{5,7},{6,0},{7,1},{8,10},{9,11},{10,... | collective-permute-start | bytes 1572872 | tf_op jit(solution)/shard_map/t_p_far/ppermute | solution.py:52
  91.3 10.0 %copy-start.9 = (bf16[2,2,64,1024]{3,2,1,0:T(8,128)(2,1)S(1)}, bf16[2,2,64,1024]{3,2,1,0:T(8,128)(2,1)}, u32[]{:S(2)}) copy-start(bf16[2,2,64,1024]{3,2,1,0:T(8,128)(2,1)} %copy-done.8) | copy-start | bytes 1572868
  97.1 6.0 %collective-permute-start.17 = (bf16[256,1024]{1,0:T(8,128)(2,1)}, bf16[256,1024]{1,0:T(8,128)(2,1)S(1)}, u32[]{:S(2)}, u32[]{:S(2)}) collective-permute-start(bf16[256,1024]{1,0:T(8,128)(2,1)} %get-tuple-element.61), channel_id=1, source_target_pairs={{0,8},{8,0},{16,24},{24,16},{32,40},{40,32},{48,56},{56,48},{64,72... | collective-permute-start | bytes 1572872 | tf_op jit(solution)/shard_map/t_sum_other_sibling/ppermute | solution.py:36
  101.4 15.5 %collective-permute-start.22 = (bf16[2,2,64,1024]{3,2,1,0:T(8,128)(2,1)S(1)}, bf16[2,2,64,1024]{3,2,1,0:T(8,128)(2,1)S(1)}, u32[]{:S(2)}, u32[]{:S(2)}) collective-permute-start(bf16[2,2,64,1024]{3,2,1,0:T(8,128)(2,1)S(1)} %copy-done.9), channel_id=1, source_target_pairs={{0,2},{1,3},{2,4},{3,5},{4,6},{5,7},{6,0},{7,1},{8,10},{9,11},{10,... | collective-permute-start | bytes 1572872 | tf_op jit(solution)/shard_map/t_q_up/ppermute | solution.py:52
  116.9 9.0 %copy-start.12 = (bf16[2,2,64,1024]{3,2,1,0:T(8,128)(2,1)}, bf16[2,2,64,1024]{3,2,1,0:T(8,128)(2,1)S(1)}, u32[]{:S(2)}) copy-start(bf16[2,2,64,1024]{3,2,1,0:T(8,128)(2,1)S(1)} %collective-permute-done.22.refs_7_.refs_11_) | copy-start | bytes 1572868
  125.9 81.4 %reduce-scatter.5.cloned.1.call-start = ((), (), s32[]{:S(2)}) async-start(), calls=%async_computation.4 | async-start | bytes 2621440 | tf_op jit(solution)/shard_map/reduce_scatter | solution.py:407
  126.0 12.4 %collective-permute-start.21 = (bf16[2,2,64,1024]{3,2,1,0:T(8,128)(2,1)}, bf16[2,2,64,1024]{3,2,1,0:T(8,128)(2,1)S(1)}, u32[]{:S(2)}, u32[]{:S(2)}) collective-permute-start(bf16[2,2,64,1024]{3,2,1,0:T(8,128)(2,1)} %collective-permute-done.20.refs_5_.refs_9_), channel_id=1, source_target_pairs={{0,6},{1,7},{2,0},{3,1},{4,2},{5,3},{6,4},{7,5},{8,14},{9,15},{10,... | collective-permute-start | bytes 1572872 | tf_op jit(solution)/shard_map/t_q_far/ppermute | solution.py:56
  138.4 0.8 copy-start.13
  144.9 4.0 %collective-permute-start.27 = (bf16[256,1024]{1,0:T(8,128)(2,1)}, bf16[256,1024]{1,0:T(8,128)(2,1)S(1)}, u32[]{:S(2)}, u32[]{:S(2)}) collective-permute-start(bf16[256,1024]{1,0:T(8,128)(2,1)} %get-tuple-element.69), channel_id=1, source_target_pairs={{0,8},{8,0},{16,24},{24,16},{32,40},{40,32},{48,56},{56,48},{64,72... | collective-permute-start | bytes 1572872 | tf_op jit(solution)/shard_map/t_sum_other_flip_sibling/ppermute | solution.py:36
  165.0 9.4 %collective-permute-start.14 = (bf16[256,1024]{1,0:T(8,128)(2,1)}, bf16[256,1024]{1,0:T(8,128)(2,1)S(1)}, u32[]{:S(2)}, u32[]{:S(2)}) collective-permute-start(bf16[256,1024]{1,0:T(8,128)(2,1)} %get-tuple-element.57), channel_id=1, source_target_pairs={{0,8},{8,0},{16,24},{24,16},{32,40},{40,32},{48,56},{56,48},{64,72... | collective-permute-start | bytes 1572872 | tf_op jit(solution)/shard_map/t_sum_near_sibling/ppermute | solution.py:36
  171.4 3.1 %collective-permute-start.28 = (bf16[256,1024]{1,0:T(8,128)(2,1)}, bf16[256,1024]{1,0:T(8,128)(2,1)S(1)}, u32[]{:S(2)}, u32[]{:S(2)}) collective-permute-start(bf16[256,1024]{1,0:T(8,128)(2,1)} %get-tuple-element.73), channel_id=1, source_target_pairs={{0,8},{8,0},{16,24},{24,16},{32,40},{40,32},{48,56},{56,48},{64,72... | collective-permute-start | bytes 1572872 | tf_op jit(solution)/shard_map/t_sum_near_flip_sibling/ppermute | solution.py:36
  171.4 14.7 %collective-permute-start.29 = (bf16[256,1024]{1,0:T(8,128)(2,1)S(1)}, bf16[256,1024]{1,0:T(8,128)(2,1)S(1)}, u32[]{:S(2)}, u32[]{:S(2)}) collective-permute-start(bf16[256,1024]{1,0:T(8,128)(2,1)S(1)} %add_convert_fusion), channel_id=1, source_target_pairs={{0,16},{8,24},{16,0},{24,8},{32,48},{40,56},{48,32},{56,40},{64,80... | collective-permute-start | bytes 1572872 | tf_op jit(solution)/shard_map/t_sum_other_flip_across/ppermute | solution.py:40
  171.8 25.5 %collective-permute-start.18 = (bf16[256,1024]{1,0:T(8,128)(2,1)S(1)}, bf16[256,1024]{1,0:T(8,128)(2,1)S(1)}, u32[]{:S(2)}, u32[]{:S(2)}) collective-permute-start(bf16[256,1024]{1,0:T(8,128)(2,1)S(1)} %add_convert_fusion.1), channel_id=1, source_target_pairs={{0,16},{8,24},{16,0},{24,8},{32,48},{40,56},{48,32},{56,40},{64,80... | collective-permute-start | bytes 1572872 | tf_op jit(solution)/shard_map/t_sum_other_across/ppermute | solution.py:40
  174.4 22.8 %copy-start.14 = (bf16[256,1024]{1,0:T(8,128)(2,1)}, bf16[256,1024]{1,0:T(8,128)(2,1)S(1)}, u32[]{:S(2)}) copy-start(bf16[256,1024]{1,0:T(8,128)(2,1)S(1)} %collective-permute-done.14.rest_1_) | copy-start | bytes 1572868
  174.4 22.8 %copy-start.15 = (bf16[256,1024]{1,0:T(8,128)(2,1)}, bf16[256,1024]{1,0:T(8,128)(2,1)S(1)}, u32[]{:S(2)}) copy-start(bf16[256,1024]{1,0:T(8,128)(2,1)S(1)} %collective-permute-done.28.rest_4_) | copy-start | bytes 1572868
  186.0 11.2 %copy-start.16 = (bf16[256,1024]{1,0:T(8,128)(2,1)}, bf16[256,1024]{1,0:T(8,128)(2,1)S(1)}, u32[]{:S(2)}) copy-start(bf16[256,1024]{1,0:T(8,128)(2,1)S(1)} %collective-permute-done.29.rest_5_) | copy-start | bytes 1572868
  197.2 0.8 copy-start.17
Sparse Core Ops, SparseCore 0:
  9.7 51.6 all-gather.1
  126.1 28.3 reduce-scatter.2
  159.4 28.7 reduce-scatter.4

commit v3 on v2

--- a/solution.py
+++ b/solution.py
@@ -30,6 +30,7 @@
 Y_UP = by_tensor(lambda i: (i + 2) % 8)
 Y_DOWN = by_tensor(lambda i: (i - 2) % 8)
 Z_GROUPS = [[z * 4 + j for z in range(4)] for j in range(4)]
+Y_GROUPS = [[y * 2 + low for y in range(4)] for low in range(2)]
 
 
 def sibling(x):
@@ -206,8 +207,8 @@
     for b in range(blocks):
         first, last = key_range(b)
         rows = pl.ds(pl.multiple_of(lax.rem(b - y + 4, 4) * half, half), half)
-        same = terms[0][rows] + terms[1][rows].astype(F32) + terms[2][rows].astype(F32)
-        flip = terms[3][rows] + terms[4][rows].astype(F32) + terms[5][rows].astype(F32)
+        same = terms[0][rows] + terms[1][0, rows].astype(F32) + terms[2][rows].astype(F32)
+        flip = terms[3][rows] + terms[4][0, rows].astype(F32) + terms[5][rows].astype(F32)
         grad = jnp.concatenate([jnp.where(low == 0, same, flip), jnp.where(low == 0, flip, same)], axis=0).astype(BF16)
         grad = jnp.concatenate([grad[:, :HD], grad[:, HD:]], axis=0)
         q2 = two_heads(q, b)
@@ -232,6 +233,7 @@
     length, wide = q.shape
     pairs, blocks = wide // (2 * HD), length // HD
     two = pl.BlockSpec((length, 2 * HD), lambda i: (0, i))
+    half = pl.BlockSpec((length // 2, 2 * HD), lambda i: (0, i))
     return pl.pallas_call(
         backward_kernel,
         grid=(pairs,),
@@ -243,7 +245,7 @@
             pl.BlockSpec((1, 2 * blocks, 2 * HD), lambda i: (i, 0, 0)),
             whole(bias.shape),
         ]
-        + [pl.BlockSpec((length // 2, 2 * HD), lambda i: (0, i))] * 6,
+        + [half, pl.BlockSpec((1, length // 2, 2 * HD), lambda i: (0, 0, i)), half] * 2,
         out_specs=[two, whole(k.shape), whole(v.shape)],
         out_shape=[jax.ShapeDtypeStruct(x.shape, BF16) for x in (q, k, v)],
         scratch_shapes=[pltpu.VMEM((HD, length), BF16), pltpu.VMEM(k.shape, F32), pltpu.VMEM(v.shape, F32)],
@@ -253,86 +255,95 @@
     )(place, q, k, v, stats, bias, *terms)
 
 
-def partial_kernel(*refs):
-    pieces, (weight, keep, give, x) = refs[:8], refs[8:]
-    _, _, seq, cols = pieces[0].shape
+def reader(place, refs):
+    y = place[0]
+    if len(refs) == 8:
+        return lambda p, i, e, k: refs[p * 4 + k][e, i]
+    return lambda p, i, e, k: refs[e][lax.rem(y + k, 4), p, i]
+
+
+def partial_kernel(count, place, *refs):
+    read = reader(place, refs[:count])
+    weight, keep_near, keep_other, give, x = refs[count:]
+    seq = refs[count - 1].shape[-2]
+    cols = refs[count - 1].shape[-1]
     half = 4 * seq
     width = weight.shape[2] // 2
 
     @pl.when(pl.program_id(0) == 0)
     def _():
         for e in range(2):
-            for i in range(2):
-                for j in range(4):
-                    at = i * half + j * seq
-                    x[at : at + seq, e * cols : (e + 1) * cols] = pieces[e * 4 + j][0, i]
+            for p in range(2):
+                for i in range(2):
+                    for k in range(4):
+                        at = (p * 2 + i) * half + k * seq
+                        x[at : at + seq, e * cols : (e + 1) * cols] = read(p, i, e, k)
 
     w = jnp.concatenate([weight[j, :, e * width : (e + 1) * width] for e in range(2) for j in range(4)], axis=1)
-    total = nt(x[...], w)
-    keep[...] = total[:half]
-    give[...] = total[half:].astype(BF16)
-
-
-def partial(pieces, weight):
-    _, _, seq, cols = pieces[0][0].shape
+    for p, keep in enumerate((keep_near, keep_other)):
+        total = nt(x[p * 2 * half : (p + 1) * 2 * half], w)
+        keep[...] = total[:half]
+        give[p] = total[half:].astype(BF16)
+
+
+def partial(place, pieces, weight):
+    seq, cols = pieces[-1].shape[-2:]
     heads = weight.shape[1]
     tile = heads // 2
     out = pl.BlockSpec((4 * seq, tile), lambda i: (0, i))
-
-    def spec(index):
-        return pl.BlockSpec((1, 2, seq, cols), lambda i: (index, 0, 0, 0))
-
+    shape = jax.ShapeDtypeStruct((4 * seq, heads), F32)
     return pl.pallas_call(
-        partial_kernel,
+        functools.partial(partial_kernel, len(pieces)),
         grid=(2,),
-        in_specs=[spec(index) for _, index in pieces] + [pl.BlockSpec((4, tile, cols // 2), lambda i: (0, i, 0))],
-        out_specs=[out, out],
-        out_shape=[jax.ShapeDtypeStruct((4 * seq, heads), F32), jax.ShapeDtypeStruct((4 * seq, heads), BF16)],
-        scratch_shapes=[pltpu.VMEM((8 * seq, 2 * cols), BF16)],
+        in_specs=[SMEM()] + [whole(x.shape) for x in pieces] + [pl.BlockSpec((4, tile, cols // 2), lambda i: (0, i, 0))],
+        out_specs=[out, out, pl.BlockSpec((2, 4 * seq, tile), lambda i: (0, 0, i))],
+        out_shape=[shape, shape, jax.ShapeDtypeStruct((2, 4 * seq, heads), BF16)],
+        scratch_shapes=[pltpu.VMEM((16 * seq, 2 * cols), BF16)],
         compiler_params=params(),
         cost_estimate=LIGHT,
         name="partial_grad",
-    )(*[x for x, _ in pieces], weight)
-
-
-def wgrad_kernel(*refs):
-    near, other, flip, outs, (out, x) = refs[:4], refs[4:8], refs[8:12], refs[12:16], refs[16:]
-    _, _, seq, cols = near[0].shape
+    )(place, *pieces, weight)
+
+
+def wgrad_kernel(place, *refs):
+    same, flip, outs, (out, x) = refs[:8], refs[8], refs[9:13], refs[13:]
+    seq = same[0].shape[2]
     length = 8 * seq
-    for i in range(2):
-        for j in range(4):
-            for row, block in ((i, near[j][0, i]), (2 + i, other[j][0, i])):
-                at = row * length + 2 * j * seq
-                x[at : at + seq] = block
-            for row, block in ((i, flip[j][0, i]), (2 + i, flip[j][1, i])):
-                at = row * length + (2 * j + 1) * seq
-                x[at : at + seq] = block
+    y = place[0]
+    for p in range(2):
+        for i in range(2):
+            for k in range(4):
+                at = (p * 2 + i) * length + 2 * k * seq
+                x[at : at + seq] = same[p * 4 + k][0, i]
+                x[at + seq : at + 2 * seq] = flip[lax.rem(y + k, 4), p, i]
     tile = 256
     width = out.shape[2]
     for m in range(0, out.shape[1], tile):
         total = nn(outs[0][m : m + tile], x[:length])
         for r in range(1, 4):
             total += nn(outs[r][m : m + tile], x[r * length : (r + 1) * length])
-        for k in range(cols // width):
+        for k in range(2):
             out[k, m : m + tile] = total[:, k * width : (k + 1) * width].astype(BF16)
 
 
-def wgrad(half, near, other, flip, outs):
-    _, _, seq, cols = near[0].shape
+def wgrad(place, half, same, flip, outs):
+    _, _, seq, cols = same[0].shape
     heads = outs[0].shape[0]
     wide = cols // 2
-    same = pl.BlockSpec((1, 2, seq, wide), lambda i: (half, 0, 0, i))
     return pl.pallas_call(
         wgrad_kernel,
         grid=(2,),
-        in_specs=[same] * 8 + [pl.BlockSpec((2, 2, seq, wide), lambda i: (0, 0, 0, i))] * 4 + [whole(outs[0].shape)] * 4,
+        in_specs=[SMEM()]
+        + [pl.BlockSpec((1, 2, seq, wide), lambda i: (half, 0, 0, i))] * 8
+        + [pl.BlockSpec((4, 2, 2, seq, wide), lambda i: (0, 0, 0, 0, i))]
+        + [whole(outs[0].shape)] * 4,
         out_specs=pl.BlockSpec((2, heads, wide // 2), lambda i: (i, 0, 0)),
         out_shape=jax.ShapeDtypeStruct((4, heads, wide // 2), BF16),
         scratch_shapes=[pltpu.VMEM((32 * seq, wide), BF16)],
         compiler_params=params(),
         cost_estimate=LIGHT,
         name="weight_grad",
-    )(*near, *other, *flip, *outs)
+    )(place, *same, flip, *outs)
 
 
 def named(name, fn, x):
@@ -374,52 +385,40 @@
     other = jnp.stack([after(from_across, n_up, n_down, ids_up, ids_down, ids_far), from_diagonal], axis=1)
     flips = [named("pair_%d" % e, pair, jnp.stack([near[e], other[e]])) for e in range(2)]
 
-    def to_row(name, pieces):
-        keep, give = partial(pieces, weight)
-        total = (keep + named(name + "_sibling", sibling, give).astype(F32)).astype(BF16)
-        return named(name + "_across", across, total), total
-
-    def for_row(name, pieces):
-        keep, give = partial(pieces, weight)
-        return keep, named(name + "_sibling", sibling, give)
-
-    n, o, p, q = near, other, flips[0], flips[1]
-    attn_out, stats, bias = forward(place, whole_segs, after(query, other, n_up, n_down), key, value)
-    out_across = named("out_across", across, after(attn_out, q))
-
-    n_far, o_down = named("n_far", y_up, after(n_up, n_down)), named("o_down", y_down, after(o, ids))
-    o_up, o_far = named("o_up", y_up, after(o, n_up, n_down, p, attn_out)), named("o_far", y_down, after(o_down, attn_out))
-    p = after(p, n_far, o_down)
-    p_up, p_down = named("p_up", y_up, p), named("p_down", y_down, p)
+    n, o = near, other
+    n_far, o_down = named("n_far", y_up, after(n_up, n_down)), named("o_down", y_down, after(o, whole_segs))
+    attn_out, stats, bias = forward(place, whole_segs, after(query, n_far, o_down), key, value)
+    out_across = named("out_across", across, attn_out)
+    o_up, o_far = named("o_up", y_up, after(o, n_up, n_down)), named("o_far", y_down, o_down)
+    flips[0] = after(flips[0], n_far, o_down)
+    flips[1] = after(flips[1], attn_out)
+    flips = [lax.all_gather(x, "tensor", axis=0, axis_index_groups=Y_GROUPS) for x in flips]
     near_blocks = [n, n_down, n_far, n_up]
     other_blocks = [o, o_down, o_far, o_up]
-    terms_same = for_row("sum_near", [(x, e) for e in range(2) for x in [n, n_down, n_far, after(n_up, o_up, o_far)]])
-    p_far = named("p_far", y_up, p_up)
-    q_down = named("q_down", y_down, after(q, o_up, o_far))
-    sent_same, sum_other = to_row("sum_other", [(x, e) for e in range(2) for x in [o, o_down, o_far, after(o_up, p_up, p_down)]])
-    q_up, q_far = named("q_up", y_up, after(q, p_up, p_down)), named("q_far", y_down, q_down)
+    same = [*near_blocks, *other_blocks]
+
+    def sums(name, pieces):
+        keep_near, keep_other, give = partial(place, pieces, weight)
+        given = named(name + "_sibling", sibling, give)
+        total = (keep_other + given[1].astype(F32)).astype(BF16)
+        return keep_near, given, named(name + "_across", across, total)
+
+    terms_same = sums("sum_same", same)
     out_near = named("out_near", sibling, after(attn_out, o_up, o_far))
     out_other = named("out_other", sibling, after(out_across, o_up, o_far))
     outs = (attn_out, out_near, out_across, out_other)
-    flip_blocks = [[p, p_down, after(p_far, q_down), p_up], [q, q_down, q_far, q_up]]
 
     def sum_z(x):
         return lax.psum_scatter(
             x.reshape(4 * heads, width // 2), "dp", scatter_dimension=0, tiled=True, axis_index_groups=Z_GROUPS
         )
 
-    first = wgrad(0, near_blocks, other_blocks, flip_blocks[0], (*outs[:3], after(out_other, sum_other, q_up)))
-    first_sum = sum_z(first)
-
-    def flipped(row):
-        return [(x, row) for e in range(2) for x in flip_blocks[e]]
-
-    sent_flip, sum_other_flip = to_row("sum_other_flip", flipped(1))
-    last = wgrad(1, near_blocks, other_blocks, flip_blocks[1], (*outs[:3], after(out_other, sum_other_flip)))
+    first = wgrad(place, 0, same, flips[0], (*outs[:3], after(out_other, terms_same[1])))
+    first_sum = sum_z(after(first, flips[1], terms_same[2]))
+    terms_flip = sums("sum_flip", [flips[0], after(flips[1], first)])
+    last = wgrad(place, 1, same, flips[1], (*outs[:3], after(out_other, terms_flip[1])))
     last_sum = sum_z(last)
-    terms_flip = for_row("sum_near_flip", [(after(x, last) if i == 0 else x, r) for i, (x, r) in enumerate(flipped(0))])
-    terms = [*terms_same, sent_same, *terms_flip, sent_flip]
-    dq, dk, dv = backward(place, query, key, value, stats, bias, terms)
+    dq, dk, dv = backward(place, query, key, value, stats, bias, [*terms_same, *terms_flip])
     weight_grad = jnp.concatenate([first_sum, last_sum], axis=1).astype(F32)
     return (dq[None], dk[None], dv[None], weight_grad)
 

time: 217 us -> 209 us (0.963)
  waiting for transfers between devices: 83.1 us -> 74.6 us
  Pallas kernels: 62.7 us -> 57.3 us
  local copies, waits for them, and re-layouts: 5.02 us -> 8.14 us
  starting transfers between devices: 40.2 us -> 42.6 us
    ppermute x7 -> x4, waiting for transfers between devices: 31.2 us -> 7.49 us  [y_up(): return lax.ppermute(x, 'tensor', Y_UP)]
    ppermute x4, waiting for transfers between devices: 32 us -> 11.9 us  [across(): return lax.ppermute(x, 'dp', ACROSS)]
    reduce_scatter x2, waiting for transfers between devices: 0.04 us -> 17.3 us  [sum_z(): lax.psum_scatter(x.reshape(4 * heads, width // 2), 'dp', scatter_dimensio...]
    all_gather x0 -> x2, waiting for transfers between devices: none -> 11.5 us  [shards(): lax.all_gather(x, 'tensor', axis=0, axis_index_groups=Y_GROUPS)]
    pallas_call x6 -> x4, Pallas kernels: 41.2 us -> 35.9 us  [the longest x2 18 us: wgrad(): pl.pallas_call(wgrad_kernel, grid=(2,), in_specs=[SMEM()] + [pl.BlockSpec...]
    ppermute x7 -> x4, waiting for transfers between devices: 12.9 us -> 18 us  [y_down(): return lax.ppermute(x, 'tensor', Y_DOWN)]
    ppermute x7 -> x4, starting transfers between devices: 10.6 us -> 6.34 us  [y_down(): return lax.ppermute(x, 'tensor', Y_DOWN)]
    ppermute x7 -> x5, starting transfers between devices: 11.7 us -> 14.8 us  [sibling(): return lax.ppermute(x, 'dp', SIBLING)]
  transfers between devices with their start and end apart: 33 -> 27, of which waited for: 16 -> 14; matrix products, arithmetic and copies ran while one was open for 5% -> 6% of each run, Pallas kernels for 25% -> 27%
where the time goes in v3:
time: 209 us; the launch traced here: 208 us
  waiting for transfers between devices  74.6 us (36%)
  Pallas kernels  57.3 us (27%)
  starting transfers between devices  42.6 us (20%)
  between operations  14 us (7%)
  other arithmetic  11.8 us (6%)
  local copies, waits for them, and re-layouts  8.14 us (4%)
    pallas_call x2, Pallas kernels, wgrad(): pl.pallas_call(wgrad_kernel, grid=(2,), in_specs=[SMEM()] + [pl.BlockSpec...  18 us
    ppermute x4, waiting for transfers between devices, y_down(): return lax.ppermute(x, 'tensor', Y_DOWN)  18 us
    pallas_call x2, Pallas kernels, partial(): pl.pallas_call(functools.partial(partial_kernel, len(pieces)), grid=(2,),...  17.8 us
    reduce_scatter x2, waiting for transfers between devices, sum_z(): lax.psum_scatter(x.reshape(4 * heads, width // 2), 'dp', scatter_dimensio...  17.3 us
    ppermute x5, starting transfers between devices, sibling(): return lax.ppermute(x, 'dp', SIBLING)  14.8 us
    ppermute x4, waiting for transfers between devices, across(): return lax.ppermute(x, 'dp', ACROSS)  11.9 us
    all_gather x2, waiting for transfers between devices, shards(): lax.all_gather(x, 'tensor', axis=0, axis_index_groups=Y_GROUPS)  11.5 us
    ppermute x4, starting transfers between devices, across(): return lax.ppermute(x, 'dp', ACROSS)  10 us
  transfers between devices with their start and end apart: 27, of which 14 were waited for; matrix products, arithmetic and copies ran while one was open for 6% of the time, Pallas kernels for 27%

profile of v3, /device:TPU:1, one launch (start us, length us, event | category | flops | bytes accessed | tf_op | source)
XLA Modules:
  0.0 208.5 jit_solution(11531173568273626393)
XLA Ops:
  7.2 0.7 all-gather.6.cloned.1.call-update
  8.0 2.1 %collective-permute-start = (s32[64]{0:T(128)}, s32[64]{0:T(128)S(1)}, u32[]{:S(2)}, u32[]{:S(2)}) collective-permute-start(s32[64]{0:T(128)} %bitcast.57), channel_id=1, source_target_pairs={{0,1},{1,0},{2,3},{3,2},{4,5},{5,4},{6,7},{7,6},{8,9},{9,8},{10,11... | collective-permute-start | bytes 776 | tf_op jit(solution)/shard_map/t_ids_pair/ppermute | solution.py:49
  10.1 0.6 pad_add_fusion.place
  10.7 1.3 broadcast_in_dim.21.segs
  12.0 3.4 %prep.1 = (bf16[2,64,1024]{2,1,0:T(8,128)(2,1)}, bf16[2,64,1024]{2,1,0:T(8,128)(2,1)}, bf16[2,64,1024]{2,1,0:T(8,128)(2,1)}, bf16[2,64,1024]{2,1,0:T(8,128)(2,1)}) custom-call(s32[4]{0:T(128)} %pad_add_fusion.place, f32[1,4]{1,0:T(1,128)} %margins.1, s32[64,128]{1,0:T(8,128)} %broadcast_in_dim.21.segs, bf16[64,8192]{1,0:T(8,128)(2,1)} %bitcast.44), custom_call_target="tpu_custom_call" | custom-call | tf_op jit(solution)/shard_map/prep/pallas_call | solution.py:105
  15.4 1.0 collective-permute-start.1
  16.5 1.4 collective-permute-done.1
  17.9 1.0 pad_maximum_fusion.refs_0_
  18.9 1.4 collective-permute-start.5
  20.2 1.5 collective-permute-start.6
  21.7 2.5 %collective-permute-start.8 = (bf16[2,64,1024]{2,1,0:T(8,128)(2,1)}, bf16[2,64,1024]{2,1,0:T(8,128)(2,1)S(1)}, u32[]{:S(2)}, u32[]{:S(2)}) collective-permute-start(bf16[2,64,1024]{2,1,0:T(8,128)(2,1)} %get-tuple-element.40), channel_id=1, source_target_pairs={{0,16},{8,24},{16,0},{24,8},{32,48},{40,56},{48,32},{56,40},{64,80... | collective-permute-start | bytes 786440 | tf_op jit(solution)/shard_map/t_other_across/ppermute | solution.py:41
  24.2 1.5 collective-permute-start.9
  25.7 1.6 collective-permute-start.2
  27.3 5.9 %collective-permute-done.2 = s32[2,64]{1,0:T(2,128)S(1)} collective-permute-done((s32[2,64]{1,0:T(2,128)S(1)}, s32[2,64]{1,0:T(2,128)S(1)}, u32[]{:S(2)}, u32[]{:S(2)}) %collective-permute-start.2) | collective-permute-done | bytes 544 | tf_op jit(solution)/shard_map/t_ids_down/ppermute | solution.py:57
  33.2 2.6 %collective-permute-start.3 = (s32[2,64]{1,0:T(2,128)S(1)}, s32[2,64]{1,0:T(2,128)S(1)}, u32[]{:S(2)}, u32[]{:S(2)}) collective-permute-start(s32[2,64]{1,0:T(2,128)S(1)} %add_select_fusion), channel_id=1, source_target_pairs={{0,4},{1,5},{2,6},{3,7},{4,0},{5,1},{6,2},{7,3},{8,12},{9,13},{10,... | collective-permute-start | bytes 1544 | tf_op jit(solution)/shard_map/t_ids_far/ppermute | solution.py:380
  35.8 1.4 collective-permute-done.3
  37.1 1.6 collective-permute-start.4
  38.8 1.8 fusion.5
  40.6 0.1 stack.79
  40.7 0.1 stack.80
  40.8 0.1 stack.81
  40.9 0.5 collective-permute-done.4
  41.4 0.1 stack.82
  41.7 0.6 copy-done.13
  42.3 0.9 broadcast_in_dim.23.segs
  43.2 1.5 collective-permute-start.10
  44.6 1.7 fusion.3
  46.4 0.4 collective-permute-start.15
  46.8 6.8 %collective-permute-done.10.refs_5_ = bf16[2,2,64,1024]{3,2,1,0:T(8,128)(2,1)S(1)} collective-permute-done((bf16[2,2,64,1024]{3,2,1,0:T(8,128)(2,1)S(1)}, bf16[2,2,64,1024]{3,2,1,0:T(8,128)(2,1)S(1)}, u32[]{:S(2)}, u32[]{:S(2)}) %collective-permute-start.10) | collective-permute-done | bytes 524320 | tf_op jit(solution)/shard_map/t_o_down/ppermute | solution.py:57
  53.6 2.3 %collective-permute-done.7.refs_2_ = bf16[2,2,64,1024]{3,2,1,0:T(8,128)(2,1)S(1)} collective-permute-done((bf16[2,2,64,1024]{3,2,1,0:T(8,128)(2,1)S(1)}, bf16[2,2,64,1024]{3,2,1,0:T(8,128)(2,1)S(1)}, u32[]{:S(2)}, u32[]{:S(2)}) %collective-permute-start.7) | collective-permute-done | bytes 524320 | tf_op jit(solution)/shard_map/t_n_far/ppermute | solution.py:53
  55.9 0.4 collective-permute-done.15
  56.4 1.1 pad_maximum_fusion.3
  57.5 0.5 collective-permute-start.16
  58.0 8.8 %attend.1 = (bf16[1024,512]{1,0:T(8,128)(2,1)}, f32[4,8,256]{2,1,0:T(8,128)}, f32[4,384,128]{2,1,0:T(8,128)}) custom-call(s32[4]{0:T(128)} %pad_add_fusion.place, s32[512,128]{1,0:T(8,128)} %broadcast_in_dim.23.segs, bf16[512,1024]{1,0:T(8,128)(2,1)} %bitcast.42, bf16[512,128]{1,0:T(8,128)(2,1)} %bitcast.53, bf16[512,128]{1,0:T(8,128)(2,1)} %bitcast.55), custom_call_target="tpu_custom_call" | custom-call | tf_op jit(solution)/shard_map/attend/pallas_call | solution.py:168
  66.8 0.8 copy-done.15
  67.7 1.0 collective-permute-start.12
  68.7 1.8 collective-permute-start.11
  70.5 2.6 %collective-permute-start.18 = (bf16[1024,512]{1,0:T(8,128)(2,1)}, bf16[1024,512]{1,0:T(8,128)(2,1)}, u32[]{:S(2)}, u32[]{:S(2)}) collective-permute-start(bf16[1024,512]{1,0:T(8,128)(2,1)} %get-tuple-element.54.refs_9_), channel_id=1, source_target_pairs={{0,16},{8,24},{16,0},{24,8},{32,48},{40,56},{48,32},{56,40},{64,80... | collective-permute-start | bytes 3145736 | tf_op jit(solution)/shard_map/t_out_across/ppermute | solution.py:41
  73.0 4.6 %collective-permute-done.12.refs_7_ = bf16[2,2,64,1024]{3,2,1,0:T(8,128)(2,1)S(1)} collective-permute-done((bf16[2,2,64,1024]{3,2,1,0:T(8,128)(2,1)S(1)}, bf16[2,2,64,1024]{3,2,1,0:T(8,128)(2,1)S(1)}, u32[]{:S(2)}, u32[]{:S(2)}) %collective-permute-start.12) | collective-permute-done | bytes 524320 | tf_op jit(solution)/shard_map/t_o_up/ppermute | solution.py:53
  77.7 5.4 %collective-permute-done.11.refs_6_ = bf16[2,2,64,1024]{3,2,1,0:T(8,128)(2,1)S(1)} collective-permute-done((bf16[2,2,64,1024]{3,2,1,0:T(8,128)(2,1)S(1)}, bf16[2,2,64,1024]{3,2,1,0:T(8,128)(2,1)S(1)}, u32[]{:S(2)}, u32[]{:S(2)}) %collective-permute-start.11) | collective-permute-done | bytes 524320 | tf_op jit(solution)/shard_map/t_o_far/ppermute | solution.py:57
  83.1 0.8 copy-done.7
  83.8 9.0 %partial_grad.2 = (f32[256,1024]{1,0:T(8,128)}, f32[256,1024]{1,0:T(8,128)}, bf16[2,256,1024]{2,1,0:T(8,128)(2,1)}) custom-call(s32[4]{0:T(128)} %pad_add_fusion.place, bf16[2,2,64,1024]{3,2,1,0:T(8,128)(2,1)} %copy-done, bf16[2,2,64,1024]{3,2,1,0:T(8,128)(2,1)} %copy-done.3, bf16[2,2,64,1024]{3,2,1,0:T(8,128)(2,1)} %copy-done.5, ...), custom_call_target="tpu_custom_call" | custom-call | tf_op jit(solution)/shard_map/partial_grad/pallas_call | solution.py:295
  92.8 12.6 %collective-permute-start.13 = (bf16[2,256,1024]{2,1,0:T(8,128)(2,1)}, bf16[2,256,1024]{2,1,0:T(8,128)(2,1)S(1)}, u32[]{:S(2)}, u32[]{:S(2)}) collective-permute-start(bf16[2,256,1024]{2,1,0:T(8,128)(2,1)} %get-tuple-element.49), channel_id=1, source_target_pairs={{0,8},{8,0},{16,24},{24,16},{32,40},{40,32},{48,56},{56,48},{64,72... | collective-permute-start | bytes 3145736 | tf_op jit(solution)/shard_map/t_sum_same_sibling/ppermute | solution.py:37
  105.5 0.1 collective-permute-start.19
  105.6 0.4 collective-permute-start.17
  106.0 2.0 collective-permute-done.13.rest_1_
  108.0 2.5 %fusion.1 = bf16[256,1024]{1,0:T(8,128)(2,1)} fusion(f32[256,1024]{1,0:T(8,128)} %get-tuple-element.50, bf16[2,256,1024]{2,1,0:T(8,128)(2,1)S(1)} %collective-permute-done.13.rest_1_), kind=kLoop, calls=%fused_computation.4 | loop fusion | flops 786432 | bytes 2097152 | tf_op jit(solution)/shard_map/convert_element_type | solution.py:403
  110.5 2.2 %collective-permute-start.14 = (bf16[256,1024]{1,0:T(8,128)(2,1)}, bf16[256,1024]{1,0:T(8,128)(2,1)}, u32[]{:S(2)}, u32[]{:S(2)}) collective-permute-start(bf16[256,1024]{1,0:T(8,128)(2,1)} %fusion.1), channel_id=1, source_target_pairs={{0,16},{8,24},{16,0},{24,8},{32,48},{40,56},{48,32},{56,40},{64,80... | collective-permute-start | bytes 1572872 | tf_op jit(solution)/shard_map/t_sum_same_across/ppermute | solution.py:41
  112.8 0.9 copy-done.8
  113.7 0.4 copy-done.9
  114.1 8.9 %weight_grad.2 = bf16[4,1024,256]{2,1,0:T(8,128)(2,1)} custom-call(s32[4]{0:T(128)} %pad_add_fusion.place, bf16[2,2,64,1024]{3,2,1,0:T(8,128)(2,1)} %copy-done, bf16[2,2,64,1024]{3,2,1,0:T(8,128)(2,1)} %copy-done.3, bf16[2,2,64,1024]{3,2,1,0:T(8,128)(2,1)} %copy-done.5, bf16[2,2,64,1024]{3,2,1,0:T(8,128)(2,1)} %copy-done.2, ...), custom_call_target="tpu_custom_call" | custom-call | tf_op jit(solution)/shard_map/weight_grad/pallas_call | solution.py:333
  123.0 11.4 %all-gather.10.cloned.1.call-done = bf16[8,2,64,1024]{3,2,1,0:T(8,128)(2,1)} async-done(((bf16[2,2,64,1024]{3,2,1,0:T(8,128)(2,1)}), bf16[8,2,64,1024]{3,2,1,0:T(8,128)(2,1)}) %all-gather.10.cloned.1.call-update) | async-done | bytes 2097168 | tf_op jit(solution)/shard_map/all_gather | solution.py:395
  134.5 8.8 %partial_grad.3 = (f32[256,1024]{1,0:T(8,128)}, f32[256,1024]{1,0:T(8,128)}, bf16[2,256,1024]{2,1,0:T(8,128)(2,1)}) custom-call(s32[4]{0:T(128)} %pad_add_fusion.place, bf16[4,2,2,64,1024]{4,3,2,1,0:T(8,128)(2,1)} %bitcast.39, bf16[4,2,2,64,1024]{4,3,2,1,0:T(8,128)(2,1)} %bitcast.40, bf16[4,1024,512]{2,1,0:T(8,128)(2,1)} %bitcast.35), custom_call_target="tpu_custom_call" | custom-call | tf_op jit(solution)/shard_map/partial_grad/pallas_call | solution.py:295
  143.3 0.7 collective-permute-start.20
  144.0 2.5 %collective-permute-done.20.rest_4_ = bf16[2,256,1024]{2,1,0:T(8,128)(2,1)S(1)} collective-permute-done((bf16[2,256,1024]{2,1,0:T(8,128)(2,1)}, bf16[2,256,1024]{2,1,0:T(8,128)(2,1)S(1)}, u32[]{:S(2)}, u32[]{:S(2)}) %collective-permute-start.20) | collective-permute-done | bytes 1048608 | tf_op jit(solution)/shard_map/t_sum_flip_sibling/ppermute | solution.py:37
  146.5 9.1 %weight_grad.3 = bf16[4,1024,256]{2,1,0:T(8,128)(2,1)} custom-call(s32[4]{0:T(128)} %pad_add_fusion.place, bf16[2,2,64,1024]{3,2,1,0:T(8,128)(2,1)} %copy-done, bf16[2,2,64,1024]{3,2,1,0:T(8,128)(2,1)} %copy-done.3, bf16[2,2,64,1024]{3,2,1,0:T(8,128)(2,1)} %copy-done.5, bf16[2,2,64,1024]{3,2,1,0:T(8,128)(2,1)} %copy-done.2, ...), custom_call_target="tpu_custom_call" | custom-call | tf_op jit(solution)/shard_map/weight_grad/pallas_call | solution.py:333
  155.7 1.2 copy-done.12
  156.9 0.1 fusion
  157.0 2.8 %collective-permute-start.21 = (bf16[256,1024]{1,0:T(8,128)(2,1)S(1)}, bf16[256,1024]{1,0:T(8,128)(2,1)S(1)}, u32[]{:S(2)}, u32[]{:S(2)}) collective-permute-start(bf16[256,1024]{1,0:T(8,128)(2,1)S(1)} %fusion), channel_id=1, source_target_pairs={{0,16},{8,24},{16,0},{24,8},{32,48},{40,56},{48,32},{56,40},{64,80... | collective-permute-start | bytes 1572872 | tf_op jit(solution)/shard_map/t_sum_flip_across/ppermute | solution.py:41
  159.8 11.9 %collective-permute-done.21.rest_5_ = bf16[256,1024]{1,0:T(8,128)(2,1)S(1)} collective-permute-done((bf16[256,1024]{1,0:T(8,128)(2,1)S(1)}, bf16[256,1024]{1,0:T(8,128)(2,1)S(1)}, u32[]{:S(2)}, u32[]{:S(2)}) %collective-permute-start.21) | collective-permute-done | bytes 524320 | tf_op jit(solution)/shard_map/t_sum_flip_across/ppermute | solution.py:41
  171.7 0.8 copy-done.16
  172.5 9.3 %attend_grad.1 = (bf16[512,1024]{1,0:T(8,128)(2,1)}, bf16[512,128]{1,0:T(8,128)(2,1)}, bf16[512,128]{1,0:T(8,128)(2,1)}) custom-call(s32[4]{0:T(128)} %pad_add_fusion.place, bf16[512,1024]{1,0:T(8,128)(2,1)} %bitcast.43, bf16[512,128]{1,0:T(8,128)(2,1)} %bitcast.54, bf16[512,128]{1,0:T(8,128)(2,1)} %bitcast.56, f32[4,8,256]{2,1,0:T(8,128)} %get-tuple-element.45.stats, ...), custom_call_target="tpu_custom_call" | custom-call | tf_op jit(solution)/shard_map/attend_grad/pallas_call | solution.py:237
  181.8 17.3 %reduce-scatter.5.cloned.1.call-done = bf16[1024,256]{1,0:T(8,128)(2,1)} async-done(((bf16[4096,256]{1,0:T(8,128)(2,1)}), bf16[1024,256]{1,0:T(8,128)(2,1)}) %reduce-scatter.5.cloned.1.call-update) | async-done | bytes 524304 | tf_op jit(solution)/shard_map/reduce_scatter | solution.py:412
  199.1 2.8 %maximum_convert_fusion = f32[1024,512]{1,0:T(8,128)} fusion(bf16[1024,256]{1,0:T(8,128)(2,1)} %reduce-scatter.5.cloned.1.call-done, bf16[1024,256]{1,0:T(8,128)(2,1)} %reduce-scatter.3.cloned.1.call-done), kind=kLoop, calls=%fused_computation | loop fusion | flops 2097152 | bytes 3145728 | tf_op jit(solution)/shard_map/convert_element_type | solution.py:422
  (57 shorter events, 0.5 us)
Async XLA Ops:
  7.2 18.5 %copy-start.17 = (s32[1,64]{1,0:T(1,128)S(1)}, s32[1,64]{1,0:T(1,128)}, u32[]{:S(2)}) copy-start(s32[1,64]{1,0:T(1,128)} %param.10) | copy-start | bytes 772
  7.2 75.9 %all-gather.6.cloned.1.call-start = ((), (), s32[]{:S(2)}) async-start(), calls=%async_computation.2 | async-start | bytes 5242880 | tf_op jit(solution)/shard_map/all_gather | solution.py:365
  7.9 104.9 %all-gather.8.cloned.1.call-start = ((), (), s32[]{:S(2)}) async-start(), calls=%async_computation.5 | async-start | bytes 2621440 | tf_op jit(solution)/shard_map/all_gather | solution.py:395
  8.0 7.5 %collective-permute-start = (s32[64]{0:T(128)}, s32[64]{0:T(128)S(1)}, u32[]{:S(2)}, u32[]{:S(2)}) collective-permute-start(s32[64]{0:T(128)} %bitcast.57), channel_id=1, source_target_pairs={{0,1},{1,0},{2,3},{3,2},{4,5},{5,4},{6,7},{7,6},{8,9},{9,8},{10,11... | collective-permute-start | bytes 776 | tf_op jit(solution)/shard_map/t_ids_pair/ppermute | solution.py:49
  15.4 2.4 %collective-permute-start.1 = (bf16[2,64,1024]{2,1,0:T(8,128)(2,1)}, bf16[2,64,1024]{2,1,0:T(8,128)(2,1)S(1)}, u32[]{:S(2)}, u32[]{:S(2)}) collective-permute-start(bf16[2,64,1024]{2,1,0:T(8,128)(2,1)} %get-tuple-element.37), channel_id=1, source_target_pairs={{0,8},{8,0},{16,24},{24,16},{32,40},{40,32},{48,56},{56,48},{64,72... | collective-permute-start | bytes 786440 | tf_op jit(solution)/shard_map/t_near_sibling/ppermute | solution.py:37
  18.9 27.5 %copy-start = (bf16[2,2,64,1024]{3,2,1,0:T(8,128)(2,1)}, bf16[2,2,64,1024]{3,2,1,0:T(8,128)(2,1)S(1)}, u32[]{:S(2)}) copy-start(bf16[2,2,64,1024]{3,2,1,0:T(8,128)(2,1)S(1)} %pad_maximum_fusion.refs_0_) | copy-start | bytes 1572868
  18.9 22.7 %collective-permute-start.5 = (bf16[2,2,64,1024]{3,2,1,0:T(8,128)(2,1)S(1)}, bf16[2,2,64,1024]{3,2,1,0:T(8,128)(2,1)S(1)}, u32[]{:S(2)}, u32[]{:S(2)}) collective-permute-start(bf16[2,2,64,1024]{3,2,1,0:T(8,128)(2,1)S(1)} %pad_maximum_fusion.refs_0_), channel_id=1, source_target_pairs={{0,2},{1,3},{2,4},{3,5},{4,6},{5,7},{6,0},{7,1},{8,10},{9,11},{10,... | collective-permute-start | bytes 1572872 | tf_op jit(solution)/shard_map/t_n_up/ppermute | solution.py:53
  20.2 21.3 %collective-permute-start.6 = (bf16[2,2,64,1024]{3,2,1,0:T(8,128)(2,1)S(1)}, bf16[2,2,64,1024]{3,2,1,0:T(8,128)(2,1)S(1)}, u32[]{:S(2)}, u32[]{:S(2)}) collective-permute-start(bf16[2,2,64,1024]{3,2,1,0:T(8,128)(2,1)S(1)} %pad_maximum_fusion.refs_0_), channel_id=1, source_target_pairs={{0,6},{1,7},{2,0},{3,1},{4,2},{5,3},{6,4},{7,5},{8,14},{9,15},{10,... | collective-permute-start | bytes 1572872 | tf_op jit(solution)/shard_map/t_n_down/ppermute | solution.py:57
  21.7 19.8 %collective-permute-start.8 = (bf16[2,64,1024]{2,1,0:T(8,128)(2,1)}, bf16[2,64,1024]{2,1,0:T(8,128)(2,1)S(1)}, u32[]{:S(2)}, u32[]{:S(2)}) collective-permute-start(bf16[2,64,1024]{2,1,0:T(8,128)(2,1)} %get-tuple-element.40), channel_id=1, source_target_pairs={{0,16},{8,24},{16,0},{24,8},{32,48},{40,56},{48,32},{56,40},{64,80... | collective-permute-start | bytes 786440 | tf_op jit(solution)/shard_map/t_other_across/ppermute | solution.py:41
  24.2 17.4 %collective-permute-start.9 = (bf16[2,64,1024]{2,1,0:T(8,128)(2,1)}, bf16[2,64,1024]{2,1,0:T(8,128)(2,1)S(1)}, u32[]{:S(2)}, u32[]{:S(2)}) collective-permute-start(bf16[2,64,1024]{2,1,0:T(8,128)(2,1)} %get-tuple-element.42), channel_id=1, source_target_pairs={{0,24},{8,16},{16,8},{24,0},{32,56},{40,48},{48,40},{56,32},{64,88... | collective-permute-start | bytes 786440 | tf_op jit(solution)/shard_map/t_other_diagonal/ppermute | solution.py:45
  25.7 7.5 %collective-permute-start.2 = (s32[2,64]{1,0:T(2,128)S(1)}, s32[2,64]{1,0:T(2,128)S(1)}, u32[]{:S(2)}, u32[]{:S(2)}) collective-permute-start(s32[2,64]{1,0:T(2,128)S(1)} %add_select_fusion), channel_id=1, source_target_pairs={{0,6},{1,7},{2,0},{3,1},{4,2},{5,3},{6,4},{7,5},{8,14},{9,15},{10,... | collective-permute-start | bytes 1544 | tf_op jit(solution)/shard_map/t_ids_down/ppermute | solution.py:57
  33.2 4.0 %collective-permute-start.3 = (s32[2,64]{1,0:T(2,128)S(1)}, s32[2,64]{1,0:T(2,128)S(1)}, u32[]{:S(2)}, u32[]{:S(2)}) collective-permute-start(s32[2,64]{1,0:T(2,128)S(1)} %add_select_fusion), channel_id=1, source_target_pairs={{0,4},{1,5},{2,6},{3,7},{4,0},{5,1},{6,2},{7,3},{8,12},{9,13},{10,... | collective-permute-start | bytes 1544 | tf_op jit(solution)/shard_map/t_ids_far/ppermute | solution.py:380
  37.1 4.2 %collective-permute-start.4 = (s32[2,64]{1,0:T(2,128)S(1)}, s32[2,64]{1,0:T(2,128)S(1)}, u32[]{:S(2)}, u32[]{:S(2)}) collective-permute-start(s32[2,64]{1,0:T(2,128)S(1)} %add_select_fusion), channel_id=1, source_target_pairs={{0,2},{1,3},{2,4},{3,5},{4,6},{5,7},{6,0},{7,1},{8,10},{9,11},{10,... | collective-permute-start | bytes 1544 | tf_op jit(solution)/shard_map/t_ids_up/ppermute | solution.py:53
  41.5 4.9 %copy-start.14 = (bf16[1,2,64,1024]{3,2,1,0:T(8,128)(2,1)S(1)}, bf16[1,2,64,1024]{3,2,1,0:T(8,128)(2,1)}, u32[]{:S(2)}) copy-start(bf16[1,2,64,1024]{3,2,1,0:T(8,128)(2,1)} %get-tuple-element.67) | copy-start | bytes 786436
  41.5 16.0 %copy-start.2 = (bf16[2,2,64,1024]{3,2,1,0:T(8,128)(2,1)}, bf16[2,2,64,1024]{3,2,1,0:T(8,128)(2,1)S(1)}, u32[]{:S(2)}) copy-start(bf16[2,2,64,1024]{3,2,1,0:T(8,128)(2,1)S(1)} %collective-permute-done.5.refs_3_) | copy-start | bytes 1572868
  41.6 16.0 %copy-start.3 = (bf16[2,2,64,1024]{3,2,1,0:T(8,128)(2,1)}, bf16[2,2,64,1024]{3,2,1,0:T(8,128)(2,1)S(1)}, u32[]{:S(2)}) copy-start(bf16[2,2,64,1024]{3,2,1,0:T(8,128)(2,1)S(1)} %collective-permute-done.6.refs_1_) | copy-start | bytes 1572868
  41.6 0.7 copy-start.13
  42.3 25.4 %copy-start.1 = (bf16[2,2,64,1024]{3,2,1,0:T(8,128)(2,1)}, bf16[2,2,64,1024]{3,2,1,0:T(8,128)(2,1)S(1)}, u32[]{:S(2)}) copy-start(bf16[2,2,64,1024]{3,2,1,0:T(8,128)(2,1)S(1)} %pad_maximum_fusion.1.refs_4_) | copy-start | bytes 1572868
  43.2 10.4 %collective-permute-start.10 = (bf16[2,2,64,1024]{3,2,1,0:T(8,128)(2,1)S(1)}, bf16[2,2,64,1024]{3,2,1,0:T(8,128)(2,1)S(1)}, u32[]{:S(2)}, u32[]{:S(2)}) collective-permute-start(bf16[2,2,64,1024]{3,2,1,0:T(8,128)(2,1)S(1)} %pad_maximum_fusion.1.refs_4_), channel_id=1, source_target_pairs={{0,6},{1,7},{2,0},{3,1},{4,2},{5,3},{6,4},{7,5},{8,14},{9,15},{10,... | collective-permute-start | bytes 1572872 | tf_op jit(solution)/shard_map/t_o_down/ppermute | solution.py:57
  44.6 11.3 %collective-permute-start.7 = (bf16[2,2,64,1024]{3,2,1,0:T(8,128)(2,1)S(1)}, bf16[2,2,64,1024]{3,2,1,0:T(8,128)(2,1)S(1)}, u32[]{:S(2)}, u32[]{:S(2)}) collective-permute-start(bf16[2,2,64,1024]{3,2,1,0:T(8,128)(2,1)S(1)} %collective-permute-done.5.refs_3_), channel_id=1, source_target_pairs={{0,2},{1,3},{2,4},{3,5},{4,6},{5,7},{6,0},{7,1},{8,10},{9,11},{10,... | collective-permute-start | bytes 1572872 | tf_op jit(solution)/shard_map/t_n_far/ppermute | solution.py:53
  46.4 9.9 %collective-permute-start.15 = (bf16[2,2,64,1024]{3,2,1,0:T(8,128)(2,1)S(1)}, bf16[2,2,64,1024]{3,2,1,0:T(8,128)(2,1)}, u32[]{:S(2)}, u32[]{:S(2)}) collective-permute-start(bf16[2,2,64,1024]{3,2,1,0:T(8,128)(2,1)S(1)} %pad_maximum_fusion.2), channel_id=1, source_target_pairs={{0,1},{1,0},{2,3},{3,2},{4,5},{5,4},{6,7},{7,6},{8,9},{9,8},{10,11... | collective-permute-start | bytes 1572872 | tf_op jit(solution)/shard_map/t_pair_0/ppermute | solution.py:49
  53.6 29.4 %copy-start.4 = (bf16[2,2,64,1024]{3,2,1,0:T(8,128)(2,1)}, bf16[2,2,64,1024]{3,2,1,0:T(8,128)(2,1)S(1)}, u32[]{:S(2)}) copy-start(bf16[2,2,64,1024]{3,2,1,0:T(8,128)(2,1)S(1)} %collective-permute-done.10.refs_5_) | copy-start | bytes 1572868
  55.9 27.1 %copy-start.5 = (bf16[2,2,64,1024]{3,2,1,0:T(8,128)(2,1)}, bf16[2,2,64,1024]{3,2,1,0:T(8,128)(2,1)S(1)}, u32[]{:S(2)}) copy-start(bf16[2,2,64,1024]{3,2,1,0:T(8,128)(2,1)S(1)} %collective-permute-done.7.refs_2_) | copy-start | bytes 1572868
  56.4 78.0 %all-gather.10.cloned.1.call-start = ((), (), s32[]{:S(2)}) async-start(), calls=%async_computation.6 | async-start | bytes 2621440 | tf_op jit(solution)/shard_map/all_gather | solution.py:395
  57.5 9.3 %collective-permute-start.16 = (bf16[2,2,64,1024]{3,2,1,0:T(8,128)(2,1)S(1)}, bf16[2,2,64,1024]{3,2,1,0:T(8,128)(2,1)S(1)}, u32[]{:S(2)}, u32[]{:S(2)}) collective-permute-start(bf16[2,2,64,1024]{3,2,1,0:T(8,128)(2,1)S(1)} %pad_maximum_fusion.3), channel_id=1, source_target_pairs={{0,1},{1,0},{2,3},{3,2},{4,5},{5,4},{6,7},{7,6},{8,9},{9,8},{10,11... | collective-permute-start | bytes 1572872 | tf_op jit(solution)/shard_map/t_pair_1/ppermute | solution.py:49
  66.8 0.8 copy-start.15
  67.7 114.2 %reduce-scatter.3.cloned.1.call-start = ((), (), s32[]{:S(2)}) async-start(), calls=%async_computation.3 | async-start | bytes 2621440 | tf_op jit(solution)/shard_map/reduce_scatter | solution.py:412
  67.7 10.0 %collective-permute-start.12 = (bf16[2,2,64,1024]{3,2,1,0:T(8,128)(2,1)S(1)}, bf16[2,2,64,1024]{3,2,1,0:T(8,128)(2,1)S(1)}, u32[]{:S(2)}, u32[]{:S(2)}) collective-permute-start(bf16[2,2,64,1024]{3,2,1,0:T(8,128)(2,1)S(1)} %pad_maximum_fusion.1.refs_4_), channel_id=1, source_target_pairs={{0,2},{1,3},{2,4},{3,5},{4,6},{5,7},{6,0},{7,1},{8,10},{9,11},{10,... | collective-permute-start | bytes 1572872 | tf_op jit(solution)/shard_map/t_o_up/ppermute | solution.py:53
  68.7 14.3 %collective-permute-start.11 = (bf16[2,2,64,1024]{3,2,1,0:T(8,128)(2,1)S(1)}, bf16[2,2,64,1024]{3,2,1,0:T(8,128)(2,1)S(1)}, u32[]{:S(2)}, u32[]{:S(2)}) collective-permute-start(bf16[2,2,64,1024]{3,2,1,0:T(8,128)(2,1)S(1)} %collective-permute-done.10.refs_5_), channel_id=1, source_target_pairs={{0,6},{1,7},{2,0},{3,1},{4,2},{5,3},{6,4},{7,5},{8,14},{9,15},{10,... | collective-permute-start | bytes 1572872 | tf_op jit(solution)/shard_map/t_o_far/ppermute | solution.py:57
  70.5 35.0 %collective-permute-start.18 = (bf16[1024,512]{1,0:T(8,128)(2,1)}, bf16[1024,512]{1,0:T(8,128)(2,1)}, u32[]{:S(2)}, u32[]{:S(2)}) collective-permute-start(bf16[1024,512]{1,0:T(8,128)(2,1)} %get-tuple-element.54.refs_9_), channel_id=1, source_target_pairs={{0,16},{8,24},{16,0},{24,8},{32,48},{40,56},{48,32},{56,40},{64,80... | collective-permute-start | bytes 3145736 | tf_op jit(solution)/shard_map/t_out_across/ppermute | solution.py:41
  77.7 5.4 %copy-start.6 = (bf16[2,2,64,1024]{3,2,1,0:T(8,128)(2,1)}, bf16[2,2,64,1024]{3,2,1,0:T(8,128)(2,1)S(1)}, u32[]{:S(2)}) copy-start(bf16[2,2,64,1024]{3,2,1,0:T(8,128)(2,1)S(1)} %collective-permute-done.12.refs_7_) | copy-start | bytes 1572868
  83.0 0.8 copy-start.7
  92.8 15.1 %collective-permute-start.13 = (bf16[2,256,1024]{2,1,0:T(8,128)(2,1)}, bf16[2,256,1024]{2,1,0:T(8,128)(2,1)S(1)}, u32[]{:S(2)}, u32[]{:S(2)}) collective-permute-start(bf16[2,256,1024]{2,1,0:T(8,128)(2,1)} %get-tuple-element.49), channel_id=1, source_target_pairs={{0,8},{8,0},{16,24},{24,16},{32,40},{40,32},{48,56},{56,48},{64,72... | collective-permute-start | bytes 3145736 | tf_op jit(solution)/shard_map/t_sum_same_sibling/ppermute | solution.py:37
  105.5 7.3 %collective-permute-start.19 = (bf16[1024,512]{1,0:T(8,128)(2,1)}, bf16[1024,512]{1,0:T(8,128)(2,1)S(1)}, u32[]{:S(2)}, u32[]{:S(2)}) collective-permute-start(bf16[1024,512]{1,0:T(8,128)(2,1)} %collective-permute-done.18.refs_11_), channel_id=1, source_target_pairs={{0,8},{8,0},{16,24},{24,16},{32,40},{40,32},{48,56},{56,48},{64,72... | collective-permute-start | bytes 3145736 | tf_op jit(solution)/shard_map/t_out_other/ppermute | solution.py:37
  105.6 7.2 %collective-permute-start.17 = (bf16[1024,512]{1,0:T(8,128)(2,1)}, bf16[1024,512]{1,0:T(8,128)(2,1)S(1)}, u32[]{:S(2)}, u32[]{:S(2)}) collective-permute-start(bf16[1024,512]{1,0:T(8,128)(2,1)} %get-tuple-element.54.refs_9_), channel_id=1, source_target_pairs={{0,8},{8,0},{16,24},{24,16},{32,40},{40,32},{48,56},{56,48},{64,72... | collective-permute-start | bytes 3145736 | tf_op jit(solution)/shard_map/t_out_near/ppermute | solution.py:37
  108.0 15.0 %copy-start.10 = (bf16[2,256,1024]{2,1,0:T(8,128)(2,1)}, bf16[2,256,1024]{2,1,0:T(8,128)(2,1)S(1)}, u32[]{:S(2)}) copy-start(bf16[2,256,1024]{2,1,0:T(8,128)(2,1)S(1)} %collective-permute-done.13.rest_1_) | copy-start | bytes 3145732
  110.5 23.9 %collective-permute-start.14 = (bf16[256,1024]{1,0:T(8,128)(2,1)}, bf16[256,1024]{1,0:T(8,128)(2,1)}, u32[]{:S(2)}, u32[]{:S(2)}) collective-permute-start(bf16[256,1024]{1,0:T(8,128)(2,1)} %fusion.1), channel_id=1, source_target_pairs={{0,16},{8,24},{16,0},{24,8},{32,48},{40,56},{48,32},{56,40},{64,80... | collective-permute-start | bytes 1572872 | tf_op jit(solution)/shard_map/t_sum_same_across/ppermute | solution.py:41
  112.7 1.0 copy-start.8
  112.8 1.3 copy-start.9
  134.5 64.7 %reduce-scatter.5.cloned.1.call-start = ((), (), s32[]{:S(2)}) async-start(), calls=%async_computation.4 | async-start | bytes 2621440 | tf_op jit(solution)/shard_map/reduce_scatter | solution.py:412
  143.3 3.2 %collective-permute-start.20 = (bf16[2,256,1024]{2,1,0:T(8,128)(2,1)}, bf16[2,256,1024]{2,1,0:T(8,128)(2,1)S(1)}, u32[]{:S(2)}, u32[]{:S(2)}) collective-permute-start(bf16[2,256,1024]{2,1,0:T(8,128)(2,1)} %get-tuple-element.59), channel_id=1, source_target_pairs={{0,8},{8,0},{16,24},{24,16},{32,40},{40,32},{48,56},{56,48},{64,72... | collective-permute-start | bytes 3145736 | tf_op jit(solution)/shard_map/t_sum_flip_sibling/ppermute | solution.py:37
  146.5 9.2 %copy-start.11 = (bf16[2,256,1024]{2,1,0:T(8,128)(2,1)}, bf16[2,256,1024]{2,1,0:T(8,128)(2,1)S(1)}, u32[]{:S(2)}) copy-start(bf16[2,256,1024]{2,1,0:T(8,128)(2,1)S(1)} %collective-permute-done.20.rest_4_) | copy-start | bytes 3145732
  155.6 1.2 copy-start.12
  157.0 14.7 %collective-permute-start.21 = (bf16[256,1024]{1,0:T(8,128)(2,1)S(1)}, bf16[256,1024]{1,0:T(8,128)(2,1)S(1)}, u32[]{:S(2)}, u32[]{:S(2)}) collective-permute-start(bf16[256,1024]{1,0:T(8,128)(2,1)S(1)} %fusion), channel_id=1, source_target_pairs={{0,16},{8,24},{16,0},{24,8},{32,48},{40,56},{48,32},{56,40},{64,80... | collective-permute-start | bytes 1572872 | tf_op jit(solution)/shard_map/t_sum_flip_across/ppermute | solution.py:41
  171.7 0.8 copy-start.16
Sparse Core Ops, SparseCore 0:
  9.7 51.7 all-gather.5
  63.1 36.9 all-gather.7
  101.8 32.5 all-gather.9
  136.7 29.9 reduce-scatter.2
  169.6 29.4 reduce-scatter.4

commit v4 on v3

--- a/solution.py
+++ b/solution.py
@@ -11,7 +11,6 @@
 F32 = jnp.float32
 BF16 = jnp.bfloat16
 SCALE = HD ** (-0.5)
-LIGHT = pl.CostEstimate(flops=0, bytes_accessed=0, transcendentals=0)
 VMEM_MOST = 60 * 1024 * 1024
 
 
@@ -29,6 +28,8 @@
 PAIR = by_tensor(lambda i: i ^ 1)
 Y_UP = by_tensor(lambda i: (i + 2) % 8)
 Y_DOWN = by_tensor(lambda i: (i - 2) % 8)
+Z_UP = by_dp(lambda i: (i + 4) % 16)
+Z_DOWN = by_dp(lambda i: (i - 4) % 16)
 Z_GROUPS = [[z * 4 + j for z in range(4)] for j in range(4)]
 Y_GROUPS = [[y * 2 + low for y in range(4)] for low in range(2)]
 
@@ -49,6 +50,14 @@
     return lax.ppermute(x, "tensor", PAIR)
 
 
+def z_up(x):
+    return lax.ppermute(x, "dp", Z_UP)
+
+
+def z_down(x):
+    return lax.ppermute(x, "dp", Z_DOWN)
+
+
 def y_up(x):
     return lax.ppermute(x, "tensor", Y_UP)
 
@@ -63,6 +72,10 @@
 
 def nt(a, b):
     return lax.dot_general(a, b, (((1,), (1,)), ((), ())), preferred_element_type=F32)
+
+
+def cost(us):
+    return pl.CostEstimate(flops=0, bytes_accessed=int(us * 3e6), transcendentals=0)
 
 
 def params():
@@ -109,7 +122,7 @@
         out_specs=[col] * 4,
         out_shape=[shape] * 4,
         compiler_params=params(),
-        cost_estimate=LIGHT,
+        cost_estimate=cost(3),
         name="prep",
     )(place, margins, segs, up)
 
@@ -187,7 +200,7 @@
         ],
         scratch_shapes=[pltpu.VMEM((HD, length), BF16)],
         compiler_params=params(),
-        cost_estimate=LIGHT,
+        cost_estimate=cost(9),
         name="attend",
     )(place, segs, q, k, v)
 
@@ -250,7 +263,7 @@
         out_shape=[jax.ShapeDtypeStruct(x.shape, BF16) for x in (q, k, v)],
         scratch_shapes=[pltpu.VMEM((HD, length), BF16), pltpu.VMEM(k.shape, F32), pltpu.VMEM(v.shape, F32)],
         compiler_params=params(),
-        cost_estimate=LIGHT,
+        cost_estimate=cost(9),
         name="attend_grad",
     )(place, q, k, v, stats, bias, *terms)
 
@@ -258,17 +271,17 @@
 def reader(place, refs):
     y = place[0]
     if len(refs) == 8:
-        return lambda p, i, e, k: refs[p * 4 + k][e, i]
-    return lambda p, i, e, k: refs[e][lax.rem(y + k, 4), p, i]
+        return lambda p, i, e, k: refs[p * 4 + k].at[e, i]
+    return lambda p, i, e, k: refs[0].at[lax.rem(y + k, 4), p, i] if e == 0 else refs[1 + k].at[p, i]
 
 
 def partial_kernel(count, place, *refs):
     read = reader(place, refs[:count])
-    weight, keep_near, keep_other, give, x = refs[count:]
+    weights, (keep_near, keep_other, give, x) = refs[count : count + 4], refs[count + 4 :]
     seq = refs[count - 1].shape[-2]
-    cols = refs[count - 1].shape[-1]
     half = 4 * seq
-    width = weight.shape[2] // 2
+    width = weights[0].shape[1] // 2
+    z = place[4]
 
     @pl.when(pl.program_id(0) == 0)
     def _():
@@ -277,36 +290,38 @@
                 for i in range(2):
                     for k in range(4):
                         at = (p * 2 + i) * half + k * seq
-                        x[at : at + seq, e * cols : (e + 1) * cols] = read(p, i, e, k)
-
-    w = jnp.concatenate([weight[j, :, e * width : (e + 1) * width] for e in range(2) for j in range(4)], axis=1)
+                        for j in range(4):
+                            col = pl.ds(pl.multiple_of(lax.rem(z + j, 4) * width, width), width)
+                            x[at : at + seq, (j * 2 + e) * width : (j * 2 + e + 1) * width] = read(p, i, e, k)[:, col]
+
+    w = jnp.concatenate([weight[...] for weight in weights], axis=1)
     for p, keep in enumerate((keep_near, keep_other)):
         total = nt(x[p * 2 * half : (p + 1) * 2 * half], w)
         keep[...] = total[:half]
         give[p] = total[half:].astype(BF16)
 
 
-def partial(place, pieces, weight):
+def partial(place, pieces, weights):
     seq, cols = pieces[-1].shape[-2:]
-    heads = weight.shape[1]
+    heads = weights[0].shape[0]
     tile = heads // 2
     out = pl.BlockSpec((4 * seq, tile), lambda i: (0, i))
     shape = jax.ShapeDtypeStruct((4 * seq, heads), F32)
     return pl.pallas_call(
         functools.partial(partial_kernel, len(pieces)),
         grid=(2,),
-        in_specs=[SMEM()] + [whole(x.shape) for x in pieces] + [pl.BlockSpec((4, tile, cols // 2), lambda i: (0, i, 0))],
+        in_specs=[SMEM()] + [whole(x.shape) for x in pieces] + [pl.BlockSpec((tile, cols // 2), lambda i: (i, 0))] * 4,
         out_specs=[out, out, pl.BlockSpec((2, 4 * seq, tile), lambda i: (0, 0, i))],
         out_shape=[shape, shape, jax.ShapeDtypeStruct((2, 4 * seq, heads), BF16)],
         scratch_shapes=[pltpu.VMEM((16 * seq, 2 * cols), BF16)],
         compiler_params=params(),
-        cost_estimate=LIGHT,
+        cost_estimate=cost(9),
         name="partial_grad",
-    )(place, *pieces, weight)
+    )(place, *pieces, *weights)
 
 
 def wgrad_kernel(place, *refs):
-    same, flip, outs, (out, x) = refs[:8], refs[8], refs[9:13], refs[13:]
+    same, flip, outs, (out, x) = refs[:8], refs[8:-6], refs[-6:-2], refs[-2:]
     seq = same[0].shape[2]
     length = 8 * seq
     y = place[0]
@@ -315,7 +330,7 @@
             for k in range(4):
                 at = (p * 2 + i) * length + 2 * k * seq
                 x[at : at + seq] = same[p * 4 + k][0, i]
-                x[at + seq : at + 2 * seq] = flip[lax.rem(y + k, 4), p, i]
+                x[at + seq : at + 2 * seq] = flip[k][p, i] if len(flip) > 1 else flip[0][lax.rem(y + k, 4), p, i]
     tile = 256
     width = out.shape[2]
     for m in range(0, out.shape[1], tile):
@@ -330,20 +345,24 @@
     _, _, seq, cols = same[0].shape
     heads = outs[0].shape[0]
     wide = cols // 2
+    if len(flip) > 1:
+        flip_spec = pl.BlockSpec((2, 2, seq, wide), lambda i: (0, 0, 0, i))
+    else:
+        flip_spec = pl.BlockSpec((4, 2, 2, seq, wide), lambda i: (0, 0, 0, 0, i))
     return pl.pallas_call(
         wgrad_kernel,
         grid=(2,),
         in_specs=[SMEM()]
         + [pl.BlockSpec((1, 2, seq, wide), lambda i: (half, 0, 0, i))] * 8
-        + [pl.BlockSpec((4, 2, 2, seq, wide), lambda i: (0, 0, 0, 0, i))]
+        + [flip_spec] * len(flip)
         + [whole(outs[0].shape)] * 4,
         out_specs=pl.BlockSpec((2, heads, wide // 2), lambda i: (i, 0, 0)),
         out_shape=jax.ShapeDtypeStruct((4, heads, wide // 2), BF16),
         scratch_shapes=[pltpu.VMEM((32 * seq, wide), BF16)],
         compiler_params=params(),
-        cost_estimate=LIGHT,
+        cost_estimate=cost(9),
         name="weight_grad",
-    )(place, *same, flip, *outs)
+    )(place, *same, *flip, *outs)
 
 
 def named(name, fn, x):
@@ -359,10 +378,9 @@
     d = lax.axis_index("dp")
     t = lax.axis_index("tensor")
     y, low = t // 2, t % 2
-    place = jnp.stack([y, low, (d // 2) % 2, d % 2]).astype(jnp.int32)
+    place = jnp.stack([y, low, (d // 2) % 2, d % 2, d // 4]).astype(jnp.int32)
     query, key, value = query_states[0], key_states[0], value_states[0]
     heads, width = out_weight.shape
-    weight = lax.all_gather(out_weight, "dp", axis=0, tiled=True, axis_index_groups=Z_GROUPS).reshape(4, heads, width)
 
     ids = segment_ids[0]
     partner = named("ids_pair", pair, ids)
@@ -385,20 +403,24 @@
     other = jnp.stack([after(from_across, n_up, n_down, ids_up, ids_down, ids_far), from_diagonal], axis=1)
     flips = [named("pair_%d" % e, pair, jnp.stack([near[e], other[e]])) for e in range(2)]
 
-    n, o = near, other
+    w_behind, w_ahead = named("w_up", z_up, out_weight), named("w_down", z_down, out_weight)
+    weights = [out_weight, w_ahead, named("w_far", z_up, w_behind), w_behind]
+
+    n, o, q = near, other, flips[1]
     n_far, o_down = named("n_far", y_up, after(n_up, n_down)), named("o_down", y_down, after(o, whole_segs))
-    attn_out, stats, bias = forward(place, whole_segs, after(query, n_far, o_down), key, value)
-    out_across = named("out_across", across, attn_out)
+    first_flip = lax.all_gather(after(flips[0], n_far, o_down), "tensor", axis=0, axis_index_groups=Y_GROUPS)
+    attn_out, stats, bias = forward(place, whole_segs, after(query, n_up, n_down, o), key, value)
+    out_across = named("out_across", across, after(attn_out, q))
     o_up, o_far = named("o_up", y_up, after(o, n_up, n_down)), named("o_far", y_down, o_down)
-    flips[0] = after(flips[0], n_far, o_down)
-    flips[1] = after(flips[1], attn_out)
-    flips = [lax.all_gather(x, "tensor", axis=0, axis_index_groups=Y_GROUPS) for x in flips]
+    q = after(q, n_far, o_down)
+    q_up, q_down = named("q_up", y_up, q), named("q_down", y_down, after(q, o_up, o_far))
+    q_far = named("q_far", y_down, q_down)
     near_blocks = [n, n_down, n_far, n_up]
     other_blocks = [o, o_down, o_far, o_up]
     same = [*near_blocks, *other_blocks]
 
     def sums(name, pieces):
-        keep_near, keep_other, give = partial(place, pieces, weight)
+        keep_near, keep_other, give = partial(place, pieces, weights)
         given = named(name + "_sibling", sibling, give)
         total = (keep_other + given[1].astype(F32)).astype(BF16)
         return keep_near, given, named(name + "_across", across, total)
@@ -413,11 +435,12 @@
             x.reshape(4 * heads, width // 2), "dp", scatter_dimension=0, tiled=True, axis_index_groups=Z_GROUPS
         )
 
-    first = wgrad(place, 0, same, flips[0], (*outs[:3], after(out_other, terms_same[1])))
-    first_sum = sum_z(after(first, flips[1], terms_same[2]))
-    terms_flip = sums("sum_flip", [flips[0], after(flips[1], first)])
-    last = wgrad(place, 1, same, flips[1], (*outs[:3], after(out_other, terms_flip[1])))
+    flip_blocks = [q, q_down, q_far, q_up]
+    first = wgrad(place, 0, same, [first_flip], (*outs[:3], after(out_other, terms_same[1], q_up, q_down)))
+    first_sum = sum_z(after(first, terms_same[2], q_far))
+    last = wgrad(place, 1, same, flip_blocks, (*outs[:3], after(out_other, first)))
     last_sum = sum_z(last)
+    terms_flip = sums("sum_flip", [after(first_flip, last), *flip_blocks])
     dq, dk, dv = backward(place, query, key, value, stats, bias, [*terms_same, *terms_flip])
     weight_grad = jnp.concatenate([first_sum, last_sum], axis=1).astype(F32)
     return (dq[None], dk[None], dv[None], weight_grad)

time: 209 us -> 209 us (level)
  starting transfers between devices: 42.6 us -> 48.6 us
  waiting for transfers between devices: 74.6 us -> 69.5 us
    ppermute x0 -> x3, waiting for transfers between devices: none -> 11.7 us  [the longest x2 11.7 us: z_up(): return lax.ppermute(x, 'dp', Z_UP)]
    all_gather x3 -> x1, waiting for transfers between devices: 11.5 us -> 0.01 us  [shards(): lax.all_gather(after(flips[0], n_far, o_down), 'tensor', axis=0, axis_ind...]
    ppermute x4 -> x6, starting transfers between devices: 6.34 us -> 13 us  [y_down(): return lax.ppermute(x, 'tensor', Y_DOWN)]
    ppermute x4 -> x6, waiting for transfers between devices: 18 us -> 22.8 us  [y_down(): return lax.ppermute(x, 'tensor', Y_DOWN)]
    ppermute x4 -> x5, waiting for transfers between devices: 7.49 us -> 2.82 us  [y_up(): return lax.ppermute(x, 'tensor', Y_UP)]
    ppermute x5, starting transfers between devices: 14.8 us -> 10.3 us  [sibling(): return lax.ppermute(x, 'dp', SIBLING)]
    ppermute x0 -> x3, starting transfers between devices: none -> 4.11 us  [the longest x1 2.47 us: z_down(): return lax.ppermute(x, 'dp', Z_DOWN)]
    reduce_scatter x2, waiting for transfers between devices: 17.3 us -> 13.9 us  [sum_z(): lax.psum_scatter(x.reshape(4 * heads, width // 2), 'dp', scatter_dimensio...]
  transfers between devices with their start and end apart: 27 -> 31, of which waited for: 14 -> 14; matrix products, arithmetic and copies ran while one was open for 6% -> 6% of each run, Pallas kernels for 27% -> 28%
where the time goes in v4:
time: 209 us
  waiting for transfers between devices  69.5 us (33%)
  Pallas kernels  58 us (28%)
  starting transfers between devices  48.6 us (23%)
  between operations  14 us (7%)
  other arithmetic  12 us (6%)
  local copies, waits for them, and re-layouts  6.57 us (3%)
    ppermute x6, waiting for transfers between devices, y_down(): return lax.ppermute(x, 'tensor', Y_DOWN)  22.8 us
    pallas_call x2, Pallas kernels, partial(): pl.pallas_call(functools.partial(partial_kernel, len(pieces)), grid=(2,),...  18.8 us
    pallas_call x2, Pallas kernels, wgrad(): pl.pallas_call(wgrad_kernel, grid=(2,), in_specs=[SMEM()] + [pl.BlockSpec...  17.8 us
    reduce_scatter x2, waiting for transfers between devices, sum_z(): lax.psum_scatter(x.reshape(4 * heads, width // 2), 'dp', scatter_dimensio...  13.9 us
    ppermute x6, starting transfers between devices, y_down(): return lax.ppermute(x, 'tensor', Y_DOWN)  13 us
    ppermute x4, waiting for transfers between devices, across(): return lax.ppermute(x, 'dp', ACROSS)  12.6 us
    ppermute x2, waiting for transfers between devices, z_up(): return lax.ppermute(x, 'dp', Z_UP)  11.7 us
    ppermute x4, starting transfers between devices, across(): return lax.ppermute(x, 'dp', ACROSS)  10.6 us
  transfers between devices with their start and end apart: 31, of which 14 were waited for; matrix products, arithmetic and copies ran while one was open for 6% of the time, Pallas kernels for 28%

profile of v4, /device:TPU:1, one launch (start us, length us, event | category | flops | bytes accessed | tf_op | source)
XLA Modules:
  0.0 208.7 jit_solution(10757945399741841820)
XLA Ops:
  7.2 2.1 %collective-permute-start = (s32[64]{0:T(128)}, s32[64]{0:T(128)S(1)}, u32[]{:S(2)}, u32[]{:S(2)}) collective-permute-start(s32[64]{0:T(128)} %bitcast.52), channel_id=1, source_target_pairs={{0,1},{1,0},{2,3},{3,2},{4,5},{5,4},{6,7},{7,6},{8,9},{9,8},{10,11... | collective-permute-start | bytes 776 | tf_op jit(solution)/shard_map/t_ids_pair/ppermute | solution.py:50
  9.3 0.7 stack.76.place
  10.0 1.3 broadcast_in_dim.21.segs
  11.4 3.4 %prep.1 = (bf16[2,64,1024]{2,1,0:T(8,128)(2,1)}, bf16[2,64,1024]{2,1,0:T(8,128)(2,1)}, bf16[2,64,1024]{2,1,0:T(8,128)(2,1)}, bf16[2,64,1024]{2,1,0:T(8,128)(2,1)}) custom-call(s32[5]{0:T(128)} %stack.76.place, f32[1,4]{1,0:T(1,128)} %margins.1, s32[64,128]{1,0:T(8,128)} %broadcast_in_dim.21.segs, bf16[64,8192]{1,0:T(8,128)(2,1)} %bitcast.39), custom_call_target="tpu_custom_call" | custom-call | bytes 9000000 | tf_op jit(solution)/shard_map/prep/pallas_call | solution.py:118
  14.8 1.0 collective-permute-start.1
  15.8 1.4 collective-permute-done.1
  17.2 1.0 pad_maximum_fusion.refs_0_
  18.2 1.4 collective-permute-start.5
  19.5 1.5 collective-permute-start.6
  21.1 2.5 %collective-permute-start.7 = (bf16[2,64,1024]{2,1,0:T(8,128)(2,1)}, bf16[2,64,1024]{2,1,0:T(8,128)(2,1)S(1)}, u32[]{:S(2)}, u32[]{:S(2)}) collective-permute-start(bf16[2,64,1024]{2,1,0:T(8,128)(2,1)} %get-tuple-element.41), channel_id=1, source_target_pairs={{0,16},{8,24},{16,0},{24,8},{32,48},{40,56},{48,32},{56,40},{64,80... | collective-permute-start | bytes 786440 | tf_op jit(solution)/shard_map/t_other_across/ppermute | solution.py:42
  23.5 1.5 collective-permute-start.8
  25.0 1.6 collective-permute-start.2
  26.6 5.8 %collective-permute-done.2 = s32[2,64]{1,0:T(2,128)S(1)} collective-permute-done((s32[2,64]{1,0:T(2,128)S(1)}, s32[2,64]{1,0:T(2,128)S(1)}, u32[]{:S(2)}, u32[]{:S(2)}) %collective-permute-start.2) | collective-permute-done | bytes 544 | tf_op jit(solution)/shard_map/t_ids_down/ppermute | solution.py:66
  32.4 2.6 %collective-permute-start.3 = (s32[2,64]{1,0:T(2,128)S(1)}, s32[2,64]{1,0:T(2,128)S(1)}, u32[]{:S(2)}, u32[]{:S(2)}) collective-permute-start(s32[2,64]{1,0:T(2,128)S(1)} %add_select_fusion), channel_id=1, source_target_pairs={{0,4},{1,5},{2,6},{3,7},{4,0},{5,1},{6,2},{7,3},{8,12},{9,13},{10,... | collective-permute-start | bytes 1544 | tf_op jit(solution)/shard_map/t_ids_far/ppermute | solution.py:398
  35.0 1.3 collective-permute-done.3
  36.3 1.3 collective-permute-start.4
  37.6 1.8 fusion.5
  39.4 0.1 stack.83
  39.5 0.1 stack.84
  39.6 0.1 stack.85
  39.7 0.5 collective-permute-done.4
  40.1 1.6 collective-permute-start.14
  41.8 0.1 stack.86
  42.0 0.6 copy-done.14
  42.7 0.9 broadcast_in_dim.23.segs
  43.6 1.5 collective-permute-start.10
  45.0 1.7 fusion.3
  46.8 0.3 collective-permute-start.18
  47.1 6.0 %collective-permute-done.10.refs_5_ = bf16[2,2,64,1024]{3,2,1,0:T(8,128)(2,1)S(1)} collective-permute-done((bf16[2,2,64,1024]{3,2,1,0:T(8,128)(2,1)S(1)}, bf16[2,2,64,1024]{3,2,1,0:T(8,128)(2,1)S(1)}, u32[]{:S(2)}, u32[]{:S(2)}) %collective-permute-start.10) | collective-permute-done | bytes 524320 | tf_op jit(solution)/shard_map/t_o_down/ppermute | solution.py:66
  53.1 2.3 %collective-permute-done.9.refs_2_ = bf16[2,2,64,1024]{3,2,1,0:T(8,128)(2,1)S(1)} collective-permute-done((bf16[2,2,64,1024]{3,2,1,0:T(8,128)(2,1)S(1)}, bf16[2,2,64,1024]{3,2,1,0:T(8,128)(2,1)S(1)}, u32[]{:S(2)}, u32[]{:S(2)}) %collective-permute-start.9) | collective-permute-done | bytes 524320 | tf_op jit(solution)/shard_map/t_n_far/ppermute | solution.py:62
  55.5 0.4 collective-permute-done.18
  56.0 2.5 %collective-permute-start.13 = (bf16[1024,512]{1,0:T(8,128)(2,1)}, bf16[1024,512]{1,0:T(8,128)(2,1)}, u32[]{:S(2)}, u32[]{:S(2)}) collective-permute-start(bf16[1024,512]{1,0:T(8,128)(2,1)} %refs_5_.1), channel_id=1, source_target_pairs={{0,96},{8,104},{16,112},{24,120},{32,0},{40,8},{48,16},{56,24},{64... | collective-permute-start | bytes 3145736 | tf_op jit(solution)/shard_map/t_w_down/ppermute | solution.py:58
  58.5 5.6 %collective-permute-done.14.refs_11_.refs_8_ = bf16[1024,512]{1,0:T(8,128)(2,1)} collective-permute-done((bf16[1024,512]{1,0:T(8,128)(2,1)}, bf16[1024,512]{1,0:T(8,128)(2,1)}, u32[]{:S(2)}, u32[]{:S(2)}) %collective-permute-start.14) | collective-permute-done | bytes 1048608 | tf_op jit(solution)/shard_map/t_w_up/ppermute | solution.py:54
  64.0 1.1 pad_maximum_fusion.3
  65.1 0.3 collective-permute-start.19
  65.5 1.0 collective-permute-start.12
  66.5 1.7 collective-permute-start.11
  68.2 8.8 %attend.1 = (bf16[1024,512]{1,0:T(8,128)(2,1)}, f32[4,8,256]{2,1,0:T(8,128)}, f32[4,384,128]{2,1,0:T(8,128)}) custom-call(s32[5]{0:T(128)} %stack.76.place, s32[512,128]{1,0:T(8,128)} %broadcast_in_dim.23.segs, bf16[512,1024]{1,0:T(8,128)(2,1)} %bitcast.37, bf16[512,128]{1,0:T(8,128)(2,1)} %bitcast.48, bf16[512,128]{1,0:T(8,128)(2,1)} %bitcast.50), custom_call_target="tpu_custom_call" | custom-call | bytes 27000000 | tf_op jit(solution)/shard_map/attend/pallas_call | solution.py:181
  76.9 2.8 %collective-permute-start.24 = (bf16[1024,512]{1,0:T(8,128)(2,1)}, bf16[1024,512]{1,0:T(8,128)(2,1)}, u32[]{:S(2)}, u32[]{:S(2)}) collective-permute-start(bf16[1024,512]{1,0:T(8,128)(2,1)} %get-tuple-element.58.refs_9_.refs_12_), channel_id=1, source_target_pairs={{0,16},{8,24},{16,0},{24,8},{32,48},{40,56},{48,32},{56,40},{64,80... | collective-permute-start | bytes 3145736 | tf_op jit(solution)/shard_map/t_out_across/ppermute | solution.py:42
  79.8 6.1 %collective-permute-done.15.refs_10_.refs_7_ = bf16[1024,512]{1,0:T(8,128)(2,1)} collective-permute-done((bf16[1024,512]{1,0:T(8,128)(2,1)}, bf16[1024,512]{1,0:T(8,128)(2,1)}, u32[]{:S(2)}, u32[]{:S(2)}) %collective-permute-start.15) | collective-permute-done | bytes 1048608 | tf_op jit(solution)/shard_map/t_w_far/ppermute | solution.py:54
  85.9 9.3 %partial_grad.2 = (f32[256,1024]{1,0:T(8,128)}, f32[256,1024]{1,0:T(8,128)}, bf16[2,256,1024]{2,1,0:T(8,128)(2,1)}) custom-call(s32[5]{0:T(128)} %stack.76.place, bf16[2,2,64,1024]{3,2,1,0:T(8,128)(2,1)} %copy-done, bf16[2,2,64,1024]{3,2,1,0:T(8,128)(2,1)} %copy-done.3, bf16[2,2,64,1024]{3,2,1,0:T(8,128)(2,1)} %copy-done.5, ...), custom_call_target="tpu_custom_call" | custom-call | bytes 27000000 | tf_op jit(solution)/shard_map/partial_grad/pallas_call | solution.py:310
  95.3 6.8 %collective-permute-start.16 = (bf16[2,256,1024]{2,1,0:T(8,128)(2,1)}, bf16[2,256,1024]{2,1,0:T(8,128)(2,1)S(1)}, u32[]{:S(2)}, u32[]{:S(2)}) collective-permute-start(bf16[2,256,1024]{2,1,0:T(8,128)(2,1)} %get-tuple-element.51), channel_id=1, source_target_pairs={{0,8},{8,0},{16,24},{24,16},{32,40},{40,32},{48,56},{56,48},{64,72... | collective-permute-start | bytes 3145736 | tf_op jit(solution)/shard_map/t_sum_same_sibling/ppermute | solution.py:38
  102.1 3.4 %collective-permute-start.20 = (bf16[2,2,64,1024]{3,2,1,0:T(8,128)(2,1)}, bf16[2,2,64,1024]{3,2,1,0:T(8,128)(2,1)S(1)}, u32[]{:S(2)}, u32[]{:S(2)}) collective-permute-start(bf16[2,2,64,1024]{3,2,1,0:T(8,128)(2,1)} %collective-permute-done.19.refs_8_.refs_1_), channel_id=1, source_target_pairs={{0,6},{1,7},{2,0},{3,1},{4,2},{5,3},{6,4},{7,5},{8,14},{9,15},{10,... | collective-permute-start | bytes 1572872 | tf_op jit(solution)/shard_map/t_q_down/ppermute | solution.py:66
  105.5 0.3 collective-permute-start.25
  105.8 0.3 collective-permute-start.23
  106.1 11.0 %collective-permute-done.20.refs_9_.refs_2_ = bf16[2,2,64,1024]{3,2,1,0:T(8,128)(2,1)S(1)} collective-permute-done((bf16[2,2,64,1024]{3,2,1,0:T(8,128)(2,1)}, bf16[2,2,64,1024]{3,2,1,0:T(8,128)(2,1)S(1)}, u32[]{:S(2)}, u32[]{:S(2)}) %collective-permute-start.20) | collective-permute-done | bytes 524320 | tf_op jit(solution)/shard_map/t_q_down/ppermute | solution.py:66
  117.1 3.3 %collective-permute-start.21 = (bf16[2,2,64,1024]{3,2,1,0:T(8,128)(2,1)S(1)}, bf16[2,2,64,1024]{3,2,1,0:T(8,128)(2,1)}, u32[]{:S(2)}, u32[]{:S(2)}) collective-permute-start(bf16[2,2,64,1024]{3,2,1,0:T(8,128)(2,1)S(1)} %collective-permute-done.20.refs_9_.refs_2_), channel_id=1, source_target_pairs={{0,6},{1,7},{2,0},{3,1},{4,2},{5,3},{6,4},{7,5},{8,14},{9,15},{10,... | collective-permute-start | bytes 1572872 | tf_op jit(solution)/shard_map/t_q_far/ppermute | solution.py:66
  120.4 1.7 fusion.1
  122.1 2.7 %collective-permute-start.17 = (bf16[256,1024]{1,0:T(8,128)(2,1)S(1)}, bf16[256,1024]{1,0:T(8,128)(2,1)S(1)}, u32[]{:S(2)}, u32[]{:S(2)}) collective-permute-start(bf16[256,1024]{1,0:T(8,128)(2,1)S(1)} %fusion.1), channel_id=1, source_target_pairs={{0,16},{8,24},{16,0},{24,8},{32,48},{40,56},{48,32},{56,40},{64,80... | collective-permute-start | bytes 1572872 | tf_op jit(solution)/shard_map/t_sum_same_across/ppermute | solution.py:42
  124.8 0.8 copy-done.13
  125.6 1.0 copy-done.9
  126.6 8.8 %weight_grad.2 = bf16[4,1024,256]{2,1,0:T(8,128)(2,1)} custom-call(s32[5]{0:T(128)} %stack.76.place, bf16[2,2,64,1024]{3,2,1,0:T(8,128)(2,1)} %copy-done, bf16[2,2,64,1024]{3,2,1,0:T(8,128)(2,1)} %copy-done.3, bf16[2,2,64,1024]{3,2,1,0:T(8,128)(2,1)} %copy-done.5, bf16[2,2,64,1024]{3,2,1,0:T(8,128)(2,1)} %copy-done.2, bf16[2,2,64,1024]{3,2,1,0:T(8,128)(2,1)} %copy-done.1, ...), custom_call_target="tpu_custom_call" | custom-call | bytes 27000000 | tf_op jit(solution)/shard_map/weight_grad/pallas_call | solution.py:352
  135.5 0.5 collective-permute-done.17.rest_2_
  136.1 9.0 %weight_grad.3 = bf16[4,1024,256]{2,1,0:T(8,128)(2,1)} custom-call(s32[5]{0:T(128)} %stack.76.place, bf16[2,2,64,1024]{3,2,1,0:T(8,128)(2,1)} %copy-done, bf16[2,2,64,1024]{3,2,1,0:T(8,128)(2,1)} %copy-done.3, bf16[2,2,64,1024]{3,2,1,0:T(8,128)(2,1)} %copy-done.5, bf16[2,2,64,1024]{3,2,1,0:T(8,128)(2,1)} %copy-done.2, bf16[2,2,64,1024]{3,2,1,0:T(8,128)(2,1)} %copy-done.1, ...), custom_call_target="tpu_custom_call" | custom-call | bytes 27000000 | tf_op jit(solution)/shard_map/weight_grad/pallas_call | solution.py:352
  145.1 9.5 %partial_grad.3 = (f32[256,1024]{1,0:T(8,128)}, f32[256,1024]{1,0:T(8,128)}, bf16[2,256,1024]{2,1,0:T(8,128)(2,1)}) custom-call(s32[5]{0:T(128)} %stack.76.place, bf16[4,2,2,64,1024]{4,3,2,1,0:T(8,128)(2,1)} %bitcast.36, bf16[2,2,64,1024]{3,2,1,0:T(8,128)(2,1)} %collective-permute-done.19.refs_8_.refs_1_, bf16[2,2,64,1024]{3,2,1,0:T(8,128)(2,1)} %copy-done.12, ...), custom_call_target="tpu_custom_call" | custom-call | bytes 27000000 | tf_op jit(solution)/shard_map/partial_grad/pallas_call | solution.py:310
  154.6 1.8 collective-permute-start.26
  156.4 2.5 %collective-permute-done.26.rest_4_ = bf16[2,256,1024]{2,1,0:T(8,128)(2,1)S(1)} collective-permute-done((bf16[2,256,1024]{2,1,0:T(8,128)(2,1)}, bf16[2,256,1024]{2,1,0:T(8,128)(2,1)S(1)}, u32[]{:S(2)}, u32[]{:S(2)}) %collective-permute-start.26) | collective-permute-done | bytes 1048608 | tf_op jit(solution)/shard_map/t_sum_flip_sibling/ppermute | solution.py:38
  158.9 1.8 fusion
  160.6 2.7 %collective-permute-start.27 = (bf16[256,1024]{1,0:T(8,128)(2,1)S(1)}, bf16[256,1024]{1,0:T(8,128)(2,1)S(1)}, u32[]{:S(2)}, u32[]{:S(2)}) collective-permute-start(bf16[256,1024]{1,0:T(8,128)(2,1)S(1)} %fusion), channel_id=1, source_target_pairs={{0,16},{8,24},{16,0},{24,8},{32,48},{40,56},{48,32},{56,40},{64,80... | collective-permute-start | bytes 1572872 | tf_op jit(solution)/shard_map/t_sum_flip_across/ppermute | solution.py:42
  163.3 12.0 %collective-permute-done.27.rest_5_ = bf16[256,1024]{1,0:T(8,128)(2,1)S(1)} collective-permute-done((bf16[256,1024]{1,0:T(8,128)(2,1)S(1)}, bf16[256,1024]{1,0:T(8,128)(2,1)S(1)}, u32[]{:S(2)}, u32[]{:S(2)}) %collective-permute-start.27) | collective-permute-done | bytes 524320 | tf_op jit(solution)/shard_map/t_sum_flip_across/ppermute | solution.py:42
  175.3 0.8 copy-done.17
  176.1 9.3 %attend_grad.1 = (bf16[512,1024]{1,0:T(8,128)(2,1)}, bf16[512,128]{1,0:T(8,128)(2,1)}, bf16[512,128]{1,0:T(8,128)(2,1)}) custom-call(s32[5]{0:T(128)} %stack.76.place, bf16[512,1024]{1,0:T(8,128)(2,1)} %bitcast.38, bf16[512,128]{1,0:T(8,128)(2,1)} %bitcast.49, bf16[512,128]{1,0:T(8,128)(2,1)} %bitcast.51, f32[4,8,256]{2,1,0:T(8,128)} %get-tuple-element.45.stats, ...), custom_call_target="tpu_custom_call" | custom-call | bytes 27000000 | tf_op jit(solution)/shard_map/attend_grad/pallas_call | solution.py:250
  185.5 13.9 %reduce-scatter.5.cloned.1.call-done = bf16[1024,256]{1,0:T(8,128)(2,1)} async-done(((bf16[4096,256]{1,0:T(8,128)(2,1)}), bf16[1024,256]{1,0:T(8,128)(2,1)}) %reduce-scatter.5.cloned.1.call-update) | async-done | bytes 524304 | tf_op jit(solution)/shard_map/reduce_scatter | solution.py:434
  199.4 2.8 %maximum_convert_fusion = f32[1024,512]{1,0:T(8,128)} fusion(bf16[1024,256]{1,0:T(8,128)(2,1)} %reduce-scatter.5.cloned.1.call-done, bf16[1024,256]{1,0:T(8,128)(2,1)} %reduce-scatter.3.cloned.1.call-done), kind=kLoop, calls=%fused_computation | loop fusion | flops 2097152 | bytes 3145728 | tf_op jit(solution)/shard_map/convert_element_type | solution.py:445
  (65 shorter events, 0.5 us)
Async XLA Ops:
  7.2 17.8 %copy-start.18 = (s32[1,64]{1,0:T(1,128)S(1)}, s32[1,64]{1,0:T(1,128)}, u32[]{:S(2)}) copy-start(s32[1,64]{1,0:T(1,128)} %param.10) | copy-start | bytes 772
  7.2 118.4 %all-gather.3.cloned.1.call-start = ((), (), s32[]{:S(2)}) async-start(), calls=%async_computation.4 | async-start | bytes 2621440 | tf_op jit(solution)/shard_map/all_gather | solution.py:411
  7.2 7.5 %collective-permute-start = (s32[64]{0:T(128)}, s32[64]{0:T(128)S(1)}, u32[]{:S(2)}, u32[]{:S(2)}) collective-permute-start(s32[64]{0:T(128)} %bitcast.52), channel_id=1, source_target_pairs={{0,1},{1,0},{2,3},{3,2},{4,5},{5,4},{6,7},{7,6},{8,9},{9,8},{10,11... | collective-permute-start | bytes 776 | tf_op jit(solution)/shard_map/t_ids_pair/ppermute | solution.py:50
  14.8 2.4 %collective-permute-start.1 = (bf16[2,64,1024]{2,1,0:T(8,128)(2,1)}, bf16[2,64,1024]{2,1,0:T(8,128)(2,1)S(1)}, u32[]{:S(2)}, u32[]{:S(2)}) collective-permute-start(bf16[2,64,1024]{2,1,0:T(8,128)(2,1)} %get-tuple-element.39), channel_id=1, source_target_pairs={{0,8},{8,0},{16,24},{24,16},{32,40},{40,32},{48,56},{56,48},{64,72... | collective-permute-start | bytes 786440 | tf_op jit(solution)/shard_map/t_near_sibling/ppermute | solution.py:38
  18.2 28.6 %copy-start = (bf16[2,2,64,1024]{3,2,1,0:T(8,128)(2,1)}, bf16[2,2,64,1024]{3,2,1,0:T(8,128)(2,1)S(1)}, u32[]{:S(2)}) copy-start(bf16[2,2,64,1024]{3,2,1,0:T(8,128)(2,1)S(1)} %pad_maximum_fusion.refs_0_) | copy-start | bytes 1572868
  18.2 23.7 %collective-permute-start.5 = (bf16[2,2,64,1024]{3,2,1,0:T(8,128)(2,1)S(1)}, bf16[2,2,64,1024]{3,2,1,0:T(8,128)(2,1)S(1)}, u32[]{:S(2)}, u32[]{:S(2)}) collective-permute-start(bf16[2,2,64,1024]{3,2,1,0:T(8,128)(2,1)S(1)} %pad_maximum_fusion.refs_0_), channel_id=1, source_target_pairs={{0,2},{1,3},{2,4},{3,5},{4,6},{5,7},{6,0},{7,1},{8,10},{9,11},{10,... | collective-permute-start | bytes 1572872 | tf_op jit(solution)/shard_map/t_n_up/ppermute | solution.py:62
  19.5 22.4 %collective-permute-start.6 = (bf16[2,2,64,1024]{3,2,1,0:T(8,128)(2,1)S(1)}, bf16[2,2,64,1024]{3,2,1,0:T(8,128)(2,1)S(1)}, u32[]{:S(2)}, u32[]{:S(2)}) collective-permute-start(bf16[2,2,64,1024]{3,2,1,0:T(8,128)(2,1)S(1)} %pad_maximum_fusion.refs_0_), channel_id=1, source_target_pairs={{0,6},{1,7},{2,0},{3,1},{4,2},{5,3},{6,4},{7,5},{8,14},{9,15},{10,... | collective-permute-start | bytes 1572872 | tf_op jit(solution)/shard_map/t_n_down/ppermute | solution.py:66
  21.1 20.9 %collective-permute-start.7 = (bf16[2,64,1024]{2,1,0:T(8,128)(2,1)}, bf16[2,64,1024]{2,1,0:T(8,128)(2,1)S(1)}, u32[]{:S(2)}, u32[]{:S(2)}) collective-permute-start(bf16[2,64,1024]{2,1,0:T(8,128)(2,1)} %get-tuple-element.41), channel_id=1, source_target_pairs={{0,16},{8,24},{16,0},{24,8},{32,48},{40,56},{48,32},{56,40},{64,80... | collective-permute-start | bytes 786440 | tf_op jit(solution)/shard_map/t_other_across/ppermute | solution.py:42
  23.5 18.5 %collective-permute-start.8 = (bf16[2,64,1024]{2,1,0:T(8,128)(2,1)}, bf16[2,64,1024]{2,1,0:T(8,128)(2,1)S(1)}, u32[]{:S(2)}, u32[]{:S(2)}) collective-permute-start(bf16[2,64,1024]{2,1,0:T(8,128)(2,1)} %get-tuple-element.43), channel_id=1, source_target_pairs={{0,24},{8,16},{16,8},{24,0},{32,56},{40,48},{48,40},{56,32},{64,88... | collective-permute-start | bytes 786440 | tf_op jit(solution)/shard_map/t_other_diagonal/ppermute | solution.py:46
  25.0 7.4 %collective-permute-start.2 = (s32[2,64]{1,0:T(2,128)S(1)}, s32[2,64]{1,0:T(2,128)S(1)}, u32[]{:S(2)}, u32[]{:S(2)}) collective-permute-start(s32[2,64]{1,0:T(2,128)S(1)} %add_select_fusion), channel_id=1, source_target_pairs={{0,6},{1,7},{2,0},{3,1},{4,2},{5,3},{6,4},{7,5},{8,14},{9,15},{10,... | collective-permute-start | bytes 1544 | tf_op jit(solution)/shard_map/t_ids_down/ppermute | solution.py:66
  32.4 3.9 %collective-permute-start.3 = (s32[2,64]{1,0:T(2,128)S(1)}, s32[2,64]{1,0:T(2,128)S(1)}, u32[]{:S(2)}, u32[]{:S(2)}) collective-permute-start(s32[2,64]{1,0:T(2,128)S(1)} %add_select_fusion), channel_id=1, source_target_pairs={{0,4},{1,5},{2,6},{3,7},{4,0},{5,1},{6,2},{7,3},{8,12},{9,13},{10,... | collective-permute-start | bytes 1544 | tf_op jit(solution)/shard_map/t_ids_far/ppermute | solution.py:398
  36.3 3.8 %collective-permute-start.4 = (s32[2,64]{1,0:T(2,128)S(1)}, s32[2,64]{1,0:T(2,128)S(1)}, u32[]{:S(2)}, u32[]{:S(2)}) collective-permute-start(s32[2,64]{1,0:T(2,128)S(1)} %add_select_fusion), channel_id=1, source_target_pairs={{0,2},{1,3},{2,4},{3,5},{4,6},{5,7},{6,0},{7,1},{8,10},{9,11},{10,... | collective-permute-start | bytes 1544 | tf_op jit(solution)/shard_map/t_ids_up/ppermute | solution.py:62
  40.1 23.9 %collective-permute-start.14 = (bf16[1024,512]{1,0:T(8,128)(2,1)}, bf16[1024,512]{1,0:T(8,128)(2,1)}, u32[]{:S(2)}, u32[]{:S(2)}) collective-permute-start(bf16[1024,512]{1,0:T(8,128)(2,1)} %refs_5_.1), channel_id=1, source_target_pairs={{0,32},{8,40},{16,48},{24,56},{32,64},{40,72},{48,80},{56,88},{64,... | collective-permute-start | bytes 3145736 | tf_op jit(solution)/shard_map/t_w_up/ppermute | solution.py:54
  41.9 4.8 %copy-start.15 = (bf16[1,2,64,1024]{3,2,1,0:T(8,128)(2,1)S(1)}, bf16[1,2,64,1024]{3,2,1,0:T(8,128)(2,1)}, u32[]{:S(2)}) copy-start(bf16[1,2,64,1024]{3,2,1,0:T(8,128)(2,1)} %get-tuple-element.71) | copy-start | bytes 786436
  41.9 23.2 %copy-start.2 = (bf16[2,2,64,1024]{3,2,1,0:T(8,128)(2,1)}, bf16[2,2,64,1024]{3,2,1,0:T(8,128)(2,1)S(1)}, u32[]{:S(2)}) copy-start(bf16[2,2,64,1024]{3,2,1,0:T(8,128)(2,1)S(1)} %collective-permute-done.5.refs_3_) | copy-start | bytes 1572868
  42.0 23.2 %copy-start.3 = (bf16[2,2,64,1024]{3,2,1,0:T(8,128)(2,1)}, bf16[2,2,64,1024]{3,2,1,0:T(8,128)(2,1)S(1)}, u32[]{:S(2)}) copy-start(bf16[2,2,64,1024]{3,2,1,0:T(8,128)(2,1)S(1)} %collective-permute-done.6.refs_1_) | copy-start | bytes 1572868
  42.0 0.7 copy-start.14
  42.7 34.2 %copy-start.1 = (bf16[2,2,64,1024]{3,2,1,0:T(8,128)(2,1)}, bf16[2,2,64,1024]{3,2,1,0:T(8,128)(2,1)S(1)}, u32[]{:S(2)}) copy-start(bf16[2,2,64,1024]{3,2,1,0:T(8,128)(2,1)S(1)} %pad_maximum_fusion.1.refs_4_) | copy-start | bytes 1572868
  43.6 9.6 %collective-permute-start.10 = (bf16[2,2,64,1024]{3,2,1,0:T(8,128)(2,1)S(1)}, bf16[2,2,64,1024]{3,2,1,0:T(8,128)(2,1)S(1)}, u32[]{:S(2)}, u32[]{:S(2)}) collective-permute-start(bf16[2,2,64,1024]{3,2,1,0:T(8,128)(2,1)S(1)} %pad_maximum_fusion.1.refs_4_), channel_id=1, source_target_pairs={{0,6},{1,7},{2,0},{3,1},{4,2},{5,3},{6,4},{7,5},{8,14},{9,15},{10,... | collective-permute-start | bytes 1572872 | tf_op jit(solution)/shard_map/t_o_down/ppermute | solution.py:66
  45.0 10.5 %collective-permute-start.9 = (bf16[2,2,64,1024]{3,2,1,0:T(8,128)(2,1)S(1)}, bf16[2,2,64,1024]{3,2,1,0:T(8,128)(2,1)S(1)}, u32[]{:S(2)}, u32[]{:S(2)}) collective-permute-start(bf16[2,2,64,1024]{3,2,1,0:T(8,128)(2,1)S(1)} %collective-permute-done.5.refs_3_), channel_id=1, source_target_pairs={{0,2},{1,3},{2,4},{3,5},{4,6},{5,7},{6,0},{7,1},{8,10},{9,11},{10,... | collective-permute-start | bytes 1572872 | tf_op jit(solution)/shard_map/t_n_far/ppermute | solution.py:62
  46.8 9.1 %collective-permute-start.18 = (bf16[2,2,64,1024]{3,2,1,0:T(8,128)(2,1)S(1)}, bf16[2,2,64,1024]{3,2,1,0:T(8,128)(2,1)}, u32[]{:S(2)}, u32[]{:S(2)}) collective-permute-start(bf16[2,2,64,1024]{3,2,1,0:T(8,128)(2,1)S(1)} %pad_maximum_fusion.2), channel_id=1, source_target_pairs={{0,1},{1,0},{2,3},{3,2},{4,5},{5,4},{6,7},{7,6},{8,9},{9,8},{10,11... | collective-permute-start | bytes 1572872 | tf_op jit(solution)/shard_map/t_pair_0/ppermute | solution.py:50
  53.1 32.8 %copy-start.4 = (bf16[2,2,64,1024]{3,2,1,0:T(8,128)(2,1)}, bf16[2,2,64,1024]{3,2,1,0:T(8,128)(2,1)S(1)}, u32[]{:S(2)}) copy-start(bf16[2,2,64,1024]{3,2,1,0:T(8,128)(2,1)S(1)} %collective-permute-done.10.refs_5_) | copy-start | bytes 1572868
  55.5 30.4 %copy-start.5 = (bf16[2,2,64,1024]{3,2,1,0:T(8,128)(2,1)}, bf16[2,2,64,1024]{3,2,1,0:T(8,128)(2,1)S(1)}, u32[]{:S(2)}) copy-start(bf16[2,2,64,1024]{3,2,1,0:T(8,128)(2,1)S(1)} %collective-permute-done.9.refs_2_) | copy-start | bytes 1572868
  55.9 129.5 %reduce-scatter.3.cloned.1.call-start = ((), (), s32[]{:S(2)}) async-start(), calls=%async_computation.2 | async-start | bytes 2621440 | tf_op jit(solution)/shard_map/reduce_scatter | solution.py:434
  56.0 23.8 %collective-permute-start.13 = (bf16[1024,512]{1,0:T(8,128)(2,1)}, bf16[1024,512]{1,0:T(8,128)(2,1)}, u32[]{:S(2)}, u32[]{:S(2)}) collective-permute-start(bf16[1024,512]{1,0:T(8,128)(2,1)} %refs_5_.1), channel_id=1, source_target_pairs={{0,96},{8,104},{16,112},{24,120},{32,0},{40,8},{48,16},{56,24},{64... | collective-permute-start | bytes 3145736 | tf_op jit(solution)/shard_map/t_w_down/ppermute | solution.py:58
  64.0 21.9 %collective-permute-start.15 = (bf16[1024,512]{1,0:T(8,128)(2,1)}, bf16[1024,512]{1,0:T(8,128)(2,1)}, u32[]{:S(2)}, u32[]{:S(2)}) collective-permute-start(bf16[1024,512]{1,0:T(8,128)(2,1)} %collective-permute-done.14.refs_11_.refs_8_), channel_id=1, source_target_pairs={{0,32},{8,40},{16,48},{24,56},{32,64},{40,72},{48,80},{56,88},{64,... | collective-permute-start | bytes 3145736 | tf_op jit(solution)/shard_map/t_w_far/ppermute | solution.py:54
  65.1 11.8 %collective-permute-start.19 = (bf16[2,2,64,1024]{3,2,1,0:T(8,128)(2,1)S(1)}, bf16[2,2,64,1024]{3,2,1,0:T(8,128)(2,1)}, u32[]{:S(2)}, u32[]{:S(2)}) collective-permute-start(bf16[2,2,64,1024]{3,2,1,0:T(8,128)(2,1)S(1)} %pad_maximum_fusion.3), channel_id=1, source_target_pairs={{0,1},{1,0},{2,3},{3,2},{4,5},{5,4},{6,7},{7,6},{8,9},{9,8},{10,11... | collective-permute-start | bytes 1572872 | tf_op jit(solution)/shard_map/t_pair_1/ppermute | solution.py:50
  65.5 14.3 %collective-permute-start.12 = (bf16[2,2,64,1024]{3,2,1,0:T(8,128)(2,1)S(1)}, bf16[2,2,64,1024]{3,2,1,0:T(8,128)(2,1)S(1)}, u32[]{:S(2)}, u32[]{:S(2)}) collective-permute-start(bf16[2,2,64,1024]{3,2,1,0:T(8,128)(2,1)S(1)} %pad_maximum_fusion.1.refs_4_), channel_id=1, source_target_pairs={{0,2},{1,3},{2,4},{3,5},{4,6},{5,7},{6,0},{7,1},{8,10},{9,11},{10,... | collective-permute-start | bytes 1572872 | tf_op jit(solution)/shard_map/t_o_up/ppermute | solution.py:62
  66.5 13.3 %collective-permute-start.11 = (bf16[2,2,64,1024]{3,2,1,0:T(8,128)(2,1)S(1)}, bf16[2,2,64,1024]{3,2,1,0:T(8,128)(2,1)S(1)}, u32[]{:S(2)}, u32[]{:S(2)}) collective-permute-start(bf16[2,2,64,1024]{3,2,1,0:T(8,128)(2,1)S(1)} %collective-permute-done.10.refs_5_), channel_id=1, source_target_pairs={{0,6},{1,7},{2,0},{3,1},{4,2},{5,3},{6,4},{7,5},{8,14},{9,15},{10,... | collective-permute-start | bytes 1572872 | tf_op jit(solution)/shard_map/t_o_far/ppermute | solution.py:66
  76.9 28.9 %copy-start.8 = (bf16[1024,512]{1,0:T(8,128)(2,1)S(1)}, bf16[1024,512]{1,0:T(8,128)(2,1)}, u32[]{:S(2)}) copy-start(bf16[1024,512]{1,0:T(8,128)(2,1)} %get-tuple-element.58.refs_9_.refs_12_) | copy-start | bytes 3145732
  76.9 28.5 %collective-permute-start.24 = (bf16[1024,512]{1,0:T(8,128)(2,1)}, bf16[1024,512]{1,0:T(8,128)(2,1)}, u32[]{:S(2)}, u32[]{:S(2)}) collective-permute-start(bf16[1024,512]{1,0:T(8,128)(2,1)} %get-tuple-element.58.refs_9_.refs_12_), channel_id=1, source_target_pairs={{0,16},{8,24},{16,0},{24,8},{32,48},{40,56},{48,32},{56,40},{64,80... | collective-permute-start | bytes 3145736 | tf_op jit(solution)/shard_map/t_out_across/ppermute | solution.py:42
  79.8 6.2 %copy-start.6 = (bf16[2,2,64,1024]{3,2,1,0:T(8,128)(2,1)}, bf16[2,2,64,1024]{3,2,1,0:T(8,128)(2,1)S(1)}, u32[]{:S(2)}) copy-start(bf16[2,2,64,1024]{3,2,1,0:T(8,128)(2,1)S(1)} %collective-permute-done.12.refs_7_) | copy-start | bytes 1572868
  79.8 6.2 %copy-start.7 = (bf16[2,2,64,1024]{3,2,1,0:T(8,128)(2,1)}, bf16[2,2,64,1024]{3,2,1,0:T(8,128)(2,1)S(1)}, u32[]{:S(2)}) copy-start(bf16[2,2,64,1024]{3,2,1,0:T(8,128)(2,1)S(1)} %collective-permute-done.11.refs_6_) | copy-start | bytes 1572868
  95.3 25.1 %collective-permute-start.16 = (bf16[2,256,1024]{2,1,0:T(8,128)(2,1)}, bf16[2,256,1024]{2,1,0:T(8,128)(2,1)S(1)}, u32[]{:S(2)}, u32[]{:S(2)}) collective-permute-start(bf16[2,256,1024]{2,1,0:T(8,128)(2,1)} %get-tuple-element.51), channel_id=1, source_target_pairs={{0,8},{8,0},{16,24},{24,16},{32,40},{40,32},{48,56},{56,48},{64,72... | collective-permute-start | bytes 3145736 | tf_op jit(solution)/shard_map/t_sum_same_sibling/ppermute | solution.py:38
  102.1 15.0 %collective-permute-start.20 = (bf16[2,2,64,1024]{3,2,1,0:T(8,128)(2,1)}, bf16[2,2,64,1024]{3,2,1,0:T(8,128)(2,1)S(1)}, u32[]{:S(2)}, u32[]{:S(2)}) collective-permute-start(bf16[2,2,64,1024]{3,2,1,0:T(8,128)(2,1)} %collective-permute-done.19.refs_8_.refs_1_), channel_id=1, source_target_pairs={{0,6},{1,7},{2,0},{3,1},{4,2},{5,3},{6,4},{7,5},{8,14},{9,15},{10,... | collective-permute-start | bytes 1572872 | tf_op jit(solution)/shard_map/t_q_down/ppermute | solution.py:66
  105.5 19.3 %collective-permute-start.25 = (bf16[1024,512]{1,0:T(8,128)(2,1)}, bf16[1024,512]{1,0:T(8,128)(2,1)S(1)}, u32[]{:S(2)}, u32[]{:S(2)}) collective-permute-start(bf16[1024,512]{1,0:T(8,128)(2,1)} %collective-permute-done.24.refs_11_.refs_14_), channel_id=1, source_target_pairs={{0,8},{8,0},{16,24},{24,16},{32,40},{40,32},{48,56},{56,48},{64,72... | collective-permute-start | bytes 3145736 | tf_op jit(solution)/shard_map/t_out_other/ppermute | solution.py:38
  105.8 19.8 %collective-permute-start.23 = (bf16[1024,512]{1,0:T(8,128)(2,1)S(1)}, bf16[1024,512]{1,0:T(8,128)(2,1)}, u32[]{:S(2)}, u32[]{:S(2)}) collective-permute-start(bf16[1024,512]{1,0:T(8,128)(2,1)S(1)} %copy-done.8), channel_id=1, source_target_pairs={{0,8},{8,0},{16,24},{24,16},{32,40},{40,32},{48,56},{56,48},{64,72... | collective-permute-start | bytes 3145736 | tf_op jit(solution)/shard_map/t_out_near/ppermute | solution.py:38
  106.1 18.7 %collective-permute-start.22 = (bf16[2,2,64,1024]{3,2,1,0:T(8,128)(2,1)}, bf16[2,2,64,1024]{3,2,1,0:T(8,128)(2,1)S(1)}, u32[]{:S(2)}, u32[]{:S(2)}) collective-permute-start(bf16[2,2,64,1024]{3,2,1,0:T(8,128)(2,1)} %collective-permute-done.19.refs_8_.refs_1_), channel_id=1, source_target_pairs={{0,2},{1,3},{2,4},{3,5},{4,6},{5,7},{6,0},{7,1},{8,10},{9,11},{10,... | collective-permute-start | bytes 1572872 | tf_op jit(solution)/shard_map/t_q_up/ppermute | solution.py:62
  117.1 18.4 %copy-start.12 = (bf16[2,2,64,1024]{3,2,1,0:T(8,128)(2,1)}, bf16[2,2,64,1024]{3,2,1,0:T(8,128)(2,1)S(1)}, u32[]{:S(2)}) copy-start(bf16[2,2,64,1024]{3,2,1,0:T(8,128)(2,1)S(1)} %collective-permute-done.20.refs_9_.refs_2_) | copy-start | bytes 1572868
  117.1 18.4 %collective-permute-start.21 = (bf16[2,2,64,1024]{3,2,1,0:T(8,128)(2,1)S(1)}, bf16[2,2,64,1024]{3,2,1,0:T(8,128)(2,1)}, u32[]{:S(2)}, u32[]{:S(2)}) collective-permute-start(bf16[2,2,64,1024]{3,2,1,0:T(8,128)(2,1)S(1)} %collective-permute-done.20.refs_9_.refs_2_), channel_id=1, source_target_pairs={{0,6},{1,7},{2,0},{3,1},{4,2},{5,3},{6,4},{7,5},{8,14},{9,15},{10,... | collective-permute-start | bytes 1572872 | tf_op jit(solution)/shard_map/t_q_far/ppermute | solution.py:66
  120.4 4.4 %copy-start.10 = (bf16[2,256,1024]{2,1,0:T(8,128)(2,1)}, bf16[2,256,1024]{2,1,0:T(8,128)(2,1)S(1)}, u32[]{:S(2)}) copy-start(bf16[2,256,1024]{2,1,0:T(8,128)(2,1)S(1)} %collective-permute-done.16.rest_1_) | copy-start | bytes 3145732
  122.1 13.9 %collective-permute-start.17 = (bf16[256,1024]{1,0:T(8,128)(2,1)S(1)}, bf16[256,1024]{1,0:T(8,128)(2,1)S(1)}, u32[]{:S(2)}, u32[]{:S(2)}) collective-permute-start(bf16[256,1024]{1,0:T(8,128)(2,1)S(1)} %fusion.1), channel_id=1, source_target_pairs={{0,16},{8,24},{16,0},{24,8},{32,48},{40,56},{48,32},{56,40},{64,80... | collective-permute-start | bytes 1572872 | tf_op jit(solution)/shard_map/t_sum_same_across/ppermute | solution.py:42
  124.8 0.8 copy-start.13
  125.6 1.0 copy-start.9
  136.0 9.0 %copy-start.16 = (bf16[256,1024]{1,0:T(8,128)(2,1)}, bf16[256,1024]{1,0:T(8,128)(2,1)S(1)}, u32[]{:S(2)}) copy-start(bf16[256,1024]{1,0:T(8,128)(2,1)S(1)} %collective-permute-done.17.rest_2_) | copy-start | bytes 1572868
  136.0 63.4 %reduce-scatter.5.cloned.1.call-start = ((), (), s32[]{:S(2)}) async-start(), calls=%async_computation.3 | async-start | bytes 2621440 | tf_op jit(solution)/shard_map/reduce_scatter | solution.py:434
  154.6 4.3 %collective-permute-start.26 = (bf16[2,256,1024]{2,1,0:T(8,128)(2,1)}, bf16[2,256,1024]{2,1,0:T(8,128)(2,1)S(1)}, u32[]{:S(2)}, u32[]{:S(2)}) collective-permute-start(bf16[2,256,1024]{2,1,0:T(8,128)(2,1)} %get-tuple-element.64), channel_id=1, source_target_pairs={{0,8},{8,0},{16,24},{24,16},{32,40},{40,32},{48,56},{56,48},{64,72... | collective-permute-start | bytes 3145736 | tf_op jit(solution)/shard_map/t_sum_flip_sibling/ppermute | solution.py:38
  158.9 16.5 %copy-start.11 = (bf16[2,256,1024]{2,1,0:T(8,128)(2,1)}, bf16[2,256,1024]{2,1,0:T(8,128)(2,1)S(1)}, u32[]{:S(2)}) copy-start(bf16[2,256,1024]{2,1,0:T(8,128)(2,1)S(1)} %collective-permute-done.26.rest_4_) | copy-start | bytes 3145732
  160.6 14.7 %collective-permute-start.27 = (bf16[256,1024]{1,0:T(8,128)(2,1)S(1)}, bf16[256,1024]{1,0:T(8,128)(2,1)S(1)}, u32[]{:S(2)}, u32[]{:S(2)}) collective-permute-start(bf16[256,1024]{1,0:T(8,128)(2,1)S(1)} %fusion), channel_id=1, source_target_pairs={{0,16},{8,24},{16,0},{24,8},{32,48},{40,56},{48,32},{56,40},{64,80... | collective-permute-start | bytes 1572872 | tf_op jit(solution)/shard_map/t_sum_flip_across/ppermute | solution.py:42
  175.3 0.8 copy-start.17
Sparse Core Ops, SparseCore 0:
  56.1 41.8 all-gather.2
  136.1 30.5 reduce-scatter.2
  169.9 29.4 reduce-scatter.4

commit v5 on v3

--- a/solution.py
+++ b/solution.py
@@ -11,7 +11,6 @@
 F32 = jnp.float32
 BF16 = jnp.bfloat16
 SCALE = HD ** (-0.5)
-LIGHT = pl.CostEstimate(flops=0, bytes_accessed=0, transcendentals=0)
 VMEM_MOST = 60 * 1024 * 1024
 
 
@@ -30,7 +29,6 @@
 Y_UP = by_tensor(lambda i: (i + 2) % 8)
 Y_DOWN = by_tensor(lambda i: (i - 2) % 8)
 Z_GROUPS = [[z * 4 + j for z in range(4)] for j in range(4)]
-Y_GROUPS = [[y * 2 + low for y in range(4)] for low in range(2)]
 
 
 def sibling(x):
@@ -63,6 +61,10 @@
 
 def nt(a, b):
     return lax.dot_general(a, b, (((1,), (1,)), ((), ())), preferred_element_type=F32)
+
+
+def cost(us):
+    return pl.CostEstimate(flops=0, bytes_accessed=int(us * 3e6), transcendentals=0)
 
 
 def params():
@@ -109,7 +111,7 @@
         out_specs=[col] * 4,
         out_shape=[shape] * 4,
         compiler_params=params(),
-        cost_estimate=LIGHT,
+        cost_estimate=cost(3),
         name="prep",
     )(place, margins, segs, up)
 
@@ -187,7 +189,7 @@
         ],
         scratch_shapes=[pltpu.VMEM((HD, length), BF16)],
         compiler_params=params(),
-        cost_estimate=LIGHT,
+        cost_estimate=cost(9),
         name="attend",
     )(place, segs, q, k, v)
 
@@ -250,23 +252,14 @@
         out_shape=[jax.ShapeDtypeStruct(x.shape, BF16) for x in (q, k, v)],
         scratch_shapes=[pltpu.VMEM((HD, length), BF16), pltpu.VMEM(k.shape, F32), pltpu.VMEM(v.shape, F32)],
         compiler_params=params(),
-        cost_estimate=LIGHT,
+        cost_estimate=cost(9),
         name="attend_grad",
     )(place, q, k, v, stats, bias, *terms)
 
 
-def reader(place, refs):
-    y = place[0]
-    if len(refs) == 8:
-        return lambda p, i, e, k: refs[p * 4 + k][e, i]
-    return lambda p, i, e, k: refs[e][lax.rem(y + k, 4), p, i]
-
-
-def partial_kernel(count, place, *refs):
-    read = reader(place, refs[:count])
-    weight, keep_near, keep_other, give, x = refs[count:]
-    seq = refs[count - 1].shape[-2]
-    cols = refs[count - 1].shape[-1]
+def partial_kernel(by_half, *refs):
+    pieces, (weight, keep_near, keep_other, give, x) = refs[:8], refs[8:]
+    _, _, seq, cols = pieces[0].shape
     half = 4 * seq
     width = weight.shape[2] // 2
 
@@ -277,7 +270,8 @@
                 for i in range(2):
                     for k in range(4):
                         at = (p * 2 + i) * half + k * seq
-                        x[at : at + seq, e * cols : (e + 1) * cols] = read(p, i, e, k)
+                        piece = pieces[e * 4 + k][p, i] if by_half else pieces[p * 4 + k][e, i]
+                        x[at : at + seq, e * cols : (e + 1) * cols] = piece
 
     w = jnp.concatenate([weight[j, :, e * width : (e + 1) * width] for e in range(2) for j in range(4)], axis=1)
     for p, keep in enumerate((keep_near, keep_other)):
@@ -286,36 +280,35 @@
         give[p] = total[half:].astype(BF16)
 
 
-def partial(place, pieces, weight):
-    seq, cols = pieces[-1].shape[-2:]
+def partial(by_half, pieces, weight):
+    _, _, seq, cols = pieces[0].shape
     heads = weight.shape[1]
     tile = heads // 2
     out = pl.BlockSpec((4 * seq, tile), lambda i: (0, i))
     shape = jax.ShapeDtypeStruct((4 * seq, heads), F32)
     return pl.pallas_call(
-        functools.partial(partial_kernel, len(pieces)),
+        functools.partial(partial_kernel, by_half),
         grid=(2,),
-        in_specs=[SMEM()] + [whole(x.shape) for x in pieces] + [pl.BlockSpec((4, tile, cols // 2), lambda i: (0, i, 0))],
+        in_specs=[whole(x.shape) for x in pieces] + [pl.BlockSpec((4, tile, cols // 2), lambda i: (0, i, 0))],
         out_specs=[out, out, pl.BlockSpec((2, 4 * seq, tile), lambda i: (0, 0, i))],
         out_shape=[shape, shape, jax.ShapeDtypeStruct((2, 4 * seq, heads), BF16)],
         scratch_shapes=[pltpu.VMEM((16 * seq, 2 * cols), BF16)],
         compiler_params=params(),
-        cost_estimate=LIGHT,
+        cost_estimate=cost(9),
         name="partial_grad",
-    )(place, *pieces, weight)
-
-
-def wgrad_kernel(place, *refs):
-    same, flip, outs, (out, x) = refs[:8], refs[8], refs[9:13], refs[13:]
+    )(*pieces, weight)
+
+
+def wgrad_kernel(*refs):
+    same, flip, outs, (out, x) = refs[:8], refs[8:12], refs[12:16], refs[-2:]
     seq = same[0].shape[2]
     length = 8 * seq
-    y = place[0]
     for p in range(2):
         for i in range(2):
             for k in range(4):
                 at = (p * 2 + i) * length + 2 * k * seq
                 x[at : at + seq] = same[p * 4 + k][0, i]
-                x[at + seq : at + 2 * seq] = flip[lax.rem(y + k, 4), p, i]
+                x[at + seq : at + 2 * seq] = flip[k][p, i]
     tile = 256
     width = out.shape[2]
     for m in range(0, out.shape[1], tile):
@@ -326,24 +319,26 @@
             out[k, m : m + tile] = total[:, k * width : (k + 1) * width].astype(BF16)
 
 
-def wgrad(place, half, same, flip, outs):
+def wgrad(half, same, flip, outs, into=None):
     _, _, seq, cols = same[0].shape
     heads = outs[0].shape[0]
     wide = cols // 2
+    kept = [] if into is None else [into]
     return pl.pallas_call(
         wgrad_kernel,
         grid=(2,),
-        in_specs=[SMEM()]
-        + [pl.BlockSpec((1, 2, seq, wide), lambda i: (half, 0, 0, i))] * 8
-        + [pl.BlockSpec((4, 2, 2, seq, wide), lambda i: (0, 0, 0, 0, i))]
-        + [whole(outs[0].shape)] * 4,
-        out_specs=pl.BlockSpec((2, heads, wide // 2), lambda i: (i, 0, 0)),
-        out_shape=jax.ShapeDtypeStruct((4, heads, wide // 2), BF16),
+        in_specs=[pl.BlockSpec((1, 2, seq, wide), lambda i: (half, 0, 0, i))] * 8
+        + [pl.BlockSpec((2, 2, seq, wide), lambda i: (0, 0, 0, i))] * 4
+        + [whole(outs[0].shape)] * 4
+        + [pl.BlockSpec(memory_space=pl.ANY)] * len(kept),
+        out_specs=pl.BlockSpec((2, heads, wide // 2), lambda i: (i, 0, half)),
+        out_shape=jax.ShapeDtypeStruct((4, heads, wide), BF16),
         scratch_shapes=[pltpu.VMEM((32 * seq, wide), BF16)],
+        input_output_aliases={16: 0} if kept else {},
         compiler_params=params(),
-        cost_estimate=LIGHT,
+        cost_estimate=cost(9),
         name="weight_grad",
-    )(place, *same, flip, *outs)
+    )(*same, *flip, *outs, *kept)
 
 
 def named(name, fn, x):
@@ -362,8 +357,8 @@
     place = jnp.stack([y, low, (d // 2) % 2, d % 2]).astype(jnp.int32)
     query, key, value = query_states[0], key_states[0], value_states[0]
     heads, width = out_weight.shape
+
     weight = lax.all_gather(out_weight, "dp", axis=0, tiled=True, axis_index_groups=Z_GROUPS).reshape(4, heads, width)
-
     ids = segment_ids[0]
     partner = named("ids_pair", pair, ids)
     segs = jnp.broadcast_to(ids[:, None], (ids.shape[0], HD))
@@ -374,53 +369,47 @@
     near = jnp.stack([own, named("near_sibling", sibling, after(to_sibling, partner))], axis=1)
     n_up, n_down = named("n_up", y_up, near), named("n_down", y_down, near)
     both = jnp.where(low == 0, jnp.stack([ids, partner]), jnp.stack([partner, ids]))
-    both = after(both, near)
-    ids_up = named("ids_up", y_up, both)
-    ids_down = named("ids_down", y_down, both)
-    ids_far = named("ids_far", lambda x: lax.ppermute(x, "tensor", by_tensor(lambda i: (i + 4) % 8)), both)
-    ring = jnp.stack([both, ids_down, ids_far, ids_up] * 2).reshape(8, -1)
-    ids = lax.dynamic_slice(ring, ((4 - y) % 4, 0), (4, ring.shape[1])).reshape(-1)
+    next_ids = named("ids_next", lambda x: lax.ppermute(x, "tensor", by_tensor(lambda i: i ^ 2)), after(both, near))
+    half = jnp.where(y % 2 == 0, jnp.stack([both, next_ids]), jnp.stack([next_ids, both]))
+    rest_ids = named("ids_rest", lambda x: lax.ppermute(x, "tensor", by_tensor(lambda i: i ^ 4)), half)
+    ids = jnp.where(y < 2, jnp.stack([half, rest_ids]), jnp.stack([rest_ids, half])).reshape(-1)
     whole_segs = jnp.broadcast_to(ids[:, None], (ids.shape[0], HD))
 
-    other = jnp.stack([after(from_across, n_up, n_down, ids_up, ids_down, ids_far), from_diagonal], axis=1)
+    other = jnp.stack([after(from_across, n_up, n_down, next_ids), from_diagonal], axis=1)
     flips = [named("pair_%d" % e, pair, jnp.stack([near[e], other[e]])) for e in range(2)]
 
-    n, o = near, other
-    n_far, o_down = named("n_far", y_up, after(n_up, n_down)), named("o_down", y_down, after(o, whole_segs))
+    n, o, p, q = near, other, flips[0], flips[1]
+    n_far, o_down = named("n_far", y_up, n_up), named("o_down", y_down, after(o, whole_segs))
     attn_out, stats, bias = forward(place, whole_segs, after(query, n_far, o_down), key, value)
-    out_across = named("out_across", across, attn_out)
+    out_across = named("out_across", across, after(attn_out, p, q))
     o_up, o_far = named("o_up", y_up, after(o, n_up, n_down)), named("o_far", y_down, o_down)
-    flips[0] = after(flips[0], n_far, o_down)
-    flips[1] = after(flips[1], attn_out)
-    flips = [lax.all_gather(x, "tensor", axis=0, axis_index_groups=Y_GROUPS) for x in flips]
+    p = after(p, n_far, o_down)
+    p_up, p_down = named("p_up", y_up, p), named("p_down", y_down, p)
+    p_far, q_down = named("p_far", y_up, p_up), named("q_down", y_down, after(q, o_up, o_far))
+    q_up, q_far = named("q_up", y_up, after(q, p_up, p_down)), named("q_far", y_down, q_down)
     near_blocks = [n, n_down, n_far, n_up]
     other_blocks = [o, o_down, o_far, o_up]
     same = [*near_blocks, *other_blocks]
 
-    def sums(name, pieces):
-        keep_near, keep_other, give = partial(place, pieces, weight)
+    def sums(name, by_half, pieces):
+        keep_near, keep_other, give = partial(by_half, pieces, weight)
         given = named(name + "_sibling", sibling, give)
         total = (keep_other + given[1].astype(F32)).astype(BF16)
         return keep_near, given, named(name + "_across", across, total)
 
-    terms_same = sums("sum_same", same)
+    terms_same = sums("sum_same", False, [after(n, p_up, p_down), *same[1:]])
     out_near = named("out_near", sibling, after(attn_out, o_up, o_far))
     out_other = named("out_other", sibling, after(out_across, o_up, o_far))
     outs = (attn_out, out_near, out_across, out_other)
 
-    def sum_z(x):
-        return lax.psum_scatter(
-            x.reshape(4 * heads, width // 2), "dp", scatter_dimension=0, tiled=True, axis_index_groups=Z_GROUPS
-        )
-
-    first = wgrad(place, 0, same, flips[0], (*outs[:3], after(out_other, terms_same[1])))
-    first_sum = sum_z(after(first, flips[1], terms_same[2]))
-    terms_flip = sums("sum_flip", [flips[0], after(flips[1], first)])
-    last = wgrad(place, 1, same, flips[1], (*outs[:3], after(out_other, terms_flip[1])))
-    last_sum = sum_z(last)
+    flips = [[p, p_down, p_far, p_up], [q, q_down, q_far, q_up]]
+    first = wgrad(0, same, flips[0], (*outs[:3], after(out_other, terms_same[1])))
+    total = wgrad(1, same, flips[1], outs, first)
+    total = after(total.reshape(4 * heads, width), terms_same[2])
+    weight_grad = lax.psum_scatter(total, "dp", scatter_dimension=0, tiled=True, axis_index_groups=Z_GROUPS)
+    terms_flip = sums("sum_flip", True, [after(p, total), *flips[0][1:], *flips[1]])
     dq, dk, dv = backward(place, query, key, value, stats, bias, [*terms_same, *terms_flip])
-    weight_grad = jnp.concatenate([first_sum, last_sum], axis=1).astype(F32)
-    return (dq[None], dk[None], dv[None], weight_grad)
+    return (dq[None], dk[None], dv[None], weight_grad.astype(F32))
 
 
 def solution(mesh):

time: 209 us -> 209 us (level)
  waiting for transfers between devices: 74.6 us -> 81.9 us
  starting transfers between devices: 42.6 us -> 36.4 us
  local copies, waits for them, and re-layouts: 8.14 us -> 5.22 us
    ppermute x4 -> x6, waiting for transfers between devices: 7.49 us -> 22 us  [y_up(): return lax.ppermute(x, 'tensor', Y_UP)]
    all_gather x2 -> x0, waiting for transfers between devices: 11.5 us -> none  [shards(): lax.all_gather(x, 'tensor', axis=0, axis_index_groups=Y_GROUPS)]
    reduce_scatter x2 -> x1, waiting for transfers between devices: 17.3 us -> 6.1 us  [shards(): lax.psum_scatter(total, 'dp', scatter_dimension=0, tiled=True, axis_index...]
    ppermute x1 -> x2, waiting for transfers between devices: 1.35 us -> 10.8 us  [the longest x1 9.37 us: shards(): lax.ppermute(x, 'tensor', by_tensor(lambda i: i ^ 2))]
    ppermute x4 -> x6, waiting for transfers between devices: 18 us -> 25.6 us  [y_down(): return lax.ppermute(x, 'tensor', Y_DOWN)]
    ppermute x5, starting transfers between devices: 14.8 us -> 8.57 us  [sibling(): return lax.ppermute(x, 'dp', SIBLING)]
    ppermute x4 -> x6, starting transfers between devices: 6.34 us -> 10.7 us  [y_down(): return lax.ppermute(x, 'tensor', Y_DOWN)]
    ppermute x4, starting transfers between devices: 10 us -> 6.4 us  [across(): return lax.ppermute(x, 'dp', ACROSS)]
  transfers between devices with their start and end apart: 27 -> 29, of which waited for: 14 -> 12; matrix products, arithmetic and copies ran while one was open for 6% -> 6% of each run, Pallas kernels for 27% -> 28%
where the time goes in v5:
time: 209 us
  waiting for transfers between devices  81.9 us (39%)
  Pallas kernels  57.5 us (28%)
  starting transfers between devices  36.4 us (17%)
  between operations  14.3 us (7%)
  other arithmetic  13.5 us (6%)
  local copies, waits for them, and re-layouts  5.22 us (2%)
    ppermute x6, waiting for transfers between devices, y_down(): return lax.ppermute(x, 'tensor', Y_DOWN)  25.6 us
    ppermute x6, waiting for transfers between devices, y_up(): return lax.ppermute(x, 'tensor', Y_UP)  22 us
    pallas_call x2, Pallas kernels, partial(): pl.pallas_call(functools.partial(partial_kernel, by_half), grid=(2,), in_...  17.9 us
    pallas_call x2, Pallas kernels, wgrad(): pl.pallas_call(wgrad_kernel, grid=(2,), in_specs=[pl.BlockSpec((1, 2, seq...  17.9 us
    ppermute x4, waiting for transfers between devices, across(): return lax.ppermute(x, 'dp', ACROSS)  14.1 us
    ppermute x6, starting transfers between devices, y_down(): return lax.ppermute(x, 'tensor', Y_DOWN)  10.7 us
    ppermute x1, waiting for transfers between devices, shards(): lax.ppermute(x, 'tensor', by_tensor(lambda i: i ^ 2))  9.37 us
    pallas_call x1, Pallas kernels, backward(): pl.pallas_call(backward_kernel, grid=(pairs,), in_specs=[SMEM(), two, who...  9.33 us
  transfers between devices with their start and end apart: 29, of which 12 were waited for; matrix products, arithmetic and copies ran while one was open for 6% of the time, Pallas kernels for 28%

profile of v5, /device:TPU:1, one launch (start us, length us, event | category | flops | bytes accessed | tf_op | source)
XLA Modules:
  0.0 208.7 jit_solution(4474144687076845139)
XLA Ops:
  7.2 0.7 all-gather.2.cloned.1.call-update
  7.9 0.0 reduce-scatter.2.cloned.1.call-start
  7.9 2.1 %collective-permute-start = (s32[64]{0:T(128)}, s32[64]{0:T(128)S(1)}, u32[]{:S(2)}, u32[]{:S(2)}) collective-permute-start(s32[64]{0:T(128)} %bitcast.54), channel_id=1, source_target_pairs={{0,1},{1,0},{2,3},{3,2},{4,5},{5,4},{6,7},{7,6},{8,9},{9,8},{10,11... | collective-permute-start | bytes 776 | tf_op jit(solution)/shard_map/t_ids_pair/ppermute | solution.py:47
  10.1 0.6 pad_add_fusion.place
  10.7 1.3 broadcast_in_dim.19.segs
  12.0 3.4 %prep.1 = (bf16[2,64,1024]{2,1,0:T(8,128)(2,1)}, bf16[2,64,1024]{2,1,0:T(8,128)(2,1)}, bf16[2,64,1024]{2,1,0:T(8,128)(2,1)}, bf16[2,64,1024]{2,1,0:T(8,128)(2,1)}) custom-call(s32[4]{0:T(128)} %pad_add_fusion.place, f32[1,4]{1,0:T(1,128)} %margins.1, s32[64,128]{1,0:T(8,128)} %broadcast_in_dim.19.segs, bf16[64,8192]{1,0:T(8,128)(2,1)} %bitcast.41), custom_call_target="tpu_custom_call" | custom-call | bytes 9000000 | tf_op jit(solution)/shard_map/prep/pallas_call | solution.py:107
  15.5 1.0 collective-permute-start.1
  16.5 2.5 %collective-permute-start.6 = (bf16[2,64,1024]{2,1,0:T(8,128)(2,1)}, bf16[2,64,1024]{2,1,0:T(8,128)(2,1)S(1)}, u32[]{:S(2)}, u32[]{:S(2)}) collective-permute-start(bf16[2,64,1024]{2,1,0:T(8,128)(2,1)} %get-tuple-element.40), channel_id=1, source_target_pairs={{0,16},{8,24},{16,0},{24,8},{32,48},{40,56},{48,32},{56,40},{64,80... | collective-permute-start | bytes 786440 | tf_op jit(solution)/shard_map/t_other_across/ppermute | solution.py:39
  19.0 0.8 collective-permute-start.8
  19.7 0.7 fusion.6
  20.5 0.7 add_select_fusion.3
  21.2 1.0 pad_maximum_fusion.refs_0_
  22.2 2.8 %collective-permute-start.7 = (bf16[2,2,64,1024]{3,2,1,0:T(8,128)(2,1)S(1)}, bf16[2,2,64,1024]{3,2,1,0:T(8,128)(2,1)S(1)}, u32[]{:S(2)}, u32[]{:S(2)}) collective-permute-start(bf16[2,2,64,1024]{3,2,1,0:T(8,128)(2,1)S(1)} %pad_maximum_fusion.refs_0_), channel_id=1, source_target_pairs={{0,6},{1,7},{2,0},{3,1},{4,2},{5,3},{6,4},{7,5},{8,14},{9,15},{10,... | collective-permute-start | bytes 1572872 | tf_op jit(solution)/shard_map/t_n_down/ppermute | solution.py:55
  25.1 0.7 add_select_fusion.4
  25.8 0.1 collective-permute-start.2
  25.9 1.0 fusion.5
  26.9 9.4 %collective-permute-done.2 = s32[2,64]{1,0:T(2,128)S(1)} collective-permute-done((s32[2,64]{1,0:T(2,128)S(1)}, s32[2,64]{1,0:T(2,128)S(1)}, u32[]{:S(2)}, u32[]{:S(2)}) %collective-permute-start.2) | collective-permute-done | bytes 544 | tf_op jit(solution)/shard_map/t_ids_next/ppermute | solution.py:372
  36.2 2.5 %collective-permute-start.3 = (s32[2,2,64]{2,1,0:T(2,128)S(1)}, s32[2,2,64]{2,1,0:T(2,128)S(1)}, u32[]{:S(2)}, u32[]{:S(2)}) collective-permute-start(s32[2,2,64]{2,1,0:T(2,128)S(1)} %add_select_fusion.2), channel_id=1, source_target_pairs={{0,4},{1,5},{2,6},{3,7},{4,0},{5,1},{6,2},{7,3},{8,12},{9,13},{10,... | collective-permute-start | bytes 3080 | tf_op jit(solution)/shard_map/t_ids_rest/ppermute | solution.py:374
  38.7 1.5 collective-permute-done.3
  40.2 0.1 select_n.104
  40.3 0.1 pad_maximum_fusion.1.refs_4_
  40.4 1.1 broadcast_in_dim.20.segs
  41.6 0.8 pad_maximum_fusion.2
  42.4 0.2 collective-permute-start.10
  42.6 2.5 %collective-permute-start.9 = (bf16[2,2,64,1024]{3,2,1,0:T(8,128)(2,1)S(1)}, bf16[2,2,64,1024]{3,2,1,0:T(8,128)(2,1)S(1)}, u32[]{:S(2)}, u32[]{:S(2)}) collective-permute-start(bf16[2,2,64,1024]{3,2,1,0:T(8,128)(2,1)S(1)} %pad_maximum_fusion.1.refs_4_), channel_id=1, source_target_pairs={{0,6},{1,7},{2,0},{3,1},{4,2},{5,3},{6,4},{7,5},{8,14},{9,15},{10,... | collective-permute-start | bytes 1572872 | tf_op jit(solution)/shard_map/t_o_down/ppermute | solution.py:55
  45.1 0.2 collective-permute-start.5
  45.3 0.8 pad_maximum_fusion.3
  46.2 1.2 collective-permute-start.17
  47.4 8.3 %collective-permute-done.9.refs_5_ = bf16[2,2,64,1024]{3,2,1,0:T(8,128)(2,1)S(1)} collective-permute-done((bf16[2,2,64,1024]{3,2,1,0:T(8,128)(2,1)S(1)}, bf16[2,2,64,1024]{3,2,1,0:T(8,128)(2,1)S(1)}, u32[]{:S(2)}, u32[]{:S(2)}) %collective-permute-start.9) | collective-permute-done | bytes 524320 | tf_op jit(solution)/shard_map/t_o_down/ppermute | solution.py:55
  55.7 1.2 collective-permute-done.5.refs_2_
  56.9 9.0 %attend.1 = (bf16[1024,512]{1,0:T(8,128)(2,1)}, f32[4,8,256]{2,1,0:T(8,128)}, f32[4,384,128]{2,1,0:T(8,128)}) custom-call(s32[4]{0:T(128)} %pad_add_fusion.place, s32[512,128]{1,0:T(8,128)} %broadcast_in_dim.20.segs, bf16[512,1024]{1,0:T(8,128)(2,1)} %bitcast.39, bf16[512,128]{1,0:T(8,128)(2,1)} %bitcast.50, bf16[512,128]{1,0:T(8,128)(2,1)} %bitcast.52), custom_call_target="tpu_custom_call" | custom-call | bytes 27000000 | tf_op jit(solution)/shard_map/attend/pallas_call | solution.py:170
  65.9 2.8 %collective-permute-start.22 = (bf16[1024,512]{1,0:T(8,128)(2,1)}, bf16[1024,512]{1,0:T(8,128)(2,1)}, u32[]{:S(2)}, u32[]{:S(2)}) collective-permute-start(bf16[1024,512]{1,0:T(8,128)(2,1)} %get-tuple-element.57.refs_12_), channel_id=1, source_target_pairs={{0,16},{8,24},{16,0},{24,8},{32,48},{40,56},{48,32},{56,40},{64,80... | collective-permute-start | bytes 3145736 | tf_op jit(solution)/shard_map/t_out_across/ppermute | solution.py:39
  68.7 1.2 collective-permute-start.12
  69.9 1.0 collective-permute-start.11
  70.9 1.5 collective-permute-start.14
  72.3 1.2 collective-permute-start.13
  73.5 6.1 %collective-permute-done.12.refs_9_.refs_1_ = bf16[2,2,64,1024]{3,2,1,0:T(8,128)(2,1)S(1)} collective-permute-done((bf16[2,2,64,1024]{3,2,1,0:T(8,128)(2,1)S(1)}, bf16[2,2,64,1024]{3,2,1,0:T(8,128)(2,1)S(1)}, u32[]{:S(2)}, u32[]{:S(2)}) %collective-permute-start.12) | collective-permute-done | bytes 524320 | tf_op jit(solution)/shard_map/t_p_down/ppermute | solution.py:55
  79.6 1.2 collective-permute-done.11.refs_11_.refs_3_
  80.8 11.2 %collective-permute-done.14.refs_7_ = bf16[2,2,64,1024]{3,2,1,0:T(8,128)(2,1)S(1)} collective-permute-done((bf16[2,2,64,1024]{3,2,1,0:T(8,128)(2,1)S(1)}, bf16[2,2,64,1024]{3,2,1,0:T(8,128)(2,1)S(1)}, u32[]{:S(2)}, u32[]{:S(2)}) %collective-permute-start.14) | collective-permute-done | bytes 524320 | tf_op jit(solution)/shard_map/t_o_up/ppermute | solution.py:51
  92.0 0.8 copy-done.6
  92.9 9.0 %partial_grad.2 = (f32[256,1024]{1,0:T(8,128)}, f32[256,1024]{1,0:T(8,128)}, bf16[2,256,1024]{2,1,0:T(8,128)(2,1)}) custom-call(bf16[2,2,64,1024]{3,2,1,0:T(8,128)(2,1)} %copy-done, bf16[2,2,64,1024]{3,2,1,0:T(8,128)(2,1)} %copy-done.2, bf16[2,2,64,1024]{3,2,1,0:T(8,128)(2,1)} %copy-done.5, bf16[2,2,64,1024]{3,2,1,0:T(8,128)(2,1)} %copy-done.3, ...), custom_call_target="tpu_custom_call" | custom-call | bytes 27000000 | tf_op jit(solution)/shard_map/partial_grad/pallas_call | solution.py:289
  101.8 4.7 %collective-permute-start.15 = (bf16[2,256,1024]{2,1,0:T(8,128)(2,1)}, bf16[2,256,1024]{2,1,0:T(8,128)(2,1)S(1)}, u32[]{:S(2)}, u32[]{:S(2)}) collective-permute-start(bf16[2,256,1024]{2,1,0:T(8,128)(2,1)} %get-tuple-element.51), channel_id=1, source_target_pairs={{0,8},{8,0},{16,24},{24,16},{32,40},{40,32},{48,56},{56,48},{64,72... | collective-permute-start | bytes 3145736 | tf_op jit(solution)/shard_map/t_sum_same_sibling/ppermute | solution.py:35
  106.5 0.1 collective-permute-start.23
  106.6 0.4 collective-permute-start.18
  106.9 0.7 collective-permute-start.21
  107.6 1.1 collective-permute-start.20
  108.7 11.2 %collective-permute-done.18.refs_9_.refs_5_ = bf16[2,2,64,1024]{3,2,1,0:T(8,128)(2,1)S(1)} collective-permute-done((bf16[2,2,64,1024]{3,2,1,0:T(8,128)(2,1)}, bf16[2,2,64,1024]{3,2,1,0:T(8,128)(2,1)S(1)}, u32[]{:S(2)}, u32[]{:S(2)}) %collective-permute-start.18) | collective-permute-done | bytes 524320 | tf_op jit(solution)/shard_map/t_q_down/ppermute | solution.py:55
  120.0 2.7 %collective-permute-start.19 = (bf16[2,2,64,1024]{3,2,1,0:T(8,128)(2,1)S(1)}, bf16[2,2,64,1024]{3,2,1,0:T(8,128)(2,1)}, u32[]{:S(2)}, u32[]{:S(2)}) collective-permute-start(bf16[2,2,64,1024]{3,2,1,0:T(8,128)(2,1)S(1)} %collective-permute-done.18.refs_9_.refs_5_), channel_id=1, source_target_pairs={{0,6},{1,7},{2,0},{3,1},{4,2},{5,3},{6,4},{7,5},{8,14},{9,15},{10,... | collective-permute-start | bytes 1572872 | tf_op jit(solution)/shard_map/t_q_far/ppermute | solution.py:55
  122.7 2.2 %fusion.1 = bf16[256,1024]{1,0:T(8,128)(2,1)} fusion(f32[256,1024]{1,0:T(8,128)} %get-tuple-element.52, bf16[2,256,1024]{2,1,0:T(8,128)(2,1)S(1)} %collective-permute-done.15.rest_1_), kind=kLoop, calls=%fused_computation.3 | loop fusion | flops 786432 | bytes 2097152 | tf_op jit(solution)/shard_map/convert_element_type | solution.py:397
  124.8 0.5 collective-permute-start.16
  125.4 8.4 %collective-permute-done.24.refs_10_.refs_2_ = bf16[2,2,64,1024]{3,2,1,0:T(8,128)(2,1)} collective-permute-done((bf16[2,2,64,1024]{3,2,1,0:T(8,128)(2,1)}, bf16[2,2,64,1024]{3,2,1,0:T(8,128)(2,1)}, u32[]{:S(2)}, u32[]{:S(2)}) %collective-permute-start.24) | collective-permute-done | bytes 524320 | tf_op jit(solution)/shard_map/t_p_far/ppermute | solution.py:51
  133.8 1.0 copy-done.8
  134.8 8.9 %weight_grad.2.refs_16_ = bf16[4,1024,512]{2,1,0:T(8,128)(2,1)} custom-call(bf16[2,2,64,1024]{3,2,1,0:T(8,128)(2,1)} %copy-done, bf16[2,2,64,1024]{3,2,1,0:T(8,128)(2,1)} %copy-done.2, bf16[2,2,64,1024]{3,2,1,0:T(8,128)(2,1)} %copy-done.5, bf16[2,2,64,1024]{3,2,1,0:T(8,128)(2,1)} %copy-done.3, bf16[2,2,64,1024]{3,2,1,0:T(8,128)(2,1)} %copy-done.1, ...), custom_call_target="tpu_custom_call" | custom-call | bytes 27000000 | tf_op jit(solution)/shard_map/weight_grad/pallas_call | solution.py:327
  143.8 8.9 %weight_grad.3 = bf16[4,1024,512]{2,1,0:T(8,128)(2,1)} custom-call(bf16[2,2,64,1024]{3,2,1,0:T(8,128)(2,1)} %copy-done, bf16[2,2,64,1024]{3,2,1,0:T(8,128)(2,1)} %copy-done.2, bf16[2,2,64,1024]{3,2,1,0:T(8,128)(2,1)} %copy-done.5, bf16[2,2,64,1024]{3,2,1,0:T(8,128)(2,1)} %copy-done.3, ...), custom_call_target="tpu_custom_call", output_to_operand_aliasing={{}: (16, {})} | custom-call | bytes 27000000 | tf_op jit(solution)/shard_map/weight_grad/pallas_call | solution.py:327
  152.8 9.0 %partial_grad.3 = (f32[256,1024]{1,0:T(8,128)}, f32[256,1024]{1,0:T(8,128)}, bf16[2,256,1024]{2,1,0:T(8,128)(2,1)}) custom-call(bf16[2,2,64,1024]{3,2,1,0:T(8,128)(2,1)} %copy-done.11, bf16[2,2,64,1024]{3,2,1,0:T(8,128)(2,1)} %copy-done.12, bf16[2,2,64,1024]{3,2,1,0:T(8,128)(2,1)} %collective-permute-done.24.refs_10_.refs_2_, ...), custom_call_target="tpu_custom_call" | custom-call | bytes 27000000 | tf_op jit(solution)/shard_map/partial_grad/pallas_call | solution.py:289
  161.7 2.1 collective-permute-start.25
  163.8 2.5 %collective-permute-done.25.rest_4_ = bf16[2,256,1024]{2,1,0:T(8,128)(2,1)S(1)} collective-permute-done((bf16[2,256,1024]{2,1,0:T(8,128)(2,1)}, bf16[2,256,1024]{2,1,0:T(8,128)(2,1)S(1)}, u32[]{:S(2)}, u32[]{:S(2)}) %collective-permute-start.25) | collective-permute-done | bytes 1048608 | tf_op jit(solution)/shard_map/t_sum_flip_sibling/ppermute | solution.py:35
  166.3 1.7 fusion
  168.1 0.6 collective-permute-start.26
  168.7 14.1 %collective-permute-done.26.rest_5_ = bf16[256,1024]{1,0:T(8,128)(2,1)S(1)} collective-permute-done((bf16[256,1024]{1,0:T(8,128)(2,1)S(1)}, bf16[256,1024]{1,0:T(8,128)(2,1)S(1)}, u32[]{:S(2)}, u32[]{:S(2)}) %collective-permute-start.26) | collective-permute-done | bytes 524320 | tf_op jit(solution)/shard_map/t_sum_flip_across/ppermute | solution.py:39
  182.8 0.8 copy-done.15
  183.6 9.3 %attend_grad.1 = (bf16[512,1024]{1,0:T(8,128)(2,1)}, bf16[512,128]{1,0:T(8,128)(2,1)}, bf16[512,128]{1,0:T(8,128)(2,1)}) custom-call(s32[4]{0:T(128)} %pad_add_fusion.place, bf16[512,1024]{1,0:T(8,128)(2,1)} %bitcast.40, bf16[512,128]{1,0:T(8,128)(2,1)} %bitcast.51, bf16[512,128]{1,0:T(8,128)(2,1)} %bitcast.53, f32[4,8,256]{2,1,0:T(8,128)} %get-tuple-element.45.stats, ...), custom_call_target="tpu_custom_call" | custom-call | bytes 27000000 | tf_op jit(solution)/shard_map/attend_grad/pallas_call | solution.py:239
  192.9 6.1 %reduce-scatter.2.cloned.1.call-done = bf16[1024,512]{1,0:T(8,128)(2,1)} async-done(((bf16[4096,512]{1,0:T(8,128)(2,1)}), bf16[1024,512]{1,0:T(8,128)(2,1)}) %reduce-scatter.2.cloned.1.call-update) | async-done | bytes 1048592 | tf_op jit(solution)/shard_map/reduce_scatter | solution.py:409
  199.0 2.8 %convert_element_type.27 = f32[1024,512]{1,0:T(8,128)} convert(bf16[1024,512]{1,0:T(8,128)(2,1)} %reduce-scatter.2.cloned.1.call-done) | non-fusion elementwise | flops 524288 | bytes 3145728 | tf_op jit(solution)/shard_map/convert_element_type | solution.py:412
  (54 shorter events, 0.2 us)
Async XLA Ops:
  7.2 85.6 %all-gather.2.cloned.1.call-start = ((), (), s32[]{:S(2)}) async-start(), calls=%async_computation.1 | async-start | bytes 5242880 | tf_op jit(solution)/shard_map/all_gather | solution.py:361
  7.9 191.1 %reduce-scatter.2.cloned.1.call-start = ((), (), s32[]{:S(2)}) async-start(), calls=%async_computation.2 | async-start | bytes 5242880 | tf_op jit(solution)/shard_map/reduce_scatter | solution.py:409
  7.9 7.5 %collective-permute-start = (s32[64]{0:T(128)}, s32[64]{0:T(128)S(1)}, u32[]{:S(2)}, u32[]{:S(2)}) collective-permute-start(s32[64]{0:T(128)} %bitcast.54), channel_id=1, source_target_pairs={{0,1},{1,0},{2,3},{3,2},{4,5},{5,4},{6,7},{7,6},{8,9},{9,8},{10,11... | collective-permute-start | bytes 776 | tf_op jit(solution)/shard_map/t_ids_pair/ppermute | solution.py:47
  15.5 5.7 %collective-permute-start.1 = (bf16[2,64,1024]{2,1,0:T(8,128)(2,1)}, bf16[2,64,1024]{2,1,0:T(8,128)(2,1)S(1)}, u32[]{:S(2)}, u32[]{:S(2)}) collective-permute-start(bf16[2,64,1024]{2,1,0:T(8,128)(2,1)} %get-tuple-element.38), channel_id=1, source_target_pairs={{0,8},{8,0},{16,24},{24,16},{32,40},{40,32},{48,56},{56,48},{64,72... | collective-permute-start | bytes 786440 | tf_op jit(solution)/shard_map/t_near_sibling/ppermute | solution.py:35
  16.5 23.8 %collective-permute-start.6 = (bf16[2,64,1024]{2,1,0:T(8,128)(2,1)}, bf16[2,64,1024]{2,1,0:T(8,128)(2,1)S(1)}, u32[]{:S(2)}, u32[]{:S(2)}) collective-permute-start(bf16[2,64,1024]{2,1,0:T(8,128)(2,1)} %get-tuple-element.40), channel_id=1, source_target_pairs={{0,16},{8,24},{16,0},{24,8},{32,48},{40,56},{48,32},{56,40},{64,80... | collective-permute-start | bytes 786440 | tf_op jit(solution)/shard_map/t_other_across/ppermute | solution.py:39
  19.0 21.4 %collective-permute-start.8 = (bf16[2,64,1024]{2,1,0:T(8,128)(2,1)}, bf16[2,64,1024]{2,1,0:T(8,128)(2,1)S(1)}, u32[]{:S(2)}, u32[]{:S(2)}) collective-permute-start(bf16[2,64,1024]{2,1,0:T(8,128)(2,1)} %get-tuple-element.42), channel_id=1, source_target_pairs={{0,24},{8,16},{16,8},{24,0},{32,56},{40,48},{48,40},{56,32},{64,88... | collective-permute-start | bytes 786440 | tf_op jit(solution)/shard_map/t_other_diagonal/ppermute | solution.py:43
  22.2 70.6 %copy-start = (bf16[2,2,64,1024]{3,2,1,0:T(8,128)(2,1)}, bf16[2,2,64,1024]{3,2,1,0:T(8,128)(2,1)S(1)}, u32[]{:S(2)}) copy-start(bf16[2,2,64,1024]{3,2,1,0:T(8,128)(2,1)S(1)} %pad_maximum_fusion.refs_0_) | copy-start | bytes 1572868
  22.2 18.0 %collective-permute-start.7 = (bf16[2,2,64,1024]{3,2,1,0:T(8,128)(2,1)S(1)}, bf16[2,2,64,1024]{3,2,1,0:T(8,128)(2,1)S(1)}, u32[]{:S(2)}, u32[]{:S(2)}) collective-permute-start(bf16[2,2,64,1024]{3,2,1,0:T(8,128)(2,1)S(1)} %pad_maximum_fusion.refs_0_), channel_id=1, source_target_pairs={{0,6},{1,7},{2,0},{3,1},{4,2},{5,3},{6,4},{7,5},{8,14},{9,15},{10,... | collective-permute-start | bytes 1572872 | tf_op jit(solution)/shard_map/t_n_down/ppermute | solution.py:55
  25.0 15.2 %collective-permute-start.4 = (bf16[2,2,64,1024]{3,2,1,0:T(8,128)(2,1)S(1)}, bf16[2,2,64,1024]{3,2,1,0:T(8,128)(2,1)S(1)}, u32[]{:S(2)}, u32[]{:S(2)}) collective-permute-start(bf16[2,2,64,1024]{3,2,1,0:T(8,128)(2,1)S(1)} %pad_maximum_fusion.refs_0_), channel_id=1, source_target_pairs={{0,2},{1,3},{2,4},{3,5},{4,6},{5,7},{6,0},{7,1},{8,10},{9,11},{10,... | collective-permute-start | bytes 1572872 | tf_op jit(solution)/shard_map/t_n_up/ppermute | solution.py:51
  25.8 10.4 %collective-permute-start.2 = (s32[2,64]{1,0:T(2,128)S(1)}, s32[2,64]{1,0:T(2,128)S(1)}, u32[]{:S(2)}, u32[]{:S(2)}) collective-permute-start(s32[2,64]{1,0:T(2,128)S(1)} %add_select_fusion.4), channel_id=1, source_target_pairs={{0,2},{1,3},{2,0},{3,1},{4,6},{5,7},{6,4},{7,5},{8,10},{9,11},{10,... | collective-permute-start | bytes 1544 | tf_op jit(solution)/shard_map/t_ids_next/ppermute | solution.py:372
  36.2 3.9 %collective-permute-start.3 = (s32[2,2,64]{2,1,0:T(2,128)S(1)}, s32[2,2,64]{2,1,0:T(2,128)S(1)}, u32[]{:S(2)}, u32[]{:S(2)}) collective-permute-start(s32[2,2,64]{2,1,0:T(2,128)S(1)} %add_select_fusion.2), channel_id=1, source_target_pairs={{0,4},{1,5},{2,6},{3,7},{4,0},{5,1},{6,2},{7,3},{8,12},{9,13},{10,... | collective-permute-start | bytes 3080 | tf_op jit(solution)/shard_map/t_ids_rest/ppermute | solution.py:374
  40.3 52.5 %copy-start.2 = (bf16[2,2,64,1024]{3,2,1,0:T(8,128)(2,1)}, bf16[2,2,64,1024]{3,2,1,0:T(8,128)(2,1)S(1)}, u32[]{:S(2)}) copy-start(bf16[2,2,64,1024]{3,2,1,0:T(8,128)(2,1)S(1)} %collective-permute-done.7.refs_1_) | copy-start | bytes 1572868
  40.3 52.5 %copy-start.3 = (bf16[2,2,64,1024]{3,2,1,0:T(8,128)(2,1)}, bf16[2,2,64,1024]{3,2,1,0:T(8,128)(2,1)S(1)}, u32[]{:S(2)}) copy-start(bf16[2,2,64,1024]{3,2,1,0:T(8,128)(2,1)S(1)} %collective-permute-done.4.refs_3_) | copy-start | bytes 1572868
  40.4 52.4 %copy-start.1 = (bf16[2,2,64,1024]{3,2,1,0:T(8,128)(2,1)}, bf16[2,2,64,1024]{3,2,1,0:T(8,128)(2,1)S(1)}, u32[]{:S(2)}) copy-start(bf16[2,2,64,1024]{3,2,1,0:T(8,128)(2,1)S(1)} %pad_maximum_fusion.1.refs_4_) | copy-start | bytes 1572868
  42.4 23.5 %collective-permute-start.10 = (bf16[2,2,64,1024]{3,2,1,0:T(8,128)(2,1)}, bf16[2,2,64,1024]{3,2,1,0:T(8,128)(2,1)S(1)}, u32[]{:S(2)}, u32[]{:S(2)}) collective-permute-start(bf16[2,2,64,1024]{3,2,1,0:T(8,128)(2,1)} %pad_maximum_fusion.2), channel_id=1, source_target_pairs={{0,1},{1,0},{2,3},{3,2},{4,5},{5,4},{6,7},{7,6},{8,9},{9,8},{10,11... | collective-permute-start | bytes 1572872 | tf_op jit(solution)/shard_map/t_pair_0/ppermute | solution.py:47
  42.6 13.1 %collective-permute-start.9 = (bf16[2,2,64,1024]{3,2,1,0:T(8,128)(2,1)S(1)}, bf16[2,2,64,1024]{3,2,1,0:T(8,128)(2,1)S(1)}, u32[]{:S(2)}, u32[]{:S(2)}) collective-permute-start(bf16[2,2,64,1024]{3,2,1,0:T(8,128)(2,1)S(1)} %pad_maximum_fusion.1.refs_4_), channel_id=1, source_target_pairs={{0,6},{1,7},{2,0},{3,1},{4,2},{5,3},{6,4},{7,5},{8,14},{9,15},{10,... | collective-permute-start | bytes 1572872 | tf_op jit(solution)/shard_map/t_o_down/ppermute | solution.py:55
  45.1 11.8 %collective-permute-start.5 = (bf16[2,2,64,1024]{3,2,1,0:T(8,128)(2,1)S(1)}, bf16[2,2,64,1024]{3,2,1,0:T(8,128)(2,1)S(1)}, u32[]{:S(2)}, u32[]{:S(2)}) collective-permute-start(bf16[2,2,64,1024]{3,2,1,0:T(8,128)(2,1)S(1)} %collective-permute-done.4.refs_3_), channel_id=1, source_target_pairs={{0,2},{1,3},{2,4},{3,5},{4,6},{5,7},{6,0},{7,1},{8,10},{9,11},{10,... | collective-permute-start | bytes 1572872 | tf_op jit(solution)/shard_map/t_n_far/ppermute | solution.py:51
  46.2 19.7 %collective-permute-start.17 = (bf16[2,2,64,1024]{3,2,1,0:T(8,128)(2,1)}, bf16[2,2,64,1024]{3,2,1,0:T(8,128)(2,1)}, u32[]{:S(2)}, u32[]{:S(2)}) collective-permute-start(bf16[2,2,64,1024]{3,2,1,0:T(8,128)(2,1)} %pad_maximum_fusion.3), channel_id=1, source_target_pairs={{0,1},{1,0},{2,3},{3,2},{4,5},{5,4},{6,7},{7,6},{8,9},{9,8},{10,11... | collective-permute-start | bytes 1572872 | tf_op jit(solution)/shard_map/t_pair_1/ppermute | solution.py:47
  55.7 37.1 %copy-start.4 = (bf16[2,2,64,1024]{3,2,1,0:T(8,128)(2,1)}, bf16[2,2,64,1024]{3,2,1,0:T(8,128)(2,1)S(1)}, u32[]{:S(2)}) copy-start(bf16[2,2,64,1024]{3,2,1,0:T(8,128)(2,1)S(1)} %collective-permute-done.9.refs_5_) | copy-start | bytes 1572868
  56.9 36.0 %copy-start.5 = (bf16[2,2,64,1024]{3,2,1,0:T(8,128)(2,1)}, bf16[2,2,64,1024]{3,2,1,0:T(8,128)(2,1)S(1)}, u32[]{:S(2)}) copy-start(bf16[2,2,64,1024]{3,2,1,0:T(8,128)(2,1)S(1)} %collective-permute-done.5.refs_2_) | copy-start | bytes 1572868
  65.8 26.2 %copy-start.11 = (bf16[2,2,64,1024]{3,2,1,0:T(8,128)(2,1)}, bf16[2,2,64,1024]{3,2,1,0:T(8,128)(2,1)S(1)}, u32[]{:S(2)}) copy-start(bf16[2,2,64,1024]{3,2,1,0:T(8,128)(2,1)S(1)} %collective-permute-done.10.refs_8_.refs_0_) | copy-start | bytes 1572868
  65.9 40.6 %collective-permute-start.22 = (bf16[1024,512]{1,0:T(8,128)(2,1)}, bf16[1024,512]{1,0:T(8,128)(2,1)}, u32[]{:S(2)}, u32[]{:S(2)}) collective-permute-start(bf16[1024,512]{1,0:T(8,128)(2,1)} %get-tuple-element.57.refs_12_), channel_id=1, source_target_pairs={{0,16},{8,24},{16,0},{24,8},{32,48},{40,56},{48,32},{56,40},{64,80... | collective-permute-start | bytes 3145736 | tf_op jit(solution)/shard_map/t_out_across/ppermute | solution.py:39
  68.7 10.9 %collective-permute-start.12 = (bf16[2,2,64,1024]{3,2,1,0:T(8,128)(2,1)S(1)}, bf16[2,2,64,1024]{3,2,1,0:T(8,128)(2,1)S(1)}, u32[]{:S(2)}, u32[]{:S(2)}) collective-permute-start(bf16[2,2,64,1024]{3,2,1,0:T(8,128)(2,1)S(1)} %collective-permute-done.10.refs_8_.refs_0_), channel_id=1, source_target_pairs={{0,6},{1,7},{2,0},{3,1},{4,2},{5,3},{6,4},{7,5},{8,14},{9,15},{10,... | collective-permute-start | bytes 1572872 | tf_op jit(solution)/shard_map/t_p_down/ppermute | solution.py:55
  69.9 10.9 %collective-permute-start.11 = (bf16[2,2,64,1024]{3,2,1,0:T(8,128)(2,1)S(1)}, bf16[2,2,64,1024]{3,2,1,0:T(8,128)(2,1)S(1)}, u32[]{:S(2)}, u32[]{:S(2)}) collective-permute-start(bf16[2,2,64,1024]{3,2,1,0:T(8,128)(2,1)S(1)} %collective-permute-done.10.refs_8_.refs_0_), channel_id=1, source_target_pairs={{0,2},{1,3},{2,4},{3,5},{4,6},{5,7},{6,0},{7,1},{8,10},{9,11},{10,... | collective-permute-start | bytes 1572872 | tf_op jit(solution)/shard_map/t_p_up/ppermute | solution.py:51
  70.9 21.1 %collective-permute-start.14 = (bf16[2,2,64,1024]{3,2,1,0:T(8,128)(2,1)S(1)}, bf16[2,2,64,1024]{3,2,1,0:T(8,128)(2,1)S(1)}, u32[]{:S(2)}, u32[]{:S(2)}) collective-permute-start(bf16[2,2,64,1024]{3,2,1,0:T(8,128)(2,1)S(1)} %pad_maximum_fusion.1.refs_4_), channel_id=1, source_target_pairs={{0,2},{1,3},{2,4},{3,5},{4,6},{5,7},{6,0},{7,1},{8,10},{9,11},{10,... | collective-permute-start | bytes 1572872 | tf_op jit(solution)/shard_map/t_o_up/ppermute | solution.py:51
  72.3 20.5 %collective-permute-start.13 = (bf16[2,2,64,1024]{3,2,1,0:T(8,128)(2,1)S(1)}, bf16[2,2,64,1024]{3,2,1,0:T(8,128)(2,1)}, u32[]{:S(2)}, u32[]{:S(2)}) collective-permute-start(bf16[2,2,64,1024]{3,2,1,0:T(8,128)(2,1)S(1)} %collective-permute-done.9.refs_5_), channel_id=1, source_target_pairs={{0,6},{1,7},{2,0},{3,1},{4,2},{5,3},{6,4},{7,5},{8,14},{9,15},{10,... | collective-permute-start | bytes 1572872 | tf_op jit(solution)/shard_map/t_o_far/ppermute | solution.py:55
  79.6 12.4 %copy-start.12 = (bf16[2,2,64,1024]{3,2,1,0:T(8,128)(2,1)}, bf16[2,2,64,1024]{3,2,1,0:T(8,128)(2,1)S(1)}, u32[]{:S(2)}) copy-start(bf16[2,2,64,1024]{3,2,1,0:T(8,128)(2,1)S(1)} %collective-permute-done.12.refs_9_.refs_1_) | copy-start | bytes 1572868
  80.8 11.2 %copy-start.13 = (bf16[2,2,64,1024]{3,2,1,0:T(8,128)(2,1)}, bf16[2,2,64,1024]{3,2,1,0:T(8,128)(2,1)S(1)}, u32[]{:S(2)}) copy-start(bf16[2,2,64,1024]{3,2,1,0:T(8,128)(2,1)S(1)} %collective-permute-done.11.refs_11_.refs_3_) | copy-start | bytes 1572868
  92.0 0.8 copy-start.6
  101.8 18.2 %collective-permute-start.15 = (bf16[2,256,1024]{2,1,0:T(8,128)(2,1)}, bf16[2,256,1024]{2,1,0:T(8,128)(2,1)S(1)}, u32[]{:S(2)}, u32[]{:S(2)}) collective-permute-start(bf16[2,256,1024]{2,1,0:T(8,128)(2,1)} %get-tuple-element.51), channel_id=1, source_target_pairs={{0,8},{8,0},{16,24},{24,16},{32,40},{40,32},{48,56},{56,48},{64,72... | collective-permute-start | bytes 3145736 | tf_op jit(solution)/shard_map/t_sum_same_sibling/ppermute | solution.py:35
  106.5 18.4 %collective-permute-start.23 = (bf16[1024,512]{1,0:T(8,128)(2,1)}, bf16[1024,512]{1,0:T(8,128)(2,1)S(1)}, u32[]{:S(2)}, u32[]{:S(2)}) collective-permute-start(bf16[1024,512]{1,0:T(8,128)(2,1)} %collective-permute-done.22.refs_14_), channel_id=1, source_target_pairs={{0,8},{8,0},{16,24},{24,16},{32,40},{40,32},{48,56},{56,48},{64,72... | collective-permute-start | bytes 3145736 | tf_op jit(solution)/shard_map/t_out_other/ppermute | solution.py:35
  106.6 13.4 %collective-permute-start.18 = (bf16[2,2,64,1024]{3,2,1,0:T(8,128)(2,1)}, bf16[2,2,64,1024]{3,2,1,0:T(8,128)(2,1)S(1)}, u32[]{:S(2)}, u32[]{:S(2)}) collective-permute-start(bf16[2,2,64,1024]{3,2,1,0:T(8,128)(2,1)} %collective-permute-done.17.refs_8_.refs_4_), channel_id=1, source_target_pairs={{0,6},{1,7},{2,0},{3,1},{4,2},{5,3},{6,4},{7,5},{8,14},{9,15},{10,... | collective-permute-start | bytes 1572872 | tf_op jit(solution)/shard_map/t_q_down/ppermute | solution.py:55
  106.9 26.8 %collective-permute-start.21 = (bf16[1024,512]{1,0:T(8,128)(2,1)}, bf16[1024,512]{1,0:T(8,128)(2,1)S(1)}, u32[]{:S(2)}, u32[]{:S(2)}) collective-permute-start(bf16[1024,512]{1,0:T(8,128)(2,1)} %get-tuple-element.57.refs_12_), channel_id=1, source_target_pairs={{0,8},{8,0},{16,24},{24,16},{32,40},{40,32},{48,56},{56,48},{64,72... | collective-permute-start | bytes 3145736 | tf_op jit(solution)/shard_map/t_out_near/ppermute | solution.py:35
  107.6 36.2 %collective-permute-start.20 = (bf16[2,2,64,1024]{3,2,1,0:T(8,128)(2,1)}, bf16[2,2,64,1024]{3,2,1,0:T(8,128)(2,1)}, u32[]{:S(2)}, u32[]{:S(2)}) collective-permute-start(bf16[2,2,64,1024]{3,2,1,0:T(8,128)(2,1)} %collective-permute-done.17.refs_8_.refs_4_), channel_id=1, source_target_pairs={{0,2},{1,3},{2,4},{3,5},{4,6},{5,7},{6,0},{7,1},{8,10},{9,11},{10,... | collective-permute-start | bytes 1572872 | tf_op jit(solution)/shard_map/t_q_up/ppermute | solution.py:51
  120.0 23.8 %copy-start.14 = (bf16[2,2,64,1024]{3,2,1,0:T(8,128)(2,1)}, bf16[2,2,64,1024]{3,2,1,0:T(8,128)(2,1)S(1)}, u32[]{:S(2)}) copy-start(bf16[2,2,64,1024]{3,2,1,0:T(8,128)(2,1)S(1)} %collective-permute-done.18.refs_9_.refs_5_) | copy-start | bytes 1572868
  120.0 13.8 %collective-permute-start.24 = (bf16[2,2,64,1024]{3,2,1,0:T(8,128)(2,1)}, bf16[2,2,64,1024]{3,2,1,0:T(8,128)(2,1)}, u32[]{:S(2)}, u32[]{:S(2)}) collective-permute-start(bf16[2,2,64,1024]{3,2,1,0:T(8,128)(2,1)} %copy-done.13), channel_id=1, source_target_pairs={{0,2},{1,3},{2,4},{3,5},{4,6},{5,7},{6,0},{7,1},{8,10},{9,11},{10,... | collective-permute-start | bytes 1572872 | tf_op jit(solution)/shard_map/t_p_far/ppermute | solution.py:51
  120.0 23.8 %copy-start.9 = (bf16[2,256,1024]{2,1,0:T(8,128)(2,1)}, bf16[2,256,1024]{2,1,0:T(8,128)(2,1)S(1)}, u32[]{:S(2)}) copy-start(bf16[2,256,1024]{2,1,0:T(8,128)(2,1)S(1)} %collective-permute-done.15.rest_1_) | copy-start | bytes 3145732
  120.0 23.8 %collective-permute-start.19 = (bf16[2,2,64,1024]{3,2,1,0:T(8,128)(2,1)S(1)}, bf16[2,2,64,1024]{3,2,1,0:T(8,128)(2,1)}, u32[]{:S(2)}, u32[]{:S(2)}) collective-permute-start(bf16[2,2,64,1024]{3,2,1,0:T(8,128)(2,1)S(1)} %collective-permute-done.18.refs_9_.refs_5_), channel_id=1, source_target_pairs={{0,6},{1,7},{2,0},{3,1},{4,2},{5,3},{6,4},{7,5},{8,14},{9,15},{10,... | collective-permute-start | bytes 1572872 | tf_op jit(solution)/shard_map/t_q_far/ppermute | solution.py:55
  124.8 8.9 %copy-start.7 = (bf16[1024,512]{1,0:T(8,128)(2,1)}, bf16[1024,512]{1,0:T(8,128)(2,1)S(1)}, u32[]{:S(2)}) copy-start(bf16[1024,512]{1,0:T(8,128)(2,1)S(1)} %collective-permute-done.23.refs_15_) | copy-start | bytes 3145732
  124.8 27.9 %collective-permute-start.16 = (bf16[256,1024]{1,0:T(8,128)(2,1)}, bf16[256,1024]{1,0:T(8,128)(2,1)}, u32[]{:S(2)}, u32[]{:S(2)}) collective-permute-start(bf16[256,1024]{1,0:T(8,128)(2,1)} %fusion.1), channel_id=1, source_target_pairs={{0,16},{8,24},{16,0},{24,8},{32,48},{40,56},{48,32},{56,40},{64,80... | collective-permute-start | bytes 1572872 | tf_op jit(solution)/shard_map/t_sum_same_across/ppermute | solution.py:39
  133.8 1.0 copy-start.8
  161.7 4.6 %collective-permute-start.25 = (bf16[2,256,1024]{2,1,0:T(8,128)(2,1)}, bf16[2,256,1024]{2,1,0:T(8,128)(2,1)S(1)}, u32[]{:S(2)}, u32[]{:S(2)}) collective-permute-start(bf16[2,256,1024]{2,1,0:T(8,128)(2,1)} %get-tuple-element.63), channel_id=1, source_target_pairs={{0,8},{8,0},{16,24},{24,16},{32,40},{40,32},{48,56},{56,48},{64,72... | collective-permute-start | bytes 3145736 | tf_op jit(solution)/shard_map/t_sum_flip_sibling/ppermute | solution.py:35
  166.3 16.5 %copy-start.10 = (bf16[2,256,1024]{2,1,0:T(8,128)(2,1)}, bf16[2,256,1024]{2,1,0:T(8,128)(2,1)S(1)}, u32[]{:S(2)}) copy-start(bf16[2,256,1024]{2,1,0:T(8,128)(2,1)S(1)} %collective-permute-done.25.rest_4_) | copy-start | bytes 3145732
  168.1 14.7 %collective-permute-start.26 = (bf16[256,1024]{1,0:T(8,128)(2,1)S(1)}, bf16[256,1024]{1,0:T(8,128)(2,1)S(1)}, u32[]{:S(2)}, u32[]{:S(2)}) collective-permute-start(bf16[256,1024]{1,0:T(8,128)(2,1)S(1)} %fusion), channel_id=1, source_target_pairs={{0,16},{8,24},{16,0},{24,8},{32,48},{40,56},{48,32},{56,40},{64,80... | collective-permute-start | bytes 1572872 | tf_op jit(solution)/shard_map/t_sum_flip_across/ppermute | solution.py:39
  182.8 0.8 copy-start.15
Sparse Core Ops, SparseCore 0:
  9.7 51.7 all-gather.1
  152.9 46.0 reduce-scatter.1

commit v6 on v5

--- a/solution.py
+++ b/solution.py
@@ -366,27 +366,28 @@
 
     from_across = named("other_across", across, to_across)
     from_diagonal = named("other_diagonal", diagonal, to_diagonal)
-    near = jnp.stack([own, named("near_sibling", sibling, after(to_sibling, partner))], axis=1)
-    n_up, n_down = named("n_up", y_up, near), named("n_down", y_down, near)
     both = jnp.where(low == 0, jnp.stack([ids, partner]), jnp.stack([partner, ids]))
-    next_ids = named("ids_next", lambda x: lax.ppermute(x, "tensor", by_tensor(lambda i: i ^ 2)), after(both, near))
+    next_ids = named("ids_next", lambda x: lax.ppermute(x, "tensor", by_tensor(lambda i: i ^ 2)), both)
     half = jnp.where(y % 2 == 0, jnp.stack([both, next_ids]), jnp.stack([next_ids, both]))
     rest_ids = named("ids_rest", lambda x: lax.ppermute(x, "tensor", by_tensor(lambda i: i ^ 4)), half)
     ids = jnp.where(y < 2, jnp.stack([half, rest_ids]), jnp.stack([rest_ids, half])).reshape(-1)
     whole_segs = jnp.broadcast_to(ids[:, None], (ids.shape[0], HD))
 
-    other = jnp.stack([after(from_across, n_up, n_down, next_ids), from_diagonal], axis=1)
+    from_sibling = named("near_sibling", sibling, after(to_sibling, partner))
+    near = jnp.stack([own, after(from_sibling, rest_ids)], axis=1)
+    n_up, n_down = named("n_up", y_up, near), named("n_down", y_down, near)
+    attn_out, stats, bias = forward(place, whole_segs, query, key, value)
+    other = jnp.stack([after(from_across, n_up, n_down, attn_out), from_diagonal], axis=1)
     flips = [named("pair_%d" % e, pair, jnp.stack([near[e], other[e]])) for e in range(2)]
 
     n, o, p, q = near, other, flips[0], flips[1]
-    n_far, o_down = named("n_far", y_up, n_up), named("o_down", y_down, after(o, whole_segs))
-    attn_out, stats, bias = forward(place, whole_segs, after(query, n_far, o_down), key, value)
-    out_across = named("out_across", across, after(attn_out, p, q))
-    o_up, o_far = named("o_up", y_up, after(o, n_up, n_down)), named("o_far", y_down, o_down)
-    p = after(p, n_far, o_down)
+    n_far, o_down = named("n_far", y_up, n_up), named("o_down", y_down, o)
+    o_up, o_far = named("o_up", y_up, o), named("o_far", y_down, o_down)
+    out_across = named("out_across", across, after(attn_out, p))
+    p, q = after(p, n_far, o_down), after(q, o_up, o_far)
     p_up, p_down = named("p_up", y_up, p), named("p_down", y_down, p)
-    p_far, q_down = named("p_far", y_up, p_up), named("q_down", y_down, after(q, o_up, o_far))
-    q_up, q_far = named("q_up", y_up, after(q, p_up, p_down)), named("q_far", y_down, q_down)
+    p_far, q_down = named("p_far", y_up, p_up), named("q_down", y_down, q)
+    q_up, q_far = named("q_up", y_up, q), named("q_far", y_down, q_down)
     near_blocks = [n, n_down, n_far, n_up]
     other_blocks = [o, o_down, o_far, o_up]
     same = [*near_blocks, *other_blocks]
@@ -397,17 +398,16 @@
         total = (keep_other + given[1].astype(F32)).astype(BF16)
         return keep_near, given, named(name + "_across", across, total)
 
-    terms_same = sums("sum_same", False, [after(n, p_up, p_down), *same[1:]])
     out_near = named("out_near", sibling, after(attn_out, o_up, o_far))
     out_other = named("out_other", sibling, after(out_across, o_up, o_far))
     outs = (attn_out, out_near, out_across, out_other)
 
     flips = [[p, p_down, p_far, p_up], [q, q_down, q_far, q_up]]
-    first = wgrad(0, same, flips[0], (*outs[:3], after(out_other, terms_same[1])))
-    total = wgrad(1, same, flips[1], outs, first)
-    total = after(total.reshape(4 * heads, width), terms_same[2])
+    first = wgrad(0, same, flips[0], outs)
+    total = wgrad(1, same, flips[1], outs, first).reshape(4 * heads, width)
     weight_grad = lax.psum_scatter(total, "dp", scatter_dimension=0, tiled=True, axis_index_groups=Z_GROUPS)
-    terms_flip = sums("sum_flip", True, [after(p, total), *flips[0][1:], *flips[1]])
+    terms_same = sums("sum_same", False, [after(n, total), *same[1:]])
+    terms_flip = sums("sum_flip", True, [after(p, terms_same[0]), *flips[0][1:], *flips[1]])
     dq, dk, dv = backward(place, query, key, value, stats, bias, [*terms_same, *terms_flip])
     return (dq[None], dk[None], dv[None], weight_grad.astype(F32))
 

time: 209 us -> 203 us (0.971)
  waiting for transfers between devices: 81.9 us -> 76 us
  other arithmetic: 13.5 us -> 9.86 us
  starting transfers between devices: 36.4 us -> 39.5 us
    ppermute x3, waiting for transfers between devices: 0.01 us -> 17.1 us  [pair(): return lax.ppermute(x, 'tensor', PAIR)]
    ppermute x6, waiting for transfers between devices: 25.6 us -> 9.81 us  [y_down(): return lax.ppermute(x, 'tensor', Y_DOWN)]
    ppermute x1, waiting for transfers between devices: 9.37 us -> 0.38 us  [shards(): lax.ppermute(x, 'tensor', by_tensor(lambda i: i ^ 2))]
    ppermute x4, waiting for transfers between devices: 14.1 us -> 20.8 us  [across(): return lax.ppermute(x, 'dp', ACROSS)]
    reduce_scatter x1, waiting for transfers between devices: 6.1 us -> 0.02 us  [shards(): lax.psum_scatter(total, 'dp', scatter_dimension=0, tiled=True, axis_index...]
    ppermute x1, starting transfers between devices: 0.76 us -> 4.94 us  [diagonal(): return lax.ppermute(x, 'dp', DIAGONAL)]
    ppermute x6, starting transfers between devices: 10.7 us -> 14.3 us  [y_down(): return lax.ppermute(x, 'tensor', Y_DOWN)]
    ppermute x6, waiting for transfers between devices: 22 us -> 24.7 us  [y_up(): return lax.ppermute(x, 'tensor', Y_UP)]
  transfers between devices with their start and end apart: 29 -> 29, of which waited for: 12 -> 12; matrix products, arithmetic and copies ran while one was open for 6% -> 5% of each run, Pallas kernels for 28% -> 28%
where the time goes in v6:
time: 203 us
  waiting for transfers between devices  76 us (37%)
  Pallas kernels  57.4 us (28%)
  starting transfers between devices  39.5 us (19%)
  between operations  14.3 us (7%)
  other arithmetic  9.86 us (5%)
  local copies, waits for them, and re-layouts  5.71 us (3%)
    ppermute x6, waiting for transfers between devices, y_up(): return lax.ppermute(x, 'tensor', Y_UP)  24.7 us
    ppermute x4, waiting for transfers between devices, across(): return lax.ppermute(x, 'dp', ACROSS)  20.8 us
    pallas_call x2, Pallas kernels, partial(): pl.pallas_call(functools.partial(partial_kernel, by_half), grid=(2,), in_...  18 us
    pallas_call x2, Pallas kernels, wgrad(): pl.pallas_call(wgrad_kernel, grid=(2,), in_specs=[pl.BlockSpec((1, 2, seq...  17.9 us
    ppermute x3, waiting for transfers between devices, pair(): return lax.ppermute(x, 'tensor', PAIR)  17.1 us
    ppermute x6, starting transfers between devices, y_down(): return lax.ppermute(x, 'tensor', Y_DOWN)  14.3 us
    ppermute x6, waiting for transfers between devices, y_down(): return lax.ppermute(x, 'tensor', Y_DOWN)  9.81 us
    pallas_call x1, Pallas kernels, backward(): pl.pallas_call(backward_kernel, grid=(pairs,), in_specs=[SMEM(), two, who...  9.37 us
  transfers between devices with their start and end apart: 29, of which 12 were waited for; matrix products, arithmetic and copies ran while one was open for 5% of the time, Pallas kernels for 28%

profile of v6, /device:TPU:1, one launch (start us, length us, event | category | flops | bytes accessed | tf_op | source)
XLA Modules:
  0.0 202.7 jit_solution(15208154902555984348)
XLA Ops:
  7.2 0.7 all-gather.2.cloned.1.call-update
  7.9 0.0 reduce-scatter.2.cloned.1.call-start
  7.9 2.1 %collective-permute-start = (s32[64]{0:T(128)}, s32[64]{0:T(128)S(1)}, u32[]{:S(2)}, u32[]{:S(2)}) collective-permute-start(s32[64]{0:T(128)} %bitcast.54), channel_id=1, source_target_pairs={{0,1},{1,0},{2,3},{3,2},{4,5},{5,4},{6,7},{7,6},{8,9},{9,8},{10,11... | collective-permute-start | bytes 776 | tf_op jit(solution)/shard_map/t_ids_pair/ppermute | solution.py:47
  10.1 0.6 pad_add_fusion.place
  10.6 1.3 broadcast_in_dim.20.segs
  12.0 3.4 %prep.1 = (bf16[2,64,1024]{2,1,0:T(8,128)(2,1)}, bf16[2,64,1024]{2,1,0:T(8,128)(2,1)}, bf16[2,64,1024]{2,1,0:T(8,128)(2,1)}, bf16[2,64,1024]{2,1,0:T(8,128)(2,1)}) custom-call(s32[4]{0:T(128)} %pad_add_fusion.place, f32[1,4]{1,0:T(1,128)} %margins.1, s32[64,128]{1,0:T(8,128)} %broadcast_in_dim.20.segs, bf16[64,8192]{1,0:T(8,128)(2,1)} %bitcast.41), custom_call_target="tpu_custom_call" | custom-call | bytes 9000000 | tf_op jit(solution)/shard_map/prep/pallas_call | solution.py:107
  15.4 1.0 collective-permute-start.3
  16.4 0.7 add_select_fusion.4
  17.2 1.3 collective-permute-start.1
  18.5 0.7 add_select_fusion.3
  19.2 0.4 collective-permute-done.1
  19.6 2.9 %collective-permute-start.2 = (s32[2,2,64]{2,1,0:T(2,128)S(1)}, s32[2,2,64]{2,1,0:T(2,128)S(1)}, u32[]{:S(2)}, u32[]{:S(2)}) collective-permute-start(s32[2,2,64]{2,1,0:T(2,128)S(1)} %add_select_fusion.2), channel_id=1, source_target_pairs={{0,4},{1,5},{2,6},{3,7},{4,0},{5,1},{6,2},{7,3},{8,12},{9,13},{10,... | collective-permute-start | bytes 3080 | tf_op jit(solution)/shard_map/t_ids_rest/ppermute | solution.py:372
  22.5 1.0 collective-permute-done.2
  23.6 1.0 pad_maximum_fusion.refs_0_
  24.6 2.8 %collective-permute-start.4 = (bf16[2,2,64,1024]{3,2,1,0:T(8,128)(2,1)S(1)}, bf16[2,2,64,1024]{3,2,1,0:T(8,128)(2,1)S(1)}, u32[]{:S(2)}, u32[]{:S(2)}) collective-permute-start(bf16[2,2,64,1024]{3,2,1,0:T(8,128)(2,1)S(1)} %pad_maximum_fusion.refs_0_), channel_id=1, source_target_pairs={{0,6},{1,7},{2,0},{3,1},{4,2},{5,3},{6,4},{7,5},{8,14},{9,15},{10,... | collective-permute-start | bytes 1572872 | tf_op jit(solution)/shard_map/t_n_down/ppermute | solution.py:55
  27.4 4.9 %collective-permute-start.8 = (bf16[2,64,1024]{2,1,0:T(8,128)(2,1)}, bf16[2,64,1024]{2,1,0:T(8,128)(2,1)S(1)}, u32[]{:S(2)}, u32[]{:S(2)}) collective-permute-start(bf16[2,64,1024]{2,1,0:T(8,128)(2,1)} %get-tuple-element.39), channel_id=1, source_target_pairs={{0,24},{8,16},{16,8},{24,0},{32,56},{40,48},{48,40},{56,32},{64,88... | collective-permute-start | bytes 786440 | tf_op jit(solution)/shard_map/t_other_diagonal/ppermute | solution.py:43
  32.3 0.5 collective-permute-start.7
  32.8 0.7 fusion.6
  33.6 0.1 select_n.104
  33.7 0.8 broadcast_in_dim.19.segs
  34.5 8.8 %attend.1 = (bf16[1024,512]{1,0:T(8,128)(2,1)}, f32[4,8,256]{2,1,0:T(8,128)}, f32[4,384,128]{2,1,0:T(8,128)}) custom-call(s32[4]{0:T(128)} %pad_add_fusion.place, s32[512,128]{1,0:T(8,128)} %broadcast_in_dim.19.segs, bf16[512,1024]{1,0:T(8,128)(2,1)} %bitcast.39, bf16[512,128]{1,0:T(8,128)(2,1)} %bitcast.50, bf16[512,128]{1,0:T(8,128)(2,1)} %bitcast.52), custom_call_target="tpu_custom_call" | custom-call | bytes 27000000 | tf_op jit(solution)/shard_map/attend/pallas_call | solution.py:170
  43.3 1.1 fusion.5
  44.4 0.7 collective-permute-done.7
  45.2 0.1 pad_maximum_fusion.3
  45.3 0.3 collective-permute-start.17
  45.6 0.1 pad_maximum_fusion.1.refs_4_
  45.7 3.0 %collective-permute-start.9 = (bf16[2,2,64,1024]{3,2,1,0:T(8,128)(2,1)S(1)}, bf16[2,2,64,1024]{3,2,1,0:T(8,128)(2,1)S(1)}, u32[]{:S(2)}, u32[]{:S(2)}) collective-permute-start(bf16[2,2,64,1024]{3,2,1,0:T(8,128)(2,1)S(1)} %pad_maximum_fusion.1.refs_4_), channel_id=1, source_target_pairs={{0,6},{1,7},{2,0},{3,1},{4,2},{5,3},{6,4},{7,5},{8,14},{9,15},{10,... | collective-permute-start | bytes 1572872 | tf_op jit(solution)/shard_map/t_o_down/ppermute | solution.py:55
  48.7 9.9 %collective-permute-done.17.refs_8_.refs_0_ = bf16[2,2,64,1024]{3,2,1,0:T(8,128)(2,1)S(1)} collective-permute-done((bf16[2,2,64,1024]{3,2,1,0:T(8,128)(2,1)S(1)}, bf16[2,2,64,1024]{3,2,1,0:T(8,128)(2,1)S(1)}, u32[]{:S(2)}, u32[]{:S(2)}) %collective-permute-start.17) | collective-permute-done | bytes 524320 | tf_op jit(solution)/shard_map/t_pair_0/ppermute | solution.py:47
  58.6 1.5 collective-permute-start.18
  60.1 1.1 collective-permute-start.6
  61.2 0.1 pad_maximum_fusion.2
  61.3 0.4 collective-permute-start.12
  61.6 1.7 collective-permute-start.10
  63.4 23.0 %collective-permute-done.6.refs_2_ = bf16[2,2,64,1024]{3,2,1,0:T(8,128)(2,1)S(1)} collective-permute-done((bf16[2,2,64,1024]{3,2,1,0:T(8,128)(2,1)S(1)}, bf16[2,2,64,1024]{3,2,1,0:T(8,128)(2,1)S(1)}, u32[]{:S(2)}, u32[]{:S(2)}) %collective-permute-start.6) | collective-permute-done | bytes 524320 | tf_op jit(solution)/shard_map/t_n_far/ppermute | solution.py:51
  86.4 0.9 collective-permute-start.20
  87.3 0.5 collective-permute-start.21
  87.8 7.2 %collective-permute-done.12.refs_8_.refs_4_ = bf16[2,2,64,1024]{3,2,1,0:T(8,128)(2,1)} collective-permute-done((bf16[2,2,64,1024]{3,2,1,0:T(8,128)(2,1)S(1)}, bf16[2,2,64,1024]{3,2,1,0:T(8,128)(2,1)}, u32[]{:S(2)}, u32[]{:S(2)}) %collective-permute-start.12) | collective-permute-done | bytes 524320 | tf_op jit(solution)/shard_map/t_pair_1/ppermute | solution.py:47
  95.1 0.8 copy-done.7
  95.9 0.4 collective-permute-start.16
  96.3 0.1 collective-permute-start.19
  96.4 2.7 %collective-permute-start.13 = (bf16[2,2,64,1024]{3,2,1,0:T(8,128)(2,1)}, bf16[2,2,64,1024]{3,2,1,0:T(8,128)(2,1)}, u32[]{:S(2)}, u32[]{:S(2)}) collective-permute-start(bf16[2,2,64,1024]{3,2,1,0:T(8,128)(2,1)} %collective-permute-done.12.refs_8_.refs_4_), channel_id=1, source_target_pairs={{0,6},{1,7},{2,0},{3,1},{4,2},{5,3},{6,4},{7,5},{8,14},{9,15},{10,... | collective-permute-start | bytes 1572872 | tf_op jit(solution)/shard_map/t_q_down/ppermute | solution.py:55
  99.2 1.6 collective-permute-done.21.refs_11_.refs_3_
  100.8 0.1 collective-permute-start.15
  100.9 9.8 %collective-permute-done.13.refs_9_.refs_5_ = bf16[2,2,64,1024]{3,2,1,0:T(8,128)(2,1)} collective-permute-done((bf16[2,2,64,1024]{3,2,1,0:T(8,128)(2,1)}, bf16[2,2,64,1024]{3,2,1,0:T(8,128)(2,1)}, u32[]{:S(2)}, u32[]{:S(2)}) %collective-permute-start.13) | collective-permute-done | bytes 524320 | tf_op jit(solution)/shard_map/t_q_down/ppermute | solution.py:55
  110.7 3.1 %collective-permute-start.14 = (bf16[2,2,64,1024]{3,2,1,0:T(8,128)(2,1)}, bf16[2,2,64,1024]{3,2,1,0:T(8,128)(2,1)}, u32[]{:S(2)}, u32[]{:S(2)}) collective-permute-start(bf16[2,2,64,1024]{3,2,1,0:T(8,128)(2,1)} %collective-permute-done.13.refs_9_.refs_5_), channel_id=1, source_target_pairs={{0,6},{1,7},{2,0},{3,1},{4,2},{5,3},{6,4},{7,5},{8,14},{9,15},{10,... | collective-permute-start | bytes 1572872 | tf_op jit(solution)/shard_map/t_q_far/ppermute | solution.py:55
  113.8 0.8 copy-done.16
  114.6 1.0 copy-done.10
  115.6 9.0 %weight_grad.2.refs_16_ = bf16[4,1024,512]{2,1,0:T(8,128)(2,1)} custom-call(bf16[2,2,64,1024]{3,2,1,0:T(8,128)(2,1)} %copy-done, bf16[2,2,64,1024]{3,2,1,0:T(8,128)(2,1)} %copy-done.2, bf16[2,2,64,1024]{3,2,1,0:T(8,128)(2,1)} %copy-done.6, bf16[2,2,64,1024]{3,2,1,0:T(8,128)(2,1)} %copy-done.3, bf16[2,2,64,1024]{3,2,1,0:T(8,128)(2,1)} %copy-done.1, ...), custom_call_target="tpu_custom_call" | custom-call | bytes 27000000 | tf_op jit(solution)/shard_map/weight_grad/pallas_call | solution.py:327
  124.6 0.1 collective-permute-done.15.refs_11_.refs_7_
  124.7 8.9 %weight_grad.3 = bf16[4,1024,512]{2,1,0:T(8,128)(2,1)} custom-call(bf16[2,2,64,1024]{3,2,1,0:T(8,128)(2,1)} %copy-done, bf16[2,2,64,1024]{3,2,1,0:T(8,128)(2,1)} %copy-done.2, bf16[2,2,64,1024]{3,2,1,0:T(8,128)(2,1)} %copy-done.6, bf16[2,2,64,1024]{3,2,1,0:T(8,128)(2,1)} %copy-done.3, ...), custom_call_target="tpu_custom_call", output_to_operand_aliasing={{}: (16, {})} | custom-call | bytes 27000000 | tf_op jit(solution)/shard_map/weight_grad/pallas_call | solution.py:327
  133.7 8.9 %partial_grad.2 = (f32[256,1024]{1,0:T(8,128)}, f32[256,1024]{1,0:T(8,128)}, bf16[2,256,1024]{2,1,0:T(8,128)(2,1)}) custom-call(bf16[2,2,64,1024]{3,2,1,0:T(8,128)(2,1)} %copy-done, bf16[2,2,64,1024]{3,2,1,0:T(8,128)(2,1)} %copy-done.2, bf16[2,2,64,1024]{3,2,1,0:T(8,128)(2,1)} %copy-done.6, bf16[2,2,64,1024]{3,2,1,0:T(8,128)(2,1)} %copy-done.3, ...), custom_call_target="tpu_custom_call" | custom-call | bytes 27000000 | tf_op jit(solution)/shard_map/partial_grad/pallas_call | solution.py:289
  142.6 5.1 %collective-permute-start.23 = (bf16[2,256,1024]{2,1,0:T(8,128)(2,1)}, bf16[2,256,1024]{2,1,0:T(8,128)(2,1)S(1)}, u32[]{:S(2)}, u32[]{:S(2)}) collective-permute-start(bf16[2,256,1024]{2,1,0:T(8,128)(2,1)} %get-tuple-element.47), channel_id=1, source_target_pairs={{0,8},{8,0},{16,24},{24,16},{32,40},{40,32},{48,56},{56,48},{64,72... | collective-permute-start | bytes 3145736 | tf_op jit(solution)/shard_map/t_sum_same_sibling/ppermute | solution.py:35
  147.7 9.0 %partial_grad.3 = (f32[256,1024]{1,0:T(8,128)}, f32[256,1024]{1,0:T(8,128)}, bf16[2,256,1024]{2,1,0:T(8,128)(2,1)}) custom-call(bf16[2,2,64,1024]{3,2,1,0:T(8,128)(2,1)} %copy-done.13, bf16[2,2,64,1024]{3,2,1,0:T(8,128)(2,1)} %copy-done.14, bf16[2,2,64,1024]{3,2,1,0:T(8,128)(2,1)} %copy-done.16, bf16[2,2,64,1024]{3,2,1,0:T(8,128)(2,1)} %copy-done.15, ...), custom_call_target="tpu_custom_call" | custom-call | bytes 27000000 | tf_op jit(solution)/shard_map/partial_grad/pallas_call | solution.py:289
  156.7 0.1 collective-permute-start.25
  156.8 0.1 fusion.1
  156.9 1.3 collective-permute-start.24
  158.2 1.4 collective-permute-done.25.rest_4_
  159.6 1.7 fusion
  161.3 1.3 collective-permute-start.26
  162.7 8.9 %collective-permute-done.24.rest_2_ = bf16[256,1024]{1,0:T(8,128)(2,1)S(1)} collective-permute-done((bf16[256,1024]{1,0:T(8,128)(2,1)S(1)}, bf16[256,1024]{1,0:T(8,128)(2,1)S(1)}, u32[]{:S(2)}, u32[]{:S(2)}) %collective-permute-start.24) | collective-permute-done | bytes 524320 | tf_op jit(solution)/shard_map/t_sum_same_across/ppermute | solution.py:39
  171.6 11.2 %collective-permute-done.26.rest_5_ = bf16[256,1024]{1,0:T(8,128)(2,1)S(1)} collective-permute-done((bf16[256,1024]{1,0:T(8,128)(2,1)S(1)}, bf16[256,1024]{1,0:T(8,128)(2,1)S(1)}, u32[]{:S(2)}, u32[]{:S(2)}) %collective-permute-start.26) | collective-permute-done | bytes 524320 | tf_op jit(solution)/shard_map/t_sum_flip_across/ppermute | solution.py:39
  182.8 0.8 copy-done.19
  183.6 9.4 %attend_grad.1 = (bf16[512,1024]{1,0:T(8,128)(2,1)}, bf16[512,128]{1,0:T(8,128)(2,1)}, bf16[512,128]{1,0:T(8,128)(2,1)}) custom-call(s32[4]{0:T(128)} %pad_add_fusion.place, bf16[512,1024]{1,0:T(8,128)(2,1)} %bitcast.40, bf16[512,128]{1,0:T(8,128)(2,1)} %bitcast.51, bf16[512,128]{1,0:T(8,128)(2,1)} %bitcast.53, f32[4,8,256]{2,1,0:T(8,128)} %get-tuple-element.30.stats, ...), custom_call_target="tpu_custom_call" | custom-call | bytes 27000000 | tf_op jit(solution)/shard_map/attend_grad/pallas_call | solution.py:239
  193.0 2.8 %convert_element_type.27 = f32[1024,512]{1,0:T(8,128)} convert(bf16[1024,512]{1,0:T(8,128)(2,1)} %reduce-scatter.2.cloned.1.call-done) | non-fusion elementwise | flops 524288 | bytes 3145728 | tf_op jit(solution)/shard_map/convert_element_type | solution.py:412
  (62 shorter events, 0.3 us)
Async XLA Ops:
  7.2 126.5 %all-gather.2.cloned.1.call-start = ((), (), s32[]{:S(2)}) async-start(), calls=%async_computation.1 | async-start | bytes 5242880 | tf_op jit(solution)/shard_map/all_gather | solution.py:361
  7.9 185.1 %reduce-scatter.2.cloned.1.call-start = ((), (), s32[]{:S(2)}) async-start(), calls=%async_computation.2 | async-start | bytes 5242880 | tf_op jit(solution)/shard_map/reduce_scatter | solution.py:408
  7.9 7.4 %collective-permute-start = (s32[64]{0:T(128)}, s32[64]{0:T(128)S(1)}, u32[]{:S(2)}, u32[]{:S(2)}) collective-permute-start(s32[64]{0:T(128)} %bitcast.54), channel_id=1, source_target_pairs={{0,1},{1,0},{2,3},{3,2},{4,5},{5,4},{6,7},{7,6},{8,9},{9,8},{10,11... | collective-permute-start | bytes 776 | tf_op jit(solution)/shard_map/t_ids_pair/ppermute | solution.py:47
  15.4 8.2 %collective-permute-start.3 = (bf16[2,64,1024]{2,1,0:T(8,128)(2,1)}, bf16[2,64,1024]{2,1,0:T(8,128)(2,1)S(1)}, u32[]{:S(2)}, u32[]{:S(2)}) collective-permute-start(bf16[2,64,1024]{2,1,0:T(8,128)(2,1)} %get-tuple-element.34), channel_id=1, source_target_pairs={{0,8},{8,0},{16,24},{24,16},{32,40},{40,32},{48,56},{56,48},{64,72... | collective-permute-start | bytes 786440 | tf_op jit(solution)/shard_map/t_near_sibling/ppermute | solution.py:35
  17.2 2.5 %collective-permute-start.1 = (s32[2,64]{1,0:T(2,128)S(1)}, s32[2,64]{1,0:T(2,128)S(1)}, u32[]{:S(2)}, u32[]{:S(2)}) collective-permute-start(s32[2,64]{1,0:T(2,128)S(1)} %add_select_fusion.4), channel_id=1, source_target_pairs={{0,2},{1,3},{2,0},{3,1},{4,6},{5,7},{6,4},{7,5},{8,10},{9,11},{10,... | collective-permute-start | bytes 1544 | tf_op jit(solution)/shard_map/t_ids_next/ppermute | solution.py:370
  19.6 3.9 %collective-permute-start.2 = (s32[2,2,64]{2,1,0:T(2,128)S(1)}, s32[2,2,64]{2,1,0:T(2,128)S(1)}, u32[]{:S(2)}, u32[]{:S(2)}) collective-permute-start(s32[2,2,64]{2,1,0:T(2,128)S(1)} %add_select_fusion.2), channel_id=1, source_target_pairs={{0,4},{1,5},{2,6},{3,7},{4,0},{5,1},{6,2},{7,3},{8,12},{9,13},{10,... | collective-permute-start | bytes 3080 | tf_op jit(solution)/shard_map/t_ids_rest/ppermute | solution.py:372
  24.6 91.0 %copy-start = (bf16[2,2,64,1024]{3,2,1,0:T(8,128)(2,1)}, bf16[2,2,64,1024]{3,2,1,0:T(8,128)(2,1)S(1)}, u32[]{:S(2)}) copy-start(bf16[2,2,64,1024]{3,2,1,0:T(8,128)(2,1)S(1)} %pad_maximum_fusion.refs_0_) | copy-start | bytes 1572868
  24.6 20.5 %collective-permute-start.4 = (bf16[2,2,64,1024]{3,2,1,0:T(8,128)(2,1)S(1)}, bf16[2,2,64,1024]{3,2,1,0:T(8,128)(2,1)S(1)}, u32[]{:S(2)}, u32[]{:S(2)}) collective-permute-start(bf16[2,2,64,1024]{3,2,1,0:T(8,128)(2,1)S(1)} %pad_maximum_fusion.refs_0_), channel_id=1, source_target_pairs={{0,6},{1,7},{2,0},{3,1},{4,2},{5,3},{6,4},{7,5},{8,14},{9,15},{10,... | collective-permute-start | bytes 1572872 | tf_op jit(solution)/shard_map/t_n_down/ppermute | solution.py:55
  27.4 17.7 %collective-permute-start.5 = (bf16[2,2,64,1024]{3,2,1,0:T(8,128)(2,1)S(1)}, bf16[2,2,64,1024]{3,2,1,0:T(8,128)(2,1)S(1)}, u32[]{:S(2)}, u32[]{:S(2)}) collective-permute-start(bf16[2,2,64,1024]{3,2,1,0:T(8,128)(2,1)S(1)} %pad_maximum_fusion.refs_0_), channel_id=1, source_target_pairs={{0,2},{1,3},{2,4},{3,5},{4,6},{5,7},{6,0},{7,1},{8,10},{9,11},{10,... | collective-permute-start | bytes 1572872 | tf_op jit(solution)/shard_map/t_n_up/ppermute | solution.py:51
  27.4 17.7 %collective-permute-start.8 = (bf16[2,64,1024]{2,1,0:T(8,128)(2,1)}, bf16[2,64,1024]{2,1,0:T(8,128)(2,1)S(1)}, u32[]{:S(2)}, u32[]{:S(2)}) collective-permute-start(bf16[2,64,1024]{2,1,0:T(8,128)(2,1)} %get-tuple-element.39), channel_id=1, source_target_pairs={{0,24},{8,16},{16,8},{24,0},{32,56},{40,48},{48,40},{56,32},{64,88... | collective-permute-start | bytes 786440 | tf_op jit(solution)/shard_map/t_other_diagonal/ppermute | solution.py:43
  32.3 12.8 %collective-permute-start.7 = (bf16[2,64,1024]{2,1,0:T(8,128)(2,1)}, bf16[2,64,1024]{2,1,0:T(8,128)(2,1)S(1)}, u32[]{:S(2)}, u32[]{:S(2)}) collective-permute-start(bf16[2,64,1024]{2,1,0:T(8,128)(2,1)} %get-tuple-element.36), channel_id=1, source_target_pairs={{0,16},{8,24},{16,0},{24,8},{32,48},{40,56},{48,32},{56,40},{64,80... | collective-permute-start | bytes 786440 | tf_op jit(solution)/shard_map/t_other_across/ppermute | solution.py:39
  43.3 15.3 %copy-start.8 = (bf16[1024,512]{1,0:T(8,128)(2,1)S(1)}, bf16[1024,512]{1,0:T(8,128)(2,1)}, u32[]{:S(2)}) copy-start(bf16[1024,512]{1,0:T(8,128)(2,1)} %get-tuple-element.42.refs_12_) | copy-start | bytes 3145732
  45.1 70.4 %copy-start.2 = (bf16[2,2,64,1024]{3,2,1,0:T(8,128)(2,1)}, bf16[2,2,64,1024]{3,2,1,0:T(8,128)(2,1)S(1)}, u32[]{:S(2)}) copy-start(bf16[2,2,64,1024]{3,2,1,0:T(8,128)(2,1)S(1)} %collective-permute-done.4.refs_1_) | copy-start | bytes 1572868
  45.1 70.4 %copy-start.3 = (bf16[2,2,64,1024]{3,2,1,0:T(8,128)(2,1)}, bf16[2,2,64,1024]{3,2,1,0:T(8,128)(2,1)S(1)}, u32[]{:S(2)}) copy-start(bf16[2,2,64,1024]{3,2,1,0:T(8,128)(2,1)S(1)} %collective-permute-done.5.refs_3_) | copy-start | bytes 1572868
  45.3 13.3 %collective-permute-start.17 = (bf16[2,2,64,1024]{3,2,1,0:T(8,128)(2,1)S(1)}, bf16[2,2,64,1024]{3,2,1,0:T(8,128)(2,1)S(1)}, u32[]{:S(2)}, u32[]{:S(2)}) collective-permute-start(bf16[2,2,64,1024]{3,2,1,0:T(8,128)(2,1)S(1)} %pad_maximum_fusion.3), channel_id=1, source_target_pairs={{0,1},{1,0},{2,3},{3,2},{4,5},{5,4},{6,7},{7,6},{8,9},{9,8},{10,11... | collective-permute-start | bytes 1572872 | tf_op jit(solution)/shard_map/t_pair_0/ppermute | solution.py:47
  45.7 69.9 %copy-start.1 = (bf16[2,2,64,1024]{3,2,1,0:T(8,128)(2,1)}, bf16[2,2,64,1024]{3,2,1,0:T(8,128)(2,1)S(1)}, u32[]{:S(2)}) copy-start(bf16[2,2,64,1024]{3,2,1,0:T(8,128)(2,1)S(1)} %pad_maximum_fusion.1.refs_4_) | copy-start | bytes 1572868
  45.7 16.0 %collective-permute-start.9 = (bf16[2,2,64,1024]{3,2,1,0:T(8,128)(2,1)S(1)}, bf16[2,2,64,1024]{3,2,1,0:T(8,128)(2,1)S(1)}, u32[]{:S(2)}, u32[]{:S(2)}) collective-permute-start(bf16[2,2,64,1024]{3,2,1,0:T(8,128)(2,1)S(1)} %pad_maximum_fusion.1.refs_4_), channel_id=1, source_target_pairs={{0,6},{1,7},{2,0},{3,1},{4,2},{5,3},{6,4},{7,5},{8,14},{9,15},{10,... | collective-permute-start | bytes 1572872 | tf_op jit(solution)/shard_map/t_o_down/ppermute | solution.py:55
  58.6 55.2 %copy-start.13 = (bf16[2,2,64,1024]{3,2,1,0:T(8,128)(2,1)}, bf16[2,2,64,1024]{3,2,1,0:T(8,128)(2,1)S(1)}, u32[]{:S(2)}) copy-start(bf16[2,2,64,1024]{3,2,1,0:T(8,128)(2,1)S(1)} %collective-permute-done.17.refs_8_.refs_0_) | copy-start | bytes 1572868
  58.6 37.8 %collective-permute-start.18 = (bf16[1024,512]{1,0:T(8,128)(2,1)S(1)}, bf16[1024,512]{1,0:T(8,128)(2,1)S(1)}, u32[]{:S(2)}, u32[]{:S(2)}) collective-permute-start(bf16[1024,512]{1,0:T(8,128)(2,1)S(1)} %copy-done.8), channel_id=1, source_target_pairs={{0,16},{8,24},{16,0},{24,8},{32,48},{40,56},{48,32},{56,40},{64,80... | collective-permute-start | bytes 3145736 | tf_op jit(solution)/shard_map/t_out_across/ppermute | solution.py:39
  60.1 27.2 %collective-permute-start.11 = (bf16[2,2,64,1024]{3,2,1,0:T(8,128)(2,1)S(1)}, bf16[2,2,64,1024]{3,2,1,0:T(8,128)(2,1)S(1)}, u32[]{:S(2)}, u32[]{:S(2)}) collective-permute-start(bf16[2,2,64,1024]{3,2,1,0:T(8,128)(2,1)S(1)} %pad_maximum_fusion.1.refs_4_), channel_id=1, source_target_pairs={{0,2},{1,3},{2,4},{3,5},{4,6},{5,7},{6,0},{7,1},{8,10},{9,11},{10,... | collective-permute-start | bytes 1572872 | tf_op jit(solution)/shard_map/t_o_up/ppermute | solution.py:51
  60.1 26.3 %collective-permute-start.6 = (bf16[2,2,64,1024]{3,2,1,0:T(8,128)(2,1)S(1)}, bf16[2,2,64,1024]{3,2,1,0:T(8,128)(2,1)S(1)}, u32[]{:S(2)}, u32[]{:S(2)}) collective-permute-start(bf16[2,2,64,1024]{3,2,1,0:T(8,128)(2,1)S(1)} %collective-permute-done.5.refs_3_), channel_id=1, source_target_pairs={{0,2},{1,3},{2,4},{3,5},{4,6},{5,7},{6,0},{7,1},{8,10},{9,11},{10,... | collective-permute-start | bytes 1572872 | tf_op jit(solution)/shard_map/t_n_far/ppermute | solution.py:51
  61.3 33.8 %collective-permute-start.12 = (bf16[2,2,64,1024]{3,2,1,0:T(8,128)(2,1)S(1)}, bf16[2,2,64,1024]{3,2,1,0:T(8,128)(2,1)}, u32[]{:S(2)}, u32[]{:S(2)}) collective-permute-start(bf16[2,2,64,1024]{3,2,1,0:T(8,128)(2,1)S(1)} %pad_maximum_fusion.2), channel_id=1, source_target_pairs={{0,1},{1,0},{2,3},{3,2},{4,5},{5,4},{6,7},{7,6},{8,9},{9,8},{10,11... | collective-permute-start | bytes 1572872 | tf_op jit(solution)/shard_map/t_pair_1/ppermute | solution.py:47
  61.6 54.0 %copy-start.4 = (bf16[2,2,64,1024]{3,2,1,0:T(8,128)(2,1)}, bf16[2,2,64,1024]{3,2,1,0:T(8,128)(2,1)S(1)}, u32[]{:S(2)}) copy-start(bf16[2,2,64,1024]{3,2,1,0:T(8,128)(2,1)S(1)} %collective-permute-done.9.refs_5_) | copy-start | bytes 1572868
  61.6 33.4 %collective-permute-start.10 = (bf16[2,2,64,1024]{3,2,1,0:T(8,128)(2,1)S(1)}, bf16[2,2,64,1024]{3,2,1,0:T(8,128)(2,1)S(1)}, u32[]{:S(2)}, u32[]{:S(2)}) collective-permute-start(bf16[2,2,64,1024]{3,2,1,0:T(8,128)(2,1)S(1)} %collective-permute-done.9.refs_5_), channel_id=1, source_target_pairs={{0,6},{1,7},{2,0},{3,1},{4,2},{5,3},{6,4},{7,5},{8,14},{9,15},{10,... | collective-permute-start | bytes 1572872 | tf_op jit(solution)/shard_map/t_o_far/ppermute | solution.py:55
  86.4 29.2 %copy-start.6 = (bf16[2,2,64,1024]{3,2,1,0:T(8,128)(2,1)}, bf16[2,2,64,1024]{3,2,1,0:T(8,128)(2,1)S(1)}, u32[]{:S(2)}) copy-start(bf16[2,2,64,1024]{3,2,1,0:T(8,128)(2,1)S(1)} %collective-permute-done.6.refs_2_) | copy-start | bytes 1572868
  86.4 14.4 %collective-permute-start.20 = (bf16[2,2,64,1024]{3,2,1,0:T(8,128)(2,1)S(1)}, bf16[2,2,64,1024]{3,2,1,0:T(8,128)(2,1)S(1)}, u32[]{:S(2)}, u32[]{:S(2)}) collective-permute-start(bf16[2,2,64,1024]{3,2,1,0:T(8,128)(2,1)S(1)} %collective-permute-done.17.refs_8_.refs_0_), channel_id=1, source_target_pairs={{0,6},{1,7},{2,0},{3,1},{4,2},{5,3},{6,4},{7,5},{8,14},{9,15},{10,... | collective-permute-start | bytes 1572872 | tf_op jit(solution)/shard_map/t_p_down/ppermute | solution.py:55
  87.3 28.3 %copy-start.5 = (bf16[2,2,64,1024]{3,2,1,0:T(8,128)(2,1)}, bf16[2,2,64,1024]{3,2,1,0:T(8,128)(2,1)S(1)}, u32[]{:S(2)}) copy-start(bf16[2,2,64,1024]{3,2,1,0:T(8,128)(2,1)S(1)} %collective-permute-done.11.refs_7_) | copy-start | bytes 1572868
  87.3 13.5 %collective-permute-start.21 = (bf16[2,2,64,1024]{3,2,1,0:T(8,128)(2,1)S(1)}, bf16[2,2,64,1024]{3,2,1,0:T(8,128)(2,1)S(1)}, u32[]{:S(2)}, u32[]{:S(2)}) collective-permute-start(bf16[2,2,64,1024]{3,2,1,0:T(8,128)(2,1)S(1)} %collective-permute-done.17.refs_8_.refs_0_), channel_id=1, source_target_pairs={{0,2},{1,3},{2,4},{3,5},{4,6},{5,7},{6,0},{7,1},{8,10},{9,11},{10,... | collective-permute-start | bytes 1572872 | tf_op jit(solution)/shard_map/t_p_up/ppermute | solution.py:51
  95.1 0.8 copy-start.7
  95.9 17.9 %collective-permute-start.16 = (bf16[1024,512]{1,0:T(8,128)(2,1)S(1)}, bf16[1024,512]{1,0:T(8,128)(2,1)S(1)}, u32[]{:S(2)}, u32[]{:S(2)}) collective-permute-start(bf16[1024,512]{1,0:T(8,128)(2,1)S(1)} %copy-done.8), channel_id=1, source_target_pairs={{0,8},{8,0},{16,24},{24,16},{32,40},{40,32},{48,56},{56,48},{64,72... | collective-permute-start | bytes 3145736 | tf_op jit(solution)/shard_map/t_out_near/ppermute | solution.py:35
  96.3 17.5 %copy-start.9 = (bf16[1024,512]{1,0:T(8,128)(2,1)}, bf16[1024,512]{1,0:T(8,128)(2,1)S(1)}, u32[]{:S(2)}) copy-start(bf16[1024,512]{1,0:T(8,128)(2,1)S(1)} %collective-permute-done.18.refs_14_) | copy-start | bytes 3145732
  96.3 19.2 %collective-permute-start.19 = (bf16[1024,512]{1,0:T(8,128)(2,1)S(1)}, bf16[1024,512]{1,0:T(8,128)(2,1)}, u32[]{:S(2)}, u32[]{:S(2)}) collective-permute-start(bf16[1024,512]{1,0:T(8,128)(2,1)S(1)} %collective-permute-done.18.refs_14_), channel_id=1, source_target_pairs={{0,8},{8,0},{16,24},{24,16},{32,40},{40,32},{48,56},{56,48},{64,72... | collective-permute-start | bytes 3145736 | tf_op jit(solution)/shard_map/t_out_other/ppermute | solution.py:35
  96.4 14.3 %collective-permute-start.13 = (bf16[2,2,64,1024]{3,2,1,0:T(8,128)(2,1)}, bf16[2,2,64,1024]{3,2,1,0:T(8,128)(2,1)}, u32[]{:S(2)}, u32[]{:S(2)}) collective-permute-start(bf16[2,2,64,1024]{3,2,1,0:T(8,128)(2,1)} %collective-permute-done.12.refs_8_.refs_4_), channel_id=1, source_target_pairs={{0,6},{1,7},{2,0},{3,1},{4,2},{5,3},{6,4},{7,5},{8,14},{9,15},{10,... | collective-permute-start | bytes 1572872 | tf_op jit(solution)/shard_map/t_q_down/ppermute | solution.py:55
  100.8 13.0 %copy-start.15 = (bf16[2,2,64,1024]{3,2,1,0:T(8,128)(2,1)}, bf16[2,2,64,1024]{3,2,1,0:T(8,128)(2,1)S(1)}, u32[]{:S(2)}) copy-start(bf16[2,2,64,1024]{3,2,1,0:T(8,128)(2,1)S(1)} %collective-permute-done.21.refs_11_.refs_3_) | copy-start | bytes 1572868
  100.8 13.0 %collective-permute-start.22 = (bf16[2,2,64,1024]{3,2,1,0:T(8,128)(2,1)S(1)}, bf16[2,2,64,1024]{3,2,1,0:T(8,128)(2,1)S(1)}, u32[]{:S(2)}, u32[]{:S(2)}) collective-permute-start(bf16[2,2,64,1024]{3,2,1,0:T(8,128)(2,1)S(1)} %collective-permute-done.21.refs_11_.refs_3_), channel_id=1, source_target_pairs={{0,2},{1,3},{2,4},{3,5},{4,6},{5,7},{6,0},{7,1},{8,10},{9,11},{10,... | collective-permute-start | bytes 1572872 | tf_op jit(solution)/shard_map/t_p_far/ppermute | solution.py:51
  100.8 13.0 %copy-start.14 = (bf16[2,2,64,1024]{3,2,1,0:T(8,128)(2,1)}, bf16[2,2,64,1024]{3,2,1,0:T(8,128)(2,1)S(1)}, u32[]{:S(2)}) copy-start(bf16[2,2,64,1024]{3,2,1,0:T(8,128)(2,1)S(1)} %collective-permute-done.20.refs_9_.refs_1_) | copy-start | bytes 1572868
  100.8 23.9 %collective-permute-start.15 = (bf16[2,2,64,1024]{3,2,1,0:T(8,128)(2,1)}, bf16[2,2,64,1024]{3,2,1,0:T(8,128)(2,1)}, u32[]{:S(2)}, u32[]{:S(2)}) collective-permute-start(bf16[2,2,64,1024]{3,2,1,0:T(8,128)(2,1)} %collective-permute-done.12.refs_8_.refs_4_), channel_id=1, source_target_pairs={{0,2},{1,3},{2,4},{3,5},{4,6},{5,7},{6,0},{7,1},{8,10},{9,11},{10,... | collective-permute-start | bytes 1572872 | tf_op jit(solution)/shard_map/t_q_up/ppermute | solution.py:51
  110.7 14.0 %collective-permute-start.14 = (bf16[2,2,64,1024]{3,2,1,0:T(8,128)(2,1)}, bf16[2,2,64,1024]{3,2,1,0:T(8,128)(2,1)}, u32[]{:S(2)}, u32[]{:S(2)}) collective-permute-start(bf16[2,2,64,1024]{3,2,1,0:T(8,128)(2,1)} %collective-permute-done.13.refs_9_.refs_5_), channel_id=1, source_target_pairs={{0,6},{1,7},{2,0},{3,1},{4,2},{5,3},{6,4},{7,5},{8,14},{9,15},{10,... | collective-permute-start | bytes 1572872 | tf_op jit(solution)/shard_map/t_q_far/ppermute | solution.py:55
  113.8 0.8 copy-start.16
  114.6 1.0 copy-start.10
  142.6 14.1 %collective-permute-start.23 = (bf16[2,256,1024]{2,1,0:T(8,128)(2,1)}, bf16[2,256,1024]{2,1,0:T(8,128)(2,1)S(1)}, u32[]{:S(2)}, u32[]{:S(2)}) collective-permute-start(bf16[2,256,1024]{2,1,0:T(8,128)(2,1)} %get-tuple-element.47), channel_id=1, source_target_pairs={{0,8},{8,0},{16,24},{24,16},{32,40},{40,32},{48,56},{56,48},{64,72... | collective-permute-start | bytes 3145736 | tf_op jit(solution)/shard_map/t_sum_same_sibling/ppermute | solution.py:35
  147.7 9.1 %copy-start.17 = (f32[256,1024]{1,0:T(8,128)S(1)}, f32[256,1024]{1,0:T(8,128)}, u32[]{:S(2)}) copy-start(f32[256,1024]{1,0:T(8,128)} %get-tuple-element.48) | copy-start | bytes 3145732
  156.7 2.9 %collective-permute-start.25 = (bf16[2,256,1024]{2,1,0:T(8,128)(2,1)}, bf16[2,256,1024]{2,1,0:T(8,128)(2,1)S(1)}, u32[]{:S(2)}, u32[]{:S(2)}) collective-permute-start(bf16[2,256,1024]{2,1,0:T(8,128)(2,1)} %get-tuple-element.51), channel_id=1, source_target_pairs={{0,8},{8,0},{16,24},{24,16},{32,40},{40,32},{48,56},{56,48},{64,72... | collective-permute-start | bytes 3145736 | tf_op jit(solution)/shard_map/t_sum_flip_sibling/ppermute | solution.py:35
  156.8 26.0 %copy-start.11 = (bf16[2,256,1024]{2,1,0:T(8,128)(2,1)}, bf16[2,256,1024]{2,1,0:T(8,128)(2,1)S(1)}, u32[]{:S(2)}) copy-start(bf16[2,256,1024]{2,1,0:T(8,128)(2,1)S(1)} %collective-permute-done.23.rest_1_) | copy-start | bytes 3145732
  156.9 14.6 %collective-permute-start.24 = (bf16[256,1024]{1,0:T(8,128)(2,1)S(1)}, bf16[256,1024]{1,0:T(8,128)(2,1)S(1)}, u32[]{:S(2)}, u32[]{:S(2)}) collective-permute-start(bf16[256,1024]{1,0:T(8,128)(2,1)S(1)} %fusion.1), channel_id=1, source_target_pairs={{0,16},{8,24},{16,0},{24,8},{32,48},{40,56},{48,32},{56,40},{64,80... | collective-permute-start | bytes 1572872 | tf_op jit(solution)/shard_map/t_sum_same_across/ppermute | solution.py:39
  159.6 23.2 %copy-start.12 = (bf16[2,256,1024]{2,1,0:T(8,128)(2,1)}, bf16[2,256,1024]{2,1,0:T(8,128)(2,1)S(1)}, u32[]{:S(2)}) copy-start(bf16[2,256,1024]{2,1,0:T(8,128)(2,1)S(1)} %collective-permute-done.25.rest_4_) | copy-start | bytes 3145732
  161.3 21.4 %collective-permute-start.26 = (bf16[256,1024]{1,0:T(8,128)(2,1)S(1)}, bf16[256,1024]{1,0:T(8,128)(2,1)S(1)}, u32[]{:S(2)}, u32[]{:S(2)}) collective-permute-start(bf16[256,1024]{1,0:T(8,128)(2,1)S(1)} %fusion), channel_id=1, source_target_pairs={{0,16},{8,24},{16,0},{24,8},{32,48},{40,56},{48,32},{56,40},{64,80... | collective-permute-start | bytes 1572872 | tf_op jit(solution)/shard_map/t_sum_flip_across/ppermute | solution.py:39
  171.5 11.2 %copy-start.18 = (bf16[256,1024]{1,0:T(8,128)(2,1)}, bf16[256,1024]{1,0:T(8,128)(2,1)S(1)}, u32[]{:S(2)}) copy-start(bf16[256,1024]{1,0:T(8,128)(2,1)S(1)} %collective-permute-done.24.rest_2_) | copy-start | bytes 1572868
  182.8 0.9 copy-start.19
Sparse Core Ops, SparseCore 0:
  9.7 51.6 all-gather.1
  133.8 50.9 reduce-scatter.1

commit v7 on v6

--- a/solution.py
+++ b/solution.py
@@ -85,31 +85,29 @@
     for p in range(1, margins.shape[1]):
         margin = jnp.where((seg >> 1) == p, margins[0, p], margin)
     factor = jax.nn.sigmoid(-margin) * jnp.where((seg & 1) == 0, -1.0, 1.0)
-    width = own.shape[2]
+    width = own.shape[1]
     factor = jnp.concatenate([factor] * (width // factor.shape[1]), axis=1)
 
-    def put(ref, hh, cc):
-        for e in range(2):
-            start = pl.multiple_of((hh * 2 + cc) * 2 * width, 2 * width) + e * width
-            ref[e] = (up[:, pl.ds(start, width)].astype(F32) * factor).astype(BF16)
-
-    put(own, h, c)
-    put(to_sibling, h, 1 - c)
-    put(to_across, 1 - h, c)
-    put(to_diagonal, 1 - h, 1 - c)
+    def grad(hh, cc):
+        start = pl.multiple_of((hh * 2 + cc) * width, width)
+        return (up[:, pl.ds(start, width)].astype(F32) * factor).astype(BF16)
+
+    own[...] = grad(h, c)
+    to_sibling[...] = grad(h, 1 - c)
+    to_across[...] = grad(1 - h, c)
+    to_diagonal[...] = grad(1 - h, 1 - c)
 
 
 def prep(place, margins, segs, up):
     seq, model = up.shape
-    width = model // 32
-    shape = jax.ShapeDtypeStruct((2, seq, 4 * width), BF16)
-    col = pl.BlockSpec((2, seq, width), lambda i: (0, 0, i))
+    width = model // 16
+    col = pl.BlockSpec((seq, width), lambda i: (0, i))
     return pl.pallas_call(
         prep_kernel,
         grid=(4,),
-        in_specs=[SMEM(), SMEM(), whole(segs.shape), pl.BlockSpec((seq, 8 * width), lambda i: (0, i))],
+        in_specs=[SMEM(), SMEM(), whole(segs.shape), pl.BlockSpec((seq, 4 * width), lambda i: (0, i))],
         out_specs=[col] * 4,
-        out_shape=[shape] * 4,
+        out_shape=[jax.ShapeDtypeStruct((seq, 4 * width), BF16)] * 4,
         compiler_params=params(),
         cost_estimate=cost(3),
         name="prep",
@@ -257,50 +255,51 @@
     )(place, q, k, v, stats, bias, *terms)
 
 
-def partial_kernel(by_half, *refs):
+def partial_kernel(*refs):
     pieces, (weight, keep_near, keep_other, give, x) = refs[:8], refs[8:]
-    _, _, seq, cols = pieces[0].shape
+    seq = pieces[0].shape[2]
     half = 4 * seq
-    width = weight.shape[2] // 2
 
     @pl.when(pl.program_id(0) == 0)
     def _():
-        for e in range(2):
-            for p in range(2):
-                for i in range(2):
-                    for k in range(4):
-                        at = (p * 2 + i) * half + k * seq
-                        piece = pieces[e * 4 + k][p, i] if by_half else pieces[p * 4 + k][e, i]
-                        x[at : at + seq, e * cols : (e + 1) * cols] = piece
-
-    w = jnp.concatenate([weight[j, :, e * width : (e + 1) * width] for e in range(2) for j in range(4)], axis=1)
+        for p in range(2):
+            for i in range(2):
+                for k in range(4):
+                    at = (p * 2 + i) * half + k * seq
+                    x[at : at + seq] = pieces[p * 4 + k][0, i]
+
+    w = jnp.concatenate([weight[j] for j in range(4)], axis=1)
     for p, keep in enumerate((keep_near, keep_other)):
         total = nt(x[p * 2 * half : (p + 1) * 2 * half], w)
         keep[...] = total[:half]
         give[p] = total[half:].astype(BF16)
 
 
-def partial(by_half, pieces, weight):
-    _, _, seq, cols = pieces[0].shape
+def partial(pieces, weight):
+    _, _, seq, cols = pieces[0][0].shape
     heads = weight.shape[1]
     tile = heads // 2
     out = pl.BlockSpec((4 * seq, tile), lambda i: (0, i))
     shape = jax.ShapeDtypeStruct((4 * seq, heads), F32)
+
+    def spec(index):
+        return pl.BlockSpec((1, 2, seq, cols), lambda i: (index, 0, 0, 0))
+
     return pl.pallas_call(
-        functools.partial(partial_kernel, by_half),
+        partial_kernel,
         grid=(2,),
-        in_specs=[whole(x.shape) for x in pieces] + [pl.BlockSpec((4, tile, cols // 2), lambda i: (0, i, 0))],
+        in_specs=[spec(index) for _, index in pieces] + [pl.BlockSpec((4, tile, cols // 4), lambda i: (0, i, 0))],
         out_specs=[out, out, pl.BlockSpec((2, 4 * seq, tile), lambda i: (0, 0, i))],
         out_shape=[shape, shape, jax.ShapeDtypeStruct((2, 4 * seq, heads), BF16)],
-        scratch_shapes=[pltpu.VMEM((16 * seq, 2 * cols), BF16)],
+        scratch_shapes=[pltpu.VMEM((16 * seq, cols), BF16)],
         compiler_params=params(),
         cost_estimate=cost(9),
         name="partial_grad",
-    )(*pieces, weight)
+    )(*[x for x, _ in pieces], weight)
 
 
 def wgrad_kernel(*refs):
-    same, flip, outs, (out, x) = refs[:8], refs[8:12], refs[12:16], refs[-2:]
+    same, flip, outs, (out, x) = refs[:8], refs[8:16], refs[16:20], refs[20:]
     seq = same[0].shape[2]
     length = 8 * seq
     for p in range(2):
@@ -308,37 +307,34 @@
             for k in range(4):
                 at = (p * 2 + i) * length + 2 * k * seq
                 x[at : at + seq] = same[p * 4 + k][0, i]
-                x[at + seq : at + 2 * seq] = flip[k][p, i]
+                x[at + seq : at + 2 * seq] = flip[p * 4 + k][0, i]
     tile = 256
-    width = out.shape[2]
     for m in range(0, out.shape[1], tile):
         total = nn(outs[0][m : m + tile], x[:length])
         for r in range(1, 4):
             total += nn(outs[r][m : m + tile], x[r * length : (r + 1) * length])
-        for k in range(2):
-            out[k, m : m + tile] = total[:, k * width : (k + 1) * width].astype(BF16)
-
-
-def wgrad(half, same, flip, outs, into=None):
-    _, _, seq, cols = same[0].shape
+        out[0, m : m + tile] = total.astype(BF16)
+
+
+def wgrad(same, flip, outs):
+    _, _, seq, cols = same[0][0].shape
     heads = outs[0].shape[0]
-    wide = cols // 2
-    kept = [] if into is None else [into]
+    width = cols // 4
+
+    def spec(index):
+        return pl.BlockSpec((1, 2, seq, width), lambda i: (index, 0, 0, i))
+
     return pl.pallas_call(
         wgrad_kernel,
-        grid=(2,),
-        in_specs=[pl.BlockSpec((1, 2, seq, wide), lambda i: (half, 0, 0, i))] * 8
-        + [pl.BlockSpec((2, 2, seq, wide), lambda i: (0, 0, 0, i))] * 4
-        + [whole(outs[0].shape)] * 4
-        + [pl.BlockSpec(memory_space=pl.ANY)] * len(kept),
-        out_specs=pl.BlockSpec((2, heads, wide // 2), lambda i: (i, 0, half)),
-        out_shape=jax.ShapeDtypeStruct((4, heads, wide), BF16),
-        scratch_shapes=[pltpu.VMEM((32 * seq, wide), BF16)],
-        input_output_aliases={16: 0} if kept else {},
+        grid=(4,),
+        in_specs=[spec(index) for _, index in same + flip] + [whole(outs[0].shape)] * 4,
+        out_specs=pl.BlockSpec((1, heads, width), lambda i: (i, 0, 0)),
+        out_shape=jax.ShapeDtypeStruct((4, heads, width), BF16),
+        scratch_shapes=[pltpu.VMEM((32 * seq, width), BF16)],
         compiler_params=params(),
-        cost_estimate=cost(9),
+        cost_estimate=cost(16),
         name="weight_grad",
-    )(*same, *flip, *outs, *kept)
+    )(*[x for x, _ in same + flip], *outs)
 
 
 def named(name, fn, x):
@@ -374,40 +370,35 @@
     whole_segs = jnp.broadcast_to(ids[:, None], (ids.shape[0], HD))
 
     from_sibling = named("near_sibling", sibling, after(to_sibling, partner))
-    near = jnp.stack([own, after(from_sibling, rest_ids)], axis=1)
+    near = jnp.stack([own, after(from_sibling, rest_ids)])
     n_up, n_down = named("n_up", y_up, near), named("n_down", y_down, near)
     attn_out, stats, bias = forward(place, whole_segs, query, key, value)
-    other = jnp.stack([after(from_across, n_up, n_down, attn_out), from_diagonal], axis=1)
-    flips = [named("pair_%d" % e, pair, jnp.stack([near[e], other[e]])) for e in range(2)]
-
-    n, o, p, q = near, other, flips[0], flips[1]
+    other = jnp.stack([after(from_across, n_up, n_down, attn_out), from_diagonal])
+
+    n, o = near, other
     n_far, o_down = named("n_far", y_up, n_up), named("o_down", y_down, o)
-    o_up, o_far = named("o_up", y_up, o), named("o_far", y_down, o_down)
-    out_across = named("out_across", across, after(attn_out, p))
-    p, q = after(p, n_far, o_down), after(q, o_up, o_far)
-    p_up, p_down = named("p_up", y_up, p), named("p_down", y_down, p)
-    p_far, q_down = named("p_far", y_up, p_up), named("q_down", y_down, q)
-    q_up, q_far = named("q_up", y_up, q), named("q_far", y_down, q_down)
-    near_blocks = [n, n_down, n_far, n_up]
-    other_blocks = [o, o_down, o_far, o_up]
-    same = [*near_blocks, *other_blocks]
-
-    def sums(name, by_half, pieces):
-        keep_near, keep_other, give = partial(by_half, pieces, weight)
+    f = named("pair", pair, jnp.stack([near, other]))
+    out_across = named("out_across", across, after(attn_out, f, n_far, o_down))
+    o_up, o_far = named("o_up", y_up, after(o, n_far, o_down)), named("o_far", y_down, o_down)
+    f = after(f, o_up, o_far)
+    f_up, f_down = named("f_up", y_up, f), named("f_down", y_down, f)
+    f_far = [named("f_far_up", y_up, f_up[0]), named("f_far_down", y_down, f_down[1])]
+    same = [(x[None], 0) for x in (n, n_down, n_far, n_up, o, o_down, o_far, o_up)]
+    flip = [x for p in range(2) for x in ((f, p), (f_down, p), (f_far[p][None], 0), (f_up, p))]
+
+    def sums(name, pieces):
+        keep_near, keep_other, give = partial(pieces, weight)
         given = named(name + "_sibling", sibling, give)
         total = (keep_other + given[1].astype(F32)).astype(BF16)
         return keep_near, given, named(name + "_across", across, total)
 
+    terms_same = sums("sum_same", same)
     out_near = named("out_near", sibling, after(attn_out, o_up, o_far))
     out_other = named("out_other", sibling, after(out_across, o_up, o_far))
-    outs = (attn_out, out_near, out_across, out_other)
-
-    flips = [[p, p_down, p_far, p_up], [q, q_down, q_far, q_up]]
-    first = wgrad(0, same, flips[0], outs)
-    total = wgrad(1, same, flips[1], outs, first).reshape(4 * heads, width)
-    weight_grad = lax.psum_scatter(total, "dp", scatter_dimension=0, tiled=True, axis_index_groups=Z_GROUPS)
-    terms_same = sums("sum_same", False, [after(n, total), *same[1:]])
-    terms_flip = sums("sum_flip", True, [after(p, terms_same[0]), *flips[0][1:], *flips[1]])
+    outs = (attn_out, out_near, out_across, after(out_other, terms_same[1]))
+    total = wgrad(same, flip, outs).reshape(4 * heads, width)
+    weight_grad = lax.psum_scatter(after(total, terms_same[2]), "dp", scatter_dimension=0, tiled=True, axis_index_groups=Z_GROUPS)
+    terms_flip = sums("sum_flip", [(after(f, total), 0), *flip[1:]])
     dq, dk, dv = backward(place, query, key, value, stats, bias, [*terms_same, *terms_flip])
     return (dq[None], dk[None], dv[None], weight_grad.astype(F32))
 

time: 203 us -> 191 us (0.941)
  waiting for transfers between devices: 76 us -> 71.1 us
  Pallas kernels: 57.4 us -> 52.8 us
  starting transfers between devices: 39.5 us -> 37.4 us
    ppermute x3 -> x2, waiting for transfers between devices: 17.1 us -> 0.01 us  [pair(): return lax.ppermute(x, 'tensor', PAIR)]
    ppermute x6 -> x5, waiting for transfers between devices: 24.7 us -> 38.3 us  [y_up(): return lax.ppermute(x, 'tensor', Y_UP)]
    reduce_scatter x1, waiting for transfers between devices: 0.02 us -> 10.3 us  [shards(): lax.psum_scatter(after(total, terms_same[2]), 'dp', scatter_dimension=0,...]
    ppermute x4, waiting for transfers between devices: 20.8 us -> 13.6 us  [across(): return lax.ppermute(x, 'dp', ACROSS)]
    ppermute x6 -> x5, waiting for transfers between devices: 9.81 us -> 4.32 us  [y_down(): return lax.ppermute(x, 'tensor', Y_DOWN)]
    pallas_call x4 -> x3, Pallas kernels: 35.9 us -> 31.4 us  [the longest x2 17.9 us: partial(): pl.pallas_call(partial_kernel, grid=(2,), in_specs=[spec(index) for _, in...]
    ppermute x4, starting transfers between devices: 4.69 us -> 7.08 us  [across(): return lax.ppermute(x, 'dp', ACROSS)]
    ppermute x6 -> x5, starting transfers between devices: 14.3 us -> 14.2 us  [y_down(): return lax.ppermute(x, 'tensor', Y_DOWN)]
  transfers between devices with their start and end apart: 29 -> 26, of which waited for: 12 -> 11; matrix products, arithmetic and copies ran while one was open for 5% -> 5% of each run, Pallas kernels for 28% -> 28%
where the time goes in v7:
time: 191 us
  waiting for transfers between devices  71.1 us (37%)
  Pallas kernels  52.8 us (28%)
  starting transfers between devices  37.4 us (20%)
  between operations  14.3 us (7%)
  other arithmetic  10 us (5%)
  local copies, waits for them, and re-layouts  4.94 us (3%)
    ppermute x5, waiting for transfers between devices, y_up(): return lax.ppermute(x, 'tensor', Y_UP)  38.3 us
    pallas_call x2, Pallas kernels, partial(): pl.pallas_call(partial_kernel, grid=(2,), in_specs=[spec(index) for _, in...  17.9 us
    ppermute x5, starting transfers between devices, y_down(): return lax.ppermute(x, 'tensor', Y_DOWN)  14.2 us
    ppermute x4, waiting for transfers between devices, across(): return lax.ppermute(x, 'dp', ACROSS)  13.6 us
    pallas_call x1, Pallas kernels, wgrad(): pl.pallas_call(wgrad_kernel, grid=(4,), in_specs=[spec(index) for _, inde...  13.5 us
    reduce_scatter x1, waiting for transfers between devices, shards(): lax.psum_scatter(after(total, terms_same[2]), 'dp', scatter_dimension=0,...  10.3 us
    pallas_call x1, Pallas kernels, backward(): pl.pallas_call(backward_kernel, grid=(pairs,), in_specs=[SMEM(), two, who...  9.28 us
    pallas_call x1, Pallas kernels, forward(): pl.pallas_call(forward_kernel, grid=(pairs,), in_specs=[SMEM(), whole(seg...  8.75 us
  transfers between devices with their start and end apart: 26, of which 11 were waited for; matrix products, arithmetic and copies ran while one was open for 5% of the time, Pallas kernels for 28%

profile of v7, /device:TPU:1, one launch (start us, length us, event | category | flops | bytes accessed | tf_op | source)
XLA Modules:
  0.0 190.6 jit_solution(8491496641167154889)
XLA Ops:
  7.2 0.0 all-gather.2.cloned.1.call-start
  7.2 0.7 all-gather.2.cloned.1.call-update
  7.9 0.0 reduce-scatter.2.cloned.1.call-start
  7.9 2.1 %collective-permute-start = (s32[64]{0:T(128)}, s32[64]{0:T(128)S(1)}, u32[]{:S(2)}, u32[]{:S(2)}) collective-permute-start(s32[64]{0:T(128)} %bitcast.82), channel_id=1, source_target_pairs={{0,1},{1,0},{2,3},{3,2},{4,5},{5,4},{6,7},{7,6},{8,9},{9,8},{10,11... | collective-permute-start | bytes 776 | tf_op jit(solution)/shard_map/t_ids_pair/ppermute | solution.py:47
  10.1 0.7 pad_add_fusion.place
  10.7 1.3 broadcast_in_dim.50.segs
  12.1 3.4 %prep.1 = (bf16[64,2048]{1,0:T(8,128)(2,1)}, bf16[64,2048]{1,0:T(8,128)(2,1)}, bf16[64,2048]{1,0:T(8,128)(2,1)}, bf16[64,2048]{1,0:T(8,128)(2,1)}) custom-call(s32[4]{0:T(128)} %pad_add_fusion.place, f32[1,4]{1,0:T(1,128)} %margins.1, s32[64,128]{1,0:T(8,128)} %broadcast_in_dim.50.segs, bf16[64,8192]{1,0:T(8,128)(2,1)} %bitcast.73), custom_call_target="tpu_custom_call" | custom-call | bytes 9000000 | tf_op jit(solution)/shard_map/prep/pallas_call | solution.py:105
  15.5 0.0 collective-permute-done
  15.5 1.0 collective-permute-start.3
  16.5 0.7 add_select_fusion.4
  17.3 1.3 collective-permute-start.1
  18.6 0.7 add_select_fusion.3
  19.3 0.4 collective-permute-done.1
  19.7 2.9 %collective-permute-start.2 = (s32[2,2,64]{2,1,0:T(2,128)S(1)}, s32[2,2,64]{2,1,0:T(2,128)S(1)}, u32[]{:S(2)}, u32[]{:S(2)}) collective-permute-start(s32[2,2,64]{2,1,0:T(2,128)S(1)} %add_select_fusion.2), channel_id=1, source_target_pairs={{0,4},{1,5},{2,6},{3,7},{4,0},{5,1},{6,2},{7,3},{8,12},{9,13},{10,... | collective-permute-start | bytes 3080 | tf_op jit(solution)/shard_map/t_ids_rest/ppermute | solution.py:368
  22.6 1.0 collective-permute-done.2
  23.7 1.0 pad_maximum_fusion.1
  24.7 2.8 %collective-permute-start.4 = (bf16[2,64,2048]{2,1,0:T(8,128)(2,1)S(1)}, bf16[2,64,2048]{2,1,0:T(8,128)(2,1)S(1)}, u32[]{:S(2)}, u32[]{:S(2)}) collective-permute-start(bf16[2,64,2048]{2,1,0:T(8,128)(2,1)S(1)} %get-tuple-element.60), channel_id=1, source_target_pairs={{0,6},{1,7},{2,0},{3,1},{4,2},{5,3},{6,4},{7,5},{8,14},{9,15},{10,... | collective-permute-start | bytes 1572872 | tf_op jit(solution)/shard_map/t_n_down/ppermute | solution.py:55
  27.5 2.4 %collective-permute-start.7 = (bf16[64,2048]{1,0:T(8,128)(2,1)}, bf16[64,2048]{1,0:T(8,128)(2,1)S(1)}, u32[]{:S(2)}, u32[]{:S(2)}) collective-permute-start(bf16[64,2048]{1,0:T(8,128)(2,1)} %get-tuple-element.37), channel_id=1, source_target_pairs={{0,16},{8,24},{16,0},{24,8},{32,48},{40,56},{48,32},{56,40},{64,80... | collective-permute-start | bytes 786440 | tf_op jit(solution)/shard_map/t_other_across/ppermute | solution.py:39
  30.0 3.3 %collective-permute-start.8 = (bf16[64,2048]{1,0:T(8,128)(2,1)}, bf16[64,2048]{1,0:T(8,128)(2,1)S(1)}, u32[]{:S(2)}, u32[]{:S(2)}) collective-permute-start(bf16[64,2048]{1,0:T(8,128)(2,1)} %get-tuple-element.40), channel_id=1, source_target_pairs={{0,24},{8,16},{16,8},{24,0},{32,56},{40,48},{48,40},{56,32},{64,88... | collective-permute-start | bytes 786440 | tf_op jit(solution)/shard_map/t_other_diagonal/ppermute | solution.py:43
  33.3 0.7 fusion.4
  34.0 0.1 select_n.104
  34.1 0.8 broadcast_in_dim.49.segs
  34.9 8.8 %attend.1 = (bf16[1024,512]{1,0:T(8,128)(2,1)}, f32[4,8,256]{2,1,0:T(8,128)}, f32[4,384,128]{2,1,0:T(8,128)}) custom-call(s32[4]{0:T(128)} %pad_add_fusion.place, s32[512,128]{1,0:T(8,128)} %broadcast_in_dim.49.segs, bf16[512,1024]{1,0:T(8,128)(2,1)} %bitcast.55, bf16[512,128]{1,0:T(8,128)(2,1)} %bitcast.74, bf16[512,128]{1,0:T(8,128)(2,1)} %bitcast.76), custom_call_target="tpu_custom_call" | custom-call | bytes 27000000 | tf_op jit(solution)/shard_map/attend/pallas_call | solution.py:168
  43.7 0.0 collective-permute-done.7
  43.7 0.0 collective-permute-done.5
  43.7 0.0 collective-permute-done.8
  43.7 0.1 pad_maximum_fusion.2
  43.8 3.0 %collective-permute-start.9 = (bf16[2,64,2048]{2,1,0:T(8,128)(2,1)S(1)}, bf16[2,64,2048]{2,1,0:T(8,128)(2,1)S(1)}, u32[]{:S(2)}, u32[]{:S(2)}) collective-permute-start(bf16[2,64,2048]{2,1,0:T(8,128)(2,1)S(1)} %get-tuple-element.41), channel_id=1, source_target_pairs={{0,6},{1,7},{2,0},{3,1},{4,2},{5,3},{6,4},{7,5},{8,14},{9,15},{10,... | collective-permute-start | bytes 1572872 | tf_op jit(solution)/shard_map/t_o_down/ppermute | solution.py:55
  46.8 0.1 pad_maximum_fusion
  46.9 0.4 collective-permute-start.14
  47.3 14.4 %collective-permute-done.6 = bf16[2,64,2048]{2,1,0:T(8,128)(2,1)S(1)} collective-permute-done((bf16[2,64,2048]{2,1,0:T(8,128)(2,1)S(1)}, bf16[2,64,2048]{2,1,0:T(8,128)(2,1)S(1)}, u32[]{:S(2)}, u32[]{:S(2)}) %collective-permute-start.6) | collective-permute-done | bytes 524320 | tf_op jit(solution)/shard_map/t_n_far/ppermute | solution.py:51
  61.7 0.0 collective-permute-done.9
  61.7 0.1 collective-permute-start.11
  61.8 2.7 %collective-permute-start.10 = (bf16[2,64,2048]{2,1,0:T(8,128)(2,1)S(1)}, bf16[2,64,2048]{2,1,0:T(8,128)(2,1)S(1)}, u32[]{:S(2)}, u32[]{:S(2)}) collective-permute-start(bf16[2,64,2048]{2,1,0:T(8,128)(2,1)S(1)} %collective-permute-done.9), channel_id=1, source_target_pairs={{0,6},{1,7},{2,0},{3,1},{4,2},{5,3},{6,4},{7,5},{8,14},{9,15},{10,... | collective-permute-start | bytes 1572872 | tf_op jit(solution)/shard_map/t_o_far/ppermute | solution.py:55
  64.5 11.3 %collective-permute-done.11 = bf16[2,64,2048]{2,1,0:T(8,128)(2,1)S(1)} collective-permute-done((bf16[2,64,2048]{2,1,0:T(8,128)(2,1)S(1)}, bf16[2,64,2048]{2,1,0:T(8,128)(2,1)S(1)}, u32[]{:S(2)}, u32[]{:S(2)}) %collective-permute-start.11) | collective-permute-done | bytes 524320 | tf_op jit(solution)/shard_map/t_o_up/ppermute | solution.py:51
  75.8 0.1 collective-permute-start.16
  76.0 1.2 collective-permute-start.20
  77.2 3.0 %collective-permute-start.15 = (bf16[2,2,64,2048]{3,2,1,0:T(8,128)(2,1)S(1)}, bf16[2,2,64,2048]{3,2,1,0:T(8,128)(2,1)S(1)}, u32[]{:S(2)}, u32[]{:S(2)}) collective-permute-start(bf16[2,2,64,2048]{3,2,1,0:T(8,128)(2,1)S(1)} %collective-permute-done.14.refs_8_.refs_12_.refs_0_.refs_4_), channel_id=1, source_target_pairs={{0,6},{1,7},{2,0},{3,1},{4,2},{5,3},{6,4},{7,5},{8,14},{9,15},{10,... | collective-permute-start | bytes 3145736 | tf_op jit(solution)/shard_map/t_f_down/ppermute | solution.py:55
  80.2 8.9 %partial_grad.2 = (f32[256,1024]{1,0:T(8,128)}, f32[256,1024]{1,0:T(8,128)}, bf16[2,256,1024]{2,1,0:T(8,128)(2,1)}) custom-call(bf16[1,2,64,2048]{3,2,1,0:T(8,128)(2,1)} %copy-done.3, bf16[1,2,64,2048]{3,2,1,0:T(8,128)(2,1)} %bitcast.57, bf16[1,2,64,2048]{3,2,1,0:T(8,128)(2,1)} %bitcast.63, bf16[1,2,64,2048]{3,2,1,0:T(8,128)(2,1)} %bitcast.59, ...), custom_call_target="tpu_custom_call" | custom-call | bytes 27000000 | tf_op jit(solution)/shard_map/partial_grad/pallas_call | solution.py:288
  89.2 1.0 collective-permute-start.12
  90.1 0.1 collective-permute-start.19
  90.2 10.1 %collective-permute-done.16.refs_11_.refs_15_.refs_3_.refs_7_ = bf16[2,2,64,2048]{3,2,1,0:T(8,128)(2,1)S(1)} collective-permute-done((bf16[2,2,64,2048]{3,2,1,0:T(8,128)(2,1)S(1)}, bf16[2,2,64,2048]{3,2,1,0:T(8,128)(2,1)S(1)}, u32[]{:S(2)}, u32[]{:S(2)}) %collective-permute-start.16) | collective-permute-done | bytes 1048608 | tf_op jit(solution)/shard_map/t_f_up/ppermute | solution.py:51
  100.4 0.1 collective-permute-start.17
  100.5 0.5 collective-permute-done.20.refs_18_
  101.0 2.5 %collective-permute-start.21 = (bf16[1024,512]{1,0:T(8,128)(2,1)}, bf16[1024,512]{1,0:T(8,128)(2,1)S(1)}, u32[]{:S(2)}, u32[]{:S(2)}) collective-permute-start(bf16[1024,512]{1,0:T(8,128)(2,1)} %collective-permute-done.20.refs_18_), channel_id=1, source_target_pairs={{0,8},{8,0},{16,24},{24,16},{32,40},{40,32},{48,56},{56,48},{64,72... | collective-permute-start | bytes 3145736 | tf_op jit(solution)/shard_map/t_out_other/ppermute | solution.py:35
  103.5 2.7 %collective-permute-start.18 = (bf16[2,64,2048]{2,1,0:T(8,128)(2,1)S(1)}, bf16[2,64,2048]{2,1,0:T(8,128)(2,1)S(1)}, u32[]{:S(2)}, u32[]{:S(2)}) collective-permute-start(bf16[2,64,2048]{2,1,0:T(8,128)(2,1)S(1)} %slice_bitcast_fusion.1), channel_id=1, source_target_pairs={{0,6},{1,7},{2,0},{3,1},{4,2},{5,3},{6,4},{7,5},{8,14},{9,15},{10,... | collective-permute-start | bytes 1572872 | tf_op jit(solution)/shard_map/t_f_far_down/ppermute | solution.py:55
  106.2 1.0 copy-done.5
  107.2 1.4 fusion.1
  108.5 1.7 collective-permute-start.13
  110.3 2.5 %collective-permute-done.17 = bf16[2,64,2048]{2,1,0:T(8,128)(2,1)S(1)} collective-permute-done((bf16[2,64,2048]{2,1,0:T(8,128)(2,1)S(1)}, bf16[2,64,2048]{2,1,0:T(8,128)(2,1)S(1)}, u32[]{:S(2)}, u32[]{:S(2)}) %collective-permute-start.17) | collective-permute-done | bytes 524320 | tf_op jit(solution)/shard_map/t_f_far_up/ppermute | solution.py:51
  112.7 4.3 %collective-permute-done.18 = bf16[2,64,2048]{2,1,0:T(8,128)(2,1)S(1)} collective-permute-done((bf16[2,64,2048]{2,1,0:T(8,128)(2,1)S(1)}, bf16[2,64,2048]{2,1,0:T(8,128)(2,1)S(1)}, u32[]{:S(2)}, u32[]{:S(2)}) %collective-permute-start.18) | collective-permute-done | bytes 524320 | tf_op jit(solution)/shard_map/t_f_far_down/ppermute | solution.py:55
  117.1 0.8 copy-done.14
  117.8 13.5 %weight_grad.1 = bf16[4,1024,512]{2,1,0:T(8,128)(2,1)} custom-call(bf16[1,2,64,2048]{3,2,1,0:T(8,128)(2,1)} %copy-done.3, bf16[1,2,64,2048]{3,2,1,0:T(8,128)(2,1)} %bitcast.58, bf16[1,2,64,2048]{3,2,1,0:T(8,128)(2,1)} %bitcast.64, bf16[1,2,64,2048]{3,2,1,0:T(8,128)(2,1)} %bitcast.60, bf16[1,2,64,2048]{3,2,1,0:T(8,128)(2,1)} %copy-done.4, ...), custom_call_target="tpu_custom_call" | custom-call | bytes 48000000 | tf_op jit(solution)/shard_map/weight_grad/pallas_call | solution.py:327
  131.4 0.0 reduce-scatter.2.cloned.1.call-update
  131.4 8.9 %partial_grad.3 = (f32[256,1024]{1,0:T(8,128)}, f32[256,1024]{1,0:T(8,128)}, bf16[2,256,1024]{2,1,0:T(8,128)(2,1)}) custom-call(bf16[2,2,64,2048]{3,2,1,0:T(8,128)(2,1)} %copy-done.2, bf16[2,2,64,2048]{3,2,1,0:T(8,128)(2,1)} %copy-done.1, bf16[1,2,64,2048]{3,2,1,0:T(8,128)(2,1)} %bitcast.70, bf16[2,2,64,2048]{3,2,1,0:T(8,128)(2,1)} %copy-done, ...), custom_call_target="tpu_custom_call" | custom-call | bytes 27000000 | tf_op jit(solution)/shard_map/partial_grad/pallas_call | solution.py:288
  140.3 1.3 collective-permute-start.22
  141.6 2.5 %collective-permute-done.22.rest_4_ = bf16[2,256,1024]{2,1,0:T(8,128)(2,1)S(1)} collective-permute-done((bf16[2,256,1024]{2,1,0:T(8,128)(2,1)}, bf16[2,256,1024]{2,1,0:T(8,128)(2,1)S(1)}, u32[]{:S(2)}, u32[]{:S(2)}) %collective-permute-start.22) | collective-permute-done | bytes 1048608 | tf_op jit(solution)/shard_map/t_sum_flip_sibling/ppermute | solution.py:35
  144.1 1.7 fusion
  145.9 1.7 collective-permute-start.23
  147.5 13.1 %collective-permute-done.23.rest_5_ = bf16[256,1024]{1,0:T(8,128)(2,1)S(1)} collective-permute-done((bf16[256,1024]{1,0:T(8,128)(2,1)S(1)}, bf16[256,1024]{1,0:T(8,128)(2,1)S(1)}, u32[]{:S(2)}, u32[]{:S(2)}) %collective-permute-start.23) | collective-permute-done | bytes 524320 | tf_op jit(solution)/shard_map/t_sum_flip_across/ppermute | solution.py:39
  160.6 0.8 copy-done.17
  161.4 9.3 %attend_grad.1 = (bf16[512,1024]{1,0:T(8,128)(2,1)}, bf16[512,128]{1,0:T(8,128)(2,1)}, bf16[512,128]{1,0:T(8,128)(2,1)}) custom-call(s32[4]{0:T(128)} %pad_add_fusion.place, bf16[512,1024]{1,0:T(8,128)(2,1)} %bitcast.56, bf16[512,128]{1,0:T(8,128)(2,1)} %bitcast.75, bf16[512,128]{1,0:T(8,128)(2,1)} %bitcast.77, f32[4,8,256]{2,1,0:T(8,128)} %get-tuple-element.31.stats, ...), custom_call_target="tpu_custom_call" | custom-call | bytes 27000000 | tf_op jit(solution)/shard_map/attend_grad/pallas_call | solution.py:237
  170.7 10.3 %reduce-scatter.2.cloned.1.call-done = bf16[1024,512]{1,0:T(8,128)(2,1)} async-done(((bf16[4096,512]{1,0:T(8,128)(2,1)}), bf16[1024,512]{1,0:T(8,128)(2,1)}) %reduce-scatter.2.cloned.1.call-update) | async-done | bytes 1048592 | tf_op jit(solution)/shard_map/reduce_scatter | solution.py:400
  181.0 2.8 %convert_element_type.27 = f32[1024,512]{1,0:T(8,128)} convert(bf16[1024,512]{1,0:T(8,128)(2,1)} %reduce-scatter.2.cloned.1.call-done) | non-fusion elementwise | flops 524288 | bytes 3145728 | tf_op jit(solution)/shard_map/convert_element_type | solution.py:403
  (50 shorter events, 0.2 us)
Async XLA Ops:
  7.2 73.1 %all-gather.2.cloned.1.call-start = ((), (), s32[]{:S(2)}) async-start(), calls=%async_computation.1 | async-start | bytes 5242880 | tf_op jit(solution)/shard_map/all_gather | solution.py:357
  7.9 173.1 %reduce-scatter.2.cloned.1.call-start = ((), (), s32[]{:S(2)}) async-start(), calls=%async_computation.2 | async-start | bytes 5242880 | tf_op jit(solution)/shard_map/reduce_scatter | solution.py:400
  7.9 7.5 %collective-permute-start = (s32[64]{0:T(128)}, s32[64]{0:T(128)S(1)}, u32[]{:S(2)}, u32[]{:S(2)}) collective-permute-start(s32[64]{0:T(128)} %bitcast.82), channel_id=1, source_target_pairs={{0,1},{1,0},{2,3},{3,2},{4,5},{5,4},{6,7},{7,6},{8,9},{9,8},{10,11... | collective-permute-start | bytes 776 | tf_op jit(solution)/shard_map/t_ids_pair/ppermute | solution.py:47
  15.5 8.2 %collective-permute-start.3 = (bf16[64,2048]{1,0:T(8,128)(2,1)}, bf16[64,2048]{1,0:T(8,128)(2,1)S(1)}, u32[]{:S(2)}, u32[]{:S(2)}) collective-permute-start(bf16[64,2048]{1,0:T(8,128)(2,1)} %get-tuple-element.35), channel_id=1, source_target_pairs={{0,8},{8,0},{16,24},{24,16},{32,40},{40,32},{48,56},{56,48},{64,72... | collective-permute-start | bytes 786440 | tf_op jit(solution)/shard_map/t_near_sibling/ppermute | solution.py:35
  17.3 2.5 %collective-permute-start.1 = (s32[2,64]{1,0:T(2,128)S(1)}, s32[2,64]{1,0:T(2,128)S(1)}, u32[]{:S(2)}, u32[]{:S(2)}) collective-permute-start(s32[2,64]{1,0:T(2,128)S(1)} %add_select_fusion.4), channel_id=1, source_target_pairs={{0,2},{1,3},{2,0},{3,1},{4,6},{5,7},{6,4},{7,5},{8,10},{9,11},{10,... | collective-permute-start | bytes 1544 | tf_op jit(solution)/shard_map/t_ids_next/ppermute | solution.py:366
  19.7 3.9 %collective-permute-start.2 = (s32[2,2,64]{2,1,0:T(2,128)S(1)}, s32[2,2,64]{2,1,0:T(2,128)S(1)}, u32[]{:S(2)}, u32[]{:S(2)}) collective-permute-start(s32[2,2,64]{2,1,0:T(2,128)S(1)} %add_select_fusion.2), channel_id=1, source_target_pairs={{0,4},{1,5},{2,6},{3,7},{4,0},{5,1},{6,2},{7,3},{8,12},{9,13},{10,... | collective-permute-start | bytes 3080 | tf_op jit(solution)/shard_map/t_ids_rest/ppermute | solution.py:368
  24.7 51.1 %copy-start.3 = (bf16[1,2,64,2048]{3,2,1,0:T(8,128)(2,1)}, bf16[1,2,64,2048]{3,2,1,0:T(8,128)(2,1)S(1)}, u32[]{:S(2)}) copy-start(bf16[1,2,64,2048]{3,2,1,0:T(8,128)(2,1)S(1)} %get-tuple-element.61.refs_0_) | copy-start | bytes 1572868
  24.7 19.0 %collective-permute-start.4 = (bf16[2,64,2048]{2,1,0:T(8,128)(2,1)S(1)}, bf16[2,64,2048]{2,1,0:T(8,128)(2,1)S(1)}, u32[]{:S(2)}, u32[]{:S(2)}) collective-permute-start(bf16[2,64,2048]{2,1,0:T(8,128)(2,1)S(1)} %get-tuple-element.60), channel_id=1, source_target_pairs={{0,6},{1,7},{2,0},{3,1},{4,2},{5,3},{6,4},{7,5},{8,14},{9,15},{10,... | collective-permute-start | bytes 1572872 | tf_op jit(solution)/shard_map/t_n_down/ppermute | solution.py:55
  27.5 16.2 %collective-permute-start.5 = (bf16[2,64,2048]{2,1,0:T(8,128)(2,1)S(1)}, bf16[2,64,2048]{2,1,0:T(8,128)(2,1)S(1)}, u32[]{:S(2)}, u32[]{:S(2)}) collective-permute-start(bf16[2,64,2048]{2,1,0:T(8,128)(2,1)S(1)} %get-tuple-element.60), channel_id=1, source_target_pairs={{0,2},{1,3},{2,4},{3,5},{4,6},{5,7},{6,0},{7,1},{8,10},{9,11},{10,... | collective-permute-start | bytes 1572872 | tf_op jit(solution)/shard_map/t_n_up/ppermute | solution.py:51
  27.5 16.2 %collective-permute-start.7 = (bf16[64,2048]{1,0:T(8,128)(2,1)}, bf16[64,2048]{1,0:T(8,128)(2,1)S(1)}, u32[]{:S(2)}, u32[]{:S(2)}) collective-permute-start(bf16[64,2048]{1,0:T(8,128)(2,1)} %get-tuple-element.37), channel_id=1, source_target_pairs={{0,16},{8,24},{16,0},{24,8},{32,48},{40,56},{48,32},{56,40},{64,80... | collective-permute-start | bytes 786440 | tf_op jit(solution)/shard_map/t_other_across/ppermute | solution.py:39
  30.0 13.8 %collective-permute-start.8 = (bf16[64,2048]{1,0:T(8,128)(2,1)}, bf16[64,2048]{1,0:T(8,128)(2,1)S(1)}, u32[]{:S(2)}, u32[]{:S(2)}) collective-permute-start(bf16[64,2048]{1,0:T(8,128)(2,1)} %get-tuple-element.40), channel_id=1, source_target_pairs={{0,24},{8,16},{16,8},{24,0},{32,56},{40,48},{48,40},{56,32},{64,88... | collective-permute-start | bytes 786440 | tf_op jit(solution)/shard_map/t_other_diagonal/ppermute | solution.py:43
  43.7 32.1 %copy-start.7 = (bf16[2,64,2048]{2,1,0:T(8,128)(2,1)}, bf16[2,64,2048]{2,1,0:T(8,128)(2,1)S(1)}, u32[]{:S(2)}) copy-start(bf16[2,64,2048]{2,1,0:T(8,128)(2,1)S(1)} %collective-permute-done.4) | copy-start | bytes 1572868
  43.7 32.2 %copy-start.8 = (bf16[2,64,2048]{2,1,0:T(8,128)(2,1)}, bf16[2,64,2048]{2,1,0:T(8,128)(2,1)S(1)}, u32[]{:S(2)}) copy-start(bf16[2,64,2048]{2,1,0:T(8,128)(2,1)S(1)} %collective-permute-done.5) | copy-start | bytes 1572868
  43.8 32.1 %copy-start.4 = (bf16[1,2,64,2048]{3,2,1,0:T(8,128)(2,1)}, bf16[1,2,64,2048]{3,2,1,0:T(8,128)(2,1)S(1)}, u32[]{:S(2)}) copy-start(bf16[1,2,64,2048]{3,2,1,0:T(8,128)(2,1)S(1)} %get-tuple-element.59.refs_4_) | copy-start | bytes 1572868
  43.8 17.9 %collective-permute-start.9 = (bf16[2,64,2048]{2,1,0:T(8,128)(2,1)S(1)}, bf16[2,64,2048]{2,1,0:T(8,128)(2,1)S(1)}, u32[]{:S(2)}, u32[]{:S(2)}) collective-permute-start(bf16[2,64,2048]{2,1,0:T(8,128)(2,1)S(1)} %get-tuple-element.41), channel_id=1, source_target_pairs={{0,6},{1,7},{2,0},{3,1},{4,2},{5,3},{6,4},{7,5},{8,14},{9,15},{10,... | collective-permute-start | bytes 1572872 | tf_op jit(solution)/shard_map/t_o_down/ppermute | solution.py:55
  46.8 14.9 %collective-permute-start.6 = (bf16[2,64,2048]{2,1,0:T(8,128)(2,1)S(1)}, bf16[2,64,2048]{2,1,0:T(8,128)(2,1)S(1)}, u32[]{:S(2)}, u32[]{:S(2)}) collective-permute-start(bf16[2,64,2048]{2,1,0:T(8,128)(2,1)S(1)} %collective-permute-done.5), channel_id=1, source_target_pairs={{0,2},{1,3},{2,4},{3,5},{4,6},{5,7},{6,0},{7,1},{8,10},{9,11},{10,... | collective-permute-start | bytes 1572872 | tf_op jit(solution)/shard_map/t_n_far/ppermute | solution.py:51
  46.9 28.9 %collective-permute-start.14 = (bf16[2,2,64,2048]{3,2,1,0:T(8,128)(2,1)S(1)}, bf16[2,2,64,2048]{3,2,1,0:T(8,128)(2,1)S(1)}, u32[]{:S(2)}, u32[]{:S(2)}) collective-permute-start(bf16[2,2,64,2048]{3,2,1,0:T(8,128)(2,1)S(1)} %pad_maximum_fusion), channel_id=1, source_target_pairs={{0,1},{1,0},{2,3},{3,2},{4,5},{5,4},{6,7},{7,6},{8,9},{9,8},{10,11... | collective-permute-start | bytes 3145736 | tf_op jit(solution)/shard_map/t_pair/ppermute | solution.py:47
  61.7 15.5 %copy-start.10 = (bf16[2,64,2048]{2,1,0:T(8,128)(2,1)}, bf16[2,64,2048]{2,1,0:T(8,128)(2,1)S(1)}, u32[]{:S(2)}) copy-start(bf16[2,64,2048]{2,1,0:T(8,128)(2,1)S(1)} %collective-permute-done.6) | copy-start | bytes 1572868
  61.7 14.2 %copy-start.9 = (bf16[2,64,2048]{2,1,0:T(8,128)(2,1)}, bf16[2,64,2048]{2,1,0:T(8,128)(2,1)S(1)}, u32[]{:S(2)}) copy-start(bf16[2,64,2048]{2,1,0:T(8,128)(2,1)S(1)} %collective-permute-done.9) | copy-start | bytes 1572868
  61.7 14.1 %collective-permute-start.11 = (bf16[2,64,2048]{2,1,0:T(8,128)(2,1)S(1)}, bf16[2,64,2048]{2,1,0:T(8,128)(2,1)S(1)}, u32[]{:S(2)}, u32[]{:S(2)}) collective-permute-start(bf16[2,64,2048]{2,1,0:T(8,128)(2,1)S(1)} %get-tuple-element.41), channel_id=1, source_target_pairs={{0,2},{1,3},{2,4},{3,5},{4,6},{5,7},{6,0},{7,1},{8,10},{9,11},{10,... | collective-permute-start | bytes 1572872 | tf_op jit(solution)/shard_map/t_o_up/ppermute | solution.py:51
  61.8 14.0 %collective-permute-start.10 = (bf16[2,64,2048]{2,1,0:T(8,128)(2,1)S(1)}, bf16[2,64,2048]{2,1,0:T(8,128)(2,1)S(1)}, u32[]{:S(2)}, u32[]{:S(2)}) collective-permute-start(bf16[2,64,2048]{2,1,0:T(8,128)(2,1)S(1)} %collective-permute-done.9), channel_id=1, source_target_pairs={{0,6},{1,7},{2,0},{3,1},{4,2},{5,3},{6,4},{7,5},{8,14},{9,15},{10,... | collective-permute-start | bytes 1572872 | tf_op jit(solution)/shard_map/t_o_far/ppermute | solution.py:55
  75.8 1.4 copy-start.11
  75.8 1.4 copy-start.12
  75.8 13.3 %copy-start.2 = (bf16[2,2,64,2048]{3,2,1,0:T(8,128)(2,1)}, bf16[2,2,64,2048]{3,2,1,0:T(8,128)(2,1)S(1)}, u32[]{:S(2)}) copy-start(bf16[2,2,64,2048]{3,2,1,0:T(8,128)(2,1)S(1)} %collective-permute-done.14.refs_8_.refs_12_.refs_0_.refs_4_) | copy-start | bytes 3145732
  75.8 24.5 %collective-permute-start.16 = (bf16[2,2,64,2048]{3,2,1,0:T(8,128)(2,1)S(1)}, bf16[2,2,64,2048]{3,2,1,0:T(8,128)(2,1)S(1)}, u32[]{:S(2)}, u32[]{:S(2)}) collective-permute-start(bf16[2,2,64,2048]{3,2,1,0:T(8,128)(2,1)S(1)} %collective-permute-done.14.refs_8_.refs_12_.refs_0_.refs_4_), channel_id=1, source_target_pairs={{0,2},{1,3},{2,4},{3,5},{4,6},{5,7},{6,0},{7,1},{8,10},{9,11},{10,... | collective-permute-start | bytes 3145736 | tf_op jit(solution)/shard_map/t_f_up/ppermute | solution.py:51
  76.0 25.0 %collective-permute-start.20 = (bf16[1024,512]{1,0:T(8,128)(2,1)}, bf16[1024,512]{1,0:T(8,128)(2,1)}, u32[]{:S(2)}, u32[]{:S(2)}) collective-permute-start(bf16[1024,512]{1,0:T(8,128)(2,1)} %get-tuple-element.47.refs_16_), channel_id=1, source_target_pairs={{0,16},{8,24},{16,0},{24,8},{32,48},{40,56},{48,32},{56,40},{64,80... | collective-permute-start | bytes 3145736 | tf_op jit(solution)/shard_map/t_out_across/ppermute | solution.py:39
  77.2 26.2 %collective-permute-start.15 = (bf16[2,2,64,2048]{3,2,1,0:T(8,128)(2,1)S(1)}, bf16[2,2,64,2048]{3,2,1,0:T(8,128)(2,1)S(1)}, u32[]{:S(2)}, u32[]{:S(2)}) collective-permute-start(bf16[2,2,64,2048]{3,2,1,0:T(8,128)(2,1)S(1)} %collective-permute-done.14.refs_8_.refs_12_.refs_0_.refs_4_), channel_id=1, source_target_pairs={{0,6},{1,7},{2,0},{3,1},{4,2},{5,3},{6,4},{7,5},{8,14},{9,15},{10,... | collective-permute-start | bytes 3145736 | tf_op jit(solution)/shard_map/t_f_down/ppermute | solution.py:55
  89.2 17.0 %collective-permute-start.12 = (bf16[2,256,1024]{2,1,0:T(8,128)(2,1)}, bf16[2,256,1024]{2,1,0:T(8,128)(2,1)S(1)}, u32[]{:S(2)}, u32[]{:S(2)}) collective-permute-start(bf16[2,256,1024]{2,1,0:T(8,128)(2,1)} %get-tuple-element.43), channel_id=1, source_target_pairs={{0,8},{8,0},{16,24},{24,16},{32,40},{40,32},{48,56},{56,48},{64,72... | collective-permute-start | bytes 3145736 | tf_op jit(solution)/shard_map/t_sum_same_sibling/ppermute | solution.py:35
  90.1 20.1 %collective-permute-start.19 = (bf16[1024,512]{1,0:T(8,128)(2,1)}, bf16[1024,512]{1,0:T(8,128)(2,1)S(1)}, u32[]{:S(2)}, u32[]{:S(2)}) collective-permute-start(bf16[1024,512]{1,0:T(8,128)(2,1)} %get-tuple-element.47.refs_16_), channel_id=1, source_target_pairs={{0,8},{8,0},{16,24},{24,16},{32,40},{40,32},{48,56},{56,48},{64,72... | collective-permute-start | bytes 3145736 | tf_op jit(solution)/shard_map/t_out_near/ppermute | solution.py:35
  100.3 16.7 %copy-start = (bf16[2,2,64,2048]{3,2,1,0:T(8,128)(2,1)}, bf16[2,2,64,2048]{3,2,1,0:T(8,128)(2,1)S(1)}, u32[]{:S(2)}) copy-start(bf16[2,2,64,2048]{3,2,1,0:T(8,128)(2,1)S(1)} %collective-permute-done.16.refs_11_.refs_15_.refs_3_.refs_7_) | copy-start | bytes 3145732
  100.4 12.3 %collective-permute-start.17 = (bf16[2,64,2048]{2,1,0:T(8,128)(2,1)S(1)}, bf16[2,64,2048]{2,1,0:T(8,128)(2,1)S(1)}, u32[]{:S(2)}, u32[]{:S(2)}) collective-permute-start(bf16[2,64,2048]{2,1,0:T(8,128)(2,1)S(1)} %slice_bitcast_fusion.2), channel_id=1, source_target_pairs={{0,2},{1,3},{2,4},{3,5},{4,6},{5,7},{6,0},{7,1},{8,10},{9,11},{10,... | collective-permute-start | bytes 1572872 | tf_op jit(solution)/shard_map/t_f_far_up/ppermute | solution.py:51
  101.0 9.3 %collective-permute-start.21 = (bf16[1024,512]{1,0:T(8,128)(2,1)}, bf16[1024,512]{1,0:T(8,128)(2,1)S(1)}, u32[]{:S(2)}, u32[]{:S(2)}) collective-permute-start(bf16[1024,512]{1,0:T(8,128)(2,1)} %collective-permute-done.20.refs_18_), channel_id=1, source_target_pairs={{0,8},{8,0},{16,24},{24,16},{32,40},{40,32},{48,56},{56,48},{64,72... | collective-permute-start | bytes 3145736 | tf_op jit(solution)/shard_map/t_out_other/ppermute | solution.py:35
  103.4 13.6 %copy-start.1 = (bf16[2,2,64,2048]{3,2,1,0:T(8,128)(2,1)}, bf16[2,2,64,2048]{3,2,1,0:T(8,128)(2,1)S(1)}, u32[]{:S(2)}) copy-start(bf16[2,2,64,2048]{3,2,1,0:T(8,128)(2,1)S(1)} %collective-permute-done.15.refs_9_.refs_13_.refs_1_.refs_5_) | copy-start | bytes 3145732
  103.5 13.5 %collective-permute-start.18 = (bf16[2,64,2048]{2,1,0:T(8,128)(2,1)S(1)}, bf16[2,64,2048]{2,1,0:T(8,128)(2,1)S(1)}, u32[]{:S(2)}, u32[]{:S(2)}) collective-permute-start(bf16[2,64,2048]{2,1,0:T(8,128)(2,1)S(1)} %slice_bitcast_fusion.1), channel_id=1, source_target_pairs={{0,6},{1,7},{2,0},{3,1},{4,2},{5,3},{6,4},{7,5},{8,14},{9,15},{10,... | collective-permute-start | bytes 1572872 | tf_op jit(solution)/shard_map/t_f_far_down/ppermute | solution.py:55
  106.2 1.0 copy-start.5
  108.5 22.8 %collective-permute-start.13 = (bf16[256,1024]{1,0:T(8,128)(2,1)S(1)}, bf16[256,1024]{1,0:T(8,128)(2,1)}, u32[]{:S(2)}, u32[]{:S(2)}) collective-permute-start(bf16[256,1024]{1,0:T(8,128)(2,1)S(1)} %fusion.1), channel_id=1, source_target_pairs={{0,16},{8,24},{16,0},{24,8},{32,48},{40,56},{48,32},{56,40},{64,80... | collective-permute-start | bytes 1572872 | tf_op jit(solution)/shard_map/t_sum_same_across/ppermute | solution.py:39
  110.3 6.8 %copy-start.16 = (bf16[1024,512]{1,0:T(8,128)(2,1)}, bf16[1024,512]{1,0:T(8,128)(2,1)S(1)}, u32[]{:S(2)}) copy-start(bf16[1024,512]{1,0:T(8,128)(2,1)S(1)} %collective-permute-done.21.refs_19_) | copy-start | bytes 3145732
  110.3 6.8 %copy-start.15 = (bf16[1024,512]{1,0:T(8,128)(2,1)}, bf16[1024,512]{1,0:T(8,128)(2,1)S(1)}, u32[]{:S(2)}) copy-start(bf16[1024,512]{1,0:T(8,128)(2,1)S(1)} %collective-permute-done.19.refs_17_) | copy-start | bytes 3145732
  112.7 4.3 %copy-start.13 = (bf16[2,64,2048]{2,1,0:T(8,128)(2,1)}, bf16[2,64,2048]{2,1,0:T(8,128)(2,1)S(1)}, u32[]{:S(2)}) copy-start(bf16[2,64,2048]{2,1,0:T(8,128)(2,1)S(1)} %collective-permute-done.17) | copy-start | bytes 1572868
  117.0 0.8 copy-start.14
  140.3 3.8 %collective-permute-start.22 = (bf16[2,256,1024]{2,1,0:T(8,128)(2,1)}, bf16[2,256,1024]{2,1,0:T(8,128)(2,1)S(1)}, u32[]{:S(2)}, u32[]{:S(2)}) collective-permute-start(bf16[2,256,1024]{2,1,0:T(8,128)(2,1)} %get-tuple-element.52), channel_id=1, source_target_pairs={{0,8},{8,0},{16,24},{24,16},{32,40},{40,32},{48,56},{56,48},{64,72... | collective-permute-start | bytes 3145736 | tf_op jit(solution)/shard_map/t_sum_flip_sibling/ppermute | solution.py:35
  144.1 16.5 %copy-start.6 = (bf16[2,256,1024]{2,1,0:T(8,128)(2,1)}, bf16[2,256,1024]{2,1,0:T(8,128)(2,1)S(1)}, u32[]{:S(2)}) copy-start(bf16[2,256,1024]{2,1,0:T(8,128)(2,1)S(1)} %collective-permute-done.22.rest_4_) | copy-start | bytes 3145732
  145.9 14.7 %collective-permute-start.23 = (bf16[256,1024]{1,0:T(8,128)(2,1)S(1)}, bf16[256,1024]{1,0:T(8,128)(2,1)S(1)}, u32[]{:S(2)}, u32[]{:S(2)}) collective-permute-start(bf16[256,1024]{1,0:T(8,128)(2,1)S(1)} %fusion), channel_id=1, source_target_pairs={{0,16},{8,24},{16,0},{24,8},{32,48},{40,56},{48,32},{56,40},{64,80... | collective-permute-start | bytes 1572872 | tf_op jit(solution)/shard_map/t_sum_flip_across/ppermute | solution.py:39
  160.6 0.8 copy-start.17
Sparse Core Ops, SparseCore 0:
  9.7 51.6 all-gather.1
  131.5 49.3 reduce-scatter.1

commit v8 on v7

--- a/solution.py
+++ b/solution.py
@@ -28,6 +28,8 @@
 PAIR = by_tensor(lambda i: i ^ 1)
 Y_UP = by_tensor(lambda i: (i + 2) % 8)
 Y_DOWN = by_tensor(lambda i: (i - 2) % 8)
+Z_UP = by_dp(lambda i: (i + 4) % 16)
+Z_DOWN = by_dp(lambda i: (i - 4) % 16)
 Z_GROUPS = [[z * 4 + j for z in range(4)] for j in range(4)]
 
 
@@ -45,6 +47,14 @@
 
 def pair(x):
     return lax.ppermute(x, "tensor", PAIR)
+
+
+def z_up(x):
+    return lax.ppermute(x, "dp", Z_UP)
+
+
+def z_down(x):
+    return lax.ppermute(x, "dp", Z_DOWN)
 
 
 def y_up(x):
@@ -206,9 +216,14 @@
 
     for b in range(blocks):
         first, last = key_range(b)
-        rows = pl.ds(pl.multiple_of(lax.rem(b - y + 4, 4) * half, half), half)
-        same = terms[0][rows] + terms[1][0, rows].astype(F32) + terms[2][rows].astype(F32)
-        flip = terms[3][rows] + terms[4][0, rows].astype(F32) + terms[5][rows].astype(F32)
+        at = lax.rem(b - y + 4, 4)
+
+        def term(first, k):
+            rows = pl.ds(pl.multiple_of(k * half, half), half)
+            return terms[first][rows] + terms[first + 1][rows].astype(F32) + terms[first + 2][rows].astype(F32)
+
+        same = term(0, at)
+        flip = term(3, at)
         grad = jnp.concatenate([jnp.where(low == 0, same, flip), jnp.where(low == 0, flip, same)], axis=0).astype(BF16)
         grad = jnp.concatenate([grad[:, :HD], grad[:, HD:]], axis=0)
         q2 = two_heads(q, b)
@@ -233,7 +248,6 @@
     length, wide = q.shape
     pairs, blocks = wide // (2 * HD), length // HD
     two = pl.BlockSpec((length, 2 * HD), lambda i: (0, i))
-    half = pl.BlockSpec((length // 2, 2 * HD), lambda i: (0, i))
     return pl.pallas_call(
         backward_kernel,
         grid=(pairs,),
@@ -245,7 +259,7 @@
             pl.BlockSpec((1, 2 * blocks, 2 * HD), lambda i: (i, 0, 0)),
             whole(bias.shape),
         ]
-        + [half, pl.BlockSpec((1, length // 2, 2 * HD), lambda i: (0, 0, i)), half] * 2,
+        + [pl.BlockSpec((x.shape[0], 2 * HD), lambda i: (0, i)) for x in terms],
         out_specs=[two, whole(k.shape), whole(v.shape)],
         out_shape=[jax.ShapeDtypeStruct(x.shape, BF16) for x in (q, k, v)],
         scratch_shapes=[pltpu.VMEM((HD, length), BF16), pltpu.VMEM(k.shape, F32), pltpu.VMEM(v.shape, F32)],
@@ -255,51 +269,52 @@
     )(place, q, k, v, stats, bias, *terms)
 
 
-def partial_kernel(*refs):
-    pieces, (weight, keep_near, keep_other, give, x) = refs[:8], refs[8:]
+def partial_kernel(count, *refs):
+    pieces, (weight, keep_near, keep_other, give_near, give_other, x) = refs[:-6], refs[-6:]
     seq = pieces[0].shape[2]
-    half = 4 * seq
+    half = count * seq
 
     @pl.when(pl.program_id(0) == 0)
     def _():
         for p in range(2):
             for i in range(2):
-                for k in range(4):
+                for k in range(count):
                     at = (p * 2 + i) * half + k * seq
-                    x[at : at + seq] = pieces[p * 4 + k][0, i]
+                    x[at : at + seq] = pieces[p * count + k][0, i]
 
     w = jnp.concatenate([weight[j] for j in range(4)], axis=1)
-    for p, keep in enumerate((keep_near, keep_other)):
+    for p, (keep, give) in enumerate(((keep_near, give_near), (keep_other, give_other))):
         total = nt(x[p * 2 * half : (p + 1) * 2 * half], w)
         keep[...] = total[:half]
-        give[p] = total[half:].astype(BF16)
-
-
-def partial(pieces, weight):
+        give[...] = total[half:].astype(BF16)
+
+
+def partial(pieces, weight, us):
     _, _, seq, cols = pieces[0][0].shape
     heads = weight.shape[1]
     tile = heads // 2
-    out = pl.BlockSpec((4 * seq, tile), lambda i: (0, i))
-    shape = jax.ShapeDtypeStruct((4 * seq, heads), F32)
+    count = len(pieces) // 2
+    rows = count * seq
+    out = pl.BlockSpec((rows, tile), lambda i: (0, i))
 
     def spec(index):
         return pl.BlockSpec((1, 2, seq, cols), lambda i: (index, 0, 0, 0))
 
     return pl.pallas_call(
-        partial_kernel,
+        functools.partial(partial_kernel, count),
         grid=(2,),
         in_specs=[spec(index) for _, index in pieces] + [pl.BlockSpec((4, tile, cols // 4), lambda i: (0, i, 0))],
-        out_specs=[out, out, pl.BlockSpec((2, 4 * seq, tile), lambda i: (0, 0, i))],
-        out_shape=[shape, shape, jax.ShapeDtypeStruct((2, 4 * seq, heads), BF16)],
-        scratch_shapes=[pltpu.VMEM((16 * seq, cols), BF16)],
+        out_specs=[out] * 4,
+        out_shape=[jax.ShapeDtypeStruct((rows, heads), dtype) for dtype in (F32, F32, BF16, BF16)],
+        scratch_shapes=[pltpu.VMEM((4 * rows, cols), BF16)],
         compiler_params=params(),
-        cost_estimate=cost(9),
+        cost_estimate=cost(us),
         name="partial_grad",
     )(*[x for x, _ in pieces], weight)
 
 
-def wgrad_kernel(*refs):
-    same, flip, outs, (out, x) = refs[:8], refs[8:16], refs[16:20], refs[20:]
+def wgrad_kernel(place, *refs):
+    same, flip, outs, results, x = refs[:8], refs[8:16], refs[16:20], refs[20:25], refs[25]
     seq = same[0].shape[2]
     length = 8 * seq
     for p in range(2):
@@ -308,33 +323,49 @@
                 at = (p * 2 + i) * length + 2 * k * seq
                 x[at : at + seq] = same[p * 4 + k][0, i]
                 x[at + seq : at + 2 * seq] = flip[p * 4 + k][0, i]
+    up, down, ahead, behind, mine = results
+    rows = ahead.shape[0]
+    places = ((up.at[0], down.at[0]), (ahead, up.at[1]), (down.at[1], behind), (mine.at[:rows], mine.at[rows:]))
     tile = 256
-    for m in range(0, out.shape[1], tile):
+    for m in range(0, 2 * rows, tile):
         total = nn(outs[0][m : m + tile], x[:length])
         for r in range(1, 4):
             total += nn(outs[r][m : m + tile], x[r * length : (r + 1) * length])
-        out[0, m : m + tile] = total.astype(BF16)
-
-
-def wgrad(same, flip, outs):
+        total = total.astype(BF16)
+        for step, halves in enumerate(places):
+
+            @pl.when(pl.program_id(0) == step)
+            def _():
+                halves[m // rows][m % rows : m % rows + tile] = total
+
+
+def wgrad(place, same, flip, outs):
     _, _, seq, cols = same[0][0].shape
     heads = outs[0].shape[0]
     width = cols // 4
 
     def spec(index):
-        return pl.BlockSpec((1, 2, seq, width), lambda i: (index, 0, 0, i))
-
+        def at(i, place):
+            return index, 0, 0, lax.rem(place[4] + jnp.where(i == 0, 2, jnp.where(i == 1, 1, jnp.where(i == 2, 3, 0))), 4)
+
+        return pl.BlockSpec((1, 2, seq, width), at)
+
+    half = (heads // 2, width)
+    results = [(2, *half), (2, *half), half, half, (heads, width)]
     return pl.pallas_call(
         wgrad_kernel,
-        grid=(4,),
-        in_specs=[spec(index) for _, index in same + flip] + [whole(outs[0].shape)] * 4,
-        out_specs=pl.BlockSpec((1, heads, width), lambda i: (i, 0, 0)),
-        out_shape=jax.ShapeDtypeStruct((4, heads, width), BF16),
-        scratch_shapes=[pltpu.VMEM((32 * seq, width), BF16)],
+        grid_spec=pltpu.PrefetchScalarGridSpec(
+            num_scalar_prefetch=1,
+            grid=(4,),
+            in_specs=[spec(index) for _, index in same + flip] + [pl.BlockSpec(outs[0].shape, lambda i, place: (0, 0))] * 4,
+            out_specs=[pl.BlockSpec(r, lambda i, place, n=len(r): (0,) * n) for r in results],
+            scratch_shapes=[pltpu.VMEM((32 * seq, width), BF16)],
+        ),
+        out_shape=[jax.ShapeDtypeStruct(r, BF16) for r in results],
         compiler_params=params(),
-        cost_estimate=cost(16),
+        cost_estimate=cost(14),
         name="weight_grad",
-    )(*[x for x, _ in same + flip], *outs)
+    )(place, *[x for x, _ in same + flip], *outs)
 
 
 def named(name, fn, x):
@@ -350,7 +381,7 @@
     d = lax.axis_index("dp")
     t = lax.axis_index("tensor")
     y, low = t // 2, t % 2
-    place = jnp.stack([y, low, (d // 2) % 2, d % 2]).astype(jnp.int32)
+    place = jnp.stack([y, low, (d // 2) % 2, d % 2, d // 4]).astype(jnp.int32)
     query, key, value = query_states[0], key_states[0], value_states[0]
     heads, width = out_weight.shape
 
@@ -382,25 +413,37 @@
     o_up, o_far = named("o_up", y_up, after(o, n_far, o_down)), named("o_far", y_down, o_down)
     f = after(f, o_up, o_far)
     f_up, f_down = named("f_up", y_up, f), named("f_down", y_down, f)
-    f_far = [named("f_far_up", y_up, f_up[0]), named("f_far_down", y_down, f_down[1])]
     same = [(x[None], 0) for x in (n, n_down, n_far, n_up, o, o_down, o_far, o_up)]
+    def sums(name, pieces, us):
+        keep_near, keep_other, give_near, give_other = partial(pieces, weight, us)
+        given = named(name + "_sibling", sibling, give_other)
+        total = (keep_other + given.astype(F32)).astype(BF16)
+        return keep_near, give_near, given, named(name + "_across", across, total)
+
+    same_near, give_same, got_same, sent_same = sums("sum_same", same, 9)
+    f_far = [named("f_far_up", y_up, after(f_up, same_near)[0]), named("f_far_down", y_down, f_down[1])]
     flip = [x for p in range(2) for x in ((f, p), (f_down, p), (f_far[p][None], 0), (f_up, p))]
-
-    def sums(name, pieces):
-        keep_near, keep_other, give = partial(pieces, weight)
-        given = named(name + "_sibling", sibling, give)
-        total = (keep_other + given[1].astype(F32)).astype(BF16)
-        return keep_near, given, named(name + "_across", across, total)
-
-    terms_same = sums("sum_same", same)
-    out_near = named("out_near", sibling, after(attn_out, o_up, o_far))
-    out_other = named("out_other", sibling, after(out_across, o_up, o_far))
-    outs = (attn_out, out_near, out_across, after(out_other, terms_same[1]))
-    total = wgrad(same, flip, outs).reshape(4 * heads, width)
-    weight_grad = lax.psum_scatter(after(total, terms_same[2]), "dp", scatter_dimension=0, tiled=True, axis_index_groups=Z_GROUPS)
-    terms_flip = sums("sum_flip", [(after(f, total), 0), *flip[1:]])
-    dq, dk, dv = backward(place, query, key, value, stats, bias, [*terms_same, *terms_flip])
-    return (dq[None], dk[None], dv[None], weight_grad.astype(F32))
+    out_near = named("out_near", sibling, after(attn_out, same_near))
+    out_other = named("out_other", sibling, after(out_across, same_near))
+    outs = (attn_out, out_near, out_across, after(out_other, got_same))
+
+    up, down, ahead, behind, mine = wgrad(place, same, flip, outs)
+    from_below, from_above = named("wg_up", z_up, after(up, sent_same)), named("wg_down", z_down, after(down, sent_same))
+
+    def add(*xs):
+        return sum(x.astype(F32) for x in xs)
+
+    given_same = named("same_near", sibling, after(give_same, mine))
+    flip_near, give_flip, got_flip, sent_flip = sums("sum_flip", [(after(f, given_same), 0), *flip[1:]], 1)
+    given_flip = named("flip_near", sibling, give_flip)
+    from_below, from_above, _ = lax.optimization_barrier((from_below, from_above, got_flip))
+    ahead_sum = named("wg_ahead", z_up, add(ahead, from_below[0]).astype(BF16))
+    behind_sum = named("wg_behind", z_down, add(behind, from_above[0]).astype(BF16))
+    terms = [same_near, given_same, sent_same, flip_near, given_flip, sent_flip]
+    dq, dk, dv = backward(place, query, key, value, stats, bias, terms)
+    ahead_sum = after(ahead_sum, dq)
+    weight_grad = add(mine, jnp.concatenate([ahead_sum, from_below[1]]), jnp.concatenate([from_above[1], behind_sum]))
+    return (dq[None], dk[None], dv[None], weight_grad)
 
 
 def solution(mesh):

time: 191 us -> 190 us (level)
  waiting for transfers between devices: 71.1 us -> 57 us
  starting transfers between devices: 37.4 us -> 46.8 us
  Pallas kernels: 52.8 us -> 57.8 us
    ppermute x5, waiting for transfers between devices: 38.3 us -> 18.5 us  [y_up(): return lax.ppermute(x, 'tensor', Y_UP)]
    ppermute x0 -> x4, waiting for transfers between devices: none -> 11.6 us  [the longest x2 8.59 us: z_down(): return lax.ppermute(x, 'dp', Z_DOWN)]
    reduce_scatter x1 -> x0, waiting for transfers between devices: 10.3 us -> none  [shards(): lax.psum_scatter(after(total, terms_same[2]), 'dp', scatter_dimension=0,...]
    ppermute x0 -> x4, starting transfers between devices: none -> 6.17 us  [the longest x2 6.17 us: z_down(): return lax.ppermute(x, 'dp', Z_DOWN)]
    ppermute x2, waiting for transfers between devices: 0.01 us -> 5.89 us  [pair(): return lax.ppermute(x, 'tensor', PAIR)]
    pallas_call x3, Pallas kernels: 31.4 us -> 36.3 us  [the longest x1 18.4 us: wgrad(): pl.pallas_call(wgrad_kernel, grid_spec=pltpu.PrefetchScalarGridSpec(num_s...]
    ppermute x4, waiting for transfers between devices: 13.6 us -> 8.86 us  [across(): return lax.ppermute(x, 'dp', ACROSS)]
    ppermute x5, waiting for transfers between devices: 4.32 us -> 7.52 us  [y_down(): return lax.ppermute(x, 'tensor', Y_DOWN)]
  transfers between devices with their start and end apart: 26 -> 31, of which waited for: 11 -> 13; matrix products, arithmetic and copies ran while one was open for 5% -> 5% of each run, Pallas kernels for 28% -> 31%
where the time goes in v8:
time: 190 us; the launch traced here: 189 us
  Pallas kernels  57.8 us (30%)
  waiting for transfers between devices  57 us (30%)
  starting transfers between devices  46.8 us (25%)
  between operations  14.4 us (8%)
  other arithmetic  8.52 us (4%)
  local copies, waits for them, and re-layouts  4.82 us (3%)
    ppermute x5, waiting for transfers between devices, y_up(): return lax.ppermute(x, 'tensor', Y_UP)  18.5 us
    pallas_call x1, Pallas kernels, wgrad(): pl.pallas_call(wgrad_kernel, grid_spec=pltpu.PrefetchScalarGridSpec(num_s...  18.4 us
    pallas_call x2, Pallas kernels, partial(): pl.pallas_call(functools.partial(partial_kernel, count), grid=(2,), in_sp...  17.9 us
    ppermute x5, starting transfers between devices, y_down(): return lax.ppermute(x, 'tensor', Y_DOWN)  12.8 us
    pallas_call x1, Pallas kernels, backward(): pl.pallas_call(backward_kernel, grid=(pairs,), in_specs=[SMEM(), two, who...  9.35 us
    ppermute x4, starting transfers between devices, across(): return lax.ppermute(x, 'dp', ACROSS)  9 us
    ppermute x4, waiting for transfers between devices, across(): return lax.ppermute(x, 'dp', ACROSS)  8.86 us
    pallas_call x1, Pallas kernels, forward(): pl.pallas_call(forward_kernel, grid=(pairs,), in_specs=[SMEM(), whole(seg...  8.77 us
  transfers between devices with their start and end apart: 31, of which 13 were waited for; matrix products, arithmetic and copies ran while one was open for 5% of the time, Pallas kernels for 31%

profile of v8, /device:TPU:1, one launch (start us, length us, event | category | flops | bytes accessed | tf_op | source)
XLA Modules:
  0.0 189.4 jit_solution(16530808051882784853)
XLA Ops:
  7.2 0.0 all-gather.2.cloned.1.call-start
  7.2 0.7 all-gather.2.cloned.1.call-update
  7.9 2.1 %collective-permute-start = (s32[64]{0:T(128)}, s32[64]{0:T(128)S(1)}, u32[]{:S(2)}, u32[]{:S(2)}) collective-permute-start(s32[64]{0:T(128)} %bitcast.81), channel_id=1, source_target_pairs={{0,1},{1,0},{2,3},{3,2},{4,5},{5,4},{6,7},{7,6},{8,9},{9,8},{10,11... | collective-permute-start | bytes 776 | tf_op jit(solution)/shard_map/t_ids_pair/ppermute | solution.py:49
  10.0 0.6 stack.96.place
  10.6 1.3 broadcast_in_dim.50.segs
  12.0 3.4 %prep.1 = (bf16[64,2048]{1,0:T(8,128)(2,1)}, bf16[64,2048]{1,0:T(8,128)(2,1)}, bf16[64,2048]{1,0:T(8,128)(2,1)}, bf16[64,2048]{1,0:T(8,128)(2,1)}) custom-call(s32[5]{0:T(128)} %stack.96.place, f32[1,4]{1,0:T(1,128)} %margins.1, s32[64,128]{1,0:T(8,128)} %broadcast_in_dim.50.segs, bf16[64,8192]{1,0:T(8,128)(2,1)} %bitcast.72), custom_call_target="tpu_custom_call" | custom-call | bytes 9000000 | tf_op jit(solution)/shard_map/prep/pallas_call | solution.py:115
  15.4 1.0 collective-permute-start.3
  16.4 1.4 collective-permute-start.1
  17.8 1.1 collective-permute-done.1
  18.9 2.9 %collective-permute-start.2 = (s32[2,2,64]{2,1,0:T(2,128)S(1)}, s32[2,2,64]{2,1,0:T(2,128)S(1)}, u32[]{:S(2)}, u32[]{:S(2)}) collective-permute-start(s32[2,2,64]{2,1,0:T(2,128)S(1)} %add_select_fusion.2), channel_id=1, source_target_pairs={{0,4},{1,5},{2,6},{3,7},{4,0},{5,1},{6,2},{7,3},{8,12},{9,13},{10,... | collective-permute-start | bytes 3080 | tf_op jit(solution)/shard_map/t_ids_rest/ppermute | solution.py:399
  21.8 1.0 collective-permute-done.2
  22.9 1.1 pad_maximum_fusion.1
  23.9 2.8 %collective-permute-start.4 = (bf16[2,64,2048]{2,1,0:T(8,128)(2,1)S(1)}, bf16[2,64,2048]{2,1,0:T(8,128)(2,1)S(1)}, u32[]{:S(2)}, u32[]{:S(2)}) collective-permute-start(bf16[2,64,2048]{2,1,0:T(8,128)(2,1)S(1)} %get-tuple-element.86), channel_id=1, source_target_pairs={{0,6},{1,7},{2,0},{3,1},{4,2},{5,3},{6,4},{7,5},{8,14},{9,15},{10,... | collective-permute-start | bytes 1572872 | tf_op jit(solution)/shard_map/t_n_down/ppermute | solution.py:65
  26.7 2.5 %collective-permute-start.7 = (bf16[64,2048]{1,0:T(8,128)(2,1)}, bf16[64,2048]{1,0:T(8,128)(2,1)S(1)}, u32[]{:S(2)}, u32[]{:S(2)}) collective-permute-start(bf16[64,2048]{1,0:T(8,128)(2,1)} %get-tuple-element.50), channel_id=1, source_target_pairs={{0,16},{8,24},{16,0},{24,8},{32,48},{40,56},{48,32},{56,40},{64,80... | collective-permute-start | bytes 786440 | tf_op jit(solution)/shard_map/t_other_across/ppermute | solution.py:41
  29.2 3.3 %collective-permute-start.8 = (bf16[64,2048]{1,0:T(8,128)(2,1)}, bf16[64,2048]{1,0:T(8,128)(2,1)S(1)}, u32[]{:S(2)}, u32[]{:S(2)}) collective-permute-start(bf16[64,2048]{1,0:T(8,128)(2,1)} %get-tuple-element.53), channel_id=1, source_target_pairs={{0,24},{8,16},{16,8},{24,0},{32,56},{40,48},{48,40},{56,32},{64,88... | collective-permute-start | bytes 786440 | tf_op jit(solution)/shard_map/t_other_diagonal/ppermute | solution.py:45
  32.5 0.1 select_n.108
  32.6 0.8 broadcast_in_dim.49.segs
  33.4 8.8 %attend.1 = (bf16[1024,512]{1,0:T(8,128)(2,1)}, f32[4,8,256]{2,1,0:T(8,128)}, f32[4,384,128]{2,1,0:T(8,128)}) custom-call(s32[5]{0:T(128)} %stack.96.place, s32[512,128]{1,0:T(8,128)} %broadcast_in_dim.49.segs, bf16[512,1024]{1,0:T(8,128)(2,1)} %bitcast.54, bf16[512,128]{1,0:T(8,128)(2,1)} %bitcast.73, bf16[512,128]{1,0:T(8,128)(2,1)} %bitcast.75), custom_call_target="tpu_custom_call" | custom-call | bytes 27000000 | tf_op jit(solution)/shard_map/attend/pallas_call | solution.py:178
  42.3 0.2 collective-permute-done.8
  42.4 0.1 pad_maximum_fusion.2
  42.5 0.1 pad_maximum_fusion
  42.6 0.7 collective-permute-start.12
  43.3 0.3 collective-permute-start.6
  43.6 2.7 %collective-permute-start.9 = (bf16[2,64,2048]{2,1,0:T(8,128)(2,1)S(1)}, bf16[2,64,2048]{2,1,0:T(8,128)(2,1)S(1)}, u32[]{:S(2)}, u32[]{:S(2)}) collective-permute-start(bf16[2,64,2048]{2,1,0:T(8,128)(2,1)S(1)} %get-tuple-element.54), channel_id=1, source_target_pairs={{0,6},{1,7},{2,0},{3,1},{4,2},{5,3},{6,4},{7,5},{8,14},{9,15},{10,... | collective-permute-start | bytes 1572872 | tf_op jit(solution)/shard_map/t_o_down/ppermute | solution.py:65
  46.2 12.6 %collective-permute-done.6 = bf16[2,64,2048]{2,1,0:T(8,128)(2,1)S(1)} collective-permute-done((bf16[2,64,2048]{2,1,0:T(8,128)(2,1)S(1)}, bf16[2,64,2048]{2,1,0:T(8,128)(2,1)S(1)}, u32[]{:S(2)}, u32[]{:S(2)}) %collective-permute-start.6) | collective-permute-done | bytes 524320 | tf_op jit(solution)/shard_map/t_n_far/ppermute | solution.py:61
  58.8 0.7 collective-permute-start.11
  59.5 2.0 %collective-permute-start.10 = (bf16[2,64,2048]{2,1,0:T(8,128)(2,1)S(1)}, bf16[2,64,2048]{2,1,0:T(8,128)(2,1)S(1)}, u32[]{:S(2)}, u32[]{:S(2)}) collective-permute-start(bf16[2,64,2048]{2,1,0:T(8,128)(2,1)S(1)} %collective-permute-done.9), channel_id=1, source_target_pairs={{0,6},{1,7},{2,0},{3,1},{4,2},{5,3},{6,4},{7,5},{8,14},{9,15},{10,... | collective-permute-start | bytes 1572872 | tf_op jit(solution)/shard_map/t_o_far/ppermute | solution.py:65
  61.5 5.9 %collective-permute-done.12.refs_8_.refs_12_.refs_0_.refs_4_ = bf16[2,2,64,2048]{3,2,1,0:T(8,128)(2,1)S(1)} collective-permute-done((bf16[2,2,64,2048]{3,2,1,0:T(8,128)(2,1)S(1)}, bf16[2,2,64,2048]{3,2,1,0:T(8,128)(2,1)S(1)}, u32[]{:S(2)}, u32[]{:S(2)}) %collective-permute-start.12) | collective-permute-done | bytes 1048608 | tf_op jit(solution)/shard_map/t_pair/ppermute | solution.py:49
  67.4 3.2 %collective-permute-start.18 = (bf16[1024,512]{1,0:T(8,128)(2,1)}, bf16[1024,512]{1,0:T(8,128)(2,1)}, u32[]{:S(2)}, u32[]{:S(2)}) collective-permute-start(bf16[1024,512]{1,0:T(8,128)(2,1)} %get-tuple-element.60.refs_16_), channel_id=1, source_target_pairs={{0,16},{8,24},{16,0},{24,8},{32,48},{40,56},{48,32},{56,40},{64,80... | collective-permute-start | bytes 3145736 | tf_op jit(solution)/shard_map/t_out_across/ppermute | solution.py:41
  70.7 2.7 %collective-permute-done.11 = bf16[2,64,2048]{2,1,0:T(8,128)(2,1)S(1)} collective-permute-done((bf16[2,64,2048]{2,1,0:T(8,128)(2,1)S(1)}, bf16[2,64,2048]{2,1,0:T(8,128)(2,1)S(1)}, u32[]{:S(2)}, u32[]{:S(2)}) %collective-permute-start.11) | collective-permute-done | bytes 524320 | tf_op jit(solution)/shard_map/t_o_up/ppermute | solution.py:61
  73.4 2.3 %collective-permute-start.13 = (bf16[2,2,64,2048]{3,2,1,0:T(8,128)(2,1)S(1)}, bf16[2,2,64,2048]{3,2,1,0:T(8,128)(2,1)S(1)}, u32[]{:S(2)}, u32[]{:S(2)}) collective-permute-start(bf16[2,2,64,2048]{3,2,1,0:T(8,128)(2,1)S(1)} %collective-permute-done.12.refs_8_.refs_12_.refs_0_.refs_4_), channel_id=1, source_target_pairs={{0,6},{1,7},{2,0},{3,1},{4,2},{5,3},{6,4},{7,5},{8,14},{9,15},{10,... | collective-permute-start | bytes 3145736 | tf_op jit(solution)/shard_map/t_f_down/ppermute | solution.py:65
  75.7 0.1 collective-permute-start.14
  75.8 0.0 all-gather.2.cloned.1.call-done
  75.8 8.9 %partial_grad.2 = (f32[256,1024]{1,0:T(8,128)}, f32[256,1024]{1,0:T(8,128)}, bf16[256,1024]{1,0:T(8,128)(2,1)}, bf16[256,1024]{1,0:T(8,128)(2,1)}) custom-call(bf16[1,2,64,2048]{3,2,1,0:T(8,128)(2,1)} %copy-done.3, bf16[1,2,64,2048]{3,2,1,0:T(8,128)(2,1)} %bitcast.56, bf16[1,2,64,2048]{3,2,1,0:T(8,128)(2,1)} %bitcast.60, bf16[1,2,64,2048]{3,2,1,0:T(8,128)(2,1)} %bitcast.58, ...), custom_call_target="tpu_custom_call" | custom-call | bytes 27000000 | tf_op jit(solution)/shard_map/partial_grad/pallas_call | solution.py:303
  84.8 8.8 %collective-permute-done.18.refs_18_ = bf16[1024,512]{1,0:T(8,128)(2,1)} collective-permute-done((bf16[1024,512]{1,0:T(8,128)(2,1)}, bf16[1024,512]{1,0:T(8,128)(2,1)}, u32[]{:S(2)}, u32[]{:S(2)}) %collective-permute-start.18) | collective-permute-done | bytes 1048608 | tf_op jit(solution)/shard_map/t_out_across/ppermute | solution.py:41
  93.7 1.4 collective-permute-start.20
  95.1 0.5 collective-permute-start.19
  95.6 1.5 collective-permute-done.13.refs_9_.refs_13_.refs_1_.refs_5_
  97.2 3.1 %collective-permute-start.16 = (bf16[2,64,2048]{2,1,0:T(8,128)(2,1)S(1)}, bf16[2,64,2048]{2,1,0:T(8,128)(2,1)S(1)}, u32[]{:S(2)}, u32[]{:S(2)}) collective-permute-start(bf16[2,64,2048]{2,1,0:T(8,128)(2,1)S(1)} %slice_bitcast_fusion), channel_id=1, source_target_pairs={{0,6},{1,7},{2,0},{3,1},{4,2},{5,3},{6,4},{7,5},{8,14},{9,15},{10,... | collective-permute-start | bytes 1572872 | tf_op jit(solution)/shard_map/t_f_far_down/ppermute | solution.py:65
  100.3 0.1 collective-permute-start.15
  100.4 1.1 add_convert_fusion.1
  101.5 1.6 collective-permute-start.22
  103.1 6.0 %collective-permute-done.16 = bf16[2,64,2048]{2,1,0:T(8,128)(2,1)S(1)} collective-permute-done((bf16[2,64,2048]{2,1,0:T(8,128)(2,1)S(1)}, bf16[2,64,2048]{2,1,0:T(8,128)(2,1)S(1)}, u32[]{:S(2)}, u32[]{:S(2)}) %collective-permute-start.16) | collective-permute-done | bytes 524320 | tf_op jit(solution)/shard_map/t_f_far_down/ppermute | solution.py:65
  109.1 3.3 %collective-permute-done.15 = bf16[2,64,2048]{2,1,0:T(8,128)(2,1)S(1)} collective-permute-done((bf16[2,64,2048]{2,1,0:T(8,128)(2,1)S(1)}, bf16[2,64,2048]{2,1,0:T(8,128)(2,1)S(1)}, u32[]{:S(2)}, u32[]{:S(2)}) %collective-permute-start.15) | collective-permute-done | bytes 524320 | tf_op jit(solution)/shard_map/t_f_far_up/ppermute | solution.py:61
  112.4 0.8 copy-done.12
  113.2 18.4 %weight_grad.1 = (bf16[2,512,512]{2,1,0:T(8,128)(2,1)}, bf16[2,512,512]{2,1,0:T(8,128)(2,1)}, bf16[512,512]{1,0:T(8,128)(2,1)}, bf16[512,512]{1,0:T(8,128)(2,1)}, bf16[1024,512]{1,0:T(8,128)(2,1)}) custom-call(s32[5]{0:T(128)} %stack.96.place, bf16[1,2,64,2048]{3,2,1,0:T(8,128)(2,1)} %copy-done.3, bf16[1,2,64,2048]{3,2,1,0:T(8,128)(2,1)} %bitcast.57, ...), custom_call_target="tpu_custom_call" | custom-call | bytes 42000000 | tf_op jit(solution)/shard_map/weight_grad/pallas_call | solution.py:355
  131.6 3.6 %collective-permute-start.21 = (bf16[256,1024]{1,0:T(8,128)(2,1)S(1)}, bf16[256,1024]{1,0:T(8,128)(2,1)}, u32[]{:S(2)}, u32[]{:S(2)}) collective-permute-start(bf16[256,1024]{1,0:T(8,128)(2,1)S(1)} %copy-done.22), channel_id=1, source_target_pairs={{0,8},{8,0},{16,24},{24,16},{32,40},{40,32},{48,56},{56,48},{64,72... | collective-permute-start | bytes 1572872 | tf_op jit(solution)/shard_map/t_same_near/ppermute | solution.py:37
  135.3 3.5 %collective-permute-start.27 = (bf16[2,512,512]{2,1,0:T(8,128)(2,1)}, bf16[2,512,512]{2,1,0:T(8,128)(2,1)S(1)}, u32[]{:S(2)}, u32[]{:S(2)}) collective-permute-start(bf16[2,512,512]{2,1,0:T(8,128)(2,1)} %get-tuple-element.79), channel_id=1, source_target_pairs={{0,96},{8,104},{16,112},{24,120},{32,0},{40,8},{48,16},{56,24},{64... | collective-permute-start | bytes 3145736 | tf_op jit(solution)/shard_map/t_wg_down/ppermute | solution.py:57
  138.8 8.9 %partial_grad.3 = (f32[256,1024]{1,0:T(8,128)}, f32[256,1024]{1,0:T(8,128)}, bf16[256,1024]{1,0:T(8,128)(2,1)}, bf16[256,1024]{1,0:T(8,128)(2,1)}) custom-call(bf16[2,2,64,2048]{3,2,1,0:T(8,128)(2,1)} %copy-done.2, bf16[2,2,64,2048]{3,2,1,0:T(8,128)(2,1)} %copy-done, bf16[1,2,64,2048]{3,2,1,0:T(8,128)(2,1)} %bitcast.71, bf16[2,2,64,2048]{3,2,1,0:T(8,128)(2,1)} %copy-done.1, ...), custom_call_target="tpu_custom_call" | custom-call | bytes 3000000 | tf_op jit(solution)/shard_map/partial_grad/pallas_call | solution.py:303
  147.7 0.4 collective-permute-start.24
  148.2 0.1 collective-permute-start.23
  148.3 1.6 collective-permute-done.24
  149.9 1.4 add_convert_fusion
  151.3 1.7 collective-permute-start.25
  153.0 8.6 %collective-permute-done.27 = bf16[2,512,512]{2,1,0:T(8,128)(2,1)S(1)} collective-permute-done((bf16[2,512,512]{2,1,0:T(8,128)(2,1)}, bf16[2,512,512]{2,1,0:T(8,128)(2,1)S(1)}, u32[]{:S(2)}, u32[]{:S(2)}) %collective-permute-start.27) | collective-permute-done | bytes 1048608 | tf_op jit(solution)/shard_map/t_wg_down/ppermute | solution.py:57
  161.6 3.0 %collective-permute-done.26 = bf16[2,512,512]{2,1,0:T(8,128)(2,1)S(1)} collective-permute-done((bf16[2,512,512]{2,1,0:T(8,128)(2,1)}, bf16[2,512,512]{2,1,0:T(8,128)(2,1)S(1)}, u32[]{:S(2)}, u32[]{:S(2)}) %collective-permute-start.26) | collective-permute-done | bytes 1048608 | tf_op jit(solution)/shard_map/t_wg_up/ppermute | solution.py:53
  164.6 0.9 fusion.1
  165.5 0.9 fusion
  166.5 2.7 %collective-permute-start.29 = (bf16[512,512]{1,0:T(8,128)(2,1)}, bf16[512,512]{1,0:T(8,128)(2,1)}, u32[]{:S(2)}, u32[]{:S(2)}) collective-permute-start(bf16[512,512]{1,0:T(8,128)(2,1)} %fusion), channel_id=1, source_target_pairs={{0,96},{8,104},{16,112},{24,120},{32,0},{40,8},{48,16},{56,24},{64... | collective-permute-start | bytes 1572872 | tf_op jit(solution)/shard_map/t_wg_behind/ppermute | solution.py:57
  169.1 0.1 slice_bitcast_fusion.1
  169.2 0.8 copy-done.20
  170.1 0.1 copy-done.19
  170.2 9.3 %attend_grad.1 = (bf16[512,1024]{1,0:T(8,128)(2,1)}, bf16[512,128]{1,0:T(8,128)(2,1)}, bf16[512,128]{1,0:T(8,128)(2,1)}) custom-call(s32[5]{0:T(128)} %stack.96.place, bf16[512,1024]{1,0:T(8,128)(2,1)} %bitcast.55, bf16[512,128]{1,0:T(8,128)(2,1)} %bitcast.74, bf16[512,128]{1,0:T(8,128)(2,1)} %bitcast.76, f32[4,8,256]{2,1,0:T(8,128)} %get-tuple-element.44.stats, ...), custom_call_target="tpu_custom_call" | custom-call | bytes 27000000 | tf_op jit(solution)/shard_map/attend_grad/pallas_call | solution.py:251
  179.6 2.9 %convert_add_fusion = f32[1024,512]{1,0:T(8,128)} fusion(bf16[1024,512]{1,0:T(8,128)(2,1)S(1)} %copy-done.13, bf16[512,512]{1,0:T(8,128)(2,1)S(1)} %get-tuple-element.89, bf16[512,512]{1,0:T(8,128)(2,1)} %collective-permute-done.28, bf16[512,512]{1,0:T(8,128)(2,1)} %collective-permute-done.29, bf16[512,512]{1,0:T(8,128)(2,1)S(1)} %get-tuple-element.88), kind=kLoop, calls=%fused_computation | loop fusion | flops 5767168 | bytes 5242880 | tf_op jit(solution)/shard_map/add | solution.py:434
  (72 shorter events, 0.3 us)
Async XLA Ops:
  7.2 9.2 %copy-start.21 = (s32[1,64]{1,0:T(1,128)S(1)}, s32[1,64]{1,0:T(1,128)}, u32[]{:S(2)}) copy-start(s32[1,64]{1,0:T(1,128)} %param.10) | copy-start | bytes 772
  7.2 68.7 %all-gather.2.cloned.1.call-start = ((), (), s32[]{:S(2)}) async-start(), calls=%async_computation | async-start | bytes 5242880 | tf_op jit(solution)/shard_map/all_gather | solution.py:388
  7.9 7.5 %collective-permute-start = (s32[64]{0:T(128)}, s32[64]{0:T(128)S(1)}, u32[]{:S(2)}, u32[]{:S(2)}) collective-permute-start(s32[64]{0:T(128)} %bitcast.81), channel_id=1, source_target_pairs={{0,1},{1,0},{2,3},{3,2},{4,5},{5,4},{6,7},{7,6},{8,9},{9,8},{10,11... | collective-permute-start | bytes 776 | tf_op jit(solution)/shard_map/t_ids_pair/ppermute | solution.py:49
  15.4 7.5 %collective-permute-start.3 = (bf16[64,2048]{1,0:T(8,128)(2,1)}, bf16[64,2048]{1,0:T(8,128)(2,1)S(1)}, u32[]{:S(2)}, u32[]{:S(2)}) collective-permute-start(bf16[64,2048]{1,0:T(8,128)(2,1)} %get-tuple-element.48), channel_id=1, source_target_pairs={{0,8},{8,0},{16,24},{24,16},{32,40},{40,32},{48,56},{56,48},{64,72... | collective-permute-start | bytes 786440 | tf_op jit(solution)/shard_map/t_near_sibling/ppermute | solution.py:37
  16.4 2.5 %collective-permute-start.1 = (s32[2,64]{1,0:T(2,128)S(1)}, s32[2,64]{1,0:T(2,128)S(1)}, u32[]{:S(2)}, u32[]{:S(2)}) collective-permute-start(s32[2,64]{1,0:T(2,128)S(1)} %add_select_fusion.4), channel_id=1, source_target_pairs={{0,2},{1,3},{2,0},{3,1},{4,6},{5,7},{6,4},{7,5},{8,10},{9,11},{10,... | collective-permute-start | bytes 1544 | tf_op jit(solution)/shard_map/t_ids_next/ppermute | solution.py:397
  18.9 3.9 %collective-permute-start.2 = (s32[2,2,64]{2,1,0:T(2,128)S(1)}, s32[2,2,64]{2,1,0:T(2,128)S(1)}, u32[]{:S(2)}, u32[]{:S(2)}) collective-permute-start(s32[2,2,64]{2,1,0:T(2,128)S(1)} %add_select_fusion.2), channel_id=1, source_target_pairs={{0,4},{1,5},{2,6},{3,7},{4,0},{5,1},{6,2},{7,3},{8,12},{9,13},{10,... | collective-permute-start | bytes 3080 | tf_op jit(solution)/shard_map/t_ids_rest/ppermute | solution.py:399
  23.9 18.7 %copy-start.3 = (bf16[1,2,64,2048]{3,2,1,0:T(8,128)(2,1)}, bf16[1,2,64,2048]{3,2,1,0:T(8,128)(2,1)S(1)}, u32[]{:S(2)}) copy-start(bf16[1,2,64,2048]{3,2,1,0:T(8,128)(2,1)S(1)} %get-tuple-element.87.refs_0_) | copy-start | bytes 1572868
  23.9 18.3 %collective-permute-start.4 = (bf16[2,64,2048]{2,1,0:T(8,128)(2,1)S(1)}, bf16[2,64,2048]{2,1,0:T(8,128)(2,1)S(1)}, u32[]{:S(2)}, u32[]{:S(2)}) collective-permute-start(bf16[2,64,2048]{2,1,0:T(8,128)(2,1)S(1)} %get-tuple-element.86), channel_id=1, source_target_pairs={{0,6},{1,7},{2,0},{3,1},{4,2},{5,3},{6,4},{7,5},{8,14},{9,15},{10,... | collective-permute-start | bytes 1572872 | tf_op jit(solution)/shard_map/t_n_down/ppermute | solution.py:65
  26.7 15.5 %collective-permute-start.5 = (bf16[2,64,2048]{2,1,0:T(8,128)(2,1)S(1)}, bf16[2,64,2048]{2,1,0:T(8,128)(2,1)S(1)}, u32[]{:S(2)}, u32[]{:S(2)}) collective-permute-start(bf16[2,64,2048]{2,1,0:T(8,128)(2,1)S(1)} %get-tuple-element.86), channel_id=1, source_target_pairs={{0,2},{1,3},{2,4},{3,5},{4,6},{5,7},{6,0},{7,1},{8,10},{9,11},{10,... | collective-permute-start | bytes 1572872 | tf_op jit(solution)/shard_map/t_n_up/ppermute | solution.py:61
  26.7 15.5 %collective-permute-start.7 = (bf16[64,2048]{1,0:T(8,128)(2,1)}, bf16[64,2048]{1,0:T(8,128)(2,1)S(1)}, u32[]{:S(2)}, u32[]{:S(2)}) collective-permute-start(bf16[64,2048]{1,0:T(8,128)(2,1)} %get-tuple-element.50), channel_id=1, source_target_pairs={{0,16},{8,24},{16,0},{24,8},{32,48},{40,56},{48,32},{56,40},{64,80... | collective-permute-start | bytes 786440 | tf_op jit(solution)/shard_map/t_other_across/ppermute | solution.py:41
  29.2 13.2 %collective-permute-start.8 = (bf16[64,2048]{1,0:T(8,128)(2,1)}, bf16[64,2048]{1,0:T(8,128)(2,1)S(1)}, u32[]{:S(2)}, u32[]{:S(2)}) collective-permute-start(bf16[64,2048]{1,0:T(8,128)(2,1)} %get-tuple-element.53), channel_id=1, source_target_pairs={{0,24},{8,16},{16,8},{24,0},{32,56},{40,48},{48,40},{56,32},{64,88... | collective-permute-start | bytes 786440 | tf_op jit(solution)/shard_map/t_other_diagonal/ppermute | solution.py:45
  42.2 31.2 %copy-start.5 = (bf16[2,64,2048]{2,1,0:T(8,128)(2,1)}, bf16[2,64,2048]{2,1,0:T(8,128)(2,1)S(1)}, u32[]{:S(2)}) copy-start(bf16[2,64,2048]{2,1,0:T(8,128)(2,1)S(1)} %collective-permute-done.4) | copy-start | bytes 1572868
  42.2 31.2 %copy-start.6 = (bf16[2,64,2048]{2,1,0:T(8,128)(2,1)}, bf16[2,64,2048]{2,1,0:T(8,128)(2,1)S(1)}, u32[]{:S(2)}) copy-start(bf16[2,64,2048]{2,1,0:T(8,128)(2,1)S(1)} %collective-permute-done.5) | copy-start | bytes 1572868
  42.5 30.9 %copy-start.4 = (bf16[1,2,64,2048]{3,2,1,0:T(8,128)(2,1)}, bf16[1,2,64,2048]{3,2,1,0:T(8,128)(2,1)S(1)}, u32[]{:S(2)}) copy-start(bf16[1,2,64,2048]{3,2,1,0:T(8,128)(2,1)S(1)} %get-tuple-element.85.refs_4_) | copy-start | bytes 1572868
  42.6 24.8 %collective-permute-start.12 = (bf16[2,2,64,2048]{3,2,1,0:T(8,128)(2,1)S(1)}, bf16[2,2,64,2048]{3,2,1,0:T(8,128)(2,1)S(1)}, u32[]{:S(2)}, u32[]{:S(2)}) collective-permute-start(bf16[2,2,64,2048]{3,2,1,0:T(8,128)(2,1)S(1)} %pad_maximum_fusion), channel_id=1, source_target_pairs={{0,1},{1,0},{2,3},{3,2},{4,5},{5,4},{6,7},{7,6},{8,9},{9,8},{10,11... | collective-permute-start | bytes 3145736 | tf_op jit(solution)/shard_map/t_pair/ppermute | solution.py:49
  43.3 15.5 %collective-permute-start.6 = (bf16[2,64,2048]{2,1,0:T(8,128)(2,1)S(1)}, bf16[2,64,2048]{2,1,0:T(8,128)(2,1)S(1)}, u32[]{:S(2)}, u32[]{:S(2)}) collective-permute-start(bf16[2,64,2048]{2,1,0:T(8,128)(2,1)S(1)} %collective-permute-done.5), channel_id=1, source_target_pairs={{0,2},{1,3},{2,4},{3,5},{4,6},{5,7},{6,0},{7,1},{8,10},{9,11},{10,... | collective-permute-start | bytes 1572872 | tf_op jit(solution)/shard_map/t_n_far/ppermute | solution.py:61
  43.6 15.2 %collective-permute-start.9 = (bf16[2,64,2048]{2,1,0:T(8,128)(2,1)S(1)}, bf16[2,64,2048]{2,1,0:T(8,128)(2,1)S(1)}, u32[]{:S(2)}, u32[]{:S(2)}) collective-permute-start(bf16[2,64,2048]{2,1,0:T(8,128)(2,1)S(1)} %get-tuple-element.54), channel_id=1, source_target_pairs={{0,6},{1,7},{2,0},{3,1},{4,2},{5,3},{6,4},{7,5},{8,14},{9,15},{10,... | collective-permute-start | bytes 1572872 | tf_op jit(solution)/shard_map/t_o_down/ppermute | solution.py:65
  58.8 14.6 %copy-start.7 = (bf16[2,64,2048]{2,1,0:T(8,128)(2,1)}, bf16[2,64,2048]{2,1,0:T(8,128)(2,1)S(1)}, u32[]{:S(2)}) copy-start(bf16[2,64,2048]{2,1,0:T(8,128)(2,1)S(1)} %collective-permute-done.6) | copy-start | bytes 1572868
  58.8 16.9 %copy-start.8 = (bf16[2,64,2048]{2,1,0:T(8,128)(2,1)}, bf16[2,64,2048]{2,1,0:T(8,128)(2,1)S(1)}, u32[]{:S(2)}) copy-start(bf16[2,64,2048]{2,1,0:T(8,128)(2,1)S(1)} %collective-permute-done.9) | copy-start | bytes 1572868
  58.8 14.6 %collective-permute-start.11 = (bf16[2,64,2048]{2,1,0:T(8,128)(2,1)S(1)}, bf16[2,64,2048]{2,1,0:T(8,128)(2,1)S(1)}, u32[]{:S(2)}, u32[]{:S(2)}) collective-permute-start(bf16[2,64,2048]{2,1,0:T(8,128)(2,1)S(1)} %get-tuple-element.54), channel_id=1, source_target_pairs={{0,2},{1,3},{2,4},{3,5},{4,6},{5,7},{6,0},{7,1},{8,10},{9,11},{10,... | collective-permute-start | bytes 1572872 | tf_op jit(solution)/shard_map/t_o_up/ppermute | solution.py:61
  59.5 13.9 %collective-permute-start.10 = (bf16[2,64,2048]{2,1,0:T(8,128)(2,1)S(1)}, bf16[2,64,2048]{2,1,0:T(8,128)(2,1)S(1)}, u32[]{:S(2)}, u32[]{:S(2)}) collective-permute-start(bf16[2,64,2048]{2,1,0:T(8,128)(2,1)S(1)} %collective-permute-done.9), channel_id=1, source_target_pairs={{0,6},{1,7},{2,0},{3,1},{4,2},{5,3},{6,4},{7,5},{8,14},{9,15},{10,... | collective-permute-start | bytes 1572872 | tf_op jit(solution)/shard_map/t_o_far/ppermute | solution.py:65
  67.4 17.4 %copy-start.2 = (bf16[2,2,64,2048]{3,2,1,0:T(8,128)(2,1)}, bf16[2,2,64,2048]{3,2,1,0:T(8,128)(2,1)S(1)}, u32[]{:S(2)}) copy-start(bf16[2,2,64,2048]{3,2,1,0:T(8,128)(2,1)S(1)} %collective-permute-done.12.refs_8_.refs_12_.refs_0_.refs_4_) | copy-start | bytes 3145732
  67.4 26.2 %collective-permute-start.18 = (bf16[1024,512]{1,0:T(8,128)(2,1)}, bf16[1024,512]{1,0:T(8,128)(2,1)}, u32[]{:S(2)}, u32[]{:S(2)}) collective-permute-start(bf16[1024,512]{1,0:T(8,128)(2,1)} %get-tuple-element.60.refs_16_), channel_id=1, source_target_pairs={{0,16},{8,24},{16,0},{24,8},{32,48},{40,56},{48,32},{56,40},{64,80... | collective-permute-start | bytes 3145736 | tf_op jit(solution)/shard_map/t_out_across/ppermute | solution.py:41
  73.4 2.3 %copy-start.9 = (bf16[2,64,2048]{2,1,0:T(8,128)(2,1)}, bf16[2,64,2048]{2,1,0:T(8,128)(2,1)S(1)}, u32[]{:S(2)}) copy-start(bf16[2,64,2048]{2,1,0:T(8,128)(2,1)S(1)} %collective-permute-done.11) | copy-start | bytes 1572868
  73.4 2.3 %copy-start.10 = (bf16[2,64,2048]{2,1,0:T(8,128)(2,1)}, bf16[2,64,2048]{2,1,0:T(8,128)(2,1)S(1)}, u32[]{:S(2)}) copy-start(bf16[2,64,2048]{2,1,0:T(8,128)(2,1)S(1)} %collective-permute-done.10) | copy-start | bytes 1572868
  73.4 23.7 %collective-permute-start.13 = (bf16[2,2,64,2048]{3,2,1,0:T(8,128)(2,1)S(1)}, bf16[2,2,64,2048]{3,2,1,0:T(8,128)(2,1)S(1)}, u32[]{:S(2)}, u32[]{:S(2)}) collective-permute-start(bf16[2,2,64,2048]{3,2,1,0:T(8,128)(2,1)S(1)} %collective-permute-done.12.refs_8_.refs_12_.refs_0_.refs_4_), channel_id=1, source_target_pairs={{0,6},{1,7},{2,0},{3,1},{4,2},{5,3},{6,4},{7,5},{8,14},{9,15},{10,... | collective-permute-start | bytes 3145736 | tf_op jit(solution)/shard_map/t_f_down/ppermute | solution.py:65
  75.7 24.5 %collective-permute-start.14 = (bf16[2,2,64,2048]{3,2,1,0:T(8,128)(2,1)S(1)}, bf16[2,2,64,2048]{3,2,1,0:T(8,128)(2,1)S(1)}, u32[]{:S(2)}, u32[]{:S(2)}) collective-permute-start(bf16[2,2,64,2048]{3,2,1,0:T(8,128)(2,1)S(1)} %collective-permute-done.12.refs_8_.refs_12_.refs_0_.refs_4_), channel_id=1, source_target_pairs={{0,2},{1,3},{2,4},{3,5},{4,6},{5,7},{6,0},{7,1},{8,10},{9,11},{10,... | collective-permute-start | bytes 3145736 | tf_op jit(solution)/shard_map/t_f_up/ppermute | solution.py:61
  84.8 15.6 %copy-start.15 = (f32[256,1024]{1,0:T(8,128)S(1)}, f32[256,1024]{1,0:T(8,128)}, u32[]{:S(2)}) copy-start(f32[256,1024]{1,0:T(8,128)} %get-tuple-element.66) | copy-start | bytes 3145732
  93.7 6.7 %collective-permute-start.20 = (bf16[256,1024]{1,0:T(8,128)(2,1)}, bf16[256,1024]{1,0:T(8,128)(2,1)S(1)}, u32[]{:S(2)}, u32[]{:S(2)}) collective-permute-start(bf16[256,1024]{1,0:T(8,128)(2,1)} %get-tuple-element.62), channel_id=1, source_target_pairs={{0,8},{8,0},{16,24},{24,16},{32,40},{40,32},{48,56},{56,48},{64,72... | collective-permute-start | bytes 1572872 | tf_op jit(solution)/shard_map/t_sum_same_sibling/ppermute | solution.py:37
  95.1 17.3 %collective-permute-start.17 = (bf16[1024,512]{1,0:T(8,128)(2,1)}, bf16[1024,512]{1,0:T(8,128)(2,1)}, u32[]{:S(2)}, u32[]{:S(2)}) collective-permute-start(bf16[1024,512]{1,0:T(8,128)(2,1)} %get-tuple-element.60.refs_16_), channel_id=1, source_target_pairs={{0,8},{8,0},{16,24},{24,16},{32,40},{40,32},{48,56},{56,48},{64,72... | collective-permute-start | bytes 3145736 | tf_op jit(solution)/shard_map/t_out_near/ppermute | solution.py:37
  95.1 8.0 %collective-permute-start.19 = (bf16[1024,512]{1,0:T(8,128)(2,1)}, bf16[1024,512]{1,0:T(8,128)(2,1)S(1)}, u32[]{:S(2)}, u32[]{:S(2)}) collective-permute-start(bf16[1024,512]{1,0:T(8,128)(2,1)} %collective-permute-done.18.refs_18_), channel_id=1, source_target_pairs={{0,8},{8,0},{16,24},{24,16},{32,40},{40,32},{48,56},{56,48},{64,72... | collective-permute-start | bytes 3145736 | tf_op jit(solution)/shard_map/t_out_other/ppermute | solution.py:37
  97.1 4.4 %copy-start = (bf16[2,2,64,2048]{3,2,1,0:T(8,128)(2,1)}, bf16[2,2,64,2048]{3,2,1,0:T(8,128)(2,1)S(1)}, u32[]{:S(2)}) copy-start(bf16[2,2,64,2048]{3,2,1,0:T(8,128)(2,1)S(1)} %collective-permute-done.13.refs_9_.refs_13_.refs_1_.refs_5_) | copy-start | bytes 3145732
  97.2 11.9 %collective-permute-start.16 = (bf16[2,64,2048]{2,1,0:T(8,128)(2,1)S(1)}, bf16[2,64,2048]{2,1,0:T(8,128)(2,1)S(1)}, u32[]{:S(2)}, u32[]{:S(2)}) collective-permute-start(bf16[2,64,2048]{2,1,0:T(8,128)(2,1)S(1)} %slice_bitcast_fusion), channel_id=1, source_target_pairs={{0,6},{1,7},{2,0},{3,1},{4,2},{5,3},{6,4},{7,5},{8,14},{9,15},{10,... | collective-permute-start | bytes 1572872 | tf_op jit(solution)/shard_map/t_f_far_down/ppermute | solution.py:65
  100.3 12.1 %copy-start.1 = (bf16[2,2,64,2048]{3,2,1,0:T(8,128)(2,1)}, bf16[2,2,64,2048]{3,2,1,0:T(8,128)(2,1)S(1)}, u32[]{:S(2)}) copy-start(bf16[2,2,64,2048]{3,2,1,0:T(8,128)(2,1)S(1)} %collective-permute-done.14.refs_11_.refs_15_.refs_3_.refs_7_) | copy-start | bytes 3145732
  100.3 12.0 %collective-permute-start.15 = (bf16[2,64,2048]{2,1,0:T(8,128)(2,1)S(1)}, bf16[2,64,2048]{2,1,0:T(8,128)(2,1)S(1)}, u32[]{:S(2)}, u32[]{:S(2)}) collective-permute-start(bf16[2,64,2048]{2,1,0:T(8,128)(2,1)S(1)} %slice_bitcast_fusion.3), channel_id=1, source_target_pairs={{0,2},{1,3},{2,4},{3,5},{4,6},{5,7},{6,0},{7,1},{8,10},{9,11},{10,... | collective-permute-start | bytes 1572872 | tf_op jit(solution)/shard_map/t_f_far_up/ppermute | solution.py:61
  101.5 33.8 %collective-permute-start.22 = (bf16[256,1024]{1,0:T(8,128)(2,1)}, bf16[256,1024]{1,0:T(8,128)(2,1)S(1)}, u32[]{:S(2)}, u32[]{:S(2)}) collective-permute-start(bf16[256,1024]{1,0:T(8,128)(2,1)} %add_convert_fusion.1), channel_id=1, source_target_pairs={{0,16},{8,24},{16,0},{24,8},{32,48},{40,56},{48,32},{56,40},{64,80... | collective-permute-start | bytes 1572872 | tf_op jit(solution)/shard_map/t_sum_same_across/ppermute | solution.py:41
  103.1 9.2 %copy-start.14 = (bf16[1024,512]{1,0:T(8,128)(2,1)}, bf16[1024,512]{1,0:T(8,128)(2,1)S(1)}, u32[]{:S(2)}) copy-start(bf16[1024,512]{1,0:T(8,128)(2,1)S(1)} %collective-permute-done.19.refs_19_) | copy-start | bytes 3145732
  109.1 3.3 %copy-start.11 = (bf16[2,64,2048]{2,1,0:T(8,128)(2,1)}, bf16[2,64,2048]{2,1,0:T(8,128)(2,1)S(1)}, u32[]{:S(2)}) copy-start(bf16[2,64,2048]{2,1,0:T(8,128)(2,1)S(1)} %collective-permute-done.16) | copy-start | bytes 1572868
  112.4 0.8 copy-start.12
  113.2 18.4 %copy-start.22 = (bf16[256,1024]{1,0:T(8,128)(2,1)S(1)}, bf16[256,1024]{1,0:T(8,128)(2,1)}, u32[]{:S(2)}) copy-start(bf16[256,1024]{1,0:T(8,128)(2,1)} %get-tuple-element.65) | copy-start | bytes 1572868
  131.6 7.2 %collective-permute-start.21 = (bf16[256,1024]{1,0:T(8,128)(2,1)S(1)}, bf16[256,1024]{1,0:T(8,128)(2,1)}, u32[]{:S(2)}, u32[]{:S(2)}) collective-permute-start(bf16[256,1024]{1,0:T(8,128)(2,1)S(1)} %copy-done.22), channel_id=1, source_target_pairs={{0,8},{8,0},{16,24},{24,16},{32,40},{40,32},{48,56},{56,48},{64,72... | collective-permute-start | bytes 1572872 | tf_op jit(solution)/shard_map/t_same_near/ppermute | solution.py:37
  135.3 12.4 %copy-start.16 = (bf16[256,1024]{1,0:T(8,128)(2,1)}, bf16[256,1024]{1,0:T(8,128)(2,1)S(1)}, u32[]{:S(2)}) copy-start(bf16[256,1024]{1,0:T(8,128)(2,1)S(1)} %collective-permute-done.22.rest_2_) | copy-start | bytes 1572868
  135.3 26.3 %collective-permute-start.27 = (bf16[2,512,512]{2,1,0:T(8,128)(2,1)}, bf16[2,512,512]{2,1,0:T(8,128)(2,1)S(1)}, u32[]{:S(2)}, u32[]{:S(2)}) collective-permute-start(bf16[2,512,512]{2,1,0:T(8,128)(2,1)} %get-tuple-element.79), channel_id=1, source_target_pairs={{0,96},{8,104},{16,112},{24,120},{32,0},{40,8},{48,16},{56,24},{64... | collective-permute-start | bytes 3145736 | tf_op jit(solution)/shard_map/t_wg_down/ppermute | solution.py:57
  138.8 25.8 %collective-permute-start.26 = (bf16[2,512,512]{2,1,0:T(8,128)(2,1)}, bf16[2,512,512]{2,1,0:T(8,128)(2,1)S(1)}, u32[]{:S(2)}, u32[]{:S(2)}) collective-permute-start(bf16[2,512,512]{2,1,0:T(8,128)(2,1)} %get-tuple-element.77), channel_id=1, source_target_pairs={{0,32},{8,40},{16,48},{24,56},{32,64},{40,72},{48,80},{56,88},{64,... | collective-permute-start | bytes 3145736 | tf_op jit(solution)/shard_map/t_wg_up/ppermute | solution.py:53
  147.7 16.9 %copy-start.18 = (bf16[512,512]{1,0:T(8,128)(2,1)S(1)}, bf16[512,512]{1,0:T(8,128)(2,1)}, u32[]{:S(2)}) copy-start(bf16[512,512]{1,0:T(8,128)(2,1)} %get-tuple-element.75) | copy-start | bytes 1572868
  147.7 17.8 %copy-start.17 = (bf16[512,512]{1,0:T(8,128)(2,1)S(1)}, bf16[512,512]{1,0:T(8,128)(2,1)}, u32[]{:S(2)}) copy-start(bf16[512,512]{1,0:T(8,128)(2,1)} %get-tuple-element.83) | copy-start | bytes 1572868
  147.7 2.2 %collective-permute-start.24 = (bf16[256,1024]{1,0:T(8,128)(2,1)}, bf16[256,1024]{1,0:T(8,128)(2,1)S(1)}, u32[]{:S(2)}, u32[]{:S(2)}) collective-permute-start(bf16[256,1024]{1,0:T(8,128)(2,1)} %get-tuple-element.71), channel_id=1, source_target_pairs={{0,8},{8,0},{16,24},{24,16},{32,40},{40,32},{48,56},{56,48},{64,72... | collective-permute-start | bytes 1572872 | tf_op jit(solution)/shard_map/t_sum_flip_sibling/ppermute | solution.py:37
  148.2 21.0 %collective-permute-start.23 = (bf16[256,1024]{1,0:T(8,128)(2,1)}, bf16[256,1024]{1,0:T(8,128)(2,1)S(1)}, u32[]{:S(2)}, u32[]{:S(2)}) collective-permute-start(bf16[256,1024]{1,0:T(8,128)(2,1)} %get-tuple-element.69), channel_id=1, source_target_pairs={{0,8},{8,0},{16,24},{24,16},{32,40},{40,32},{48,56},{56,48},{64,72... | collective-permute-start | bytes 1572872 | tf_op jit(solution)/shard_map/t_flip_near/ppermute | solution.py:37
  151.3 17.9 %collective-permute-start.25 = (bf16[256,1024]{1,0:T(8,128)(2,1)S(1)}, bf16[256,1024]{1,0:T(8,128)(2,1)S(1)}, u32[]{:S(2)}, u32[]{:S(2)}) collective-permute-start(bf16[256,1024]{1,0:T(8,128)(2,1)S(1)} %add_convert_fusion), channel_id=1, source_target_pairs={{0,16},{8,24},{16,0},{24,8},{32,48},{40,56},{48,32},{56,40},{64,80... | collective-permute-start | bytes 1572872 | tf_op jit(solution)/shard_map/t_sum_flip_across/ppermute | solution.py:41
  165.5 14.1 %collective-permute-start.28 = (bf16[512,512]{1,0:T(8,128)(2,1)}, bf16[512,512]{1,0:T(8,128)(2,1)}, u32[]{:S(2)}, u32[]{:S(2)}) collective-permute-start(bf16[512,512]{1,0:T(8,128)(2,1)} %fusion.1), channel_id=1, source_target_pairs={{0,32},{8,40},{16,48},{24,56},{32,64},{40,72},{48,80},{56,88},{64,... | collective-permute-start | bytes 1572872 | tf_op jit(solution)/shard_map/t_wg_ahead/ppermute | solution.py:53
  166.5 13.1 %collective-permute-start.29 = (bf16[512,512]{1,0:T(8,128)(2,1)}, bf16[512,512]{1,0:T(8,128)(2,1)}, u32[]{:S(2)}, u32[]{:S(2)}) collective-permute-start(bf16[512,512]{1,0:T(8,128)(2,1)} %fusion), channel_id=1, source_target_pairs={{0,96},{8,104},{16,112},{24,120},{32,0},{40,8},{48,16},{56,24},{64... | collective-permute-start | bytes 1572872 | tf_op jit(solution)/shard_map/t_wg_behind/ppermute | solution.py:57
  169.2 1.0 copy-start.19
  169.2 0.9 copy-start.20
  170.2 9.4 %copy-start.13 = (bf16[1024,512]{1,0:T(8,128)(2,1)S(1)}, bf16[1024,512]{1,0:T(8,128)(2,1)}, u32[]{:S(2)}) copy-start(bf16[1024,512]{1,0:T(8,128)(2,1)} %get-tuple-element.64) | copy-start | bytes 3145732
Sparse Core Ops, SparseCore 0:
  9.7 51.6 all-gather.1

commit v9 on v8

--- a/solution.py
+++ b/solution.py
@@ -314,7 +314,7 @@
 
 
 def wgrad_kernel(place, *refs):
-    same, flip, outs, results, x = refs[:8], refs[8:16], refs[16:20], refs[20:25], refs[25]
+    same, flip, outs, results, (x, block) = refs[:8], refs[8:16], refs[16:20], refs[20:25], refs[25:]
     seq = same[0].shape[2]
     length = 8 * seq
     for p in range(2):
@@ -331,12 +331,13 @@
         total = nn(outs[0][m : m + tile], x[:length])
         for r in range(1, 4):
             total += nn(outs[r][m : m + tile], x[r * length : (r + 1) * length])
-        total = total.astype(BF16)
-        for step, halves in enumerate(places):
-
-            @pl.when(pl.program_id(0) == step)
-            def _():
-                halves[m // rows][m % rows : m % rows + tile] = total
+        block[m : m + tile] = total.astype(BF16)
+    for step, (first, second) in enumerate(places):
+
+        @pl.when(pl.program_id(0) == step)
+        def _():
+            first[...] = block[:rows]
+            second[...] = block[rows:]
 
 
 def wgrad(place, same, flip, outs):
@@ -359,7 +360,7 @@
             grid=(4,),
             in_specs=[spec(index) for _, index in same + flip] + [pl.BlockSpec(outs[0].shape, lambda i, place: (0, 0))] * 4,
             out_specs=[pl.BlockSpec(r, lambda i, place, n=len(r): (0,) * n) for r in results],
-            scratch_shapes=[pltpu.VMEM((32 * seq, width), BF16)],
+            scratch_shapes=[pltpu.VMEM((32 * seq, width), BF16), pltpu.VMEM((heads, width), BF16)],
         ),
         out_shape=[jax.ShapeDtypeStruct(r, BF16) for r in results],
         compiler_params=params(),

time: 190 us -> 188 us (0.989)
  Pallas kernels: 57.8 us -> 55.7 us
    pallas_call x1, Pallas kernels: 18.4 us -> 16.3 us  [wgrad(): pl.pallas_call(wgrad_kernel, grid_spec=pltpu.PrefetchScalarGridSpec(num_s...]
  transfers between devices with their start and end apart: 31 -> 31, of which waited for: 13 -> 13; matrix products, arithmetic and copies ran while one was open for 5% -> 5% of each run, Pallas kernels for 31% -> 30%
where the time goes in v9:
time: 188 us; the launch traced here: 187 us
  waiting for transfers between devices  57 us (30%)
  Pallas kernels  55.7 us (30%)
  starting transfers between devices  46.8 us (25%)
  between operations  14.4 us (8%)
  other arithmetic  8.52 us (5%)
  local copies, waits for them, and re-layouts  4.82 us (3%)
    ppermute x5, waiting for transfers between devices, y_up(): return lax.ppermute(x, 'tensor', Y_UP)  18.5 us
    pallas_call x2, Pallas kernels, partial(): pl.pallas_call(functools.partial(partial_kernel, count), grid=(2,), in_sp...  17.9 us
    pallas_call x1, Pallas kernels, wgrad(): pl.pallas_call(wgrad_kernel, grid_spec=pltpu.PrefetchScalarGridSpec(num_s...  16.3 us
    ppermute x5, starting transfers between devices, y_down(): return lax.ppermute(x, 'tensor', Y_DOWN)  12.8 us
    pallas_call x1, Pallas kernels, backward(): pl.pallas_call(backward_kernel, grid=(pairs,), in_specs=[SMEM(), two, who...  9.35 us
    ppermute x4, starting transfers between devices, across(): return lax.ppermute(x, 'dp', ACROSS)  9 us
    ppermute x4, waiting for transfers between devices, across(): return lax.ppermute(x, 'dp', ACROSS)  8.86 us
    pallas_call x1, Pallas kernels, forward(): pl.pallas_call(forward_kernel, grid=(pairs,), in_specs=[SMEM(), whole(seg...  8.77 us
  transfers between devices with their start and end apart: 31, of which 13 were waited for; matrix products, arithmetic and copies ran while one was open for 5% of the time, Pallas kernels for 30%

profile of v9, /device:TPU:1, one launch (start us, length us, event | category | flops | bytes accessed | tf_op | source)
XLA Modules:
  0.0 187.3 jit_solution(3270146063193637343)
XLA Ops:
  7.2 0.0 all-gather.2.cloned.1.call-start
  7.2 0.7 all-gather.2.cloned.1.call-update
  7.9 2.1 %collective-permute-start = (s32[64]{0:T(128)}, s32[64]{0:T(128)S(1)}, u32[]{:S(2)}, u32[]{:S(2)}) collective-permute-start(s32[64]{0:T(128)} %bitcast.81), channel_id=1, source_target_pairs={{0,1},{1,0},{2,3},{3,2},{4,5},{5,4},{6,7},{7,6},{8,9},{9,8},{10,11... | collective-permute-start | bytes 776 | tf_op jit(solution)/shard_map/t_ids_pair/ppermute | solution.py:49
  10.0 0.6 stack.96.place
  10.6 1.3 broadcast_in_dim.50.segs
  12.0 3.4 %prep.1 = (bf16[64,2048]{1,0:T(8,128)(2,1)}, bf16[64,2048]{1,0:T(8,128)(2,1)}, bf16[64,2048]{1,0:T(8,128)(2,1)}, bf16[64,2048]{1,0:T(8,128)(2,1)}) custom-call(s32[5]{0:T(128)} %stack.96.place, f32[1,4]{1,0:T(1,128)} %margins.1, s32[64,128]{1,0:T(8,128)} %broadcast_in_dim.50.segs, bf16[64,8192]{1,0:T(8,128)(2,1)} %bitcast.72), custom_call_target="tpu_custom_call" | custom-call | bytes 9000000 | tf_op jit(solution)/shard_map/prep/pallas_call | solution.py:115
  15.4 1.0 collective-permute-start.3
  16.4 1.4 collective-permute-start.1
  17.8 1.1 collective-permute-done.1
  18.9 2.9 %collective-permute-start.2 = (s32[2,2,64]{2,1,0:T(2,128)S(1)}, s32[2,2,64]{2,1,0:T(2,128)S(1)}, u32[]{:S(2)}, u32[]{:S(2)}) collective-permute-start(s32[2,2,64]{2,1,0:T(2,128)S(1)} %add_select_fusion.2), channel_id=1, source_target_pairs={{0,4},{1,5},{2,6},{3,7},{4,0},{5,1},{6,2},{7,3},{8,12},{9,13},{10,... | collective-permute-start | bytes 3080 | tf_op jit(solution)/shard_map/t_ids_rest/ppermute | solution.py:400
  21.8 1.0 collective-permute-done.2
  22.9 1.1 pad_maximum_fusion.1
  23.9 2.8 %collective-permute-start.4 = (bf16[2,64,2048]{2,1,0:T(8,128)(2,1)S(1)}, bf16[2,64,2048]{2,1,0:T(8,128)(2,1)S(1)}, u32[]{:S(2)}, u32[]{:S(2)}) collective-permute-start(bf16[2,64,2048]{2,1,0:T(8,128)(2,1)S(1)} %get-tuple-element.86), channel_id=1, source_target_pairs={{0,6},{1,7},{2,0},{3,1},{4,2},{5,3},{6,4},{7,5},{8,14},{9,15},{10,... | collective-permute-start | bytes 1572872 | tf_op jit(solution)/shard_map/t_n_down/ppermute | solution.py:65
  26.7 2.5 %collective-permute-start.7 = (bf16[64,2048]{1,0:T(8,128)(2,1)}, bf16[64,2048]{1,0:T(8,128)(2,1)S(1)}, u32[]{:S(2)}, u32[]{:S(2)}) collective-permute-start(bf16[64,2048]{1,0:T(8,128)(2,1)} %get-tuple-element.50), channel_id=1, source_target_pairs={{0,16},{8,24},{16,0},{24,8},{32,48},{40,56},{48,32},{56,40},{64,80... | collective-permute-start | bytes 786440 | tf_op jit(solution)/shard_map/t_other_across/ppermute | solution.py:41
  29.2 3.3 %collective-permute-start.8 = (bf16[64,2048]{1,0:T(8,128)(2,1)}, bf16[64,2048]{1,0:T(8,128)(2,1)S(1)}, u32[]{:S(2)}, u32[]{:S(2)}) collective-permute-start(bf16[64,2048]{1,0:T(8,128)(2,1)} %get-tuple-element.53), channel_id=1, source_target_pairs={{0,24},{8,16},{16,8},{24,0},{32,56},{40,48},{48,40},{56,32},{64,88... | collective-permute-start | bytes 786440 | tf_op jit(solution)/shard_map/t_other_diagonal/ppermute | solution.py:45
  32.5 0.1 select_n.108
  32.6 0.8 broadcast_in_dim.49.segs
  33.4 8.8 %attend.1 = (bf16[1024,512]{1,0:T(8,128)(2,1)}, f32[4,8,256]{2,1,0:T(8,128)}, f32[4,384,128]{2,1,0:T(8,128)}) custom-call(s32[5]{0:T(128)} %stack.96.place, s32[512,128]{1,0:T(8,128)} %broadcast_in_dim.49.segs, bf16[512,1024]{1,0:T(8,128)(2,1)} %bitcast.54, bf16[512,128]{1,0:T(8,128)(2,1)} %bitcast.73, bf16[512,128]{1,0:T(8,128)(2,1)} %bitcast.75), custom_call_target="tpu_custom_call" | custom-call | bytes 27000000 | tf_op jit(solution)/shard_map/attend/pallas_call | solution.py:178
  42.3 0.2 collective-permute-done.8
  42.4 0.1 pad_maximum_fusion.2
  42.5 0.1 pad_maximum_fusion
  42.6 0.7 collective-permute-start.12
  43.3 0.3 collective-permute-start.6
  43.6 2.7 %collective-permute-start.9 = (bf16[2,64,2048]{2,1,0:T(8,128)(2,1)S(1)}, bf16[2,64,2048]{2,1,0:T(8,128)(2,1)S(1)}, u32[]{:S(2)}, u32[]{:S(2)}) collective-permute-start(bf16[2,64,2048]{2,1,0:T(8,128)(2,1)S(1)} %get-tuple-element.54), channel_id=1, source_target_pairs={{0,6},{1,7},{2,0},{3,1},{4,2},{5,3},{6,4},{7,5},{8,14},{9,15},{10,... | collective-permute-start | bytes 1572872 | tf_op jit(solution)/shard_map/t_o_down/ppermute | solution.py:65
  46.2 12.6 %collective-permute-done.6 = bf16[2,64,2048]{2,1,0:T(8,128)(2,1)S(1)} collective-permute-done((bf16[2,64,2048]{2,1,0:T(8,128)(2,1)S(1)}, bf16[2,64,2048]{2,1,0:T(8,128)(2,1)S(1)}, u32[]{:S(2)}, u32[]{:S(2)}) %collective-permute-start.6) | collective-permute-done | bytes 524320 | tf_op jit(solution)/shard_map/t_n_far/ppermute | solution.py:61
  58.8 0.7 collective-permute-start.11
  59.5 2.0 %collective-permute-start.10 = (bf16[2,64,2048]{2,1,0:T(8,128)(2,1)S(1)}, bf16[2,64,2048]{2,1,0:T(8,128)(2,1)S(1)}, u32[]{:S(2)}, u32[]{:S(2)}) collective-permute-start(bf16[2,64,2048]{2,1,0:T(8,128)(2,1)S(1)} %collective-permute-done.9), channel_id=1, source_target_pairs={{0,6},{1,7},{2,0},{3,1},{4,2},{5,3},{6,4},{7,5},{8,14},{9,15},{10,... | collective-permute-start | bytes 1572872 | tf_op jit(solution)/shard_map/t_o_far/ppermute | solution.py:65
  61.5 5.9 %collective-permute-done.12.refs_8_.refs_12_.refs_0_.refs_4_ = bf16[2,2,64,2048]{3,2,1,0:T(8,128)(2,1)S(1)} collective-permute-done((bf16[2,2,64,2048]{3,2,1,0:T(8,128)(2,1)S(1)}, bf16[2,2,64,2048]{3,2,1,0:T(8,128)(2,1)S(1)}, u32[]{:S(2)}, u32[]{:S(2)}) %collective-permute-start.12) | collective-permute-done | bytes 1048608 | tf_op jit(solution)/shard_map/t_pair/ppermute | solution.py:49
  67.4 3.2 %collective-permute-start.18 = (bf16[1024,512]{1,0:T(8,128)(2,1)}, bf16[1024,512]{1,0:T(8,128)(2,1)}, u32[]{:S(2)}, u32[]{:S(2)}) collective-permute-start(bf16[1024,512]{1,0:T(8,128)(2,1)} %get-tuple-element.60.refs_16_), channel_id=1, source_target_pairs={{0,16},{8,24},{16,0},{24,8},{32,48},{40,56},{48,32},{56,40},{64,80... | collective-permute-start | bytes 3145736 | tf_op jit(solution)/shard_map/t_out_across/ppermute | solution.py:41
  70.7 2.7 %collective-permute-done.11 = bf16[2,64,2048]{2,1,0:T(8,128)(2,1)S(1)} collective-permute-done((bf16[2,64,2048]{2,1,0:T(8,128)(2,1)S(1)}, bf16[2,64,2048]{2,1,0:T(8,128)(2,1)S(1)}, u32[]{:S(2)}, u32[]{:S(2)}) %collective-permute-start.11) | collective-permute-done | bytes 524320 | tf_op jit(solution)/shard_map/t_o_up/ppermute | solution.py:61
  73.4 2.3 %collective-permute-start.13 = (bf16[2,2,64,2048]{3,2,1,0:T(8,128)(2,1)S(1)}, bf16[2,2,64,2048]{3,2,1,0:T(8,128)(2,1)S(1)}, u32[]{:S(2)}, u32[]{:S(2)}) collective-permute-start(bf16[2,2,64,2048]{3,2,1,0:T(8,128)(2,1)S(1)} %collective-permute-done.12.refs_8_.refs_12_.refs_0_.refs_4_), channel_id=1, source_target_pairs={{0,6},{1,7},{2,0},{3,1},{4,2},{5,3},{6,4},{7,5},{8,14},{9,15},{10,... | collective-permute-start | bytes 3145736 | tf_op jit(solution)/shard_map/t_f_down/ppermute | solution.py:65
  75.7 0.1 collective-permute-start.14
  75.8 0.0 all-gather.2.cloned.1.call-done
  75.8 8.9 %partial_grad.2 = (f32[256,1024]{1,0:T(8,128)}, f32[256,1024]{1,0:T(8,128)}, bf16[256,1024]{1,0:T(8,128)(2,1)}, bf16[256,1024]{1,0:T(8,128)(2,1)}) custom-call(bf16[1,2,64,2048]{3,2,1,0:T(8,128)(2,1)} %copy-done.3, bf16[1,2,64,2048]{3,2,1,0:T(8,128)(2,1)} %bitcast.56, bf16[1,2,64,2048]{3,2,1,0:T(8,128)(2,1)} %bitcast.60, bf16[1,2,64,2048]{3,2,1,0:T(8,128)(2,1)} %bitcast.58, ...), custom_call_target="tpu_custom_call" | custom-call | bytes 27000000 | tf_op jit(solution)/shard_map/partial_grad/pallas_call | solution.py:303
  84.8 8.8 %collective-permute-done.18.refs_18_ = bf16[1024,512]{1,0:T(8,128)(2,1)} collective-permute-done((bf16[1024,512]{1,0:T(8,128)(2,1)}, bf16[1024,512]{1,0:T(8,128)(2,1)}, u32[]{:S(2)}, u32[]{:S(2)}) %collective-permute-start.18) | collective-permute-done | bytes 1048608 | tf_op jit(solution)/shard_map/t_out_across/ppermute | solution.py:41
  93.7 1.4 collective-permute-start.20
  95.1 0.5 collective-permute-start.19
  95.6 1.5 collective-permute-done.13.refs_9_.refs_13_.refs_1_.refs_5_
  97.2 3.1 %collective-permute-start.16 = (bf16[2,64,2048]{2,1,0:T(8,128)(2,1)S(1)}, bf16[2,64,2048]{2,1,0:T(8,128)(2,1)S(1)}, u32[]{:S(2)}, u32[]{:S(2)}) collective-permute-start(bf16[2,64,2048]{2,1,0:T(8,128)(2,1)S(1)} %slice_bitcast_fusion), channel_id=1, source_target_pairs={{0,6},{1,7},{2,0},{3,1},{4,2},{5,3},{6,4},{7,5},{8,14},{9,15},{10,... | collective-permute-start | bytes 1572872 | tf_op jit(solution)/shard_map/t_f_far_down/ppermute | solution.py:65
  100.3 0.1 collective-permute-start.15
  100.4 1.1 add_convert_fusion.1
  101.5 1.6 collective-permute-start.22
  103.1 6.0 %collective-permute-done.16 = bf16[2,64,2048]{2,1,0:T(8,128)(2,1)S(1)} collective-permute-done((bf16[2,64,2048]{2,1,0:T(8,128)(2,1)S(1)}, bf16[2,64,2048]{2,1,0:T(8,128)(2,1)S(1)}, u32[]{:S(2)}, u32[]{:S(2)}) %collective-permute-start.16) | collective-permute-done | bytes 524320 | tf_op jit(solution)/shard_map/t_f_far_down/ppermute | solution.py:65
  109.1 3.3 %collective-permute-done.15 = bf16[2,64,2048]{2,1,0:T(8,128)(2,1)S(1)} collective-permute-done((bf16[2,64,2048]{2,1,0:T(8,128)(2,1)S(1)}, bf16[2,64,2048]{2,1,0:T(8,128)(2,1)S(1)}, u32[]{:S(2)}, u32[]{:S(2)}) %collective-permute-start.15) | collective-permute-done | bytes 524320 | tf_op jit(solution)/shard_map/t_f_far_up/ppermute | solution.py:61
  112.4 0.8 copy-done.12
  113.2 16.3 %weight_grad.1 = (bf16[2,512,512]{2,1,0:T(8,128)(2,1)}, bf16[2,512,512]{2,1,0:T(8,128)(2,1)}, bf16[512,512]{1,0:T(8,128)(2,1)}, bf16[512,512]{1,0:T(8,128)(2,1)}, bf16[1024,512]{1,0:T(8,128)(2,1)}) custom-call(s32[5]{0:T(128)} %stack.96.place, bf16[1,2,64,2048]{3,2,1,0:T(8,128)(2,1)} %copy-done.3, bf16[1,2,64,2048]{3,2,1,0:T(8,128)(2,1)} %bitcast.57, ...), custom_call_target="tpu_custom_call" | custom-call | bytes 42000000 | tf_op jit(solution)/shard_map/weight_grad/pallas_call | solution.py:356
  129.5 3.7 %collective-permute-start.21 = (bf16[256,1024]{1,0:T(8,128)(2,1)S(1)}, bf16[256,1024]{1,0:T(8,128)(2,1)}, u32[]{:S(2)}, u32[]{:S(2)}) collective-permute-start(bf16[256,1024]{1,0:T(8,128)(2,1)S(1)} %copy-done.22), channel_id=1, source_target_pairs={{0,8},{8,0},{16,24},{24,16},{32,40},{40,32},{48,56},{56,48},{64,72... | collective-permute-start | bytes 1572872 | tf_op jit(solution)/shard_map/t_same_near/ppermute | solution.py:37
  133.2 3.5 %collective-permute-start.27 = (bf16[2,512,512]{2,1,0:T(8,128)(2,1)}, bf16[2,512,512]{2,1,0:T(8,128)(2,1)S(1)}, u32[]{:S(2)}, u32[]{:S(2)}) collective-permute-start(bf16[2,512,512]{2,1,0:T(8,128)(2,1)} %get-tuple-element.79), channel_id=1, source_target_pairs={{0,96},{8,104},{16,112},{24,120},{32,0},{40,8},{48,16},{56,24},{64... | collective-permute-start | bytes 3145736 | tf_op jit(solution)/shard_map/t_wg_down/ppermute | solution.py:57
  136.7 8.9 %partial_grad.3 = (f32[256,1024]{1,0:T(8,128)}, f32[256,1024]{1,0:T(8,128)}, bf16[256,1024]{1,0:T(8,128)(2,1)}, bf16[256,1024]{1,0:T(8,128)(2,1)}) custom-call(bf16[2,2,64,2048]{3,2,1,0:T(8,128)(2,1)} %copy-done.2, bf16[2,2,64,2048]{3,2,1,0:T(8,128)(2,1)} %copy-done, bf16[1,2,64,2048]{3,2,1,0:T(8,128)(2,1)} %bitcast.71, bf16[2,2,64,2048]{3,2,1,0:T(8,128)(2,1)} %copy-done.1, ...), custom_call_target="tpu_custom_call" | custom-call | bytes 3000000 | tf_op jit(solution)/shard_map/partial_grad/pallas_call | solution.py:303
  145.6 0.4 collective-permute-start.24
  146.1 0.1 collective-permute-start.23
  146.2 1.6 collective-permute-done.24
  147.8 1.4 add_convert_fusion
  149.2 1.7 collective-permute-start.25
  150.9 8.6 %collective-permute-done.27 = bf16[2,512,512]{2,1,0:T(8,128)(2,1)S(1)} collective-permute-done((bf16[2,512,512]{2,1,0:T(8,128)(2,1)}, bf16[2,512,512]{2,1,0:T(8,128)(2,1)S(1)}, u32[]{:S(2)}, u32[]{:S(2)}) %collective-permute-start.27) | collective-permute-done | bytes 1048608 | tf_op jit(solution)/shard_map/t_wg_down/ppermute | solution.py:57
  159.5 3.0 %collective-permute-done.26 = bf16[2,512,512]{2,1,0:T(8,128)(2,1)S(1)} collective-permute-done((bf16[2,512,512]{2,1,0:T(8,128)(2,1)}, bf16[2,512,512]{2,1,0:T(8,128)(2,1)S(1)}, u32[]{:S(2)}, u32[]{:S(2)}) %collective-permute-start.26) | collective-permute-done | bytes 1048608 | tf_op jit(solution)/shard_map/t_wg_up/ppermute | solution.py:53
  162.5 0.9 fusion.1
  163.4 0.9 fusion
  164.3 2.7 %collective-permute-start.29 = (bf16[512,512]{1,0:T(8,128)(2,1)}, bf16[512,512]{1,0:T(8,128)(2,1)}, u32[]{:S(2)}, u32[]{:S(2)}) collective-permute-start(bf16[512,512]{1,0:T(8,128)(2,1)} %fusion), channel_id=1, source_target_pairs={{0,96},{8,104},{16,112},{24,120},{32,0},{40,8},{48,16},{56,24},{64... | collective-permute-start | bytes 1572872 | tf_op jit(solution)/shard_map/t_wg_behind/ppermute | solution.py:57
  167.0 0.1 slice_bitcast_fusion.1
  167.1 0.8 copy-done.20
  168.0 0.1 copy-done.19
  168.1 9.4 %attend_grad.1 = (bf16[512,1024]{1,0:T(8,128)(2,1)}, bf16[512,128]{1,0:T(8,128)(2,1)}, bf16[512,128]{1,0:T(8,128)(2,1)}) custom-call(s32[5]{0:T(128)} %stack.96.place, bf16[512,1024]{1,0:T(8,128)(2,1)} %bitcast.55, bf16[512,128]{1,0:T(8,128)(2,1)} %bitcast.74, bf16[512,128]{1,0:T(8,128)(2,1)} %bitcast.76, f32[4,8,256]{2,1,0:T(8,128)} %get-tuple-element.44.stats, ...), custom_call_target="tpu_custom_call" | custom-call | bytes 27000000 | tf_op jit(solution)/shard_map/attend_grad/pallas_call | solution.py:251
  177.5 2.9 %convert_add_fusion = f32[1024,512]{1,0:T(8,128)} fusion(bf16[1024,512]{1,0:T(8,128)(2,1)S(1)} %copy-done.13, bf16[512,512]{1,0:T(8,128)(2,1)S(1)} %get-tuple-element.89, bf16[512,512]{1,0:T(8,128)(2,1)} %collective-permute-done.28, bf16[512,512]{1,0:T(8,128)(2,1)} %collective-permute-done.29, bf16[512,512]{1,0:T(8,128)(2,1)S(1)} %get-tuple-element.88), kind=kLoop, calls=%fused_computation | loop fusion | flops 5767168 | bytes 5242880 | tf_op jit(solution)/shard_map/add | solution.py:435
  (72 shorter events, 0.3 us)
Async XLA Ops:
  7.2 9.2 %copy-start.21 = (s32[1,64]{1,0:T(1,128)S(1)}, s32[1,64]{1,0:T(1,128)}, u32[]{:S(2)}) copy-start(s32[1,64]{1,0:T(1,128)} %param.10) | copy-start | bytes 772
  7.2 68.7 %all-gather.2.cloned.1.call-start = ((), (), s32[]{:S(2)}) async-start(), calls=%async_computation | async-start | bytes 5242880 | tf_op jit(solution)/shard_map/all_gather | solution.py:389
  7.9 7.5 %collective-permute-start = (s32[64]{0:T(128)}, s32[64]{0:T(128)S(1)}, u32[]{:S(2)}, u32[]{:S(2)}) collective-permute-start(s32[64]{0:T(128)} %bitcast.81), channel_id=1, source_target_pairs={{0,1},{1,0},{2,3},{3,2},{4,5},{5,4},{6,7},{7,6},{8,9},{9,8},{10,11... | collective-permute-start | bytes 776 | tf_op jit(solution)/shard_map/t_ids_pair/ppermute | solution.py:49
  15.4 7.5 %collective-permute-start.3 = (bf16[64,2048]{1,0:T(8,128)(2,1)}, bf16[64,2048]{1,0:T(8,128)(2,1)S(1)}, u32[]{:S(2)}, u32[]{:S(2)}) collective-permute-start(bf16[64,2048]{1,0:T(8,128)(2,1)} %get-tuple-element.48), channel_id=1, source_target_pairs={{0,8},{8,0},{16,24},{24,16},{32,40},{40,32},{48,56},{56,48},{64,72... | collective-permute-start | bytes 786440 | tf_op jit(solution)/shard_map/t_near_sibling/ppermute | solution.py:37
  16.4 2.5 %collective-permute-start.1 = (s32[2,64]{1,0:T(2,128)S(1)}, s32[2,64]{1,0:T(2,128)S(1)}, u32[]{:S(2)}, u32[]{:S(2)}) collective-permute-start(s32[2,64]{1,0:T(2,128)S(1)} %add_select_fusion.4), channel_id=1, source_target_pairs={{0,2},{1,3},{2,0},{3,1},{4,6},{5,7},{6,4},{7,5},{8,10},{9,11},{10,... | collective-permute-start | bytes 1544 | tf_op jit(solution)/shard_map/t_ids_next/ppermute | solution.py:398
  18.9 3.9 %collective-permute-start.2 = (s32[2,2,64]{2,1,0:T(2,128)S(1)}, s32[2,2,64]{2,1,0:T(2,128)S(1)}, u32[]{:S(2)}, u32[]{:S(2)}) collective-permute-start(s32[2,2,64]{2,1,0:T(2,128)S(1)} %add_select_fusion.2), channel_id=1, source_target_pairs={{0,4},{1,5},{2,6},{3,7},{4,0},{5,1},{6,2},{7,3},{8,12},{9,13},{10,... | collective-permute-start | bytes 3080 | tf_op jit(solution)/shard_map/t_ids_rest/ppermute | solution.py:400
  23.9 18.7 %copy-start.3 = (bf16[1,2,64,2048]{3,2,1,0:T(8,128)(2,1)}, bf16[1,2,64,2048]{3,2,1,0:T(8,128)(2,1)S(1)}, u32[]{:S(2)}) copy-start(bf16[1,2,64,2048]{3,2,1,0:T(8,128)(2,1)S(1)} %get-tuple-element.87.refs_0_) | copy-start | bytes 1572868
  23.9 18.3 %collective-permute-start.4 = (bf16[2,64,2048]{2,1,0:T(8,128)(2,1)S(1)}, bf16[2,64,2048]{2,1,0:T(8,128)(2,1)S(1)}, u32[]{:S(2)}, u32[]{:S(2)}) collective-permute-start(bf16[2,64,2048]{2,1,0:T(8,128)(2,1)S(1)} %get-tuple-element.86), channel_id=1, source_target_pairs={{0,6},{1,7},{2,0},{3,1},{4,2},{5,3},{6,4},{7,5},{8,14},{9,15},{10,... | collective-permute-start | bytes 1572872 | tf_op jit(solution)/shard_map/t_n_down/ppermute | solution.py:65
  26.7 15.5 %collective-permute-start.5 = (bf16[2,64,2048]{2,1,0:T(8,128)(2,1)S(1)}, bf16[2,64,2048]{2,1,0:T(8,128)(2,1)S(1)}, u32[]{:S(2)}, u32[]{:S(2)}) collective-permute-start(bf16[2,64,2048]{2,1,0:T(8,128)(2,1)S(1)} %get-tuple-element.86), channel_id=1, source_target_pairs={{0,2},{1,3},{2,4},{3,5},{4,6},{5,7},{6,0},{7,1},{8,10},{9,11},{10,... | collective-permute-start | bytes 1572872 | tf_op jit(solution)/shard_map/t_n_up/ppermute | solution.py:61
  26.7 15.5 %collective-permute-start.7 = (bf16[64,2048]{1,0:T(8,128)(2,1)}, bf16[64,2048]{1,0:T(8,128)(2,1)S(1)}, u32[]{:S(2)}, u32[]{:S(2)}) collective-permute-start(bf16[64,2048]{1,0:T(8,128)(2,1)} %get-tuple-element.50), channel_id=1, source_target_pairs={{0,16},{8,24},{16,0},{24,8},{32,48},{40,56},{48,32},{56,40},{64,80... | collective-permute-start | bytes 786440 | tf_op jit(solution)/shard_map/t_other_across/ppermute | solution.py:41
  29.2 13.2 %collective-permute-start.8 = (bf16[64,2048]{1,0:T(8,128)(2,1)}, bf16[64,2048]{1,0:T(8,128)(2,1)S(1)}, u32[]{:S(2)}, u32[]{:S(2)}) collective-permute-start(bf16[64,2048]{1,0:T(8,128)(2,1)} %get-tuple-element.53), channel_id=1, source_target_pairs={{0,24},{8,16},{16,8},{24,0},{32,56},{40,48},{48,40},{56,32},{64,88... | collective-permute-start | bytes 786440 | tf_op jit(solution)/shard_map/t_other_diagonal/ppermute | solution.py:45
  42.2 31.2 %copy-start.5 = (bf16[2,64,2048]{2,1,0:T(8,128)(2,1)}, bf16[2,64,2048]{2,1,0:T(8,128)(2,1)S(1)}, u32[]{:S(2)}) copy-start(bf16[2,64,2048]{2,1,0:T(8,128)(2,1)S(1)} %collective-permute-done.4) | copy-start | bytes 1572868
  42.2 31.2 %copy-start.6 = (bf16[2,64,2048]{2,1,0:T(8,128)(2,1)}, bf16[2,64,2048]{2,1,0:T(8,128)(2,1)S(1)}, u32[]{:S(2)}) copy-start(bf16[2,64,2048]{2,1,0:T(8,128)(2,1)S(1)} %collective-permute-done.5) | copy-start | bytes 1572868
  42.5 30.9 %copy-start.4 = (bf16[1,2,64,2048]{3,2,1,0:T(8,128)(2,1)}, bf16[1,2,64,2048]{3,2,1,0:T(8,128)(2,1)S(1)}, u32[]{:S(2)}) copy-start(bf16[1,2,64,2048]{3,2,1,0:T(8,128)(2,1)S(1)} %get-tuple-element.85.refs_4_) | copy-start | bytes 1572868
  42.6 24.8 %collective-permute-start.12 = (bf16[2,2,64,2048]{3,2,1,0:T(8,128)(2,1)S(1)}, bf16[2,2,64,2048]{3,2,1,0:T(8,128)(2,1)S(1)}, u32[]{:S(2)}, u32[]{:S(2)}) collective-permute-start(bf16[2,2,64,2048]{3,2,1,0:T(8,128)(2,1)S(1)} %pad_maximum_fusion), channel_id=1, source_target_pairs={{0,1},{1,0},{2,3},{3,2},{4,5},{5,4},{6,7},{7,6},{8,9},{9,8},{10,11... | collective-permute-start | bytes 3145736 | tf_op jit(solution)/shard_map/t_pair/ppermute | solution.py:49
  43.3 15.5 %collective-permute-start.6 = (bf16[2,64,2048]{2,1,0:T(8,128)(2,1)S(1)}, bf16[2,64,2048]{2,1,0:T(8,128)(2,1)S(1)}, u32[]{:S(2)}, u32[]{:S(2)}) collective-permute-start(bf16[2,64,2048]{2,1,0:T(8,128)(2,1)S(1)} %collective-permute-done.5), channel_id=1, source_target_pairs={{0,2},{1,3},{2,4},{3,5},{4,6},{5,7},{6,0},{7,1},{8,10},{9,11},{10,... | collective-permute-start | bytes 1572872 | tf_op jit(solution)/shard_map/t_n_far/ppermute | solution.py:61
  43.6 15.2 %collective-permute-start.9 = (bf16[2,64,2048]{2,1,0:T(8,128)(2,1)S(1)}, bf16[2,64,2048]{2,1,0:T(8,128)(2,1)S(1)}, u32[]{:S(2)}, u32[]{:S(2)}) collective-permute-start(bf16[2,64,2048]{2,1,0:T(8,128)(2,1)S(1)} %get-tuple-element.54), channel_id=1, source_target_pairs={{0,6},{1,7},{2,0},{3,1},{4,2},{5,3},{6,4},{7,5},{8,14},{9,15},{10,... | collective-permute-start | bytes 1572872 | tf_op jit(solution)/shard_map/t_o_down/ppermute | solution.py:65
  58.8 14.6 %copy-start.7 = (bf16[2,64,2048]{2,1,0:T(8,128)(2,1)}, bf16[2,64,2048]{2,1,0:T(8,128)(2,1)S(1)}, u32[]{:S(2)}) copy-start(bf16[2,64,2048]{2,1,0:T(8,128)(2,1)S(1)} %collective-permute-done.6) | copy-start | bytes 1572868
  58.8 16.9 %copy-start.8 = (bf16[2,64,2048]{2,1,0:T(8,128)(2,1)}, bf16[2,64,2048]{2,1,0:T(8,128)(2,1)S(1)}, u32[]{:S(2)}) copy-start(bf16[2,64,2048]{2,1,0:T(8,128)(2,1)S(1)} %collective-permute-done.9) | copy-start | bytes 1572868
  58.8 14.6 %collective-permute-start.11 = (bf16[2,64,2048]{2,1,0:T(8,128)(2,1)S(1)}, bf16[2,64,2048]{2,1,0:T(8,128)(2,1)S(1)}, u32[]{:S(2)}, u32[]{:S(2)}) collective-permute-start(bf16[2,64,2048]{2,1,0:T(8,128)(2,1)S(1)} %get-tuple-element.54), channel_id=1, source_target_pairs={{0,2},{1,3},{2,4},{3,5},{4,6},{5,7},{6,0},{7,1},{8,10},{9,11},{10,... | collective-permute-start | bytes 1572872 | tf_op jit(solution)/shard_map/t_o_up/ppermute | solution.py:61
  59.5 13.9 %collective-permute-start.10 = (bf16[2,64,2048]{2,1,0:T(8,128)(2,1)S(1)}, bf16[2,64,2048]{2,1,0:T(8,128)(2,1)S(1)}, u32[]{:S(2)}, u32[]{:S(2)}) collective-permute-start(bf16[2,64,2048]{2,1,0:T(8,128)(2,1)S(1)} %collective-permute-done.9), channel_id=1, source_target_pairs={{0,6},{1,7},{2,0},{3,1},{4,2},{5,3},{6,4},{7,5},{8,14},{9,15},{10,... | collective-permute-start | bytes 1572872 | tf_op jit(solution)/shard_map/t_o_far/ppermute | solution.py:65
  67.4 17.4 %copy-start.2 = (bf16[2,2,64,2048]{3,2,1,0:T(8,128)(2,1)}, bf16[2,2,64,2048]{3,2,1,0:T(8,128)(2,1)S(1)}, u32[]{:S(2)}) copy-start(bf16[2,2,64,2048]{3,2,1,0:T(8,128)(2,1)S(1)} %collective-permute-done.12.refs_8_.refs_12_.refs_0_.refs_4_) | copy-start | bytes 3145732
  67.4 26.2 %collective-permute-start.18 = (bf16[1024,512]{1,0:T(8,128)(2,1)}, bf16[1024,512]{1,0:T(8,128)(2,1)}, u32[]{:S(2)}, u32[]{:S(2)}) collective-permute-start(bf16[1024,512]{1,0:T(8,128)(2,1)} %get-tuple-element.60.refs_16_), channel_id=1, source_target_pairs={{0,16},{8,24},{16,0},{24,8},{32,48},{40,56},{48,32},{56,40},{64,80... | collective-permute-start | bytes 3145736 | tf_op jit(solution)/shard_map/t_out_across/ppermute | solution.py:41
  73.4 2.3 %copy-start.9 = (bf16[2,64,2048]{2,1,0:T(8,128)(2,1)}, bf16[2,64,2048]{2,1,0:T(8,128)(2,1)S(1)}, u32[]{:S(2)}) copy-start(bf16[2,64,2048]{2,1,0:T(8,128)(2,1)S(1)} %collective-permute-done.11) | copy-start | bytes 1572868
  73.4 2.3 %copy-start.10 = (bf16[2,64,2048]{2,1,0:T(8,128)(2,1)}, bf16[2,64,2048]{2,1,0:T(8,128)(2,1)S(1)}, u32[]{:S(2)}) copy-start(bf16[2,64,2048]{2,1,0:T(8,128)(2,1)S(1)} %collective-permute-done.10) | copy-start | bytes 1572868
  73.4 23.7 %collective-permute-start.13 = (bf16[2,2,64,2048]{3,2,1,0:T(8,128)(2,1)S(1)}, bf16[2,2,64,2048]{3,2,1,0:T(8,128)(2,1)S(1)}, u32[]{:S(2)}, u32[]{:S(2)}) collective-permute-start(bf16[2,2,64,2048]{3,2,1,0:T(8,128)(2,1)S(1)} %collective-permute-done.12.refs_8_.refs_12_.refs_0_.refs_4_), channel_id=1, source_target_pairs={{0,6},{1,7},{2,0},{3,1},{4,2},{5,3},{6,4},{7,5},{8,14},{9,15},{10,... | collective-permute-start | bytes 3145736 | tf_op jit(solution)/shard_map/t_f_down/ppermute | solution.py:65
  75.7 24.5 %collective-permute-start.14 = (bf16[2,2,64,2048]{3,2,1,0:T(8,128)(2,1)S(1)}, bf16[2,2,64,2048]{3,2,1,0:T(8,128)(2,1)S(1)}, u32[]{:S(2)}, u32[]{:S(2)}) collective-permute-start(bf16[2,2,64,2048]{3,2,1,0:T(8,128)(2,1)S(1)} %collective-permute-done.12.refs_8_.refs_12_.refs_0_.refs_4_), channel_id=1, source_target_pairs={{0,2},{1,3},{2,4},{3,5},{4,6},{5,7},{6,0},{7,1},{8,10},{9,11},{10,... | collective-permute-start | bytes 3145736 | tf_op jit(solution)/shard_map/t_f_up/ppermute | solution.py:61
  84.8 15.6 %copy-start.15 = (f32[256,1024]{1,0:T(8,128)S(1)}, f32[256,1024]{1,0:T(8,128)}, u32[]{:S(2)}) copy-start(f32[256,1024]{1,0:T(8,128)} %get-tuple-element.66) | copy-start | bytes 3145732
  93.7 6.7 %collective-permute-start.20 = (bf16[256,1024]{1,0:T(8,128)(2,1)}, bf16[256,1024]{1,0:T(8,128)(2,1)S(1)}, u32[]{:S(2)}, u32[]{:S(2)}) collective-permute-start(bf16[256,1024]{1,0:T(8,128)(2,1)} %get-tuple-element.62), channel_id=1, source_target_pairs={{0,8},{8,0},{16,24},{24,16},{32,40},{40,32},{48,56},{56,48},{64,72... | collective-permute-start | bytes 1572872 | tf_op jit(solution)/shard_map/t_sum_same_sibling/ppermute | solution.py:37
  95.1 17.3 %collective-permute-start.17 = (bf16[1024,512]{1,0:T(8,128)(2,1)}, bf16[1024,512]{1,0:T(8,128)(2,1)}, u32[]{:S(2)}, u32[]{:S(2)}) collective-permute-start(bf16[1024,512]{1,0:T(8,128)(2,1)} %get-tuple-element.60.refs_16_), channel_id=1, source_target_pairs={{0,8},{8,0},{16,24},{24,16},{32,40},{40,32},{48,56},{56,48},{64,72... | collective-permute-start | bytes 3145736 | tf_op jit(solution)/shard_map/t_out_near/ppermute | solution.py:37
  95.1 8.0 %collective-permute-start.19 = (bf16[1024,512]{1,0:T(8,128)(2,1)}, bf16[1024,512]{1,0:T(8,128)(2,1)S(1)}, u32[]{:S(2)}, u32[]{:S(2)}) collective-permute-start(bf16[1024,512]{1,0:T(8,128)(2,1)} %collective-permute-done.18.refs_18_), channel_id=1, source_target_pairs={{0,8},{8,0},{16,24},{24,16},{32,40},{40,32},{48,56},{56,48},{64,72... | collective-permute-start | bytes 3145736 | tf_op jit(solution)/shard_map/t_out_other/ppermute | solution.py:37
  97.1 4.4 %copy-start = (bf16[2,2,64,2048]{3,2,1,0:T(8,128)(2,1)}, bf16[2,2,64,2048]{3,2,1,0:T(8,128)(2,1)S(1)}, u32[]{:S(2)}) copy-start(bf16[2,2,64,2048]{3,2,1,0:T(8,128)(2,1)S(1)} %collective-permute-done.13.refs_9_.refs_13_.refs_1_.refs_5_) | copy-start | bytes 3145732
  97.2 11.9 %collective-permute-start.16 = (bf16[2,64,2048]{2,1,0:T(8,128)(2,1)S(1)}, bf16[2,64,2048]{2,1,0:T(8,128)(2,1)S(1)}, u32[]{:S(2)}, u32[]{:S(2)}) collective-permute-start(bf16[2,64,2048]{2,1,0:T(8,128)(2,1)S(1)} %slice_bitcast_fusion), channel_id=1, source_target_pairs={{0,6},{1,7},{2,0},{3,1},{4,2},{5,3},{6,4},{7,5},{8,14},{9,15},{10,... | collective-permute-start | bytes 1572872 | tf_op jit(solution)/shard_map/t_f_far_down/ppermute | solution.py:65
  100.3 12.1 %copy-start.1 = (bf16[2,2,64,2048]{3,2,1,0:T(8,128)(2,1)}, bf16[2,2,64,2048]{3,2,1,0:T(8,128)(2,1)S(1)}, u32[]{:S(2)}) copy-start(bf16[2,2,64,2048]{3,2,1,0:T(8,128)(2,1)S(1)} %collective-permute-done.14.refs_11_.refs_15_.refs_3_.refs_7_) | copy-start | bytes 3145732
  100.3 12.0 %collective-permute-start.15 = (bf16[2,64,2048]{2,1,0:T(8,128)(2,1)S(1)}, bf16[2,64,2048]{2,1,0:T(8,128)(2,1)S(1)}, u32[]{:S(2)}, u32[]{:S(2)}) collective-permute-start(bf16[2,64,2048]{2,1,0:T(8,128)(2,1)S(1)} %slice_bitcast_fusion.3), channel_id=1, source_target_pairs={{0,2},{1,3},{2,4},{3,5},{4,6},{5,7},{6,0},{7,1},{8,10},{9,11},{10,... | collective-permute-start | bytes 1572872 | tf_op jit(solution)/shard_map/t_f_far_up/ppermute | solution.py:61
  101.5 31.7 %collective-permute-start.22 = (bf16[256,1024]{1,0:T(8,128)(2,1)}, bf16[256,1024]{1,0:T(8,128)(2,1)S(1)}, u32[]{:S(2)}, u32[]{:S(2)}) collective-permute-start(bf16[256,1024]{1,0:T(8,128)(2,1)} %add_convert_fusion.1), channel_id=1, source_target_pairs={{0,16},{8,24},{16,0},{24,8},{32,48},{40,56},{48,32},{56,40},{64,80... | collective-permute-start | bytes 1572872 | tf_op jit(solution)/shard_map/t_sum_same_across/ppermute | solution.py:41
  103.1 9.2 %copy-start.14 = (bf16[1024,512]{1,0:T(8,128)(2,1)}, bf16[1024,512]{1,0:T(8,128)(2,1)S(1)}, u32[]{:S(2)}) copy-start(bf16[1024,512]{1,0:T(8,128)(2,1)S(1)} %collective-permute-done.19.refs_19_) | copy-start | bytes 3145732
  109.1 3.3 %copy-start.11 = (bf16[2,64,2048]{2,1,0:T(8,128)(2,1)}, bf16[2,64,2048]{2,1,0:T(8,128)(2,1)S(1)}, u32[]{:S(2)}) copy-start(bf16[2,64,2048]{2,1,0:T(8,128)(2,1)S(1)} %collective-permute-done.16) | copy-start | bytes 1572868
  112.4 0.8 copy-start.12
  113.2 16.3 %copy-start.22 = (bf16[256,1024]{1,0:T(8,128)(2,1)S(1)}, bf16[256,1024]{1,0:T(8,128)(2,1)}, u32[]{:S(2)}) copy-start(bf16[256,1024]{1,0:T(8,128)(2,1)} %get-tuple-element.65) | copy-start | bytes 1572868
  129.5 7.2 %collective-permute-start.21 = (bf16[256,1024]{1,0:T(8,128)(2,1)S(1)}, bf16[256,1024]{1,0:T(8,128)(2,1)}, u32[]{:S(2)}, u32[]{:S(2)}) collective-permute-start(bf16[256,1024]{1,0:T(8,128)(2,1)S(1)} %copy-done.22), channel_id=1, source_target_pairs={{0,8},{8,0},{16,24},{24,16},{32,40},{40,32},{48,56},{56,48},{64,72... | collective-permute-start | bytes 1572872 | tf_op jit(solution)/shard_map/t_same_near/ppermute | solution.py:37
  133.2 12.4 %copy-start.16 = (bf16[256,1024]{1,0:T(8,128)(2,1)}, bf16[256,1024]{1,0:T(8,128)(2,1)S(1)}, u32[]{:S(2)}) copy-start(bf16[256,1024]{1,0:T(8,128)(2,1)S(1)} %collective-permute-done.22.rest_2_) | copy-start | bytes 1572868
  133.2 26.3 %collective-permute-start.27 = (bf16[2,512,512]{2,1,0:T(8,128)(2,1)}, bf16[2,512,512]{2,1,0:T(8,128)(2,1)S(1)}, u32[]{:S(2)}, u32[]{:S(2)}) collective-permute-start(bf16[2,512,512]{2,1,0:T(8,128)(2,1)} %get-tuple-element.79), channel_id=1, source_target_pairs={{0,96},{8,104},{16,112},{24,120},{32,0},{40,8},{48,16},{56,24},{64... | collective-permute-start | bytes 3145736 | tf_op jit(solution)/shard_map/t_wg_down/ppermute | solution.py:57
  136.7 25.8 %collective-permute-start.26 = (bf16[2,512,512]{2,1,0:T(8,128)(2,1)}, bf16[2,512,512]{2,1,0:T(8,128)(2,1)S(1)}, u32[]{:S(2)}, u32[]{:S(2)}) collective-permute-start(bf16[2,512,512]{2,1,0:T(8,128)(2,1)} %get-tuple-element.77), channel_id=1, source_target_pairs={{0,32},{8,40},{16,48},{24,56},{32,64},{40,72},{48,80},{56,88},{64,... | collective-permute-start | bytes 3145736 | tf_op jit(solution)/shard_map/t_wg_up/ppermute | solution.py:53
  145.6 16.9 %copy-start.18 = (bf16[512,512]{1,0:T(8,128)(2,1)S(1)}, bf16[512,512]{1,0:T(8,128)(2,1)}, u32[]{:S(2)}) copy-start(bf16[512,512]{1,0:T(8,128)(2,1)} %get-tuple-element.75) | copy-start | bytes 1572868
  145.6 17.8 %copy-start.17 = (bf16[512,512]{1,0:T(8,128)(2,1)S(1)}, bf16[512,512]{1,0:T(8,128)(2,1)}, u32[]{:S(2)}) copy-start(bf16[512,512]{1,0:T(8,128)(2,1)} %get-tuple-element.83) | copy-start | bytes 1572868
  145.6 2.2 %collective-permute-start.24 = (bf16[256,1024]{1,0:T(8,128)(2,1)}, bf16[256,1024]{1,0:T(8,128)(2,1)S(1)}, u32[]{:S(2)}, u32[]{:S(2)}) collective-permute-start(bf16[256,1024]{1,0:T(8,128)(2,1)} %get-tuple-element.71), channel_id=1, source_target_pairs={{0,8},{8,0},{16,24},{24,16},{32,40},{40,32},{48,56},{56,48},{64,72... | collective-permute-start | bytes 1572872 | tf_op jit(solution)/shard_map/t_sum_flip_sibling/ppermute | solution.py:37
  146.1 21.0 %collective-permute-start.23 = (bf16[256,1024]{1,0:T(8,128)(2,1)}, bf16[256,1024]{1,0:T(8,128)(2,1)S(1)}, u32[]{:S(2)}, u32[]{:S(2)}) collective-permute-start(bf16[256,1024]{1,0:T(8,128)(2,1)} %get-tuple-element.69), channel_id=1, source_target_pairs={{0,8},{8,0},{16,24},{24,16},{32,40},{40,32},{48,56},{56,48},{64,72... | collective-permute-start | bytes 1572872 | tf_op jit(solution)/shard_map/t_flip_near/ppermute | solution.py:37
  149.2 17.9 %collective-permute-start.25 = (bf16[256,1024]{1,0:T(8,128)(2,1)S(1)}, bf16[256,1024]{1,0:T(8,128)(2,1)S(1)}, u32[]{:S(2)}, u32[]{:S(2)}) collective-permute-start(bf16[256,1024]{1,0:T(8,128)(2,1)S(1)} %add_convert_fusion), channel_id=1, source_target_pairs={{0,16},{8,24},{16,0},{24,8},{32,48},{40,56},{48,32},{56,40},{64,80... | collective-permute-start | bytes 1572872 | tf_op jit(solution)/shard_map/t_sum_flip_across/ppermute | solution.py:41
  163.4 14.1 %collective-permute-start.28 = (bf16[512,512]{1,0:T(8,128)(2,1)}, bf16[512,512]{1,0:T(8,128)(2,1)}, u32[]{:S(2)}, u32[]{:S(2)}) collective-permute-start(bf16[512,512]{1,0:T(8,128)(2,1)} %fusion.1), channel_id=1, source_target_pairs={{0,32},{8,40},{16,48},{24,56},{32,64},{40,72},{48,80},{56,88},{64,... | collective-permute-start | bytes 1572872 | tf_op jit(solution)/shard_map/t_wg_ahead/ppermute | solution.py:53
  164.3 13.1 %collective-permute-start.29 = (bf16[512,512]{1,0:T(8,128)(2,1)}, bf16[512,512]{1,0:T(8,128)(2,1)}, u32[]{:S(2)}, u32[]{:S(2)}) collective-permute-start(bf16[512,512]{1,0:T(8,128)(2,1)} %fusion), channel_id=1, source_target_pairs={{0,96},{8,104},{16,112},{24,120},{32,0},{40,8},{48,16},{56,24},{64... | collective-permute-start | bytes 1572872 | tf_op jit(solution)/shard_map/t_wg_behind/ppermute | solution.py:57
  167.1 1.0 copy-start.19
  167.1 0.9 copy-start.20
  168.1 9.4 %copy-start.13 = (bf16[1024,512]{1,0:T(8,128)(2,1)S(1)}, bf16[1024,512]{1,0:T(8,128)(2,1)}, u32[]{:S(2)}) copy-start(bf16[1024,512]{1,0:T(8,128)(2,1)} %get-tuple-element.64) | copy-start | bytes 3145732
Sparse Core Ops, SparseCore 0:
  9.7 51.6 all-gather.1
